TPU v7x, 512 devices: a whole 4x8x8 slice. The times are simulated.
512 devices in a mesh: patch: 32 (over x, y_hi, core), section: 8 (over z), cfg: 2 (over y_lo).
Axes of the slice: x: 4, y: 8 (y_hi: 4, y_lo: 2; y = y_hi * 2 + y_lo), z: 8, core: 2. Of those that a mesh axis runs over, the one named last changes fastest.
Arguments:
- hidden: bfloat16 [2, 512, 1536], P('cfg', 'patch'), may hold values from -6 to 6
- timestep: int32 [1], replicated, may hold values from 0 to 27
- patch_order: int32 [64], replicated, may hold values from 0 to 63, each once
- modulation: float32 [8, 2, 28, 4608], P('section', 'cfg'), may hold values from -4 to 4
- qkv_weight: bfloat16 [8, 1536, 4608], P('section', None, 'patch'), may hold values from -0.15625 to 0.15625
- stale_kv: bfloat16 [8, 2, 512, 3072], P('section', 'cfg', 'patch'), may hold values from -6 to 6
Outputs:
- guided: bfloat16 [512, 1536], P(('patch', 'section'), 'cfg')
- fresh_kv: bfloat16 [8, 2, 512, 3072], P('section', 'cfg', 'patch')
Inputs may be any that keep to these rules, and one draw needn't show every extreme that they name: `patch_order`: each patch appears once.
All inputs are finite; a program needn't handle non-finite values.
Results may differ from a plain program's by a relative error of at most 0.023.
Values may be sent and summed in bfloat16 or wider, within the bound.
No kernel may reach another device: no remote copies, remote signals or barrier semaphores. Data moves between devices by JAX's collectives and lax.ppermute only.
A program may use at most 64 MiB of HBM per device.

v0:
```python
import math

import jax
import jax.numpy as jnp
from jax import lax
from jax.sharding import PartitionSpec as P

HEADS = 12
HDIM = 128
ROWS = 8


guide_weight = 3.5
norm_eps = 1e-06


def passed_along(block, axis, distance):
    devices = range(lax.axis_size(axis))
    route = [(i - distance, i) for i in devices if i - distance in devices]
    return lax.ppermute(block, axis, route)


def head_norm(values):
    shaped = values.astype(jnp.float32).reshape(values.shape[0], HEADS, HDIM)
    return shaped * lax.rsqrt(jnp.mean(shaped * shaped, axis=-1, keepdims=True) + norm_eps)


def rotate(shaped, positions):
    halfway = HDIM // 2
    inverse = jnp.exp(-math.log(10000.0) * jnp.arange(halfway, dtype=jnp.float32) / halfway)
    angles = positions.astype(jnp.float32)[:, None] * inverse[None, :]
    cosine = jnp.cos(angles)[:, None, :]
    sine_part = jnp.sin(angles)[:, None, :]
    first_half = shaped[..., :halfway]
    second = shaped[..., halfway:]
    return jnp.concatenate(
        [first_half * cosine - second * sine_part, first_half * sine_part + second * cosine],
        axis=-1,
    )


def body(hidden, timestep, patch_order, modulation, qkv_weight, stale_kv):
    n_sections = lax.axis_size("section")
    section_id = lax.axis_index("section")
    patch_id = lax.axis_index("patch")
    local_rows = hidden.shape[1]
    feat_width = hidden.shape[2]
    table_row = lax.dynamic_index_in_dim(modulation[0, 0], timestep[0], 0, keepdims=False)
    shifts = table_row[:feat_width]
    scales = table_row[feat_width : 2 * feat_width]
    gate_vector = table_row[2 * feat_width :]
    weight = qkv_weight[0]
    stale_rows = stale_kv[0, 0]
    scale_factor = 1.0 / math.sqrt(HDIM)
    gathered = lax.all_gather(stale_rows, "patch", axis=0, tiled=True)
    total_keys = gathered.shape[0]
    stale_keys = gathered[:, :feat_width].reshape(total_keys, HEADS, HDIM)
    stale_values = gathered[:, feat_width:].reshape(total_keys, HEADS, HDIM)
    key_blocks = jnp.arange(total_keys, dtype=jnp.int32) // ROWS
    group = 1
    group_rows = group * ROWS
    groups = local_rows // group_rows
    ticks = n_sections + groups - 1
    blocks_here = local_rows // ROWS
    is_last = section_id == n_sections - 1
    incoming = jnp.zeros((group_rows, feat_width), jnp.bfloat16)
    finals = jnp.zeros((local_rows, feat_width), jnp.bfloat16)
    fresh_all = jnp.zeros((local_rows, 2 * feat_width), jnp.bfloat16)
    for tick in range(ticks):
        micro = tick - section_id
        active = (micro >= 0) & (micro < groups)
        clipped = jnp.clip(micro, 0, groups - 1)
        start = clipped * group_rows
        entering = lax.dynamic_slice_in_dim(hidden[0], start, group_rows, 0)
        source = jnp.where(section_id == 0, entering, incoming)
        first_block = patch_id * blocks_here + clipped * group
        row_index = jnp.arange(group_rows, dtype=jnp.int32)
        row_blocks = first_block + row_index // ROWS
        positions = patch_order[row_blocks] * ROWS + row_index % ROWS
        values32 = source.astype(jnp.float32)
        center = jnp.mean(values32, axis=-1, keepdims=True)
        spread = jnp.mean((values32 - center) ** 2, axis=-1, keepdims=True)
        normed = (
            (values32 - center) * lax.rsqrt(spread + norm_eps) * (1.0 + scales) + shifts
        ).astype(jnp.bfloat16)
        column_part = jnp.dot(
            lax.all_gather(normed, "patch", axis=0, tiled=True),
            weight,
            preferred_element_type=jnp.float32,
        ).astype(jnp.bfloat16)
        projected = lax.all_to_all(column_part, "patch", split_axis=0, concat_axis=1, tiled=True)
        queries = rotate(head_norm(projected[:, :feat_width]), positions).astype(jnp.bfloat16)
        fresh_keys = rotate(head_norm(projected[:, feat_width : 2 * feat_width]), positions).astype(
            jnp.bfloat16
        )
        fresh_values = projected[:, 2 * feat_width :]
        scores = (
            jnp.einsum("rhd,thd->hrt", queries, stale_keys, preferred_element_type=jnp.float32)
            * scale_factor
        )
        outside = key_blocks[None, :] == row_blocks[:, None]
        weights = jnp.where(outside[None, :, :], 0.0, jnp.exp(scores))
        numerator = jnp.einsum(
            "hrt,thd->rhd",
            weights.astype(jnp.bfloat16),
            stale_values,
            preferred_element_type=jnp.float32,
        )
        denominator = jnp.sum(weights, axis=-1)
        own_scores = (
            jnp.einsum("rhd,thd->hrt", queries, fresh_keys, preferred_element_type=jnp.float32)
            * scale_factor
        )
        same_block = row_blocks[:, None] == row_blocks[None, :]
        own_weights = jnp.where(same_block[None, :, :], jnp.exp(own_scores), 0.0)
        numerator = numerator + jnp.einsum(
            "hrt,thd->rhd",
            own_weights.astype(jnp.bfloat16),
            fresh_values.reshape(group_rows, HEADS, HDIM),
            preferred_element_type=jnp.float32,
        )
        denominator = denominator + jnp.sum(own_weights, axis=-1)
        attended = (numerator / jnp.transpose(denominator)[:, :, None]).reshape(
            group_rows, feat_width
        )
        new_states = (values32 + gate_vector * attended).astype(jnp.bfloat16)
        fresh = jnp.concatenate([fresh_keys.reshape(group_rows, feat_width), fresh_values], axis=1)
        outgoing, fresh = (new_states, fresh)
        fresh_all = jnp.where(
            active, lax.dynamic_update_slice_in_dim(fresh_all, fresh, start, 0), fresh_all
        )
        finals = jnp.where(
            active & is_last, lax.dynamic_update_slice_in_dim(finals, outgoing, start, 0), finals
        )
        if tick + 1 < ticks:
            incoming = passed_along(outgoing, "section", 1)
    slice_rows = local_rows // n_sections
    masked = jnp.where(is_last, finals.astype(jnp.float32), 0.0)
    my_rows = lax.psum_scatter(
        masked.astype(jnp.bfloat16), "section", scatter_dimension=0, tiled=True
    )
    both_halves = lax.all_to_all(my_rows, "cfg", split_axis=1, concat_axis=0, tiled=True).astype(
        jnp.float32
    )
    uncond = both_halves[:slice_rows]
    conditioned = both_halves[slice_rows:]
    guided = (uncond + guide_weight * (conditioned - uncond)).astype(jnp.bfloat16)
    return (guided, fresh_all[None, None])


def solution(mesh):
    placed = (
        P("cfg", "patch", None),
        P(),
        P(),
        P("section", "cfg", None, None),
        P("section", None, "patch"),
        P("section", "cfg", "patch", None),
    )
    return jax.shard_map(
        body,
        mesh=mesh,
        in_specs=placed,
        out_specs=(P(("patch", "section"), "cfg"), P("section", "cfg", "patch", None)),
        check_vma=False,
    )
```

profile of v0, /device:TPU:1, one launch (start us, length us, event | category | flops | bytes accessed | tf_op | source)
XLA Modules:
  0.0 685.9 jit_solution(7431425884993635439)
XLA Ops:
  12.0 50.3 %all_gather.30 = bf16[256,1536]{1,0:T(8,128)(2,1)S(1)} all-gather(bf16[8,1536]{1,0:T(8,128)(2,1)S(1)} %fusion.146), channel_id=1, replica_groups=mesh['patch'=32,'section'=8,'cfg'=2] {'patch'}, dimensions={0}, use_global_device_ids=true | all-gather | bytes 811008 | tf_op jit(solution)/shard_map/all_gather | solution.py:87
  63.5 3.7 all-to-all-start
  76.5 4.5 all-to-all-done
  82.5 4.7 copy.279
  90.6 3.7 collective-permute-start
  95.6 45.3 %all_gather.32 = bf16[256,1536]{1,0:T(8,128)(2,1)S(1)} all-gather(bf16[8,1536]{1,0:T(8,128)(2,1)S(1)} %fusion.142), channel_id=1, replica_groups=mesh['patch'=32,'section'=8,'cfg'=2] {'patch'}, dimensions={0}, use_global_device_ids=true | all-gather | bytes 811008 | tf_op jit(solution)/shard_map/all_gather | solution.py:87
  145.8 11.4 %all-to-all-done.1 = bf16[32,8,144]{2,1,0:T(8,128)(2,1)S(1)} async-done(((bf16[32,8,144]{2,1,0:T(8,128)(2,1)}), bf16[32,8,144]{2,1,0:T(8,128)(2,1)S(1)}, u32[]{:S(2)}, u32[]{:S(2)}) %all-to-all-start.1) | async-done | bytes 73760 | tf_op jit(solution)/shard_map/all_to_all | solution.py:91
  161.0 4.2 collective-permute-start.1
  166.6 43.3 %all_gather.33 = bf16[256,1536]{1,0:T(8,128)(2,1)S(1)} all-gather(bf16[8,1536]{1,0:T(8,128)(2,1)S(1)} %fusion.138), channel_id=1, replica_groups=mesh['patch'=32,'section'=8,'cfg'=2] {'patch'}, dimensions={0}, use_global_device_ids=true | all-gather | bytes 811008 | tf_op jit(solution)/shard_map/all_gather | solution.py:87
  214.8 11.1 %all-to-all-done.2 = bf16[32,8,144]{2,1,0:T(8,128)(2,1)S(1)} async-done(((bf16[32,8,144]{2,1,0:T(8,128)(2,1)}), bf16[32,8,144]{2,1,0:T(8,128)(2,1)S(1)}, u32[]{:S(2)}, u32[]{:S(2)}) %all-to-all-start.2) | async-done | bytes 73760 | tf_op jit(solution)/shard_map/all_to_all | solution.py:91
  229.7 4.4 collective-permute-start.2
  235.5 43.8 %all_gather.34 = bf16[256,1536]{1,0:T(8,128)(2,1)S(1)} all-gather(bf16[8,1536]{1,0:T(8,128)(2,1)S(1)} %fusion.134), channel_id=1, replica_groups=mesh['patch'=32,'section'=8,'cfg'=2] {'patch'}, dimensions={0}, use_global_device_ids=true | all-gather | bytes 811008 | tf_op jit(solution)/shard_map/all_gather | solution.py:87
  284.1 10.7 %all-to-all-done.3 = bf16[32,8,144]{2,1,0:T(8,128)(2,1)S(1)} async-done(((bf16[32,8,144]{2,1,0:T(8,128)(2,1)}), bf16[32,8,144]{2,1,0:T(8,128)(2,1)S(1)}, u32[]{:S(2)}, u32[]{:S(2)}) %all-to-all-start.3) | async-done | bytes 73760 | tf_op jit(solution)/shard_map/all_to_all | solution.py:91
  298.7 3.9 collective-permute-start.3
  304.0 43.9 %all_gather.35 = bf16[256,1536]{1,0:T(8,128)(2,1)S(1)} all-gather(bf16[8,1536]{1,0:T(8,128)(2,1)S(1)} %fusion.130), channel_id=1, replica_groups=mesh['patch'=32,'section'=8,'cfg'=2] {'patch'}, dimensions={0}, use_global_device_ids=true | all-gather | bytes 811008 | tf_op jit(solution)/shard_map/all_gather | solution.py:87
  349.0 3.8 all-to-all-start.4
  352.9 10.8 %all-to-all-done.4 = bf16[32,8,144]{2,1,0:T(8,128)(2,1)S(1)} async-done(((bf16[32,8,144]{2,1,0:T(8,128)(2,1)}), bf16[32,8,144]{2,1,0:T(8,128)(2,1)S(1)}, u32[]{:S(2)}, u32[]{:S(2)}) %all-to-all-start.4) | async-done | bytes 73760 | tf_op jit(solution)/shard_map/all_to_all | solution.py:91
  367.5 3.8 collective-permute-start.4
  372.6 43.5 %all_gather.36 = bf16[256,1536]{1,0:T(8,128)(2,1)S(1)} all-gather(bf16[8,1536]{1,0:T(8,128)(2,1)S(1)} %fusion.126), channel_id=1, replica_groups=mesh['patch'=32,'section'=8,'cfg'=2] {'patch'}, dimensions={0}, use_global_device_ids=true | all-gather | bytes 811008 | tf_op jit(solution)/shard_map/all_gather | solution.py:87
  417.3 3.7 all-to-all-start.5
  421.0 10.7 %all-to-all-done.5 = bf16[32,8,144]{2,1,0:T(8,128)(2,1)S(1)} async-done(((bf16[32,8,144]{2,1,0:T(8,128)(2,1)}), bf16[32,8,144]{2,1,0:T(8,128)(2,1)S(1)}, u32[]{:S(2)}, u32[]{:S(2)}) %all-to-all-start.5) | async-done | bytes 73760 | tf_op jit(solution)/shard_map/all_to_all | solution.py:91
  435.5 5.2 collective-permute-start.5
  442.2 43.3 %all_gather.37 = bf16[256,1536]{1,0:T(8,128)(2,1)S(1)} all-gather(bf16[8,1536]{1,0:T(8,128)(2,1)S(1)} %fusion.122), channel_id=1, replica_groups=mesh['patch'=32,'section'=8,'cfg'=2] {'patch'}, dimensions={0}, use_global_device_ids=true | all-gather | bytes 811008 | tf_op jit(solution)/shard_map/all_gather | solution.py:87
  486.6 3.7 all-to-all-start.6
  490.3 10.7 %all-to-all-done.6 = bf16[32,8,144]{2,1,0:T(8,128)(2,1)S(1)} async-done(((bf16[32,8,144]{2,1,0:T(8,128)(2,1)}), bf16[32,8,144]{2,1,0:T(8,128)(2,1)S(1)}, u32[]{:S(2)}, u32[]{:S(2)}) %all-to-all-start.6) | async-done | bytes 73760 | tf_op jit(solution)/shard_map/all_to_all | solution.py:91
  504.9 5.1 collective-permute-start.6
  511.4 43.3 %all_gather.38 = bf16[256,1536]{1,0:T(8,128)(2,1)S(1)} all-gather(bf16[8,1536]{1,0:T(8,128)(2,1)S(1)} %fusion.118), channel_id=1, replica_groups=mesh['patch'=32,'section'=8,'cfg'=2] {'patch'}, dimensions={0}, use_global_device_ids=true | all-gather | bytes 811008 | tf_op jit(solution)/shard_map/all_gather | solution.py:87
  559.6 10.7 %all-to-all-done.7 = bf16[32,8,144]{2,1,0:T(8,128)(2,1)S(1)} async-done(((bf16[32,8,144]{2,1,0:T(8,128)(2,1)}), bf16[32,8,144]{2,1,0:T(8,128)(2,1)S(1)}, u32[]{:S(2)}, u32[]{:S(2)}) %all-to-all-start.7) | async-done | bytes 73760 | tf_op jit(solution)/shard_map/all_to_all | solution.py:91
  574.2 5.0 collective-permute-start.7
  580.6 43.4 %all_gather.39 = bf16[256,1536]{1,0:T(8,128)(2,1)S(1)} all-gather(bf16[8,1536]{1,0:T(8,128)(2,1)S(1)} %fusion.114), channel_id=1, replica_groups=mesh['patch'=32,'section'=8,'cfg'=2] {'patch'}, dimensions={0}, use_global_device_ids=true | all-gather | bytes 811008 | tf_op jit(solution)/shard_map/all_gather | solution.py:87
  628.9 10.7 %all-to-all-done.8 = bf16[32,8,144]{2,1,0:T(8,128)(2,1)S(1)} async-done(((bf16[32,8,144]{2,1,0:T(8,128)(2,1)}), bf16[32,8,144]{2,1,0:T(8,128)(2,1)S(1)}, u32[]{:S(2)}, u32[]{:S(2)}) %all-to-all-start.8) | async-done | bytes 73760 | tf_op jit(solution)/shard_map/all_to_all | solution.py:91
  643.5 28.5 %all-reduce = bf16[16,1536]{1,0:T(8,128)(2,1)S(1)} all-reduce(bf16[16,1536]{1,0:T(8,128)(2,1)S(1)} %select_convert_fusion), channel_id=3, replica_groups=mesh['patch'=32,'section'=8,'cfg'=2] {'section'}, use_global_device_ids=true, to_apply=%region_54.55.clone | all-reduce | flops 24576 | bytes 98304
  (354 shorter events, 93.9 us)
Async XLA Ops:
  7.2 55.1 %copy-start = (bf16[1,1536,144]{1,2,0:T(8,128)(2,1)S(1)}, bf16[1,1536,144]{1,2,0:T(8,128)(2,1)}, u32[]{:S(2)}) copy-start(bf16[1,1536,144]{1,2,0:T(8,128)(2,1)} %param.10) | copy-start | bytes 1327108
  7.2 60.4 %copy-start.1 = (s32[64]{0:T(128)S(1)}, s32[64]{0:T(128)}, u32[]{:S(2)}) copy-start(s32[64]{0:T(128)} %param.8) | copy-start | bytes 772
  7.2 75.3 %all-gather.3.cloned.1.call-start = ((), (), s32[]{:S(2)}) async-start(), calls=%async_computation.10 | async-start | bytes 3244032 | tf_op jit(solution)/shard_map/all_gather | solution.py:55
  63.5 17.6 %all-to-all-start = ((bf16[32,8,144]{2,1,0:T(8,128)(2,1)}), bf16[32,8,144]{2,1,0:T(8,128)(2,1)S(1)}, u32[]{:S(2)}, u32[]{:S(2)}) async-start(bf16[32,8,144]{2,1,0:T(8,128)(2,1)} %bitcast.3), calls=%async_computation | async-start | bytes 262144 | tf_op jit(solution)/shard_map/all_to_all | solution.py:91
  81.2 13.1 %copy-start.4 = (bf16[8,4608]{1,0:T(8,128)(2,1)}, bf16[8,4608]{1,0:T(8,128)(2,1)S(1)}, u32[]{:S(2)}) copy-start(bf16[8,4608]{1,0:T(8,128)(2,1)S(1)} %all_to_all.139) | copy-start | bytes 221188
  90.6 4.6 collective-permute-start
  94.4 51.4 %slice-start = ((bf16[8,4608]{1,0:T(8,128)(2,1)}), bf16[8,1536]{1,0:T(8,128)(2,1)S(1)}, s32[]{:S(2)}) async-start(bf16[8,4608]{1,0:T(8,128)(2,1)} %copy-done.4), calls=%async_computation.11 | async-start | bytes 49152 | tf_op jit(solution)/shard_map/slice | solution.py:96
  142.1 15.1 %all-to-all-start.1 = ((bf16[32,8,144]{2,1,0:T(8,128)(2,1)}), bf16[32,8,144]{2,1,0:T(8,128)(2,1)S(1)}, u32[]{:S(2)}, u32[]{:S(2)}) async-start(bf16[32,8,144]{2,1,0:T(8,128)(2,1)} %bitcast.19), calls=%async_computation.1 | async-start | bytes 262144 | tf_op jit(solution)/shard_map/all_to_all | solution.py:91
  161.0 5.1 collective-permute-start.1
  165.3 49.4 %slice-start.1 = ((bf16[8,4608]{1,0:T(8,128)(2,1)}), bf16[8,1536]{1,0:T(8,128)(2,1)S(1)}, s32[]{:S(2)}) async-start(bf16[8,4608]{1,0:T(8,128)(2,1)} %copy-done.5), calls=%async_computation.12 | async-start | bytes 49152 | tf_op jit(solution)/shard_map/slice | solution.py:96
  211.1 14.8 %all-to-all-start.2 = ((bf16[32,8,144]{2,1,0:T(8,128)(2,1)}), bf16[32,8,144]{2,1,0:T(8,128)(2,1)S(1)}, u32[]{:S(2)}, u32[]{:S(2)}) async-start(bf16[32,8,144]{2,1,0:T(8,128)(2,1)} %bitcast.32), calls=%async_computation.2 | async-start | bytes 262144 | tf_op jit(solution)/shard_map/all_to_all | solution.py:91
  229.7 5.3 collective-permute-start.2
  234.2 49.9 %slice-start.2 = ((bf16[8,4608]{1,0:T(8,128)(2,1)}), bf16[8,1536]{1,0:T(8,128)(2,1)S(1)}, s32[]{:S(2)}) async-start(bf16[8,4608]{1,0:T(8,128)(2,1)} %copy-done.6), calls=%async_computation.13 | async-start | bytes 49152 | tf_op jit(solution)/shard_map/slice | solution.py:96
  280.4 14.4 %all-to-all-start.3 = ((bf16[32,8,144]{2,1,0:T(8,128)(2,1)}), bf16[32,8,144]{2,1,0:T(8,128)(2,1)S(1)}, u32[]{:S(2)}, u32[]{:S(2)}) async-start(bf16[32,8,144]{2,1,0:T(8,128)(2,1)} %bitcast.45), calls=%async_computation.3 | async-start | bytes 262144 | tf_op jit(solution)/shard_map/all_to_all | solution.py:91
  298.7 4.9 collective-permute-start.3
  302.7 50.2 %slice-start.3 = ((bf16[8,4608]{1,0:T(8,128)(2,1)}), bf16[8,1536]{1,0:T(8,128)(2,1)S(1)}, s32[]{:S(2)}) async-start(bf16[8,4608]{1,0:T(8,128)(2,1)} %copy-done.7), calls=%async_computation.14 | async-start | bytes 49152 | tf_op jit(solution)/shard_map/slice | solution.py:96
  349.0 14.7 %all-to-all-start.4 = ((bf16[32,8,144]{2,1,0:T(8,128)(2,1)}), bf16[32,8,144]{2,1,0:T(8,128)(2,1)S(1)}, u32[]{:S(2)}, u32[]{:S(2)}) async-start(bf16[32,8,144]{2,1,0:T(8,128)(2,1)} %bitcast.58), calls=%async_computation.4 | async-start | bytes 262144 | tf_op jit(solution)/shard_map/all_to_all | solution.py:91
  367.5 4.7 collective-permute-start.4
  371.4 49.6 %slice-start.4 = ((bf16[8,4608]{1,0:T(8,128)(2,1)}), bf16[8,1536]{1,0:T(8,128)(2,1)S(1)}, s32[]{:S(2)}) async-start(bf16[8,4608]{1,0:T(8,128)(2,1)} %copy-done.8), calls=%async_computation.15 | async-start | bytes 49152 | tf_op jit(solution)/shard_map/slice | solution.py:96
  417.3 14.4 %all-to-all-start.5 = ((bf16[32,8,144]{2,1,0:T(8,128)(2,1)}), bf16[32,8,144]{2,1,0:T(8,128)(2,1)S(1)}, u32[]{:S(2)}, u32[]{:S(2)}) async-start(bf16[32,8,144]{2,1,0:T(8,128)(2,1)} %bitcast.71), calls=%async_computation.5 | async-start | bytes 262144 | tf_op jit(solution)/shard_map/all_to_all | solution.py:91
  431.9 9.0 %copy-start.9 = (bf16[8,4608]{1,0:T(8,128)(2,1)}, bf16[8,4608]{1,0:T(8,128)(2,1)S(1)}, u32[]{:S(2)}) copy-start(bf16[8,4608]{1,0:T(8,128)(2,1)S(1)} %all_to_all.159) | copy-start | bytes 221188
  435.5 6.2 collective-permute-start.5
  440.9 49.4 %slice-start.5 = ((bf16[8,4608]{1,0:T(8,128)(2,1)}), bf16[8,1536]{1,0:T(8,128)(2,1)S(1)}, s32[]{:S(2)}) async-start(bf16[8,4608]{1,0:T(8,128)(2,1)} %copy-done.9), calls=%async_computation.16 | async-start | bytes 49152 | tf_op jit(solution)/shard_map/slice | solution.py:96
  486.6 14.4 %all-to-all-start.6 = ((bf16[32,8,144]{2,1,0:T(8,128)(2,1)}), bf16[32,8,144]{2,1,0:T(8,128)(2,1)S(1)}, u32[]{:S(2)}, u32[]{:S(2)}) async-start(bf16[32,8,144]{2,1,0:T(8,128)(2,1)} %bitcast.84), calls=%async_computation.6 | async-start | bytes 262144 | tf_op jit(solution)/shard_map/all_to_all | solution.py:91
  501.3 8.9 %copy-start.10 = (bf16[8,4608]{1,0:T(8,128)(2,1)}, bf16[8,4608]{1,0:T(8,128)(2,1)S(1)}, u32[]{:S(2)}) copy-start(bf16[8,4608]{1,0:T(8,128)(2,1)S(1)} %all_to_all.163) | copy-start | bytes 221188
  504.9 6.1 collective-permute-start.6
  510.1 49.4 %slice-start.6 = ((bf16[8,4608]{1,0:T(8,128)(2,1)}), bf16[8,1536]{1,0:T(8,128)(2,1)S(1)}, s32[]{:S(2)}) async-start(bf16[8,4608]{1,0:T(8,128)(2,1)} %copy-done.10), calls=%async_computation.17 | async-start | bytes 49152 | tf_op jit(solution)/shard_map/slice | solution.py:96
  555.9 14.4 %all-to-all-start.7 = ((bf16[32,8,144]{2,1,0:T(8,128)(2,1)}), bf16[32,8,144]{2,1,0:T(8,128)(2,1)S(1)}, u32[]{:S(2)}, u32[]{:S(2)}) async-start(bf16[32,8,144]{2,1,0:T(8,128)(2,1)} %bitcast.97), calls=%async_computation.7 | async-start | bytes 262144 | tf_op jit(solution)/shard_map/all_to_all | solution.py:91
  574.2 5.9 collective-permute-start.7
  579.3 49.5 %slice-start.7 = ((bf16[8,4608]{1,0:T(8,128)(2,1)}), bf16[8,1536]{1,0:T(8,128)(2,1)S(1)}, s32[]{:S(2)}) async-start(bf16[8,4608]{1,0:T(8,128)(2,1)} %copy-done.11), calls=%async_computation.18 | async-start | bytes 49152 | tf_op jit(solution)/shard_map/slice | solution.py:96
  625.1 14.4 %all-to-all-start.8 = ((bf16[32,8,144]{2,1,0:T(8,128)(2,1)}), bf16[32,8,144]{2,1,0:T(8,128)(2,1)S(1)}, u32[]{:S(2)}, u32[]{:S(2)}) async-start(bf16[32,8,144]{2,1,0:T(8,128)(2,1)} %bitcast.110), calls=%async_computation.8 | async-start | bytes 262144 | tf_op jit(solution)/shard_map/all_to_all | solution.py:91
  672.6 5.9 all-to-all-start.9
  (8 other events, 45.3 us)
Sparse Core Ops, SparseCore 0:
  11.2 71.2 all-gather.2
where the time goes:
time: 694 us; the launch traced here: 686 us
  blocking collectives  429 us (62%)
  waiting for transfers between devices  101 us (15%)
  starting transfers between devices  71.8 us (10%)
  local copies, waits for them, and re-layouts  26.7 us (4%)
  matrix products  26.7 us (4%)
  between operations  17.1 us (2%)
  other arithmetic  13.7 us (2%)
    all_gather x9, blocking collectives, body(): lax.all_gather(normed, 'patch', axis=0, tiled=True)  400 us
    all_to_all x9, waiting for transfers between devices, body(): lax.all_to_all(column_part, 'patch', split_axis=0, concat_axis=1, tiled=T...  91.4 us
    ppermute x8, starting transfers between devices, passed_along(): return lax.ppermute(block, axis, route)  35.4 us
    all_to_all x9, starting transfers between devices, body(): lax.all_to_all(column_part, 'patch', split_axis=0, concat_axis=1, tiled=T...  33.1 us
    unnamed x1, blocking collectives  28.5 us
    dot_general x9, matrix products, body(): jnp.einsum('rhd,thd->hrt', queries, stale_keys, preferred_element_type=jn...  15.4 us
  transfers between devices with their start and end apart: 19, of which 19 were waited for; matrix products, arithmetic and copies ran while one was open for 2% of the time, Pallas kernels for 0%

commit v1 on v0

v1 whole, which is shorter than its diff:
```python
import functools
import math

import jax
import jax.numpy as jnp
import numpy as np
from jax import lax
from jax.experimental import pallas as pl
from jax.experimental.pallas import tpu as pltpu
from jax.sharding import Mesh, PartitionSpec as P

HEADS = 12
HDIM = 128
ROWS = 8
D = HEADS * HDIM
TOKENS = 512
SECTIONS = 8
MEMBERS = 4
PART = D // MEMBERS
LOCAL = 16
GROUP = LOCAL * MEMBERS
RING = 16
UNIT = 24
SHARE = 3 * UNIT

guide_weight = 3.5
norm_eps = 1e-06

AXES = ("xh", "xl", "yh", "core", "section", "cfg")
SIZES = (2, 2, 4, 2, 8, 2)


def ring_place(place):
    return (0, place) if place < 8 else (1, 15 - place)


def plan_weight_moves():
    def plane(xh, xl, y, core):
        return (((xh * 2 + xl) * 4 + y // 2) * 2 + core) * 2 + y % 2

    left = [[] for _ in range(64)]
    for unit in range(3 * D // UNIT):
        source, slot = divmod(unit, 3)
        part, within = divmod(unit, D // UNIT)
        member, within = divmod(within, PART // UNIT)
        place, target_slot = divmod(part * (PART // UNIT) + within, 3)
        xh, y = ring_place(place)
        target = plane(xh, member // 2, y, member % 2)
        left[source].append((target, slot, target_slot))
    rounds = []
    for _ in range(3):
        owner = {}

        def place_edge(source, seen):
            for edge in sorted(left[source], key=lambda e: e[0] != source):
                if edge[0] in seen:
                    continue
                seen.add(edge[0])
                if edge[0] not in owner or place_edge(owner[edge[0]][0], seen):
                    owner[edge[0]] = (source, edge)
                    return True
            return False

        for source in range(64):
            if not place_edge(source, set()):
                raise ValueError("no matching")
        for source, edge in owner.values():
            left[source].remove(edge)
        rounds.append([(source, edge) for source, edge in owner.values()])
    routes, send_slot, take = [], np.zeros((3, 64), np.int32), np.zeros((3, 64), np.int32)
    for number, matched in enumerate(rounds):
        route = []
        for source, (target, slot, target_slot) in matched:
            send_slot[number, source] = slot
            take[target_slot, target] = number
            for s in range(SECTIONS):
                route.append(((source // 2 * 8 + s) * 2 + source % 2, (target // 2 * 8 + s) * 2 + target % 2))
        routes.append(route)
    return routes, send_slot, take


ROUTES, SEND_SLOT, TAKE = plan_weight_moves()
RING_GROUPS = [[xh * 8 + y for xh, y in map(ring_place, range(RING))]]
PAIRS = (
    [[s, s + 1] for s in range(0, SECTIONS, 2)],
    [[s, (s + 1) % SECTIONS] for s in range(1, SECTIONS, 2)],
)


def nt_dot(a, b):
    return lax.dot_general(a, b, (((1,), (1,)), ((), ())), preferred_element_type=jnp.float32)


def block_kernel(tick, who, x_ref, w_ref, kv_ref, mod_ref, gate_ref, cos_ref, sin_ref, block_ref, old_ref, state_ref, fresh_ref):
    member = who[0]
    active = who[1] == tick
    xs = [x_ref[i].astype(jnp.float32) for i in range(MEMBERS)]
    center = sum(jnp.sum(x, axis=-1, keepdims=True) for x in xs) / D
    xs = [x - center for x in xs]
    spread = sum(jnp.sum(x * x, axis=-1, keepdims=True) for x in xs) / D
    inv = lax.rsqrt(spread + norm_eps)
    normed = jnp.concatenate(
        [
            (
                xs[i] * inv * (1.0 + mod_ref[1:2, i * PART : (i + 1) * PART])
                + mod_ref[0:1, i * PART : (i + 1) * PART]
            ).astype(jnp.bfloat16)
            for i in range(MEMBERS)
        ],
        axis=1,
    )
    projected = nt_dot(normed, w_ref[...]).astype(jnp.bfloat16)
    row_block = block_ref[...]
    stale_mask = lax.broadcasted_iota(jnp.int32, (GROUP, TOKENS), 1) // ROWS == row_block
    own_mask = (
        lax.broadcasted_iota(jnp.int32, (GROUP, GROUP), 0) // ROWS
        == lax.broadcasted_iota(jnp.int32, (GROUP, GROUP), 1) // ROWS
    )
    cosine, sine = cos_ref[...], sin_ref[...]

    def turned(values):
        values = values.astype(jnp.float32)
        values = values * lax.rsqrt(jnp.mean(values * values, axis=-1, keepdims=True) + norm_eps)
        return (values * cosine + pltpu.roll(values, HDIM // 2, 1) * sine).astype(jnp.bfloat16)

    scale = 1.0 / math.sqrt(HDIM)
    for head in range(PART // HDIM):
        cols = slice(head * HDIM, (head + 1) * HDIM)
        query = turned(projected[:, head * HDIM : (head + 1) * HDIM])
        key = turned(projected[:, PART + head * HDIM : PART + (head + 1) * HDIM])
        value = projected[:, 2 * PART + head * HDIM : 2 * PART + (head + 1) * HDIM]
        weights = jnp.where(stale_mask, 0.0, jnp.exp(nt_dot(query, kv_ref[:, cols]) * scale))
        own = jnp.where(own_mask, jnp.exp(nt_dot(query, key) * scale), 0.0)
        total = jnp.sum(weights, axis=-1, keepdims=True) + jnp.sum(own, axis=-1, keepdims=True)
        attended = jnp.dot(
            weights.astype(jnp.bfloat16),
            kv_ref[:, PART + head * HDIM : PART + (head + 1) * HDIM],
            preferred_element_type=jnp.float32,
        ) + jnp.dot(own.astype(jnp.bfloat16), value, preferred_element_type=jnp.float32)
        attended = attended / total
        state = x_ref[member, :, cols].astype(jnp.float32) + gate_ref[0:1, cols] * attended
        state_ref[:, cols] = state.astype(jnp.bfloat16)
        fresh_ref[:, cols] = jnp.where(active, key, old_ref[:, cols])
        vcols = slice(PART + head * HDIM, PART + (head + 1) * HDIM)
        fresh_ref[:, vcols] = jnp.where(active, value, old_ref[:, vcols])


def run_block(tick, who, x, weight, kv, mod, gate, cosine, sine, blocks, old):
    vmem = pl.BlockSpec(memory_space=pltpu.VMEM)
    return pl.pallas_call(
        functools.partial(block_kernel, tick),
        out_shape=(
            jax.ShapeDtypeStruct((GROUP, PART), jnp.bfloat16),
            jax.ShapeDtypeStruct((GROUP, 2 * PART), jnp.bfloat16),
        ),
        in_specs=[pl.BlockSpec(memory_space=pltpu.SMEM)] + [vmem] * 9,
        out_specs=(vmem, vmem),
        compiler_params=pltpu.CompilerParams(vmem_limit_bytes=24 * 1024 * 1024),
        name="block_step",
    )(who, x, weight, kv, mod, gate, cosine, sine, blocks, old)


def body(hidden, timestep, patch_order, modulation, qkv_weight, stale_kv):
    index = {a: lax.axis_index(a) for a in AXES}
    section = index["section"]
    member = index["xl"] * 2 + index["core"]
    place = (((index["xh"] * 2 + index["xl"]) * 4 + index["yh"]) * 2 + index["core"]) * 2 + index["cfg"]

    columns = jnp.transpose(qkv_weight[0])
    half = lax.dynamic_slice_in_dim(columns, index["cfg"] * SHARE, SHARE, 0).reshape(3, UNIT, D)
    moved = []
    for number in range(3):
        slot = jnp.asarray(SEND_SLOT[number])[place]
        moved.append(lax.ppermute(lax.dynamic_index_in_dim(half, slot, 0, keepdims=False), AXES, ROUTES[number]))
    moved = jnp.stack(moved)
    share = jnp.concatenate(
        [lax.dynamic_index_in_dim(moved, jnp.asarray(TAKE[j])[place], 0, keepdims=False) for j in range(3)]
    )
    weight = lax.all_gather(share, ("xh", "yh", "cfg"), axis=0, tiled=True, axis_index_groups=RING_GROUPS)

    share, stale_rows, entering = lax.optimization_barrier((share, stale_kv[0, 0], hidden[0]))
    pieces = [
        jnp.concatenate(
            [stale_rows[:, m * PART : (m + 1) * PART], stale_rows[:, D + m * PART : D + (m + 1) * PART]], axis=1
        )
        for m in range(MEMBERS)
    ]
    outgoing = jnp.stack([pieces[(p // 8 % 2) * 2 + p % 2] for p in range(32)])
    kv = lax.all_to_all(outgoing, ("xh", "xl", "yh", "core"), split_axis=0, concat_axis=0, tiled=True)
    kv = kv.reshape(TOKENS, 2 * PART)

    x = lax.all_gather(entering, ("xl", "core"), axis=0, tiled=True)
    x = jnp.transpose(x.reshape(GROUP, MEMBERS, PART), (1, 0, 2))

    row = lax.dynamic_index_in_dim(modulation[0, 0], timestep[0], 0, keepdims=False)
    mod = row[: 2 * D].reshape(2, D)
    gate = lax.dynamic_slice_in_dim(row, 2 * D + member * PART, PART, 0).reshape(1, PART)

    lane = jnp.arange(GROUP, dtype=jnp.int32)
    source = lane // LOCAL
    patch = ((index["xh"] * 2 + source // 2) * 4 + index["yh"]) * 2 + source % 2
    blocks = patch * (LOCAL // ROWS) + lane % LOCAL // ROWS
    positions = (patch_order[blocks] * ROWS + lane % ROWS).astype(jnp.float32)
    halfway = HDIM // 2
    inverse = jnp.exp(-math.log(10000.0) * jnp.arange(halfway, dtype=jnp.float32) / halfway)
    angles = positions[:, None] * inverse[None, :]
    cosine, sine = jnp.cos(angles), jnp.sin(angles)
    cosine = jnp.concatenate([cosine, cosine], axis=1)
    sine = jnp.concatenate([-sine, sine], axis=1)

    who = jnp.stack([member, section]).astype(jnp.int32)
    fresh = jnp.zeros((GROUP, 2 * PART), jnp.bfloat16)
    for tick in range(SECTIONS):
        state, fresh = run_block(tick, who, x, weight, kv, mod, gate, cosine, sine, blocks[:, None], fresh)
        if tick + 1 < SECTIONS:
            state = lax.all_gather(state, "section", axis=0, tiled=False, axis_index_groups=PAIRS[tick % 2])[0]
            x = lax.all_gather(state, ("xl", "core"), axis=0, tiled=False)

    ends = lax.all_gather(jnp.concatenate([state, fresh], axis=1), ("xl", "core"), axis=0, tiled=False)
    ends = lax.dynamic_slice_in_dim(ends, member * LOCAL, LOCAL, 1)
    ends = jnp.transpose(ends, (1, 0, 2))
    finals = ends[:, :, :PART].reshape(SECTIONS, LOCAL // SECTIONS, 2, D // 2)
    fresh_all = jnp.concatenate(
        [ends[:, :, PART : 2 * PART].reshape(LOCAL, D), ends[:, :, 2 * PART :].reshape(LOCAL, D)], axis=1
    )
    finals = jnp.transpose(finals, (0, 2, 1, 3)).reshape(SECTIONS * 2, LOCAL // SECTIONS, D // 2)
    spread = lax.all_to_all(finals, ("section", "cfg"), split_axis=0, concat_axis=0, tiled=True)
    uncond = spread[2 * SECTIONS - 2].astype(jnp.float32)
    conditioned = spread[2 * SECTIONS - 1].astype(jnp.float32)
    guided = (uncond + guide_weight * (conditioned - uncond)).astype(jnp.bfloat16)
    return guided, fresh_all[None, None]


def solution(mesh):
    fine = Mesh(mesh.devices.reshape(SIZES), AXES)
    patch = ("xh", "xl", "yh", "core")
    return jax.shard_map(
        body,
        mesh=fine,
        in_specs=(
            P("cfg", patch, None),
            P(),
            P(),
            P("section", "cfg", None, None),
            P("section", None, patch),
            P("section", "cfg", patch, None),
        ),
        out_specs=(P((*patch, "section"), "cfg"), P("section", "cfg", patch, None)),
        check_vma=False,
    )
```

time: 694 us -> 255 us (0.37); the launches traced: 686 us -> 254 us
  blocking collectives: 429 us -> 101 us
  waiting for transfers between devices: 101 us -> 50.2 us
  starting transfers between devices: 71.8 us -> 30.7 us
  matrix products: 26.7 us -> 0 us
  Pallas kernels: 0 us -> 19.8 us
  local copies, waits for them, and re-layouts: 26.7 us -> 9.52 us
  other arithmetic: 13.7 us -> 21.9 us
    all_gather x9 -> x16, blocking collectives: 400 us -> 101 us  [the longest x7 53.7 us: body(): x = lax.all_gather(state, ('xl', 'core'), axis=0, tiled=False)]
    all_to_all x10 -> x2, waiting for transfers between devices: 94 us -> 27.8 us  [the longest x1 20.8 us: body(): lax.all_to_all(outgoing, ('xh', 'xl', 'yh', 'core'), split_axis=0, concat...]
    unnamed x1 -> x0, blocking collectives: 28.5 us -> none
    dot_general x45 -> x0, matrix products: 26.7 us -> none  [the longest x9 15.4 us: body(): jnp.einsum('rhd,thd->hrt', queries, stale_keys, preferred_element_type=jn...]
    all_gather x1, waiting for transfers between devices: 0.16 us -> 22.4 us  [body(): lax.all_gather(share, ('xh', 'yh', 'cfg'), axis=0, tiled=True, axis_index...]
    ppermute x8 -> x3, starting transfers between devices: 35.4 us -> 13.2 us  [body(): lax.ppermute(lax.dynamic_index_in_dim(half, slot, 0, keepdims=False), AXE...]
    pallas_call x0 -> x8, Pallas kernels: none -> 19.8 us  [run_block(): pl.pallas_call(functools.partial(block_kernel, tick), out_shape=(jax.Shap...]
    all_to_all x10 -> x2, starting transfers between devices: 36.4 us -> 17.4 us  [the longest x1 10.5 us: body(): lax.all_to_all(outgoing, ('xh', 'xl', 'yh', 'core'), split_axis=0, concat...]
  transfers between devices with their start and end apart: 19 -> 6, of which waited for: 19 -> 3; matrix products, arithmetic and copies ran while one was open for 2% -> 10% of each run, Pallas kernels for 0% -> 0%
where the time goes in v1:
time: 255 us; the launch traced here: 254 us
  blocking collectives  101 us (40%)
  waiting for transfers between devices  50.2 us (20%)
  starting transfers between devices  30.7 us (12%)
  other arithmetic  21.9 us (9%)
  between operations  20.8 us (8%)
  Pallas kernels  19.8 us (8%)
  local copies, waits for them, and re-layouts  9.52 us (4%)
    all_gather x7, blocking collectives, body(): x = lax.all_gather(state, ('xl', 'core'), axis=0, tiled=False)  53.7 us
    all_gather x7, blocking collectives, body(): lax.all_gather(state, 'section', axis=0, tiled=False, axis_index_groups=P...  31.6 us
    all_gather x1, waiting for transfers between devices, body(): lax.all_gather(share, ('xh', 'yh', 'cfg'), axis=0, tiled=True, axis_index...  22.4 us
    all_to_all x1, waiting for transfers between devices, body(): lax.all_to_all(outgoing, ('xh', 'xl', 'yh', 'core'), split_axis=0, concat...  20.8 us
    pallas_call x8, Pallas kernels, run_block(): pl.pallas_call(functools.partial(block_kernel, tick), out_shape=(jax.Shap...  19.8 us
    unnamed x31, other arithmetic  18.8 us
    ppermute x3, starting transfers between devices, body(): lax.ppermute(lax.dynamic_index_in_dim(half, slot, 0, keepdims=False), AXE...  13.2 us
    all_to_all x1, starting transfers between devices, body(): lax.all_to_all(outgoing, ('xh', 'xl', 'yh', 'core'), split_axis=0, concat...  10.5 us
  transfers between devices with their start and end apart: 6, of which 3 were waited for; matrix products, arithmetic and copies ran while one was open for 10% of the time, Pallas kernels for 0%

profile of v1, /device:TPU:1, one launch (start us, length us, event | category | flops | bytes accessed | tf_op | source)
XLA Modules:
  0.0 253.8 jit_solution(10642555283839091057)
XLA Ops:
  8.3 5.6 %collective-permute-start = (bf16[24,1536]{1,0:T(8,128)(2,1)S(1)}, bf16[24,1536]{1,0:T(8,128)(2,1)S(1)}, u32[]{:S(2)}, u32[]{:S(2)}) collective-permute-start(bf16[24,1536]{1,0:T(8,128)(2,1)S(1)} %get-tuple-element.41), channel_id=1, source_target_pairs={{0,0},{2,2},{4,4},{6,6},{8,8},{10,10},{12,12},{14,14},{1,1},{3,3},... | collective-permute-start | bytes 221192 | tf_op jit(solution)/shard_map/ppermute | solution.py:174
  13.9 5.7 %collective-permute-start.1 = (bf16[24,1536]{1,0:T(8,128)(2,1)S(1)}, bf16[24,1536]{1,0:T(8,128)(2,1)S(1)}, u32[]{:S(2)}, u32[]{:S(2)}) collective-permute-start(bf16[24,1536]{1,0:T(8,128)(2,1)S(1)} %get-tuple-element.42), channel_id=1, source_target_pairs={{0,0},{2,2},{4,4},{6,6},{8,8},{10,10},{12,12},{14,14},{1,1},{3,3},... | collective-permute-start | bytes 221192 | tf_op jit(solution)/shard_map/ppermute | solution.py:174
  52.2 10.5 %all-to-all-start = ((bf16[32,16,768]{2,1,0:T(8,128)(2,1)}), bf16[32,16,768]{2,1,0:T(8,128)(2,1)S(1)}, u32[]{:S(2)}, u32[]{:S(2)}) async-start(bf16[32,16,768]{2,1,0:T(8,128)(2,1)} %constant_dynamic-update-slice_fusion), calls=%async_computation | async-start | bytes 1572864 | tf_op jit(solution)/shard_map/all_to_all | solution.py:189
  64.9 8.0 %all_gather.75 = bf16[64,1536]{1,0:T(8,128)(2,1)S(1)} all-gather(bf16[16,1536]{1,0:T(8,128)(2,1)S(1)} %bitcast.163), channel_id=1, replica_groups=mesh['xh'=2,'xl'=2,'yh'=4,'core'=2,'section'=8,'cfg'=2] {'xl','core'}, dimensions={0}, use_global_device_ids=true | all-gather | bytes 245760 | tf_op jit(solution)/shard_map/all_gather | solution.py:192
  72.9 20.8 %all-to-all-done = bf16[32,16,768]{2,1,0:T(8,128)(2,1)S(1)} async-done(((bf16[32,16,768]{2,1,0:T(8,128)(2,1)}), bf16[32,16,768]{2,1,0:T(8,128)(2,1)S(1)}, u32[]{:S(2)}, u32[]{:S(2)}) %all-to-all-start) | async-done | bytes 786464 | tf_op jit(solution)/shard_map/all_to_all | solution.py:189
  93.8 22.4 %all-gather.17.cloned.1.call-done.w_ref = bf16[1152,1536]{1,0:T(8,128)(2,1)} async-done(((bf16[72,1536]{1,0:T(8,128)(2,1)}), bf16[1152,1536]{1,0:T(8,128)(2,1)}) %all-gather.17.cloned.1.call-update) | async-done | bytes 3538960 | tf_op jit(solution)/shard_map/all_gather | solution.py:179
  116.2 2.0 copy-done.1
  118.2 2.5 block_step.8
  120.7 3.6 %all-gather = bf16[128,384]{1,0:T(8,128)(2,1)S(1)} all-gather(bf16[64,384]{1,0:T(8,128)(2,1)S(1)} %get-tuple-element.22), channel_id=2, replica_groups={{0,2},{4,6},{8,10},{12,14},{1,3},{5,7},{9,11},{13,15},{16,18},{20,22},{..., dimensions={0}, use_global_device_ids=true | all-gather | bytes 147456 | tf_op jit(solution)/shard_map/all_gather | solution.py:216
  124.3 13.9 %all-gather.8 = bf16[256,384]{1,0:T(8,128)(2,1)S(1)} all-gather(bf16[64,384]{1,0:T(8,128)(2,1)S(1)} %slice.103), channel_id=10, replica_groups=mesh['xh'=2,'xl'=2,'yh'=4,'core'=2,'section'=8,'cfg'=2] {'xl','core'}, dimensions={0}, use_global_device_ids=true | all-gather | bytes 245760 | tf_op jit(solution)/shard_map/all_gather | solution.py:217
  138.2 2.5 block_step.9
  140.6 7.3 %all-gather.1 = bf16[128,384]{1,0:T(8,128)(2,1)S(1)} all-gather(bf16[64,384]{1,0:T(8,128)(2,1)S(1)} %get-tuple-element.24), channel_id=3, replica_groups={{2,4},{6,8},{10,12},{14,0},{3,5},{7,9},{11,13},{15,1},{18,20},{22,24},{..., dimensions={0}, use_global_device_ids=true | all-gather | bytes 147456 | tf_op jit(solution)/shard_map/all_gather | solution.py:216
  147.9 6.2 %all-gather.9 = bf16[256,384]{1,0:T(8,128)(2,1)S(1)} all-gather(bf16[64,384]{1,0:T(8,128)(2,1)S(1)} %slice.104), channel_id=11, replica_groups=mesh['xh'=2,'xl'=2,'yh'=4,'core'=2,'section'=8,'cfg'=2] {'xl','core'}, dimensions={0}, use_global_device_ids=true | all-gather | bytes 245760 | tf_op jit(solution)/shard_map/all_gather | solution.py:217
  154.1 2.5 block_step.10
  156.6 3.6 %all-gather.2 = bf16[128,384]{1,0:T(8,128)(2,1)S(1)} all-gather(bf16[64,384]{1,0:T(8,128)(2,1)S(1)} %get-tuple-element.26), channel_id=4, replica_groups={{0,2},{4,6},{8,10},{12,14},{1,3},{5,7},{9,11},{13,15},{16,18},{20,22},{..., dimensions={0}, use_global_device_ids=true | all-gather | bytes 147456 | tf_op jit(solution)/shard_map/all_gather | solution.py:216
  160.2 6.7 %all-gather.10 = bf16[256,384]{1,0:T(8,128)(2,1)S(1)} all-gather(bf16[64,384]{1,0:T(8,128)(2,1)S(1)} %slice.105), channel_id=12, replica_groups=mesh['xh'=2,'xl'=2,'yh'=4,'core'=2,'section'=8,'cfg'=2] {'xl','core'}, dimensions={0}, use_global_device_ids=true | all-gather | bytes 245760 | tf_op jit(solution)/shard_map/all_gather | solution.py:217
  166.9 2.5 block_step.11
  169.4 4.9 %all-gather.3 = bf16[128,384]{1,0:T(8,128)(2,1)S(1)} all-gather(bf16[64,384]{1,0:T(8,128)(2,1)S(1)} %get-tuple-element.28), channel_id=5, replica_groups={{2,4},{6,8},{10,12},{14,0},{3,5},{7,9},{11,13},{15,1},{18,20},{22,24},{..., dimensions={0}, use_global_device_ids=true | all-gather | bytes 147456 | tf_op jit(solution)/shard_map/all_gather | solution.py:216
  174.3 6.7 %all-gather.11 = bf16[256,384]{1,0:T(8,128)(2,1)S(1)} all-gather(bf16[64,384]{1,0:T(8,128)(2,1)S(1)} %slice.106), channel_id=13, replica_groups=mesh['xh'=2,'xl'=2,'yh'=4,'core'=2,'section'=8,'cfg'=2] {'xl','core'}, dimensions={0}, use_global_device_ids=true | all-gather | bytes 245760 | tf_op jit(solution)/shard_map/all_gather | solution.py:217
  181.0 2.5 block_step.12
  183.5 3.6 %all-gather.4 = bf16[128,384]{1,0:T(8,128)(2,1)S(1)} all-gather(bf16[64,384]{1,0:T(8,128)(2,1)S(1)} %get-tuple-element.30), channel_id=6, replica_groups={{0,2},{4,6},{8,10},{12,14},{1,3},{5,7},{9,11},{13,15},{16,18},{20,22},{..., dimensions={0}, use_global_device_ids=true | all-gather | bytes 147456 | tf_op jit(solution)/shard_map/all_gather | solution.py:216
  187.1 6.7 %all-gather.12 = bf16[256,384]{1,0:T(8,128)(2,1)S(1)} all-gather(bf16[64,384]{1,0:T(8,128)(2,1)S(1)} %slice.107), channel_id=14, replica_groups=mesh['xh'=2,'xl'=2,'yh'=4,'core'=2,'section'=8,'cfg'=2] {'xl','core'}, dimensions={0}, use_global_device_ids=true | all-gather | bytes 245760 | tf_op jit(solution)/shard_map/all_gather | solution.py:217
  193.8 2.5 block_step.13
  196.3 4.9 %all-gather.5 = bf16[128,384]{1,0:T(8,128)(2,1)S(1)} all-gather(bf16[64,384]{1,0:T(8,128)(2,1)S(1)} %get-tuple-element.32), channel_id=7, replica_groups={{2,4},{6,8},{10,12},{14,0},{3,5},{7,9},{11,13},{15,1},{18,20},{22,24},{..., dimensions={0}, use_global_device_ids=true | all-gather | bytes 147456 | tf_op jit(solution)/shard_map/all_gather | solution.py:216
  201.2 6.8 %all-gather.13 = bf16[256,384]{1,0:T(8,128)(2,1)S(1)} all-gather(bf16[64,384]{1,0:T(8,128)(2,1)S(1)} %slice.108), channel_id=15, replica_groups=mesh['xh'=2,'xl'=2,'yh'=4,'core'=2,'section'=8,'cfg'=2] {'xl','core'}, dimensions={0}, use_global_device_ids=true | all-gather | bytes 245760 | tf_op jit(solution)/shard_map/all_gather | solution.py:217
  208.1 2.5 block_step.14
  210.6 3.6 %all-gather.6 = bf16[128,384]{1,0:T(8,128)(2,1)S(1)} all-gather(bf16[64,384]{1,0:T(8,128)(2,1)S(1)} %get-tuple-element.34), channel_id=8, replica_groups={{0,2},{4,6},{8,10},{12,14},{1,3},{5,7},{9,11},{13,15},{16,18},{20,22},{..., dimensions={0}, use_global_device_ids=true | all-gather | bytes 147456 | tf_op jit(solution)/shard_map/all_gather | solution.py:216
  214.2 6.7 %all-gather.14 = bf16[256,384]{1,0:T(8,128)(2,1)S(1)} all-gather(bf16[64,384]{1,0:T(8,128)(2,1)S(1)} %slice.109), channel_id=16, replica_groups=mesh['xh'=2,'xl'=2,'yh'=4,'core'=2,'section'=8,'cfg'=2] {'xl','core'}, dimensions={0}, use_global_device_ids=true | all-gather | bytes 245760 | tf_op jit(solution)/shard_map/all_gather | solution.py:217
  220.9 2.5 block_step.15
  223.4 7.6 %all-gather.7 = bf16[256,1152]{1,0:T(8,128)(2,1)S(1)} all-gather(bf16[64,1152]{1,0:T(8,128)(2,1)S(1)} %pad_maximum_fusion.2), channel_id=9, replica_groups=mesh['xh'=2,'xl'=2,'yh'=4,'core'=2,'section'=8,'cfg'=2] {'xl','core'}, dimensions={0}, use_global_device_ids=true | all-gather | bytes 737280 | tf_op jit(solution)/shard_map/all_gather | solution.py:219
  232.0 6.9 %all-to-all-start.1 = ((bf16[16,2,768]{2,1,0:T(2,128)(2,1)}), bf16[16,2,768]{2,1,0:T(2,128)(2,1)S(1)}, u32[]{:S(2)}, u32[]{:S(2)}) async-start(bf16[16,2,768]{2,1,0:T(2,128)(2,1)} %bitcast.34), calls=%async_computation.1 | async-start | bytes 98304 | tf_op jit(solution)/shard_map/all_to_all | solution.py:227
  239.5 6.9 %all-to-all-done.1 = bf16[16,2,768]{2,1,0:T(2,128)(2,1)S(1)} async-done(((bf16[16,2,768]{2,1,0:T(2,128)(2,1)}), bf16[16,2,768]{2,1,0:T(2,128)(2,1)S(1)}, u32[]{:S(2)}, u32[]{:S(2)}) %all-to-all-start.1) | async-done | bytes 49184 | tf_op jit(solution)/shard_map/all_to_all | solution.py:227
  (87 shorter events, 31.4 us)
Async XLA Ops:
  7.2 56.3 %copy-start = (f32[1,1,28,4608]{3,1,2,0:T(1,128)S(1)}, f32[1,1,28,4608]{3,1,2,0:T(1,128)}, u32[]{:S(2)}) copy-start(f32[1,1,28,4608]{3,1,2,0:T(1,128)} %param.15) | copy-start | bytes 1548292
  7.2 57.8 %copy-start.4 = (bf16[1,16,1536]{2,1,0:T(8,128)(2,1)S(1)}, bf16[1,16,1536]{2,1,0:T(8,128)(2,1)}, u32[]{:S(2)}) copy-start(bf16[1,16,1536]{2,1,0:T(8,128)(2,1)} %param.12) | copy-start | bytes 147460
  7.2 56.4 %copy-start.3 = (s32[64]{0:T(128)S(1)}, s32[64]{0:T(128)}, u32[]{:S(2)}) copy-start(s32[64]{0:T(128)} %param.14) | copy-start | bytes 772
  7.2 109.0 %all-gather.17.cloned.1.call-start = ((), (), s32[]{:S(2)}) async-start(), calls=%async_computation.2 | async-start | bytes 3760128 | tf_op jit(solution)/shard_map/all_gather | solution.py:179
  8.3 22.8 %collective-permute-start = (bf16[24,1536]{1,0:T(8,128)(2,1)S(1)}, bf16[24,1536]{1,0:T(8,128)(2,1)S(1)}, u32[]{:S(2)}, u32[]{:S(2)}) collective-permute-start(bf16[24,1536]{1,0:T(8,128)(2,1)S(1)} %get-tuple-element.41), channel_id=1, source_target_pairs={{0,0},{2,2},{4,4},{6,6},{8,8},{10,10},{12,12},{14,14},{1,1},{3,3},... | collective-permute-start | bytes 221192 | tf_op jit(solution)/shard_map/ppermute | solution.py:174
  13.9 17.2 %collective-permute-start.1 = (bf16[24,1536]{1,0:T(8,128)(2,1)S(1)}, bf16[24,1536]{1,0:T(8,128)(2,1)S(1)}, u32[]{:S(2)}, u32[]{:S(2)}) collective-permute-start(bf16[24,1536]{1,0:T(8,128)(2,1)S(1)} %get-tuple-element.42), channel_id=1, source_target_pairs={{0,0},{2,2},{4,4},{6,6},{8,8},{10,10},{12,12},{14,14},{1,1},{3,3},... | collective-permute-start | bytes 221192 | tf_op jit(solution)/shard_map/ppermute | solution.py:174
  19.6 11.5 %collective-permute-start.2 = (bf16[24,1536]{1,0:T(8,128)(2,1)S(1)}, bf16[24,1536]{1,0:T(8,128)(2,1)S(1)}, u32[]{:S(2)}, u32[]{:S(2)}) collective-permute-start(bf16[24,1536]{1,0:T(8,128)(2,1)S(1)} %get-tuple-element.43), channel_id=1, source_target_pairs={{0,0},{2,2},{4,4},{6,6},{8,8},{10,10},{12,12},{14,14},{1,1},{3,3},... | collective-permute-start | bytes 221192 | tf_op jit(solution)/shard_map/ppermute | solution.py:174
  52.2 41.6 %all-to-all-start = ((bf16[32,16,768]{2,1,0:T(8,128)(2,1)}), bf16[32,16,768]{2,1,0:T(8,128)(2,1)S(1)}, u32[]{:S(2)}, u32[]{:S(2)}) async-start(bf16[32,16,768]{2,1,0:T(8,128)(2,1)} %constant_dynamic-update-slice_fusion), calls=%async_computation | async-start | bytes 1572864 | tf_op jit(solution)/shard_map/all_to_all | solution.py:189
  116.2 2.0 copy-start.1
  118.2 20.0 %copy-start.2 = (bf16[1152,1536]{1,0:T(8,128)(2,1)S(1)}, bf16[1152,1536]{1,0:T(8,128)(2,1)}, u32[]{:S(2)}) copy-start(bf16[1152,1536]{1,0:T(8,128)(2,1)} %all-gather.17.cloned.1.call-done.w_ref) | copy-start | bytes 10616836
  232.0 14.4 %all-to-all-start.1 = ((bf16[16,2,768]{2,1,0:T(2,128)(2,1)}), bf16[16,2,768]{2,1,0:T(2,128)(2,1)S(1)}, u32[]{:S(2)}, u32[]{:S(2)}) async-start(bf16[16,2,768]{2,1,0:T(2,128)(2,1)} %bitcast.34), calls=%async_computation.1 | async-start | bytes 98304 | tf_op jit(solution)/shard_map/all_to_all | solution.py:227
Sparse Core Ops, SparseCore 0:
  32.1 84.0 all-gather.16

commit v2 on v1

--- a/solution.py
+++ b/solution.py
@@ -19,7 +19,6 @@
 PART = D // MEMBERS
 LOCAL = 16
 GROUP = LOCAL * MEMBERS
-RING = 16
 UNIT = 24
 SHARE = 3 * UNIT
 
@@ -28,10 +27,6 @@
 
 AXES = ("xh", "xl", "yh", "core", "section", "cfg")
 SIZES = (2, 2, 4, 2, 8, 2)
-
-
-def ring_place(place):
-    return (0, place) if place < 8 else (1, 15 - place)
 
 
 def plan_weight_moves():
@@ -44,7 +39,7 @@
         part, within = divmod(unit, D // UNIT)
         member, within = divmod(within, PART // UNIT)
         place, target_slot = divmod(part * (PART // UNIT) + within, 3)
-        xh, y = ring_place(place)
+        y, xh = divmod(place, 2)
         target = plane(xh, member // 2, y, member % 2)
         left[source].append((target, slot, target_slot))
     rounds = []
@@ -80,7 +75,7 @@
 
 
 ROUTES, SEND_SLOT, TAKE = plan_weight_moves()
-RING_GROUPS = [[xh * 8 + y for xh, y in map(ring_place, range(RING))]]
+SLOTS = np.concatenate([SEND_SLOT.reshape(-1), TAKE.reshape(-1)])
 PAIRS = (
     [[s, s + 1] for s in range(0, SECTIONS, 2)],
     [[s, (s + 1) % SECTIONS] for s in range(1, SECTIONS, 2)],
@@ -160,23 +155,48 @@
     )(who, x, weight, kv, mod, gate, cosine, sine, blocks, old)
 
 
+def pick_kernel(place, slots, half_ref, *outs):
+    for number in range(3):
+        outs[number][...] = half_ref[slots[number * 64 + place[0]]]
+
+
+def arrange_kernel(place, slots, *refs):
+    moved, out = refs[:3], refs[3]
+    for j in range(3):
+        number = slots[(3 + j) * 64 + place[0]]
+        for n in range(3):
+
+            @pl.when(number == n)
+            def _():
+                out[j] = moved[n][...]
+
+
+def move_units(kernel, place, units, outs):
+    smem = pl.BlockSpec(memory_space=pltpu.SMEM)
+    vmem = pl.BlockSpec(memory_space=pltpu.VMEM)
+    return pl.pallas_call(
+        kernel,
+        out_shape=[jax.ShapeDtypeStruct(shape, jnp.bfloat16) for shape in outs],
+        in_specs=[smem, smem] + [vmem] * len(units),
+        out_specs=[vmem] * len(outs),
+        name=kernel.__name__,
+    )(place, jnp.asarray(SLOTS), *units)
+
+
 def body(hidden, timestep, patch_order, modulation, qkv_weight, stale_kv):
     index = {a: lax.axis_index(a) for a in AXES}
     section = index["section"]
     member = index["xl"] * 2 + index["core"]
     place = (((index["xh"] * 2 + index["xl"]) * 4 + index["yh"]) * 2 + index["core"]) * 2 + index["cfg"]
+    place = place.astype(jnp.int32).reshape(1)
 
     columns = jnp.transpose(qkv_weight[0])
     half = lax.dynamic_slice_in_dim(columns, index["cfg"] * SHARE, SHARE, 0).reshape(3, UNIT, D)
-    moved = []
-    for number in range(3):
-        slot = jnp.asarray(SEND_SLOT[number])[place]
-        moved.append(lax.ppermute(lax.dynamic_index_in_dim(half, slot, 0, keepdims=False), AXES, ROUTES[number]))
-    moved = jnp.stack(moved)
-    share = jnp.concatenate(
-        [lax.dynamic_index_in_dim(moved, jnp.asarray(TAKE[j])[place], 0, keepdims=False) for j in range(3)]
-    )
-    weight = lax.all_gather(share, ("xh", "yh", "cfg"), axis=0, tiled=True, axis_index_groups=RING_GROUPS)
+    sent = move_units(pick_kernel, place, [half], [(UNIT, D)] * 3)
+    moved = [lax.ppermute(sent[number], AXES, ROUTES[number]) for number in range(3)]
+    (share,) = move_units(arrange_kernel, place, moved, [(3, UNIT, D)])
+    share = lax.all_gather(share.reshape(SHARE, D), "xh", axis=0, tiled=True)
+    weight = lax.all_gather(share, ("yh", "cfg"), axis=0, tiled=True)
 
     share, stale_rows, entering = lax.optimization_barrier((share, stale_kv[0, 0], hidden[0]))
     pieces = [
@@ -185,7 +205,8 @@
         )
         for m in range(MEMBERS)
     ]
-    outgoing = jnp.stack([pieces[(p // 8 % 2) * 2 + p % 2] for p in range(32)])
+    pieces = lax.optimization_barrier(jnp.stack(pieces)).reshape(1, 2, 1, 2, LOCAL, 2 * PART)
+    outgoing = jnp.broadcast_to(pieces, (2, 2, 4, 2, LOCAL, 2 * PART)).reshape(32, LOCAL, 2 * PART)
     kv = lax.all_to_all(outgoing, ("xh", "xl", "yh", "core"), split_axis=0, concat_axis=0, tiled=True)
     kv = kv.reshape(TOKENS, 2 * PART)
 
@@ -216,19 +237,19 @@
             state = lax.all_gather(state, "section", axis=0, tiled=False, axis_index_groups=PAIRS[tick % 2])[0]
             x = lax.all_gather(state, ("xl", "core"), axis=0, tiled=False)
 
-    ends = lax.all_gather(jnp.concatenate([state, fresh], axis=1), ("xl", "core"), axis=0, tiled=False)
-    ends = lax.dynamic_slice_in_dim(ends, member * LOCAL, LOCAL, 1)
-    ends = jnp.transpose(ends, (1, 0, 2))
-    finals = ends[:, :, :PART].reshape(SECTIONS, LOCAL // SECTIONS, 2, D // 2)
-    fresh_all = jnp.concatenate(
-        [ends[:, :, PART : 2 * PART].reshape(LOCAL, D), ends[:, :, 2 * PART :].reshape(LOCAL, D)], axis=1
-    )
+    ends = lax.all_gather(state, ("xl", "core"), axis=0, tiled=False)
+    ends, fresh = lax.optimization_barrier((ends, fresh))
+    finals = lax.dynamic_slice_in_dim(ends, member * LOCAL, LOCAL, 1)
+    finals = jnp.transpose(finals, (1, 0, 2)).reshape(SECTIONS, LOCAL // SECTIONS, 2, D // 2)
     finals = jnp.transpose(finals, (0, 2, 1, 3)).reshape(SECTIONS * 2, LOCAL // SECTIONS, D // 2)
     spread = lax.all_to_all(finals, ("section", "cfg"), split_axis=0, concat_axis=0, tiled=True)
+    kept = lax.all_gather(fresh, ("xl", "core"), axis=0, tiled=False)
+    kept = lax.dynamic_slice_in_dim(kept, member * LOCAL, LOCAL, 1)
+    kept = jnp.transpose(kept.reshape(MEMBERS, LOCAL, 2, PART), (1, 2, 0, 3)).reshape(LOCAL, 2 * D)
     uncond = spread[2 * SECTIONS - 2].astype(jnp.float32)
     conditioned = spread[2 * SECTIONS - 1].astype(jnp.float32)
     guided = (uncond + guide_weight * (conditioned - uncond)).astype(jnp.bfloat16)
-    return guided, fresh_all[None, None]
+    return guided, kept[None, None]
 
 
 def solution(mesh):

time: 255 us -> 246 us (0.965)
  other arithmetic: 21.9 us -> 1.16 us
  blocking collectives: 101 us -> 116 us
  between operations: 20.8 us -> 15 us
  waiting for transfers between devices: 50.2 us -> 55.7 us
  starting transfers between devices: 30.7 us -> 25.6 us
  Pallas kernels: 19.8 us -> 23.1 us
    unnamed x31 -> x0, other arithmetic: 18.8 us -> none
    all_gather x1 -> x3, blocking collectives: 7.65 us -> 25.4 us  [the longest x1 13.2 us: body(): share = lax.all_gather(share.reshape(SHARE, D), 'xh', axis=0, tiled=True)]
    all_gather x7, blocking collectives: 53.7 us -> 46.5 us  [body(): x = lax.all_gather(state, ('xl', 'core'), axis=0, tiled=False)]
    all_gather x1, waiting for transfers between devices: 22.4 us -> 28.1 us  [body(): weight = lax.all_gather(share, ('yh', 'cfg'), axis=0, tiled=True)]
    dynamic_slice x6 -> x1, local copies, waits for them, and re-layouts: 4.84 us -> 0.02 us  [body(): kept = lax.dynamic_slice_in_dim(kept, member * LOCAL, LOCAL, 1)]
    all_gather x7, blocking collectives: 31.6 us -> 36.1 us  [body(): lax.all_gather(state, 'section', axis=0, tiled=False, axis_index_groups=P...]
    all_to_all x1, starting transfers between devices: 10.5 us -> 6.87 us  [body(): lax.all_to_all(outgoing, ('xh', 'xl', 'yh', 'core'), split_axis=0, concat...]
    all_to_all x1, waiting for transfers between devices: 20.8 us -> 17.4 us  [body(): lax.all_to_all(outgoing, ('xh', 'xl', 'yh', 'core'), split_axis=0, concat...]
  transfers between devices with their start and end apart: 6 -> 6, of which waited for: 3 -> 5; matrix products, arithmetic and copies ran while one was open for 10% -> 2% of each run, Pallas kernels for 0% -> 0%
where the time goes in v2:
time: 246 us; the launch traced here: 245 us
  blocking collectives  116 us (47%)
  waiting for transfers between devices  55.7 us (23%)
  starting transfers between devices  25.6 us (10%)
  Pallas kernels  23.1 us (9%)
  between operations  15 us (6%)
  local copies, waits for them, and re-layouts  8.8 us (4%)
    all_gather x7, blocking collectives, body(): x = lax.all_gather(state, ('xl', 'core'), axis=0, tiled=False)  46.5 us
    all_gather x7, blocking collectives, body(): lax.all_gather(state, 'section', axis=0, tiled=False, axis_index_groups=P...  36.1 us
    all_gather x1, waiting for transfers between devices, body(): weight = lax.all_gather(share, ('yh', 'cfg'), axis=0, tiled=True)  28.1 us
    pallas_call x8, Pallas kernels, run_block(): pl.pallas_call(functools.partial(block_kernel, tick), out_shape=(jax.Shap...  19.8 us
    all_to_all x1, waiting for transfers between devices, body(): lax.all_to_all(outgoing, ('xh', 'xl', 'yh', 'core'), split_axis=0, concat...  17.4 us
    ppermute x3, starting transfers between devices, body(): lax.ppermute(sent[number], AXES, ROUTES[number])  14.5 us
    all_gather x1, blocking collectives, body(): share = lax.all_gather(share.reshape(SHARE, D), 'xh', axis=0, tiled=True)  13.2 us
    all_gather x1, blocking collectives, body(): x = lax.all_gather(entering, ('xl', 'core'), axis=0, tiled=True)  7.75 us
  transfers between devices with their start and end apart: 6, of which 5 were waited for; matrix products, arithmetic and copies ran while one was open for 2% of the time, Pallas kernels for 0%

profile of v2, /device:TPU:1, one launch (start us, length us, event | category | flops | bytes accessed | tf_op | source)
XLA Modules:
  0.0 245.1 jit_solution(8441838797774285186)
XLA Ops:
  10.6 4.6 %collective-permute-start = (bf16[24,1536]{1,0:T(8,128)(2,1)}, bf16[24,1536]{1,0:T(8,128)(2,1)S(1)}, u32[]{:S(2)}, u32[]{:S(2)}) collective-permute-start(bf16[24,1536]{1,0:T(8,128)(2,1)} %get-tuple-element.25), channel_id=1, source_target_pairs={{0,0},{2,2},{4,4},{6,6},{8,8},{10,10},{12,12},{14,14},{1,256},{3,2... | collective-permute-start | bytes 221192 | tf_op jit(solution)/shard_map/ppermute | solution.py:196
  15.2 4.8 %collective-permute-start.1 = (bf16[24,1536]{1,0:T(8,128)(2,1)}, bf16[24,1536]{1,0:T(8,128)(2,1)S(1)}, u32[]{:S(2)}, u32[]{:S(2)}) collective-permute-start(bf16[24,1536]{1,0:T(8,128)(2,1)} %get-tuple-element.26), channel_id=1, source_target_pairs={{0,0},{2,2},{4,4},{6,6},{8,8},{10,10},{12,12},{14,14},{1,256},{3,2... | collective-permute-start | bytes 221192 | tf_op jit(solution)/shard_map/ppermute | solution.py:196
  20.0 5.1 %collective-permute-start.2 = (bf16[24,1536]{1,0:T(8,128)(2,1)}, bf16[24,1536]{1,0:T(8,128)(2,1)S(1)}, u32[]{:S(2)}, u32[]{:S(2)}) collective-permute-start(bf16[24,1536]{1,0:T(8,128)(2,1)} %get-tuple-element.27), channel_id=1, source_target_pairs={{0,0},{2,2},{4,4},{6,6},{8,8},{10,10},{12,12},{14,14},{1,256},{3,2... | collective-permute-start | bytes 221192 | tf_op jit(solution)/shard_map/ppermute | solution.py:196
  25.7 2.9 %collective-permute-done.2.refs_2_ = bf16[24,1536]{1,0:T(8,128)(2,1)S(1)} collective-permute-done((bf16[24,1536]{1,0:T(8,128)(2,1)}, bf16[24,1536]{1,0:T(8,128)(2,1)S(1)}, u32[]{:S(2)}, u32[]{:S(2)}) %collective-permute-start.2) | collective-permute-done | bytes 73760 | tf_op jit(solution)/shard_map/ppermute | solution.py:196
  31.0 13.2 %all_gather.84 = bf16[144,1536]{1,0:T(8,128)(2,1)} all-gather(bf16[72,1536]{1,0:T(8,128)(2,1)} %bitcast.76), channel_id=1, replica_groups=mesh['xh'=2,'xl'=2,'yh'=4,'core'=2,'section'=8,'cfg'=2] {'xh'}, dimensions={0}, use_global_device_ids=true | all-gather | bytes 663552 | tf_op jit(solution)/shard_map/all_gather | solution.py:198
  46.1 6.9 %all-to-all-start = ((bf16[32,16,768]{2,1,0:T(8,128)(2,1)}), bf16[32,16,768]{2,1,0:T(8,128)(2,1)S(1)}, u32[]{:S(2)}, u32[]{:S(2)}) async-start(bf16[32,16,768]{2,1,0:T(8,128)(2,1)} %bitcast.15), calls=%async_computation | async-start | bytes 1572864 | tf_op jit(solution)/shard_map/all_to_all | solution.py:210
  55.1 7.8 %all_gather.85 = bf16[64,1536]{1,0:T(8,128)(2,1)S(1)} all-gather(bf16[16,1536]{1,0:T(8,128)(2,1)S(1)} %bitcast.84), channel_id=1, replica_groups=mesh['xh'=2,'xl'=2,'yh'=4,'core'=2,'section'=8,'cfg'=2] {'xl','core'}, dimensions={0}, use_global_device_ids=true | all-gather | bytes 245760 | tf_op jit(solution)/shard_map/all_gather | solution.py:213
  62.9 17.4 %all-to-all-done = bf16[32,16,768]{2,1,0:T(8,128)(2,1)S(1)} async-done(((bf16[32,16,768]{2,1,0:T(8,128)(2,1)}), bf16[32,16,768]{2,1,0:T(8,128)(2,1)S(1)}, u32[]{:S(2)}, u32[]{:S(2)}) %all-to-all-start) | async-done | bytes 786464 | tf_op jit(solution)/shard_map/all_to_all | solution.py:210
  80.3 28.1 %all-gather.18.cloned.1.call-done.w_ref = bf16[1152,1536]{1,0:T(8,128)(2,1)} async-done(((bf16[144,1536]{1,0:T(8,128)(2,1)}), bf16[1152,1536]{1,0:T(8,128)(2,1)}) %all-gather.18.cloned.1.call-update) | async-done | bytes 3538960 | tf_op jit(solution)/shard_map/all_gather | solution.py:199
  112.9 4.2 %all-gather = bf16[128,384]{1,0:T(8,128)(2,1)S(1)} all-gather(bf16[64,384]{1,0:T(8,128)(2,1)S(1)} %get-tuple-element.30), channel_id=2, replica_groups={{0,2},{4,6},{8,10},{12,14},{1,3},{5,7},{9,11},{13,15},{16,18},{20,22},{..., dimensions={0}, use_global_device_ids=true | all-gather | bytes 147456 | tf_op jit(solution)/shard_map/all_gather | solution.py:237
  117.1 6.7 %all-gather.9 = bf16[256,384]{1,0:T(8,128)(2,1)S(1)} all-gather(bf16[64,384]{1,0:T(8,128)(2,1)S(1)} %slice.82), channel_id=11, replica_groups=mesh['xh'=2,'xl'=2,'yh'=4,'core'=2,'section'=8,'cfg'=2] {'xl','core'}, dimensions={0}, use_global_device_ids=true | all-gather | bytes 245760 | tf_op jit(solution)/shard_map/all_gather | solution.py:238
  126.3 11.1 %all-gather.1 = bf16[128,384]{1,0:T(8,128)(2,1)S(1)} all-gather(bf16[64,384]{1,0:T(8,128)(2,1)S(1)} %get-tuple-element.32), channel_id=3, replica_groups={{2,4},{6,8},{10,12},{14,0},{3,5},{7,9},{11,13},{15,1},{18,20},{22,24},{..., dimensions={0}, use_global_device_ids=true | all-gather | bytes 147456 | tf_op jit(solution)/shard_map/all_gather | solution.py:237
  137.5 6.1 %all-gather.10 = bf16[256,384]{1,0:T(8,128)(2,1)S(1)} all-gather(bf16[64,384]{1,0:T(8,128)(2,1)S(1)} %slice.83), channel_id=12, replica_groups=mesh['xh'=2,'xl'=2,'yh'=4,'core'=2,'section'=8,'cfg'=2] {'xl','core'}, dimensions={0}, use_global_device_ids=true | all-gather | bytes 245760 | tf_op jit(solution)/shard_map/all_gather | solution.py:238
  143.6 2.5 %block_step.10 = (bf16[64,384]{1,0:T(8,128)(2,1)S(1)}, bf16[64,768]{1,0:T(8,128)(2,1)S(1)}) custom-call(s32[2]{0:T(128)S(1)} %pad_add_fusion.who, bf16[4,64,384]{2,1,0:T(8,128)(2,1)S(1)} %bitcast.70, bf16[1152,1536]{1,0:T(8,128)(2,1)S(1)} %copy-done.2, bf16[512,768]{1,0:T(8,128)(2,1)S(1)} %bitcast.61, f32[2,1536]{1,0:T(2,128)S(1)} %reshape.267.mod_ref, ...), custom_call_target="tpu_custom_call" | custom-call | tf_op jit(solution)/shard_map/block_step/pallas_call | solution.py:145
  146.0 3.6 %all-gather.2 = bf16[128,384]{1,0:T(8,128)(2,1)S(1)} all-gather(bf16[64,384]{1,0:T(8,128)(2,1)S(1)} %get-tuple-element.34), channel_id=4, replica_groups={{0,2},{4,6},{8,10},{12,14},{1,3},{5,7},{9,11},{13,15},{16,18},{20,22},{..., dimensions={0}, use_global_device_ids=true | all-gather | bytes 147456 | tf_op jit(solution)/shard_map/all_gather | solution.py:237
  149.7 6.7 %all-gather.11 = bf16[256,384]{1,0:T(8,128)(2,1)S(1)} all-gather(bf16[64,384]{1,0:T(8,128)(2,1)S(1)} %slice.84), channel_id=13, replica_groups=mesh['xh'=2,'xl'=2,'yh'=4,'core'=2,'section'=8,'cfg'=2] {'xl','core'}, dimensions={0}, use_global_device_ids=true | all-gather | bytes 245760 | tf_op jit(solution)/shard_map/all_gather | solution.py:238
  156.4 2.5 %block_step.11 = (bf16[64,384]{1,0:T(8,128)(2,1)S(1)}, bf16[64,768]{1,0:T(8,128)(2,1)S(1)}) custom-call(s32[2]{0:T(128)S(1)} %pad_add_fusion.who, bf16[4,64,384]{2,1,0:T(8,128)(2,1)S(1)} %bitcast.71, bf16[1152,1536]{1,0:T(8,128)(2,1)S(1)} %copy-done.2, bf16[512,768]{1,0:T(8,128)(2,1)S(1)} %bitcast.62, f32[2,1536]{1,0:T(2,128)S(1)} %reshape.267.mod_ref, ...), custom_call_target="tpu_custom_call" | custom-call | tf_op jit(solution)/shard_map/block_step/pallas_call | solution.py:145
  158.9 4.9 %all-gather.3 = bf16[128,384]{1,0:T(8,128)(2,1)S(1)} all-gather(bf16[64,384]{1,0:T(8,128)(2,1)S(1)} %get-tuple-element.36), channel_id=5, replica_groups={{2,4},{6,8},{10,12},{14,0},{3,5},{7,9},{11,13},{15,1},{18,20},{22,24},{..., dimensions={0}, use_global_device_ids=true | all-gather | bytes 147456 | tf_op jit(solution)/shard_map/all_gather | solution.py:237
  163.8 6.6 %all-gather.12 = bf16[256,384]{1,0:T(8,128)(2,1)S(1)} all-gather(bf16[64,384]{1,0:T(8,128)(2,1)S(1)} %slice.85), channel_id=14, replica_groups=mesh['xh'=2,'xl'=2,'yh'=4,'core'=2,'section'=8,'cfg'=2] {'xl','core'}, dimensions={0}, use_global_device_ids=true | all-gather | bytes 245760 | tf_op jit(solution)/shard_map/all_gather | solution.py:238
  170.5 2.5 %block_step.12 = (bf16[64,384]{1,0:T(8,128)(2,1)S(1)}, bf16[64,768]{1,0:T(8,128)(2,1)S(1)}) custom-call(s32[2]{0:T(128)S(1)} %pad_add_fusion.who, bf16[4,64,384]{2,1,0:T(8,128)(2,1)S(1)} %bitcast.72, bf16[1152,1536]{1,0:T(8,128)(2,1)S(1)} %copy-done.2, bf16[512,768]{1,0:T(8,128)(2,1)S(1)} %bitcast.63, f32[2,1536]{1,0:T(2,128)S(1)} %reshape.267.mod_ref, ...), custom_call_target="tpu_custom_call" | custom-call | tf_op jit(solution)/shard_map/block_step/pallas_call | solution.py:145
  173.0 3.6 %all-gather.4 = bf16[128,384]{1,0:T(8,128)(2,1)S(1)} all-gather(bf16[64,384]{1,0:T(8,128)(2,1)S(1)} %get-tuple-element.38), channel_id=6, replica_groups={{0,2},{4,6},{8,10},{12,14},{1,3},{5,7},{9,11},{13,15},{16,18},{20,22},{..., dimensions={0}, use_global_device_ids=true | all-gather | bytes 147456 | tf_op jit(solution)/shard_map/all_gather | solution.py:237
  176.6 6.7 %all-gather.13 = bf16[256,384]{1,0:T(8,128)(2,1)S(1)} all-gather(bf16[64,384]{1,0:T(8,128)(2,1)S(1)} %slice.86), channel_id=15, replica_groups=mesh['xh'=2,'xl'=2,'yh'=4,'core'=2,'section'=8,'cfg'=2] {'xl','core'}, dimensions={0}, use_global_device_ids=true | all-gather | bytes 245760 | tf_op jit(solution)/shard_map/all_gather | solution.py:238
  183.3 2.5 %block_step.13 = (bf16[64,384]{1,0:T(8,128)(2,1)S(1)}, bf16[64,768]{1,0:T(8,128)(2,1)S(1)}) custom-call(s32[2]{0:T(128)S(1)} %pad_add_fusion.who, bf16[4,64,384]{2,1,0:T(8,128)(2,1)S(1)} %bitcast.73, bf16[1152,1536]{1,0:T(8,128)(2,1)S(1)} %copy-done.2, bf16[512,768]{1,0:T(8,128)(2,1)S(1)} %bitcast.64, f32[2,1536]{1,0:T(2,128)S(1)} %reshape.267.mod_ref, ...), custom_call_target="tpu_custom_call" | custom-call | tf_op jit(solution)/shard_map/block_step/pallas_call | solution.py:145
  185.8 4.9 %all-gather.5 = bf16[128,384]{1,0:T(8,128)(2,1)S(1)} all-gather(bf16[64,384]{1,0:T(8,128)(2,1)S(1)} %get-tuple-element.40), channel_id=7, replica_groups={{2,4},{6,8},{10,12},{14,0},{3,5},{7,9},{11,13},{15,1},{18,20},{22,24},{..., dimensions={0}, use_global_device_ids=true | all-gather | bytes 147456 | tf_op jit(solution)/shard_map/all_gather | solution.py:237
  190.7 6.8 %all-gather.14 = bf16[256,384]{1,0:T(8,128)(2,1)S(1)} all-gather(bf16[64,384]{1,0:T(8,128)(2,1)S(1)} %slice.87), channel_id=16, replica_groups=mesh['xh'=2,'xl'=2,'yh'=4,'core'=2,'section'=8,'cfg'=2] {'xl','core'}, dimensions={0}, use_global_device_ids=true | all-gather | bytes 245760 | tf_op jit(solution)/shard_map/all_gather | solution.py:238
  200.0 3.6 %all-gather.6 = bf16[128,384]{1,0:T(8,128)(2,1)S(1)} all-gather(bf16[64,384]{1,0:T(8,128)(2,1)S(1)} %get-tuple-element.42), channel_id=8, replica_groups={{0,2},{4,6},{8,10},{12,14},{1,3},{5,7},{9,11},{13,15},{16,18},{20,22},{..., dimensions={0}, use_global_device_ids=true | all-gather | bytes 147456 | tf_op jit(solution)/shard_map/all_gather | solution.py:237
  203.7 6.7 %all-gather.15 = bf16[256,384]{1,0:T(8,128)(2,1)S(1)} all-gather(bf16[64,384]{1,0:T(8,128)(2,1)S(1)} %slice.88), channel_id=17, replica_groups=mesh['xh'=2,'xl'=2,'yh'=4,'core'=2,'section'=8,'cfg'=2] {'xl','core'}, dimensions={0}, use_global_device_ids=true | all-gather | bytes 245760 | tf_op jit(solution)/shard_map/all_gather | solution.py:238
  210.4 2.5 %block_step.15 = (bf16[64,384]{1,0:T(8,128)(2,1)S(1)}, bf16[64,768]{1,0:T(8,128)(2,1)S(1)}) custom-call(s32[2]{0:T(128)S(1)} %pad_add_fusion.who, bf16[4,64,384]{2,1,0:T(8,128)(2,1)S(1)} %bitcast.68, bf16[1152,1536]{1,0:T(8,128)(2,1)S(1)} %copy-done.2, bf16[512,768]{1,0:T(8,128)(2,1)S(1)} %bitcast.66, f32[2,1536]{1,0:T(2,128)S(1)} %reshape.267.mod_ref, ...), custom_call_target="tpu_custom_call" | custom-call | tf_op jit(solution)/shard_map/block_step/pallas_call | solution.py:145
  212.9 5.6 %all-gather.7 = bf16[256,384]{1,0:T(8,128)(2,1)S(1)} all-gather(bf16[64,384]{1,0:T(8,128)(2,1)S(1)} %get-tuple-element.44), channel_id=9, replica_groups=mesh['xh'=2,'xl'=2,'yh'=4,'core'=2,'section'=8,'cfg'=2] {'xl','core'}, dimensions={0}, use_global_device_ids=true | all-gather | bytes 245760 | tf_op jit(solution)/shard_map/all_gather | solution.py:240
  218.5 6.6 %all-gather.8 = bf16[256,768]{1,0:T(8,128)(2,1)S(1)} all-gather(bf16[64,768]{1,0:T(8,128)(2,1)S(1)} %get-tuple-element.47), channel_id=10, replica_groups=mesh['xh'=2,'xl'=2,'yh'=4,'core'=2,'section'=8,'cfg'=2] {'xl','core'}, dimensions={0}, use_global_device_ids=true | all-gather | bytes 491520 | tf_op jit(solution)/shard_map/all_gather | solution.py:246
  225.9 4.2 %all-to-all-start.1 = ((bf16[16,2,768]{2,1,0:T(2,128)(2,1)}), bf16[16,2,768]{2,1,0:T(2,128)(2,1)S(1)}, u32[]{:S(2)}, u32[]{:S(2)}) async-start(bf16[16,2,768]{2,1,0:T(2,128)(2,1)} %bitcast.29), calls=%async_computation.1 | async-start | bytes 98304 | tf_op jit(solution)/shard_map/all_to_all | solution.py:245
  230.9 6.8 %all-to-all-done.1 = bf16[16,2,768]{2,1,0:T(2,128)(2,1)S(1)} async-done(((bf16[16,2,768]{2,1,0:T(2,128)(2,1)}), bf16[16,2,768]{2,1,0:T(2,128)(2,1)S(1)}, u32[]{:S(2)}, u32[]{:S(2)}) %all-to-all-start.1) | async-done | bytes 49184 | tf_op jit(solution)/shard_map/all_to_all | solution.py:245
  (61 shorter events, 21.3 us)
Async XLA Ops:
  7.2 46.5 %copy-start = (f32[1,1,28,4608]{3,1,2,0:T(1,128)S(1)}, f32[1,1,28,4608]{3,1,2,0:T(1,128)}, u32[]{:S(2)}) copy-start(f32[1,1,28,4608]{3,1,2,0:T(1,128)} %param.10) | copy-start | bytes 1548292
  7.2 48.0 %copy-start.7 = (bf16[1,16,1536]{2,1,0:T(8,128)(2,1)S(1)}, bf16[1,16,1536]{2,1,0:T(8,128)(2,1)}, u32[]{:S(2)}) copy-start(bf16[1,16,1536]{2,1,0:T(8,128)(2,1)} %param.7) | copy-start | bytes 147460
  7.2 46.7 %copy-start.3 = (s32[64]{0:T(128)S(1)}, s32[64]{0:T(128)}, u32[]{:S(2)}) copy-start(s32[64]{0:T(128)} %param.9) | copy-start | bytes 772
  7.2 101.2 %all-gather.18.cloned.1.call-start = ((), (), s32[]{:S(2)}) async-start(), calls=%async_computation.2 | async-start | bytes 3981312 | tf_op jit(solution)/shard_map/all_gather | solution.py:199
  10.6 14.6 %collective-permute-start = (bf16[24,1536]{1,0:T(8,128)(2,1)}, bf16[24,1536]{1,0:T(8,128)(2,1)S(1)}, u32[]{:S(2)}, u32[]{:S(2)}) collective-permute-start(bf16[24,1536]{1,0:T(8,128)(2,1)} %get-tuple-element.25), channel_id=1, source_target_pairs={{0,0},{2,2},{4,4},{6,6},{8,8},{10,10},{12,12},{14,14},{1,256},{3,2... | collective-permute-start | bytes 221192 | tf_op jit(solution)/shard_map/ppermute | solution.py:196
  15.2 10.5 %collective-permute-start.1 = (bf16[24,1536]{1,0:T(8,128)(2,1)}, bf16[24,1536]{1,0:T(8,128)(2,1)S(1)}, u32[]{:S(2)}, u32[]{:S(2)}) collective-permute-start(bf16[24,1536]{1,0:T(8,128)(2,1)} %get-tuple-element.26), channel_id=1, source_target_pairs={{0,0},{2,2},{4,4},{6,6},{8,8},{10,10},{12,12},{14,14},{1,256},{3,2... | collective-permute-start | bytes 221192 | tf_op jit(solution)/shard_map/ppermute | solution.py:196
  20.0 8.6 %collective-permute-start.2 = (bf16[24,1536]{1,0:T(8,128)(2,1)}, bf16[24,1536]{1,0:T(8,128)(2,1)S(1)}, u32[]{:S(2)}, u32[]{:S(2)}) collective-permute-start(bf16[24,1536]{1,0:T(8,128)(2,1)} %get-tuple-element.27), channel_id=1, source_target_pairs={{0,0},{2,2},{4,4},{6,6},{8,8},{10,10},{12,12},{14,14},{1,256},{3,2... | collective-permute-start | bytes 221192 | tf_op jit(solution)/shard_map/ppermute | solution.py:196
  25.2 3.5 %copy-start.4 = (bf16[24,1536]{1,0:T(8,128)(2,1)}, bf16[24,1536]{1,0:T(8,128)(2,1)S(1)}, u32[]{:S(2)}) copy-start(bf16[24,1536]{1,0:T(8,128)(2,1)S(1)} %collective-permute-done.refs_0_) | copy-start | bytes 221188
  25.7 2.9 %copy-start.5 = (bf16[24,1536]{1,0:T(8,128)(2,1)}, bf16[24,1536]{1,0:T(8,128)(2,1)S(1)}, u32[]{:S(2)}) copy-start(bf16[24,1536]{1,0:T(8,128)(2,1)S(1)} %collective-permute-done.1.refs_1_) | copy-start | bytes 221188
  28.6 0.6 copy-start.6
  46.1 34.3 %all-to-all-start = ((bf16[32,16,768]{2,1,0:T(8,128)(2,1)}), bf16[32,16,768]{2,1,0:T(8,128)(2,1)S(1)}, u32[]{:S(2)}, u32[]{:S(2)}) async-start(bf16[32,16,768]{2,1,0:T(8,128)(2,1)} %bitcast.15), calls=%async_computation | async-start | bytes 1572864 | tf_op jit(solution)/shard_map/all_to_all | solution.py:210
  108.4 2.0 copy-start.1
  110.4 13.5 %copy-start.2 = (bf16[1152,1536]{1,0:T(8,128)(2,1)S(1)}, bf16[1152,1536]{1,0:T(8,128)(2,1)}, u32[]{:S(2)}) copy-start(bf16[1152,1536]{1,0:T(8,128)(2,1)} %all-gather.18.cloned.1.call-done.w_ref) | copy-start | bytes 10616836
  225.9 11.8 %all-to-all-start.1 = ((bf16[16,2,768]{2,1,0:T(2,128)(2,1)}), bf16[16,2,768]{2,1,0:T(2,128)(2,1)S(1)}, u32[]{:S(2)}, u32[]{:S(2)}) async-start(bf16[16,2,768]{2,1,0:T(2,128)(2,1)} %bitcast.29), calls=%async_computation.1 | async-start | bytes 98304 | tf_op jit(solution)/shard_map/all_to_all | solution.py:245
Sparse Core Ops, SparseCore 0:
  44.3 64.0 all-gather.17

commit v3 on v2

--- a/solution.py
+++ b/solution.py
@@ -19,8 +19,11 @@
 PART = D // MEMBERS
 LOCAL = 16
 GROUP = LOCAL * MEMBERS
-UNIT = 24
-SHARE = 3 * UNIT
+UNIT = 48
+UNITS = 3
+COLUMNS = UNIT * UNITS
+HALF = D // 2
+BLOCK = 2 * COLUMNS
 
 guide_weight = 3.5
 norm_eps = 1e-06
@@ -29,53 +32,26 @@
 SIZES = (2, 2, 4, 2, 8, 2)
 
 
-def plan_weight_moves():
-    def plane(xh, xl, y, core):
-        return (((xh * 2 + xl) * 4 + y // 2) * 2 + core) * 2 + y % 2
-
-    left = [[] for _ in range(64)]
-    for unit in range(3 * D // UNIT):
-        source, slot = divmod(unit, 3)
-        part, within = divmod(unit, D // UNIT)
-        member, within = divmod(within, PART // UNIT)
-        place, target_slot = divmod(part * (PART // UNIT) + within, 3)
-        y, xh = divmod(place, 2)
-        target = plane(xh, member // 2, y, member % 2)
-        left[source].append((target, slot, target_slot))
-    rounds = []
-    for _ in range(3):
-        owner = {}
-
-        def place_edge(source, seen):
-            for edge in sorted(left[source], key=lambda e: e[0] != source):
-                if edge[0] in seen:
-                    continue
-                seen.add(edge[0])
-                if edge[0] not in owner or place_edge(owner[edge[0]][0], seen):
-                    owner[edge[0]] = (source, edge)
-                    return True
-            return False
-
-        for source in range(64):
-            if not place_edge(source, set()):
-                raise ValueError("no matching")
-        for source, edge in owner.values():
-            left[source].remove(edge)
-        rounds.append([(source, edge) for source, edge in owner.values()])
-    routes, send_slot, take = [], np.zeros((3, 64), np.int32), np.zeros((3, 64), np.int32)
-    for number, matched in enumerate(rounds):
-        route = []
-        for source, (target, slot, target_slot) in matched:
-            send_slot[number, source] = slot
-            take[target_slot, target] = number
-            for s in range(SECTIONS):
-                route.append(((source // 2 * 8 + s) * 2 + source % 2, (target // 2 * 8 + s) * 2 + target % 2))
-        routes.append(route)
-    return routes, send_slot, take
-
-
-ROUTES, SEND_SLOT, TAKE = plan_weight_moves()
-SLOTS = np.concatenate([SEND_SLOT.reshape(-1), TAKE.reshape(-1)])
+def route(step):
+    def number(x, y, core, section):
+        return (((x * 4 + y // 2) * 2 + core) * 8 + section) * 2 + y % 2
+
+    return [
+        (number(x, y, core, s), number(*step(x, y, core), s))
+        for x in range(4)
+        for y in range(8)
+        for core in range(2)
+        for s in range(SECTIONS)
+    ]
+
+
+SWAP = route(lambda x, y, core: (x, y, 1 - core))
+UP = route(lambda x, y, core: (x, (y + 1) % 8, core))
+DOWN = route(lambda x, y, core: (x, (y - 1) % 8, core))
+STARTS = np.zeros((MEMBERS, 3), np.int32)
+for _member in range(MEMBERS):
+    for _third in range(3):
+        STARTS[_member, (COLUMNS * 8 * ((_third - _member) % 4) + PART * _third) // D] = PART * _third
 PAIRS = (
     [[s, s + 1] for s in range(0, SECTIONS, 2)],
     [[s, (s + 1) % SECTIONS] for s in range(1, SECTIONS, 2)],
@@ -86,7 +62,7 @@
     return lax.dot_general(a, b, (((1,), (1,)), ((), ())), preferred_element_type=jnp.float32)
 
 
-def block_kernel(tick, who, x_ref, w_ref, kv_ref, mod_ref, gate_ref, cos_ref, sin_ref, block_ref, old_ref, state_ref, fresh_ref):
+def block_kernel(tick, who, x_ref, w_ref, kv_ref, mod_ref, gate_ref, cos_ref, sin_ref, block_ref, old_ref, state_ref, fresh_ref, projected):
     member = who[0]
     active = who[1] == tick
     xs = [x_ref[i].astype(jnp.float32) for i in range(MEMBERS)]
@@ -104,7 +80,7 @@
         ],
         axis=1,
     )
-    projected = nt_dot(normed, w_ref[...]).astype(jnp.bfloat16)
+    projected[...] = nt_dot(normed, w_ref[...]).astype(jnp.bfloat16)
     row_block = block_ref[...]
     stale_mask = lax.broadcasted_iota(jnp.int32, (GROUP, TOKENS), 1) // ROWS == row_block
     own_mask = (
@@ -121,9 +97,10 @@
     scale = 1.0 / math.sqrt(HDIM)
     for head in range(PART // HDIM):
         cols = slice(head * HDIM, (head + 1) * HDIM)
-        query = turned(projected[:, head * HDIM : (head + 1) * HDIM])
-        key = turned(projected[:, PART + head * HDIM : PART + (head + 1) * HDIM])
-        value = projected[:, 2 * PART + head * HDIM : 2 * PART + (head + 1) * HDIM]
+        query, key, value = (
+            projected[:, pl.ds(pl.multiple_of(who[2 + part] + head * HDIM, HDIM), HDIM)] for part in range(3)
+        )
+        query, key = turned(query), turned(key)
         weights = jnp.where(stale_mask, 0.0, jnp.exp(nt_dot(query, kv_ref[:, cols]) * scale))
         own = jnp.where(own_mask, jnp.exp(nt_dot(query, key) * scale), 0.0)
         total = jnp.sum(weights, axis=-1, keepdims=True) + jnp.sum(own, axis=-1, keepdims=True)
@@ -150,55 +127,72 @@
         ),
         in_specs=[pl.BlockSpec(memory_space=pltpu.SMEM)] + [vmem] * 9,
         out_specs=(vmem, vmem),
+        scratch_shapes=[pltpu.VMEM((GROUP, 3 * PART), jnp.bfloat16)],
         compiler_params=pltpu.CompilerParams(vmem_limit_bytes=24 * 1024 * 1024),
         name="block_step",
     )(who, x, weight, kv, mod, gate, cosine, sine, blocks, old)
 
 
-def pick_kernel(place, slots, half_ref, *outs):
-    for number in range(3):
-        outs[number][...] = half_ref[slots[number * 64 + place[0]]]
-
-
-def arrange_kernel(place, slots, *refs):
-    moved, out = refs[:3], refs[3]
-    for j in range(3):
-        number = slots[(3 + j) * 64 + place[0]]
-        for n in range(3):
-
-            @pl.when(number == n)
-            def _():
-                out[j] = moved[n][...]
-
-
-def move_units(kernel, place, units, outs):
-    smem = pl.BlockSpec(memory_space=pltpu.SMEM)
+def pick_kernel(where, x_ref, keep_ref, send_ref):
+    member, first, core = where[0], where[1], where[2]
+    peer = member + 1 - 2 * core
+    for j in range(UNITS):
+        third = (first + j * UNIT) // PART
+        keep_ref[j * UNIT : (j + 1) * UNIT, :] = x_ref[(third - member + 4) % 4, j * UNIT : (j + 1) * UNIT, :]
+        send_ref[j * UNIT : (j + 1) * UNIT, :] = x_ref[(third - peer + 4) % 4, j * UNIT : (j + 1) * UNIT, :]
+
+
+def place_kernel(where, own, up1, up2, up3, down1, down2, down3, up4, down4, out_ref):
+    core, y = where[2], where[3]
+
+    def put(source, part, ref):
+        at = (y + source + 8) % 8
+        row = pl.multiple_of(at // 2 * BLOCK + (core + part) % 2 * COLUMNS, 16)
+        col = pl.multiple_of(at % 2 * HALF, 128)
+        out_ref[pl.ds(row, COLUMNS), pl.ds(col, HALF)] = ref[...]
+
+    for source, ref in ((0, own), (-1, up1), (-2, up2), (-3, up3), (1, down1), (2, down2), (3, down3)):
+        put(source, 0, ref.at[:COLUMNS])
+        put(source, 1, ref.at[COLUMNS:])
+    put(4, 0, up4)
+    put(4, 1, down4)
+
+
+def whole_call(kernel, where, arrays, outs):
     vmem = pl.BlockSpec(memory_space=pltpu.VMEM)
     return pl.pallas_call(
         kernel,
         out_shape=[jax.ShapeDtypeStruct(shape, jnp.bfloat16) for shape in outs],
-        in_specs=[smem, smem] + [vmem] * len(units),
+        in_specs=[pl.BlockSpec(memory_space=pltpu.SMEM)] + [vmem] * len(arrays),
         out_specs=[vmem] * len(outs),
+        compiler_params=pltpu.CompilerParams(vmem_limit_bytes=24 * 1024 * 1024),
         name=kernel.__name__,
-    )(place, jnp.asarray(SLOTS), *units)
+    )(where, *arrays)
 
 
 def body(hidden, timestep, patch_order, modulation, qkv_weight, stale_kv):
     index = {a: lax.axis_index(a) for a in AXES}
     section = index["section"]
     member = index["xl"] * 2 + index["core"]
-    place = (((index["xh"] * 2 + index["xl"]) * 4 + index["yh"]) * 2 + index["core"]) * 2 + index["cfg"]
-    place = place.astype(jnp.int32).reshape(1)
-
-    columns = jnp.transpose(qkv_weight[0])
-    half = lax.dynamic_slice_in_dim(columns, index["cfg"] * SHARE, SHARE, 0).reshape(3, UNIT, D)
-    sent = move_units(pick_kernel, place, [half], [(UNIT, D)] * 3)
-    moved = [lax.ppermute(sent[number], AXES, ROUTES[number]) for number in range(3)]
-    (share,) = move_units(arrange_kernel, place, moved, [(3, UNIT, D)])
-    share = lax.all_gather(share.reshape(SHARE, D), "xh", axis=0, tiled=True)
-    weight = lax.all_gather(share, ("yh", "cfg"), axis=0, tiled=True)
-
-    share, stale_rows, entering = lax.optimization_barrier((share, stale_kv[0, 0], hidden[0]))
+    y = index["yh"] * 2 + index["cfg"]
+    first = (index["yh"] * 2 + index["core"]) * COLUMNS
+    starts = jnp.asarray(STARTS)[member]
+    where = jnp.stack([member, first, index["core"], y]).astype(jnp.int32)
+    who = jnp.concatenate([jnp.stack([member, section]).astype(jnp.int32), starts])
+
+    columns = lax.dynamic_slice_in_dim(jnp.transpose(qkv_weight[0]), index["cfg"] * HALF, HALF, 1)
+    columns = lax.all_gather(columns, ("xh", "xl"), axis=0, tiled=False)
+    keep, send = whole_call(pick_kernel, where, [columns], [(COLUMNS, HALF)] * 2)
+    own = jnp.concatenate([keep, lax.ppermute(send, AXES, SWAP)])
+    own, stale_rows = lax.optimization_barrier((own, stale_kv[0, 0]))
+    up, down = [own], [own]
+    for _ in range(3):
+        up.append(lax.ppermute(up[-1], AXES, UP))
+        down.append(lax.ppermute(down[-1], AXES, DOWN))
+    up4 = lax.ppermute(up[3][:COLUMNS], AXES, UP)
+    down4 = lax.ppermute(down[3][COLUMNS:], AXES, DOWN)
+    (weight,) = whole_call(place_kernel, where, [own, *up[1:], *down[1:], up4, down4], [(3 * PART, D)])
+
     pieces = [
         jnp.concatenate(
             [stale_rows[:, m * PART : (m + 1) * PART], stale_rows[:, D + m * PART : D + (m + 1) * PART]], axis=1
@@ -210,6 +204,7 @@
     kv = lax.all_to_all(outgoing, ("xh", "xl", "yh", "core"), split_axis=0, concat_axis=0, tiled=True)
     kv = kv.reshape(TOKENS, 2 * PART)
 
+    entering, _ = lax.optimization_barrier((hidden[0], up[1]))
     x = lax.all_gather(entering, ("xl", "core"), axis=0, tiled=True)
     x = jnp.transpose(x.reshape(GROUP, MEMBERS, PART), (1, 0, 2))
 
@@ -229,7 +224,6 @@
     cosine = jnp.concatenate([cosine, cosine], axis=1)
     sine = jnp.concatenate([-sine, sine], axis=1)
 
-    who = jnp.stack([member, section]).astype(jnp.int32)
     fresh = jnp.zeros((GROUP, 2 * PART), jnp.bfloat16)
     for tick in range(SECTIONS):
         state, fresh = run_block(tick, who, x, weight, kv, mod, gate, cosine, sine, blocks[:, None], fresh)

time: 246 us -> 233 us (0.947)
  waiting for transfers between devices: 55.7 us -> 17.6 us
  starting transfers between devices: 25.6 us -> 55.1 us
  between operations: 15 us -> 1.7 us
  local copies, waits for them, and re-layouts: 8.8 us -> 15.7 us
    ppermute x3 -> x9, starting transfers between devices: 14.5 us -> 45.1 us  [the longest x3 22.7 us: body(): down.append(lax.ppermute(down[-1], AXES, DOWN))]
    all_gather x1 -> x0, waiting for transfers between devices: 28.1 us -> none  [body(): weight = lax.all_gather(share, ('yh', 'cfg'), axis=0, tiled=True)]
    all_to_all x1, waiting for transfers between devices: 17.4 us -> 0.01 us  [body(): lax.all_to_all(outgoing, ('xh', 'xl', 'yh', 'core'), split_axis=0, concat...]
    ppermute x3 -> x9, waiting for transfers between devices: 3.44 us -> 17.4 us  [the longest x3 16.3 us: body(): up.append(lax.ppermute(up[-1], AXES, UP))]
    all_to_all x1, waiting for transfers between devices: 6.78 us -> 0.22 us  [body(): lax.all_to_all(finals, ('section', 'cfg'), split_axis=0, concat_axis=0, t...]
    unnamed x16 -> x20, local copies, waits for them, and re-layouts: 2.66 us -> 7.55 us
    pallas_call x8, Pallas kernels: 19.8 us -> 23.4 us  [run_block(): pl.pallas_call(functools.partial(block_kernel, tick), out_shape=(jax.Shap...]
  transfers between devices with their start and end apart: 6 -> 11, of which waited for: 5 -> 4; matrix products, arithmetic and copies ran while one was open for 2% -> 3% of each run, Pallas kernels for 0% -> 1%
where the time goes in v3:
time: 233 us; the launch traced here: 232 us
  blocking collectives  115 us (49%)
  starting transfers between devices  55.1 us (24%)
  Pallas kernels  25.2 us (11%)
  waiting for transfers between devices  17.6 us (8%)
  local copies, waits for them, and re-layouts  15.7 us (7%)
    all_gather x7, blocking collectives, body(): x = lax.all_gather(state, ('xl', 'core'), axis=0, tiled=False)  45.9 us
    all_gather x7, blocking collectives, body(): lax.all_gather(state, 'section', axis=0, tiled=False, axis_index_groups=P...  36.4 us
    pallas_call x8, Pallas kernels, run_block(): pl.pallas_call(functools.partial(block_kernel, tick), out_shape=(jax.Shap...  23.4 us
    ppermute x3, starting transfers between devices, body(): down.append(lax.ppermute(down[-1], AXES, DOWN))  22.7 us
    ppermute x3, waiting for transfers between devices, body(): up.append(lax.ppermute(up[-1], AXES, UP))  16.3 us
    all_gather x1, blocking collectives, body(): columns = lax.all_gather(columns, ('xh', 'xl'), axis=0, tiled=False)  12.3 us
    ppermute x1, starting transfers between devices, body(): own = jnp.concatenate([keep, lax.ppermute(send, AXES, SWAP)])  10.2 us
    all_gather x1, blocking collectives, body(): x = lax.all_gather(entering, ('xl', 'core'), axis=0, tiled=True)  7.82 us
  transfers between devices with their start and end apart: 11, of which 4 were waited for; matrix products, arithmetic and copies ran while one was open for 3% of the time, Pallas kernels for 1%

profile of v3, /device:TPU:1, one launch (start us, length us, event | category | flops | bytes accessed | tf_op | source)
XLA Modules:
  0.0 231.8 jit_solution(4822745719785702566)
XLA Ops:
  1.7 12.3 %all-gather = bf16[576,768]{1,0:T(8,128)(2,1)S(1)} all-gather(bf16[144,768]{1,0:T(8,128)(2,1)S(1)} %dynamic-slice_bitcast_fusion), channel_id=2, replica_groups=mesh['xh'=2,'xl'=2,'yh'=4,'core'=2,'section'=8,'cfg'=2] {'xh','xl'}, dimensions={0}, use_global_device_ids=true | all-gather | bytes 1105920 | tf_op jit(solution)/shard_map/all_gather | solution.py:184
  14.6 10.2 %collective-permute-start = (bf16[144,768]{1,0:T(8,128)(2,1)S(1)}, bf16[144,768]{1,0:T(8,128)(2,1)S(1)}, u32[]{:S(2)}, u32[]{:S(2)}) collective-permute-start(bf16[144,768]{1,0:T(8,128)(2,1)S(1)} %get-tuple-element.26), channel_id=1, source_target_pairs={{0,16},{2,18},{4,20},{6,22},{8,24},{10,26},{12,28},{14,30},{16,0},... | collective-permute-start | bytes 663560 | tf_op jit(solution)/shard_map/ppermute | solution.py:186
  27.9 4.6 %collective-permute-start.4 = (bf16[288,768]{1,0:T(8,128)(2,1)S(1)}, bf16[288,768]{1,0:T(8,128)(2,1)S(1)}, u32[]{:S(2)}, u32[]{:S(2)}) collective-permute-start(bf16[288,768]{1,0:T(8,128)(2,1)S(1)} %pad_maximum_fusion.own), channel_id=1, source_target_pairs={{0,97},{2,99},{4,101},{6,103},{8,105},{10,107},{12,109},{14,111},{... | collective-permute-start | bytes 1327112 | tf_op jit(solution)/shard_map/ppermute | solution.py:191
  34.4 5.8 %all-to-all-start = ((bf16[32,16,768]{2,1,0:T(8,128)(2,1)}), bf16[32,16,768]{2,1,0:T(8,128)(2,1)S(1)}, u32[]{:S(2)}, u32[]{:S(2)}) async-start(bf16[32,16,768]{2,1,0:T(8,128)(2,1)} %bitcast.17), calls=%async_computation | async-start | bytes 1572864 | tf_op jit(solution)/shard_map/all_to_all | solution.py:204
  44.3 13.6 %collective-permute-start.5 = (bf16[288,768]{1,0:T(8,128)(2,1)S(1)}, bf16[288,768]{1,0:T(8,128)(2,1)S(1)}, u32[]{:S(2)}, u32[]{:S(2)}) collective-permute-start(bf16[288,768]{1,0:T(8,128)(2,1)S(1)} %collective-permute-done.4.down1), channel_id=1, source_target_pairs={{0,97},{2,99},{4,101},{6,103},{8,105},{10,107},{12,109},{14,111},{... | collective-permute-start | bytes 1327112 | tf_op jit(solution)/shard_map/ppermute | solution.py:191
  59.4 9.6 %collective-permute-done.2.up2 = bf16[288,768]{1,0:T(8,128)(2,1)S(1)} collective-permute-done((bf16[288,768]{1,0:T(8,128)(2,1)S(1)}, bf16[288,768]{1,0:T(8,128)(2,1)S(1)}, u32[]{:S(2)}, u32[]{:S(2)}) %collective-permute-start.2) | collective-permute-done | bytes 442400 | tf_op jit(solution)/shard_map/ppermute | solution.py:190
  71.0 4.6 %collective-permute-start.6 = (bf16[288,768]{1,0:T(8,128)(2,1)S(1)}, bf16[288,768]{1,0:T(8,128)(2,1)S(1)}, u32[]{:S(2)}, u32[]{:S(2)}) collective-permute-start(bf16[288,768]{1,0:T(8,128)(2,1)S(1)} %collective-permute-done.5.down2), channel_id=1, source_target_pairs={{0,97},{2,99},{4,101},{6,103},{8,105},{10,107},{12,109},{14,111},{... | collective-permute-start | bytes 1327112 | tf_op jit(solution)/shard_map/ppermute | solution.py:191
  76.4 6.7 %collective-permute-done.3.up3 = bf16[288,768]{1,0:T(8,128)(2,1)S(1)} collective-permute-done((bf16[288,768]{1,0:T(8,128)(2,1)S(1)}, bf16[288,768]{1,0:T(8,128)(2,1)S(1)}, u32[]{:S(2)}, u32[]{:S(2)}) %collective-permute-start.3) | collective-permute-done | bytes 442400 | tf_op jit(solution)/shard_map/ppermute | solution.py:190
  86.4 4.6 %collective-permute-start.8 = (bf16[144,768]{1,0:T(8,128)(2,1)}, bf16[144,768]{1,0:T(8,128)(2,1)}, u32[]{:S(2)}, u32[]{:S(2)}) collective-permute-start(bf16[144,768]{1,0:T(8,128)(2,1)} %slice.91), channel_id=1, source_target_pairs={{0,97},{2,99},{4,101},{6,103},{8,105},{10,107},{12,109},{14,111},{... | collective-permute-start | bytes 663560 | tf_op jit(solution)/shard_map/ppermute | solution.py:193
  91.2 7.8 %all_gather.86 = bf16[64,1536]{1,0:T(8,128)(2,1)S(1)} all-gather(bf16[16,1536]{1,0:T(8,128)(2,1)} %bitcast.86), channel_id=1, replica_groups=mesh['xh'=2,'xl'=2,'yh'=4,'core'=2,'section'=8,'cfg'=2] {'xl','core'}, dimensions={0}, use_global_device_ids=true | all-gather | bytes 245760 | tf_op jit(solution)/shard_map/all_gather | solution.py:208
  107.2 2.9 %block_step.8 = (bf16[64,384]{1,0:T(8,128)(2,1)S(1)}, bf16[64,768]{1,0:T(8,128)(2,1)S(1)}) custom-call(s32[5]{0:T(128)S(1)} %pad_add_fusion.who, bf16[4,64,384]{2,1,0:T(8,128)(2,1)S(1)} %bitcast.71, bf16[1152,1536]{1,0:T(8,128)(2,1)S(1)} %copy-done.2, bf16[512,768]{1,0:T(8,128)(2,1)S(1)} %bitcast.62, f32[2,1536]{1,0:T(2,128)S(1)} %reshape.255.mod_ref, ...), custom_call_target="tpu_custom_call" | custom-call | tf_op jit(solution)/shard_map/block_step/pallas_call | solution.py:122
  110.1 4.8 %all-gather.1 = bf16[128,384]{1,0:T(8,128)(2,1)S(1)} all-gather(bf16[64,384]{1,0:T(8,128)(2,1)S(1)} %get-tuple-element.30), channel_id=3, replica_groups={{0,2},{4,6},{8,10},{12,14},{1,3},{5,7},{9,11},{13,15},{16,18},{20,22},{..., dimensions={0}, use_global_device_ids=true | all-gather | bytes 147456 | tf_op jit(solution)/shard_map/all_gather | solution.py:231
  114.9 6.1 %all-gather.10 = bf16[256,384]{1,0:T(8,128)(2,1)S(1)} all-gather(bf16[64,384]{1,0:T(8,128)(2,1)S(1)} %slice.92), channel_id=12, replica_groups=mesh['xh'=2,'xl'=2,'yh'=4,'core'=2,'section'=8,'cfg'=2] {'xl','core'}, dimensions={0}, use_global_device_ids=true | all-gather | bytes 245760 | tf_op jit(solution)/shard_map/all_gather | solution.py:232
  123.9 10.9 %all-gather.2 = bf16[128,384]{1,0:T(8,128)(2,1)S(1)} all-gather(bf16[64,384]{1,0:T(8,128)(2,1)S(1)} %get-tuple-element.32), channel_id=4, replica_groups={{2,4},{6,8},{10,12},{14,0},{3,5},{7,9},{11,13},{15,1},{18,20},{22,24},{..., dimensions={0}, use_global_device_ids=true | all-gather | bytes 147456 | tf_op jit(solution)/shard_map/all_gather | solution.py:231
  134.8 6.2 %all-gather.11 = bf16[256,384]{1,0:T(8,128)(2,1)S(1)} all-gather(bf16[64,384]{1,0:T(8,128)(2,1)S(1)} %slice.93), channel_id=13, replica_groups=mesh['xh'=2,'xl'=2,'yh'=4,'core'=2,'section'=8,'cfg'=2] {'xl','core'}, dimensions={0}, use_global_device_ids=true | all-gather | bytes 245760 | tf_op jit(solution)/shard_map/all_gather | solution.py:232
  141.0 2.9 %block_step.10 = (bf16[64,384]{1,0:T(8,128)(2,1)S(1)}, bf16[64,768]{1,0:T(8,128)(2,1)S(1)}) custom-call(s32[5]{0:T(128)S(1)} %pad_add_fusion.who, bf16[4,64,384]{2,1,0:T(8,128)(2,1)S(1)} %bitcast.74, bf16[1152,1536]{1,0:T(8,128)(2,1)S(1)} %copy-done.2, bf16[512,768]{1,0:T(8,128)(2,1)S(1)} %bitcast.64, f32[2,1536]{1,0:T(2,128)S(1)} %reshape.255.mod_ref, ...), custom_call_target="tpu_custom_call" | custom-call | tf_op jit(solution)/shard_map/block_step/pallas_call | solution.py:122
  143.9 3.6 %all-gather.3 = bf16[128,384]{1,0:T(8,128)(2,1)S(1)} all-gather(bf16[64,384]{1,0:T(8,128)(2,1)S(1)} %get-tuple-element.34), channel_id=5, replica_groups={{0,2},{4,6},{8,10},{12,14},{1,3},{5,7},{9,11},{13,15},{16,18},{20,22},{..., dimensions={0}, use_global_device_ids=true | all-gather | bytes 147456 | tf_op jit(solution)/shard_map/all_gather | solution.py:231
  147.5 6.7 %all-gather.12 = bf16[256,384]{1,0:T(8,128)(2,1)S(1)} all-gather(bf16[64,384]{1,0:T(8,128)(2,1)S(1)} %slice.94), channel_id=14, replica_groups=mesh['xh'=2,'xl'=2,'yh'=4,'core'=2,'section'=8,'cfg'=2] {'xl','core'}, dimensions={0}, use_global_device_ids=true | all-gather | bytes 245760 | tf_op jit(solution)/shard_map/all_gather | solution.py:232
  154.3 2.9 %block_step.11 = (bf16[64,384]{1,0:T(8,128)(2,1)S(1)}, bf16[64,768]{1,0:T(8,128)(2,1)S(1)}) custom-call(s32[5]{0:T(128)S(1)} %pad_add_fusion.who, bf16[4,64,384]{2,1,0:T(8,128)(2,1)S(1)} %bitcast.75, bf16[1152,1536]{1,0:T(8,128)(2,1)S(1)} %copy-done.2, bf16[512,768]{1,0:T(8,128)(2,1)S(1)} %bitcast.65, f32[2,1536]{1,0:T(2,128)S(1)} %reshape.255.mod_ref, ...), custom_call_target="tpu_custom_call" | custom-call | tf_op jit(solution)/shard_map/block_step/pallas_call | solution.py:122
  157.2 4.9 %all-gather.4 = bf16[128,384]{1,0:T(8,128)(2,1)S(1)} all-gather(bf16[64,384]{1,0:T(8,128)(2,1)S(1)} %get-tuple-element.36), channel_id=6, replica_groups={{2,4},{6,8},{10,12},{14,0},{3,5},{7,9},{11,13},{15,1},{18,20},{22,24},{..., dimensions={0}, use_global_device_ids=true | all-gather | bytes 147456 | tf_op jit(solution)/shard_map/all_gather | solution.py:231
  162.1 6.6 %all-gather.13 = bf16[256,384]{1,0:T(8,128)(2,1)S(1)} all-gather(bf16[64,384]{1,0:T(8,128)(2,1)S(1)} %slice.95), channel_id=15, replica_groups=mesh['xh'=2,'xl'=2,'yh'=4,'core'=2,'section'=8,'cfg'=2] {'xl','core'}, dimensions={0}, use_global_device_ids=true | all-gather | bytes 245760 | tf_op jit(solution)/shard_map/all_gather | solution.py:232
  168.8 2.9 %block_step.12 = (bf16[64,384]{1,0:T(8,128)(2,1)S(1)}, bf16[64,768]{1,0:T(8,128)(2,1)S(1)}) custom-call(s32[5]{0:T(128)S(1)} %pad_add_fusion.who, bf16[4,64,384]{2,1,0:T(8,128)(2,1)S(1)} %bitcast.76, bf16[1152,1536]{1,0:T(8,128)(2,1)S(1)} %copy-done.2, bf16[512,768]{1,0:T(8,128)(2,1)S(1)} %bitcast.66, f32[2,1536]{1,0:T(2,128)S(1)} %reshape.255.mod_ref, ...), custom_call_target="tpu_custom_call" | custom-call | tf_op jit(solution)/shard_map/block_step/pallas_call | solution.py:122
  171.7 3.6 %all-gather.5 = bf16[128,384]{1,0:T(8,128)(2,1)S(1)} all-gather(bf16[64,384]{1,0:T(8,128)(2,1)S(1)} %get-tuple-element.38), channel_id=7, replica_groups={{0,2},{4,6},{8,10},{12,14},{1,3},{5,7},{9,11},{13,15},{16,18},{20,22},{..., dimensions={0}, use_global_device_ids=true | all-gather | bytes 147456 | tf_op jit(solution)/shard_map/all_gather | solution.py:231
  175.3 6.9 %all-gather.14 = bf16[256,384]{1,0:T(8,128)(2,1)S(1)} all-gather(bf16[64,384]{1,0:T(8,128)(2,1)S(1)} %slice.96), channel_id=16, replica_groups=mesh['xh'=2,'xl'=2,'yh'=4,'core'=2,'section'=8,'cfg'=2] {'xl','core'}, dimensions={0}, use_global_device_ids=true | all-gather | bytes 245760 | tf_op jit(solution)/shard_map/all_gather | solution.py:232
  185.2 4.9 %all-gather.6 = bf16[128,384]{1,0:T(8,128)(2,1)S(1)} all-gather(bf16[64,384]{1,0:T(8,128)(2,1)S(1)} %get-tuple-element.40), channel_id=8, replica_groups={{2,4},{6,8},{10,12},{14,0},{3,5},{7,9},{11,13},{15,1},{18,20},{22,24},{..., dimensions={0}, use_global_device_ids=true | all-gather | bytes 147456 | tf_op jit(solution)/shard_map/all_gather | solution.py:231
  190.1 6.6 %all-gather.15 = bf16[256,384]{1,0:T(8,128)(2,1)S(1)} all-gather(bf16[64,384]{1,0:T(8,128)(2,1)S(1)} %slice.97), channel_id=17, replica_groups=mesh['xh'=2,'xl'=2,'yh'=4,'core'=2,'section'=8,'cfg'=2] {'xl','core'}, dimensions={0}, use_global_device_ids=true | all-gather | bytes 245760 | tf_op jit(solution)/shard_map/all_gather | solution.py:232
  199.7 3.6 %all-gather.7 = bf16[128,384]{1,0:T(8,128)(2,1)S(1)} all-gather(bf16[64,384]{1,0:T(8,128)(2,1)S(1)} %get-tuple-element.42), channel_id=9, replica_groups={{0,2},{4,6},{8,10},{12,14},{1,3},{5,7},{9,11},{13,15},{16,18},{20,22},{..., dimensions={0}, use_global_device_ids=true | all-gather | bytes 147456 | tf_op jit(solution)/shard_map/all_gather | solution.py:231
  203.3 6.7 %all-gather.16 = bf16[256,384]{1,0:T(8,128)(2,1)S(1)} all-gather(bf16[64,384]{1,0:T(8,128)(2,1)S(1)} %slice.98), channel_id=18, replica_groups=mesh['xh'=2,'xl'=2,'yh'=4,'core'=2,'section'=8,'cfg'=2] {'xl','core'}, dimensions={0}, use_global_device_ids=true | all-gather | bytes 245760 | tf_op jit(solution)/shard_map/all_gather | solution.py:232
  210.0 2.9 %block_step.15 = (bf16[64,384]{1,0:T(8,128)(2,1)S(1)}, bf16[64,768]{1,0:T(8,128)(2,1)S(1)}) custom-call(s32[5]{0:T(128)S(1)} %pad_add_fusion.who, bf16[4,64,384]{2,1,0:T(8,128)(2,1)S(1)} %bitcast.72, bf16[1152,1536]{1,0:T(8,128)(2,1)S(1)} %copy-done.2, bf16[512,768]{1,0:T(8,128)(2,1)S(1)} %bitcast.69, f32[2,1536]{1,0:T(2,128)S(1)} %reshape.255.mod_ref, ...), custom_call_target="tpu_custom_call" | custom-call | tf_op jit(solution)/shard_map/block_step/pallas_call | solution.py:122
  213.0 5.6 %all-gather.8 = bf16[256,384]{1,0:T(8,128)(2,1)S(1)} all-gather(bf16[64,384]{1,0:T(8,128)(2,1)S(1)} %get-tuple-element.44), channel_id=10, replica_groups=mesh['xh'=2,'xl'=2,'yh'=4,'core'=2,'section'=8,'cfg'=2] {'xl','core'}, dimensions={0}, use_global_device_ids=true | all-gather | bytes 245760 | tf_op jit(solution)/shard_map/all_gather | solution.py:234
  219.5 4.2 %all-to-all-start.1 = ((bf16[16,2,768]{2,1,0:T(2,128)(2,1)}), bf16[16,2,768]{2,1,0:T(2,128)(2,1)S(1)}, u32[]{:S(2)}, u32[]{:S(2)}) async-start(bf16[16,2,768]{2,1,0:T(2,128)(2,1)} %bitcast.31), calls=%async_computation.1 | async-start | bytes 98304 | tf_op jit(solution)/shard_map/all_to_all | solution.py:239
  223.6 6.6 %all-gather.9 = bf16[256,768]{1,0:T(8,128)(2,1)S(1)} all-gather(bf16[64,768]{1,0:T(8,128)(2,1)S(1)} %get-tuple-element.47), channel_id=11, replica_groups=mesh['xh'=2,'xl'=2,'yh'=4,'core'=2,'section'=8,'cfg'=2] {'xl','core'}, dimensions={0}, use_global_device_ids=true | all-gather | bytes 491520 | tf_op jit(solution)/shard_map/all_gather | solution.py:240
  (79 shorter events, 37.2 us)
Async XLA Ops:
  0.6 58.7 %copy-start = (f32[1,1,28,4608]{3,1,2,0:T(1,128)S(1)}, f32[1,1,28,4608]{3,1,2,0:T(1,128)}, u32[]{:S(2)}) copy-start(f32[1,1,28,4608]{3,1,2,0:T(1,128)} %param.10) | copy-start | bytes 1548292
  0.6 40.3 %copy-start.9 = (s32[64]{0:T(128)S(1)}, s32[64]{0:T(128)}, u32[]{:S(2)}) copy-start(s32[64]{0:T(128)} %param.9) | copy-start | bytes 772
  14.6 11.3 %collective-permute-start = (bf16[144,768]{1,0:T(8,128)(2,1)S(1)}, bf16[144,768]{1,0:T(8,128)(2,1)S(1)}, u32[]{:S(2)}, u32[]{:S(2)}) collective-permute-start(bf16[144,768]{1,0:T(8,128)(2,1)S(1)} %get-tuple-element.26), channel_id=1, source_target_pairs={{0,16},{2,18},{4,20},{6,22},{8,24},{10,26},{12,28},{14,30},{16,0},... | collective-permute-start | bytes 663560 | tf_op jit(solution)/shard_map/ppermute | solution.py:186
  26.0 16.4 %collective-permute-start.1 = (bf16[288,768]{1,0:T(8,128)(2,1)S(1)}, bf16[288,768]{1,0:T(8,128)(2,1)S(1)}, u32[]{:S(2)}, u32[]{:S(2)}) collective-permute-start(bf16[288,768]{1,0:T(8,128)(2,1)S(1)} %pad_maximum_fusion.own), channel_id=1, source_target_pairs={{0,1},{2,3},{4,5},{6,7},{8,9},{10,11},{12,13},{14,15},{16,17},{18,... | collective-permute-start | bytes 1327112 | tf_op jit(solution)/shard_map/ppermute | solution.py:190
  27.9 16.4 %collective-permute-start.4 = (bf16[288,768]{1,0:T(8,128)(2,1)S(1)}, bf16[288,768]{1,0:T(8,128)(2,1)S(1)}, u32[]{:S(2)}, u32[]{:S(2)}) collective-permute-start(bf16[288,768]{1,0:T(8,128)(2,1)S(1)} %pad_maximum_fusion.own), channel_id=1, source_target_pairs={{0,97},{2,99},{4,101},{6,103},{8,105},{10,107},{12,109},{14,111},{... | collective-permute-start | bytes 1327112 | tf_op jit(solution)/shard_map/ppermute | solution.py:191
  34.4 70.9 %all-to-all-start = ((bf16[32,16,768]{2,1,0:T(8,128)(2,1)}), bf16[32,16,768]{2,1,0:T(8,128)(2,1)S(1)}, u32[]{:S(2)}, u32[]{:S(2)}) async-start(bf16[32,16,768]{2,1,0:T(8,128)(2,1)} %bitcast.17), calls=%async_computation | async-start | bytes 1572864 | tf_op jit(solution)/shard_map/all_to_all | solution.py:204
  42.3 26.7 %collective-permute-start.2 = (bf16[288,768]{1,0:T(8,128)(2,1)S(1)}, bf16[288,768]{1,0:T(8,128)(2,1)S(1)}, u32[]{:S(2)}, u32[]{:S(2)}) collective-permute-start(bf16[288,768]{1,0:T(8,128)(2,1)S(1)} %collective-permute-done.1.up1), channel_id=1, source_target_pairs={{0,1},{2,3},{4,5},{6,7},{8,9},{10,11},{12,13},{14,15},{16,17},{18,... | collective-permute-start | bytes 1327112 | tf_op jit(solution)/shard_map/ppermute | solution.py:190
  44.3 26.7 %collective-permute-start.5 = (bf16[288,768]{1,0:T(8,128)(2,1)S(1)}, bf16[288,768]{1,0:T(8,128)(2,1)S(1)}, u32[]{:S(2)}, u32[]{:S(2)}) collective-permute-start(bf16[288,768]{1,0:T(8,128)(2,1)S(1)} %collective-permute-done.4.down1), channel_id=1, source_target_pairs={{0,97},{2,99},{4,101},{6,103},{8,105},{10,107},{12,109},{14,111},{... | collective-permute-start | bytes 1327112 | tf_op jit(solution)/shard_map/ppermute | solution.py:191
  57.8 0.8 copy-start.3
  69.0 22.1 %copy-start.5 = (bf16[288,768]{1,0:T(8,128)(2,1)}, bf16[288,768]{1,0:T(8,128)(2,1)S(1)}, u32[]{:S(2)}) copy-start(bf16[288,768]{1,0:T(8,128)(2,1)S(1)} %collective-permute-done.2.up2) | copy-start | bytes 1327108
  69.0 14.1 %collective-permute-start.3 = (bf16[288,768]{1,0:T(8,128)(2,1)S(1)}, bf16[288,768]{1,0:T(8,128)(2,1)S(1)}, u32[]{:S(2)}, u32[]{:S(2)}) collective-permute-start(bf16[288,768]{1,0:T(8,128)(2,1)S(1)} %collective-permute-done.2.up2), channel_id=1, source_target_pairs={{0,1},{2,3},{4,5},{6,7},{8,9},{10,11},{12,13},{14,15},{16,17},{18,... | collective-permute-start | bytes 1327112 | tf_op jit(solution)/shard_map/ppermute | solution.py:190
  71.0 20.1 %copy-start.7 = (bf16[288,768]{1,0:T(8,128)(2,1)}, bf16[288,768]{1,0:T(8,128)(2,1)S(1)}, u32[]{:S(2)}) copy-start(bf16[288,768]{1,0:T(8,128)(2,1)S(1)} %collective-permute-done.5.down2) | copy-start | bytes 1327108
  71.0 14.8 %collective-permute-start.6 = (bf16[288,768]{1,0:T(8,128)(2,1)S(1)}, bf16[288,768]{1,0:T(8,128)(2,1)S(1)}, u32[]{:S(2)}, u32[]{:S(2)}) collective-permute-start(bf16[288,768]{1,0:T(8,128)(2,1)S(1)} %collective-permute-done.5.down2), channel_id=1, source_target_pairs={{0,97},{2,99},{4,101},{6,103},{8,105},{10,107},{12,109},{14,111},{... | collective-permute-start | bytes 1327112 | tf_op jit(solution)/shard_map/ppermute | solution.py:191
  83.8 15.3 %collective-permute-start.7 = (bf16[144,768]{1,0:T(8,128)(2,1)}, bf16[144,768]{1,0:T(8,128)(2,1)}, u32[]{:S(2)}, u32[]{:S(2)}) collective-permute-start(bf16[144,768]{1,0:T(8,128)(2,1)} %slice.90), channel_id=1, source_target_pairs={{0,1},{2,3},{4,5},{6,7},{8,9},{10,11},{12,13},{14,15},{16,17},{18,... | collective-permute-start | bytes 663560 | tf_op jit(solution)/shard_map/ppermute | solution.py:192
  86.4 12.7 %collective-permute-start.8 = (bf16[144,768]{1,0:T(8,128)(2,1)}, bf16[144,768]{1,0:T(8,128)(2,1)}, u32[]{:S(2)}, u32[]{:S(2)}) collective-permute-start(bf16[144,768]{1,0:T(8,128)(2,1)} %slice.91), channel_id=1, source_target_pairs={{0,97},{2,99},{4,101},{6,103},{8,105},{10,107},{12,109},{14,111},{... | collective-permute-start | bytes 663560 | tf_op jit(solution)/shard_map/ppermute | solution.py:193
  99.1 1.0 copy-start.4
  100.1 1.0 copy-start.6
  101.1 1.0 copy-start.8
  103.5 1.8 copy-start.1
  105.2 2.0 copy-start.2
  219.5 11.8 %all-to-all-start.1 = ((bf16[16,2,768]{2,1,0:T(2,128)(2,1)}), bf16[16,2,768]{2,1,0:T(2,128)(2,1)S(1)}, u32[]{:S(2)}, u32[]{:S(2)}) async-start(bf16[16,2,768]{2,1,0:T(2,128)(2,1)} %bitcast.31), calls=%async_computation.1 | async-start | bytes 98304 | tf_op jit(solution)/shard_map/all_to_all | solution.py:239

commit v4 on v3

v4 whole, which is shorter than its diff:
```python
import functools
import math

import jax
import jax.numpy as jnp
import numpy as np
from jax import lax
from jax.experimental import pallas as pl
from jax.experimental.pallas import tpu as pltpu
from jax.sharding import Mesh, PartitionSpec as P

HEADS = 12
HDIM = 128
ROWS = 8
D = HEADS * HDIM
TOKENS = 512
SECTIONS = 8
MEMBERS = 4
PART = D // MEMBERS
LOCAL = 16
GROUP = LOCAL * MEMBERS
UNIT = 48
UNITS = 3
COLUMNS = UNIT * UNITS
HALF = D // 2
BLOCK = 2 * COLUMNS

guide_weight = 3.5
norm_eps = 1e-06

AXES = ("xh", "xl", "yh", "core", "section", "cfg")
SIZES = (2, 2, 4, 2, 8, 2)


def route(step):
    def number(x, y, core, section):
        return (((x * 4 + y // 2) * 2 + core) * 8 + section) * 2 + y % 2

    return [
        (number(x, y, core, s), number(*step(x, y, core), s))
        for x in range(4)
        for y in range(8)
        for core in range(2)
        for s in range(SECTIONS)
    ]


SWAP = route(lambda x, y, core: (x, y, 1 - core))
UP = route(lambda x, y, core: (x, (y + 1 - 2 * core) % 8, core))
DOWN = route(lambda x, y, core: (x, (y - 1 + 2 * core) % 8, core))
ACROSS = [(i, (i + 256) % 512) for i in range(512)]
PAIRS = (
    [[s, s + 1] for s in range(0, SECTIONS, 2)],
    [[s, (s + 1) % SECTIONS] for s in range(1, SECTIONS, 2)],
)


def nt_dot(a, b):
    return lax.dot_general(a, b, (((1,), (1,)), ((), ())), preferred_element_type=jnp.float32)


def block_kernel(tick, who, x_ref, w_ref, kv_ref, other_ref, mod_ref, gate_ref, cos_ref, sin_ref, block_ref, old_ref, state_ref, fresh_ref):
    member = who[0]
    active = who[1] == tick
    xs = [x_ref[i].astype(jnp.float32) for i in range(MEMBERS)]
    center = sum(jnp.sum(x, axis=-1, keepdims=True) for x in xs) / D
    xs = [x - center for x in xs]
    spread = sum(jnp.sum(x * x, axis=-1, keepdims=True) for x in xs) / D
    inv = lax.rsqrt(spread + norm_eps)
    normed = jnp.concatenate(
        [
            (
                xs[i] * inv * (1.0 + mod_ref[1:2, i * PART : (i + 1) * PART])
                + mod_ref[0:1, i * PART : (i + 1) * PART]
            ).astype(jnp.bfloat16)
            for i in range(MEMBERS)
        ],
        axis=1,
    )
    projected = jnp.dot(normed, w_ref[...], preferred_element_type=jnp.float32).astype(jnp.bfloat16)
    row_block = block_ref[...]
    stale_mask = lax.broadcasted_iota(jnp.int32, (GROUP, TOKENS // 2), 1) // ROWS == row_block
    own_mask = (
        lax.broadcasted_iota(jnp.int32, (GROUP, GROUP), 0) // ROWS
        == lax.broadcasted_iota(jnp.int32, (GROUP, GROUP), 1) // ROWS
    )
    cosine, sine = cos_ref[...], sin_ref[...]

    def turned(values):
        values = values.astype(jnp.float32)
        values = values * lax.rsqrt(jnp.mean(values * values, axis=-1, keepdims=True) + norm_eps)
        return (values * cosine + pltpu.roll(values, HDIM // 2, 1) * sine).astype(jnp.bfloat16)

    heads = range(PART // HDIM)
    cols = [slice(h * HDIM, (h + 1) * HDIM) for h in heads]
    vcols = [slice(PART + h * HDIM, PART + (h + 1) * HDIM) for h in heads]
    scale = 1.0 / math.sqrt(HDIM)
    query = [turned(projected[:, cols[h]]) for h in heads]
    key = [turned(projected[:, vcols[h]]) for h in heads]
    value = [projected[:, 2 * PART + h * HDIM : 2 * PART + (h + 1) * HDIM] for h in heads]
    scores = [nt_dot(query[h], kv_ref[:, cols[h]]) for h in heads]
    other_scores = [nt_dot(query[h], other_ref[:, cols[h]]) for h in heads]
    own_scores = [nt_dot(query[h], key[h]) for h in heads]
    weights = [jnp.where(stale_mask, 0.0, jnp.exp(scores[h] * scale)) for h in heads]
    others = [jnp.exp(other_scores[h] * scale) for h in heads]
    own = [jnp.where(own_mask, jnp.exp(own_scores[h] * scale), 0.0) for h in heads]
    total = [
        jnp.sum(weights[h] + others[h], axis=-1, keepdims=True) + jnp.sum(own[h], axis=-1, keepdims=True)
        for h in heads
    ]
    attended = [
        jnp.dot(weights[h].astype(jnp.bfloat16), kv_ref[:, vcols[h]], preferred_element_type=jnp.float32)
        + jnp.dot(others[h].astype(jnp.bfloat16), other_ref[:, vcols[h]], preferred_element_type=jnp.float32)
        + jnp.dot(own[h].astype(jnp.bfloat16), value[h], preferred_element_type=jnp.float32)
        for h in heads
    ]
    for h in heads:
        state = x_ref[member, :, cols[h]].astype(jnp.float32) + gate_ref[0:1, cols[h]] * (attended[h] / total[h])
        state_ref[:, cols[h]] = state.astype(jnp.bfloat16)
        fresh_ref[:, cols[h]] = jnp.where(active, key[h], old_ref[:, cols[h]])
        fresh_ref[:, vcols[h]] = jnp.where(active, value[h], old_ref[:, vcols[h]])


def run_block(tick, who, x, weight, kv, other, mod, gate, cosine, sine, blocks, old):
    vmem = pl.BlockSpec(memory_space=pltpu.VMEM)
    weight = pltpu.with_memory_space_constraint(weight, pltpu.VMEM)
    return pl.pallas_call(
        functools.partial(block_kernel, tick),
        out_shape=(
            jax.ShapeDtypeStruct((GROUP, PART), jnp.bfloat16),
            jax.ShapeDtypeStruct((GROUP, 2 * PART), jnp.bfloat16),
        ),
        in_specs=[pl.BlockSpec(memory_space=pltpu.SMEM)] + [vmem] * 10,
        out_specs=(vmem, vmem),
        compiler_params=pltpu.CompilerParams(vmem_limit_bytes=24 * 1024 * 1024),
        name="block_step",
    )(who, x, weight, kv, other, mod, gate, cosine, sine, blocks, old)


def prepare_kernel(where, stale_ref, columns_ref, out_ref, half_ref):
    for slot in range(2 * 4 * 2):
        m = slot // 8 * 2 + slot % 2
        out_ref[slot, :, :PART] = stale_ref[:, m * PART : (m + 1) * PART]
        out_ref[slot, :, PART:] = stale_ref[:, D + m * PART : D + (m + 1) * PART]
    half_ref[...] = columns_ref[:, pl.ds(pl.multiple_of(where[3] % 2 * HALF, 128), HALF)]


def pick_kernel(where, x_ref, keep_ref, send_ref):
    member, first, core = where[0], where[1], where[2]
    peer = member + 1 - 2 * core
    for j in range(UNITS):
        third = (first + j * UNIT) // PART
        keep_ref[j * UNIT : (j + 1) * UNIT, :] = x_ref[(third - member + 4) % 4, j * UNIT : (j + 1) * UNIT, :]
        send_ref[j * UNIT : (j + 1) * UNIT, :] = x_ref[(third - peer + 4) % 4, j * UNIT : (j + 1) * UNIT, :]


def place_kernel(where, own, up1, up2, up3, down1, down2, down3, up4, down4, out_ref, rows, sem):
    member, core, y = where[0], where[2], where[3]
    sign = 1 - 2 * core
    copies = []

    def home(unit):
        third = unit // 8
        part = (COLUMNS * 8 * ((third - member + 4) % 4) + PART * third) // D
        return part * PART + unit % 8 * UNIT

    def put(source, part, ref, begin):
        at = (y + sign * source + 8) % 8
        first = (at // 2 * 2 + (core + part) % 2) * UNITS
        for j in range(UNITS):
            unit = first + j
            row = pl.multiple_of(home(unit), 16)
            col = pl.multiple_of(at % 2 * HALF, 128)
            copy = pltpu.make_async_copy(
                ref.at[pl.ds(begin + j * UNIT, UNIT)], rows.at[pl.ds(row, UNIT), pl.ds(col, HALF)], sem
            )
            copy.start()
            copies.append(copy)

    for source, ref in ((0, own), (-1, up1), (-2, up2), (-3, up3), (1, down1), (2, down2), (3, down3)):
        put(source, 0, ref, 0)
        put(source, 1, ref, COLUMNS)
    put(4, 0, up4, 0)
    put(4, 1, down4, 0)
    for copy in copies:
        copy.wait()
    for c in range(0, D, HDIM):
        out_ref[c : c + HDIM, :] = jnp.transpose(rows[:, c : c + HDIM])


def place(where, blocks):
    return pl.pallas_call(
        place_kernel,
        out_shape=jax.ShapeDtypeStruct((D, 3 * PART), jnp.bfloat16),
        in_specs=[pl.BlockSpec(memory_space=pltpu.SMEM)] + [pl.BlockSpec(memory_space=pl.ANY)] * len(blocks),
        out_specs=pl.BlockSpec(memory_space=pltpu.VMEM),
        scratch_shapes=[pltpu.VMEM((3 * PART, D), jnp.bfloat16), pltpu.SemaphoreType.DMA],
        compiler_params=pltpu.CompilerParams(vmem_limit_bytes=12 * 1024 * 1024),
        name="place_weight",
    )(where, *blocks)


def whole_call(kernel, where, arrays, outs):
    vmem = pl.BlockSpec(memory_space=pltpu.VMEM)
    return pl.pallas_call(
        kernel,
        out_shape=[jax.ShapeDtypeStruct(shape, jnp.bfloat16) for shape in outs],
        in_specs=[pl.BlockSpec(memory_space=pltpu.SMEM)] + [vmem] * len(arrays),
        out_specs=[vmem] * len(outs),
        compiler_params=pltpu.CompilerParams(vmem_limit_bytes=24 * 1024 * 1024),
        name=kernel.__name__,
    )(where, *arrays)


def body(hidden, timestep, patch_order, modulation, qkv_weight, stale_kv):
    index = {a: lax.axis_index(a) for a in AXES}
    section = index["section"]
    member = index["xl"] * 2 + index["core"]
    y = index["yh"] * 2 + index["cfg"]
    first = (index["yh"] * 2 + index["core"]) * COLUMNS
    where = jnp.stack([member, first, index["core"], y]).astype(jnp.int32)
    who = jnp.stack([member, section]).astype(jnp.int32)

    outgoing, columns = whole_call(
        prepare_kernel,
        where,
        [stale_kv[0, 0], jnp.transpose(qkv_weight[0])],
        [(2 * 4 * 2, LOCAL, 2 * PART), (COLUMNS, HALF)],
    )
    kv = lax.all_to_all(outgoing, ("xl", "yh", "core"), split_axis=0, concat_axis=0, tiled=True)
    kv = kv.reshape(TOKENS // 2, 2 * PART)

    columns = lax.all_gather(columns, ("xh", "xl"), axis=0, tiled=False)
    keep, send = whole_call(pick_kernel, where, [columns], [(COLUMNS, HALF)] * 2)
    own = jnp.concatenate([keep, lax.ppermute(send, AXES, SWAP)])
    own, kv = lax.optimization_barrier((own, kv))
    up1, down1 = lax.ppermute(own, AXES, UP), lax.ppermute(own, AXES, DOWN)
    up1, entering, kv = lax.optimization_barrier((up1, hidden[0], kv))
    kv_other = lax.ppermute(kv, AXES, ACROSS)
    x = lax.all_gather(entering, ("xl", "core"), axis=0, tiled=True)
    up2, down2 = lax.ppermute(up1, AXES, UP), lax.ppermute(down1, AXES, DOWN)
    down2, x = lax.optimization_barrier((down2, x))
    up3, down3 = lax.ppermute(up2, AXES, UP), lax.ppermute(down2, AXES, DOWN)
    up4 = lax.ppermute(up3[:COLUMNS], AXES, UP)
    down4 = lax.ppermute(down3[COLUMNS:], AXES, DOWN)
    weight = place(where, [own, up1, up2, up3, down1, down2, down3, up4, down4])
    x = jnp.transpose(x.reshape(GROUP, MEMBERS, PART), (1, 0, 2))

    row = lax.dynamic_index_in_dim(modulation[0, 0], timestep[0], 0, keepdims=False)
    mod = row[: 2 * D].reshape(2, D)
    gate = lax.dynamic_slice_in_dim(row, 2 * D + member * PART, PART, 0).reshape(1, PART)

    lane = jnp.arange(GROUP, dtype=jnp.int32)
    source = lane // LOCAL
    patch = (source // 2 * 4 + index["yh"]) * 2 + source % 2
    blocks = patch * (LOCAL // ROWS) + lane % LOCAL // ROWS
    positions = (patch_order[index["xh"] * (TOKENS // 2 // ROWS) + blocks] * ROWS + lane % ROWS).astype(jnp.float32)
    halfway = HDIM // 2
    inverse = jnp.exp(-math.log(10000.0) * jnp.arange(halfway, dtype=jnp.float32) / halfway)
    angles = positions[:, None] * inverse[None, :]
    cosine, sine = jnp.cos(angles), jnp.sin(angles)
    cosine = jnp.concatenate([cosine, cosine], axis=1)
    sine = jnp.concatenate([-sine, sine], axis=1)

    fresh = jnp.zeros((GROUP, 2 * PART), jnp.bfloat16)
    for tick in range(SECTIONS):
        state, fresh = run_block(tick, who, x, weight, kv, kv_other, mod, gate, cosine, sine, blocks[:, None], fresh)
        if tick + 1 < SECTIONS:
            state = lax.all_gather(state, "section", axis=0, tiled=False, axis_index_groups=PAIRS[tick % 2])[0]
            x = lax.all_gather(state, ("xl", "core"), axis=0, tiled=False)

    ends = lax.all_gather(state, ("xl", "core"), axis=0, tiled=False)
    finals = lax.dynamic_slice_in_dim(ends, member * LOCAL, LOCAL, 1)
    finals = jnp.transpose(finals, (1, 0, 2)).reshape(SECTIONS, LOCAL // SECTIONS, 2, D // 2)
    finals = jnp.transpose(finals, (0, 2, 1, 3)).reshape(SECTIONS * 2, LOCAL // SECTIONS, D // 2)
    spread = lax.all_to_all(finals, ("section", "cfg"), split_axis=0, concat_axis=0, tiled=True)
    kept = lax.all_gather(fresh, ("xl", "core"), axis=0, tiled=False)
    spread, kept = lax.optimization_barrier((spread, kept))
    kept = lax.dynamic_slice_in_dim(kept, member * LOCAL, LOCAL, 1)
    kept = jnp.transpose(kept.reshape(MEMBERS, LOCAL, 2, PART), (1, 2, 0, 3)).reshape(LOCAL, 2 * D)
    uncond = spread[2 * SECTIONS - 2].astype(jnp.float32)
    conditioned = spread[2 * SECTIONS - 1].astype(jnp.float32)
    guided = (uncond + guide_weight * (conditioned - uncond)).astype(jnp.bfloat16)
    return guided, kept[None, None]


def solution(mesh):
    fine = Mesh(mesh.devices.reshape(SIZES), AXES)
    patch = ("xh", "xl", "yh", "core")
    return jax.shard_map(
        body,
        mesh=fine,
        in_specs=(
            P("cfg", patch, None),
            P(),
            P(),
            P("section", "cfg", None, None),
            P("section", None, patch),
            P("section", "cfg", patch, None),
        ),
        out_specs=(P((*patch, "section"), "cfg"), P("section", "cfg", patch, None)),
        check_vma=False,
    )
```

time: 233 us -> 217 us (0.931)
  the two profiles are of different devices: /device:TPU:1 before, /device:TPU:16 now
where the time goes in v4:
time: 217 us; the launch traced here: 216 us
  blocking collectives  115 us (53%)
  starting transfers between devices  48.7 us (22%)
  waiting for transfers between devices  21.7 us (10%)
  Pallas kernels  20.9 us (10%)
  local copies, waits for them, and re-layouts  5.35 us (2%)
  other arithmetic  2.7 us (1%)
    all_gather x7, blocking collectives, body(): lax.all_gather(state, 'section', axis=0, tiled=False, axis_index_groups=P...  42.9 us
    all_gather x7, blocking collectives, body(): x = lax.all_gather(state, ('xl', 'core'), axis=0, tiled=False)  39.3 us
    pallas_call x8, Pallas kernels, run_block(): pl.pallas_call(functools.partial(block_kernel, tick), out_shape=(jax.Shap...  15.1 us
    all_gather x1, blocking collectives, body(): columns = lax.all_gather(columns, ('xh', 'xl'), axis=0, tiled=False)  14.6 us
    all_to_all x1, starting transfers between devices, body(): lax.all_to_all(outgoing, ('xl', 'yh', 'core'), split_axis=0, concat_axis=...  9.06 us
    ppermute x2, waiting for transfers between devices, body(): up1, down1 = (lax.ppermute(own, AXES, UP), lax.ppermute(own, AXES, DOWN))  7.16 us
    all_to_all x1, starting transfers between devices, body(): lax.all_to_all(finals, ('section', 'cfg'), split_axis=0, concat_axis=0, t...  7.11 us
    ppermute x2, starting transfers between devices, body(): up3, down3 = (lax.ppermute(up2, AXES, UP), lax.ppermute(down2, AXES, DOWN))  7.04 us
  transfers between devices with their start and end apart: 12, of which 6 were waited for; matrix products, arithmetic and copies ran while one was open for 2% of the time, Pallas kernels for 2%

profile of v4, /device:TPU:16, one launch (start us, length us, event | category | flops | bytes accessed | tf_op | source)
XLA Modules:
  0.0 215.7 jit_solution(1425685276020650367)
XLA Ops:
  4.0 9.1 %all-to-all-start = ((bf16[16,16,768]{2,1,0:T(8,128)(2,1)}), bf16[16,16,768]{2,1,0:T(8,128)(2,1)S(1)}, u32[]{:S(2)}, u32[]{:S(2)}) async-start(bf16[16,16,768]{2,1,0:T(8,128)(2,1)} %get-tuple-element.34), calls=%async_computation | async-start | bytes 786432 | tf_op jit(solution)/shard_map/all_to_all | solution.py:230
  13.0 14.6 %all-gather = bf16[576,768]{1,0:T(8,128)(2,1)S(1)} all-gather(bf16[144,768]{1,0:T(8,128)(2,1)S(1)} %get-tuple-element.31), channel_id=2, replica_groups=mesh['xh'=2,'xl'=2,'yh'=4,'core'=2,'section'=8,'cfg'=2] {'xh','xl'}, dimensions={0}, use_global_device_ids=true | all-gather | bytes 1105920 | tf_op jit(solution)/shard_map/all_gather | solution.py:233
  31.6 3.1 %collective-permute-start.3 = (bf16[288,768]{1,0:T(8,128)(2,1)S(1)}, bf16[288,768]{1,0:T(8,128)(2,1)S(1)}, u32[]{:S(2)}, u32[]{:S(2)}) collective-permute-start(bf16[288,768]{1,0:T(8,128)(2,1)S(1)} %pad_maximum_fusion.own), channel_id=1, source_target_pairs={{0,1},{2,3},{4,5},{6,7},{8,9},{10,11},{12,13},{14,15},{16,113},{18... | collective-permute-start | bytes 1327112 | tf_op jit(solution)/shard_map/ppermute | solution.py:237
  34.7 2.8 %collective-permute-start.1 = (bf16[288,768]{1,0:T(8,128)(2,1)S(1)}, bf16[288,768]{1,0:T(8,128)(2,1)S(1)}, u32[]{:S(2)}, u32[]{:S(2)}) collective-permute-start(bf16[288,768]{1,0:T(8,128)(2,1)S(1)} %pad_maximum_fusion.own), channel_id=1, source_target_pairs={{0,97},{2,99},{4,101},{6,103},{8,105},{10,107},{12,109},{14,111},{... | collective-permute-start | bytes 1327112 | tf_op jit(solution)/shard_map/ppermute | solution.py:237
  37.6 7.2 %collective-permute-done.3.up1 = bf16[288,768]{1,0:T(8,128)(2,1)S(1)} collective-permute-done((bf16[288,768]{1,0:T(8,128)(2,1)S(1)}, bf16[288,768]{1,0:T(8,128)(2,1)S(1)}, u32[]{:S(2)}, u32[]{:S(2)}) %collective-permute-start.3) | collective-permute-done | bytes 442400 | tf_op jit(solution)/shard_map/ppermute | solution.py:237
  44.8 4.8 %collective-permute-start.4 = (bf16[288,768]{1,0:T(8,128)(2,1)S(1)}, bf16[288,768]{1,0:T(8,128)(2,1)}, u32[]{:S(2)}, u32[]{:S(2)}) collective-permute-start(bf16[288,768]{1,0:T(8,128)(2,1)S(1)} %collective-permute-done.3.up1), channel_id=1, source_target_pairs={{0,1},{2,3},{4,5},{6,7},{8,9},{10,11},{12,13},{14,15},{16,113},{18... | collective-permute-start | bytes 1327112 | tf_op jit(solution)/shard_map/ppermute | solution.py:241
  53.1 6.1 %all_gather.86 = bf16[64,1536]{1,0:T(8,128)(2,1)} all-gather(bf16[16,1536]{1,0:T(8,128)(2,1)S(1)} %bitcast.72), channel_id=1, replica_groups=mesh['xh'=2,'xl'=2,'yh'=4,'core'=2,'section'=8,'cfg'=2] {'xl','core'}, dimensions={0}, use_global_device_ids=true | all-gather | bytes 245760 | tf_op jit(solution)/shard_map/all_gather | solution.py:240
  59.1 2.5 %collective-permute-done.2.down2 = bf16[288,768]{1,0:T(8,128)(2,1)} collective-permute-done((bf16[288,768]{1,0:T(8,128)(2,1)S(1)}, bf16[288,768]{1,0:T(8,128)(2,1)}, u32[]{:S(2)}, u32[]{:S(2)}) %collective-permute-start.2) | collective-permute-done | bytes 442400 | tf_op jit(solution)/shard_map/ppermute | solution.py:241
  63.6 5.1 %collective-permute-start.5 = (bf16[288,768]{1,0:T(8,128)(2,1)}, bf16[288,768]{1,0:T(8,128)(2,1)S(1)}, u32[]{:S(2)}, u32[]{:S(2)}) collective-permute-start(bf16[288,768]{1,0:T(8,128)(2,1)} %collective-permute-done.4.up2), channel_id=1, source_target_pairs={{0,1},{2,3},{4,5},{6,7},{8,9},{10,11},{12,13},{14,15},{16,113},{18... | collective-permute-start | bytes 1327112 | tf_op jit(solution)/shard_map/ppermute | solution.py:243
  69.5 3.4 %collective-permute-start.9 = (bf16[256,768]{1,0:T(8,128)(2,1)S(1)}, bf16[256,768]{1,0:T(8,128)(2,1)S(1)}, u32[]{:S(2)}, u32[]{:S(2)}) collective-permute-start(bf16[256,768]{1,0:T(8,128)(2,1)S(1)} %bitcast.46), channel_id=1, source_target_pairs={{0,256},{1,257},{2,258},{3,259},{4,260},{5,261},{6,262},{7,263},{8... | collective-permute-start | bytes 1179656 | tf_op jit(solution)/shard_map/ppermute | solution.py:239
  73.1 2.6 %collective-permute-done.5.up3 = bf16[288,768]{1,0:T(8,128)(2,1)S(1)} collective-permute-done((bf16[288,768]{1,0:T(8,128)(2,1)}, bf16[288,768]{1,0:T(8,128)(2,1)S(1)}, u32[]{:S(2)}, u32[]{:S(2)}) %collective-permute-start.5) | collective-permute-done | bytes 442400 | tf_op jit(solution)/shard_map/ppermute | solution.py:243
  75.7 5.7 %collective-permute-start.7 = (bf16[144,768]{1,0:T(8,128)(2,1)S(1)}, bf16[144,768]{1,0:T(8,128)(2,1)S(1)}, u32[]{:S(2)}, u32[]{:S(2)}) collective-permute-start(bf16[144,768]{1,0:T(8,128)(2,1)S(1)} %slice.58), channel_id=1, source_target_pairs={{0,1},{2,3},{4,5},{6,7},{8,9},{10,11},{12,13},{14,15},{16,113},{18... | collective-permute-start | bytes 663560 | tf_op jit(solution)/shard_map/ppermute | solution.py:244
  85.3 5.5 %collective-permute-done.8.down4 = bf16[144,768]{1,0:T(8,128)(2,1)S(1)} collective-permute-done((bf16[144,768]{1,0:T(8,128)(2,1)S(1)}, bf16[144,768]{1,0:T(8,128)(2,1)S(1)}, u32[]{:S(2)}, u32[]{:S(2)}) %collective-permute-start.8) | collective-permute-done | bytes 221216 | tf_op jit(solution)/shard_map/ppermute | solution.py:245
  90.9 3.9 %place_weight.1.w_ref = bf16[1536,1152]{1,0:T(8,128)(2,1)S(1)} custom-call(s32[4]{0:T(128)S(1)} %pad_add_fusion.1.where, bf16[288,768]{1,0:T(8,128)(2,1)S(1)} %pad_maximum_fusion.own, bf16[288,768]{1,0:T(8,128)(2,1)S(1)} %collective-permute-done.3.up1, bf16[288,768]{1,0:T(8,128)(2,1)} %collective-permute-done.4.up2, ...), custom_call_target="tpu_custom_call" | custom-call | tf_op jit(solution)/shard_map/place_weight/pallas_call | solution.py:192
  96.7 5.0 %all-gather.1 = bf16[128,384]{1,0:T(8,128)(2,1)S(1)} all-gather(bf16[64,384]{1,0:T(8,128)(2,1)S(1)} %get-tuple-element.42), channel_id=3, replica_groups={{0,2},{4,6},{8,10},{12,14},{1,3},{5,7},{9,11},{13,15},{16,18},{20,22},{..., dimensions={0}, use_global_device_ids=true | all-gather | bytes 147456 | tf_op jit(solution)/shard_map/all_gather | solution.py:269
  101.7 5.6 %all-gather.10 = bf16[256,384]{1,0:T(8,128)(2,1)S(1)} all-gather(bf16[64,384]{1,0:T(8,128)(2,1)S(1)} %slice.60), channel_id=12, replica_groups=mesh['xh'=2,'xl'=2,'yh'=4,'core'=2,'section'=8,'cfg'=2] {'xl','core'}, dimensions={0}, use_global_device_ids=true | all-gather | bytes 245760 | tf_op jit(solution)/shard_map/all_gather | solution.py:270
  109.2 11.6 %all-gather.2 = bf16[128,384]{1,0:T(8,128)(2,1)S(1)} all-gather(bf16[64,384]{1,0:T(8,128)(2,1)S(1)} %get-tuple-element.44), channel_id=4, replica_groups={{2,4},{6,8},{10,12},{14,0},{3,5},{7,9},{11,13},{15,1},{18,20},{22,24},{..., dimensions={0}, use_global_device_ids=true | all-gather | bytes 147456 | tf_op jit(solution)/shard_map/all_gather | solution.py:269
  120.8 5.6 %all-gather.11 = bf16[256,384]{1,0:T(8,128)(2,1)S(1)} all-gather(bf16[64,384]{1,0:T(8,128)(2,1)S(1)} %slice.61), channel_id=13, replica_groups=mesh['xh'=2,'xl'=2,'yh'=4,'core'=2,'section'=8,'cfg'=2] {'xl','core'}, dimensions={0}, use_global_device_ids=true | all-gather | bytes 245760 | tf_op jit(solution)/shard_map/all_gather | solution.py:270
  128.3 4.8 %all-gather.3 = bf16[128,384]{1,0:T(8,128)(2,1)S(1)} all-gather(bf16[64,384]{1,0:T(8,128)(2,1)S(1)} %get-tuple-element.46), channel_id=5, replica_groups={{0,2},{4,6},{8,10},{12,14},{1,3},{5,7},{9,11},{13,15},{16,18},{20,22},{..., dimensions={0}, use_global_device_ids=true | all-gather | bytes 147456 | tf_op jit(solution)/shard_map/all_gather | solution.py:269
  133.0 5.6 %all-gather.12 = bf16[256,384]{1,0:T(8,128)(2,1)S(1)} all-gather(bf16[64,384]{1,0:T(8,128)(2,1)S(1)} %slice.62), channel_id=14, replica_groups=mesh['xh'=2,'xl'=2,'yh'=4,'core'=2,'section'=8,'cfg'=2] {'xl','core'}, dimensions={0}, use_global_device_ids=true | all-gather | bytes 245760 | tf_op jit(solution)/shard_map/all_gather | solution.py:270
  140.5 6.0 %all-gather.4 = bf16[128,384]{1,0:T(8,128)(2,1)S(1)} all-gather(bf16[64,384]{1,0:T(8,128)(2,1)S(1)} %get-tuple-element.48), channel_id=6, replica_groups={{2,4},{6,8},{10,12},{14,0},{3,5},{7,9},{11,13},{15,1},{18,20},{22,24},{..., dimensions={0}, use_global_device_ids=true | all-gather | bytes 147456 | tf_op jit(solution)/shard_map/all_gather | solution.py:269
  146.5 5.6 %all-gather.13 = bf16[256,384]{1,0:T(8,128)(2,1)S(1)} all-gather(bf16[64,384]{1,0:T(8,128)(2,1)S(1)} %slice.63), channel_id=15, replica_groups=mesh['xh'=2,'xl'=2,'yh'=4,'core'=2,'section'=8,'cfg'=2] {'xl','core'}, dimensions={0}, use_global_device_ids=true | all-gather | bytes 245760 | tf_op jit(solution)/shard_map/all_gather | solution.py:270
  154.0 4.8 %all-gather.5 = bf16[128,384]{1,0:T(8,128)(2,1)S(1)} all-gather(bf16[64,384]{1,0:T(8,128)(2,1)S(1)} %get-tuple-element.50), channel_id=7, replica_groups={{0,2},{4,6},{8,10},{12,14},{1,3},{5,7},{9,11},{13,15},{16,18},{20,22},{..., dimensions={0}, use_global_device_ids=true | all-gather | bytes 147456 | tf_op jit(solution)/shard_map/all_gather | solution.py:269
  158.8 5.8 %all-gather.14 = bf16[256,384]{1,0:T(8,128)(2,1)S(1)} all-gather(bf16[64,384]{1,0:T(8,128)(2,1)S(1)} %slice.64), channel_id=16, replica_groups=mesh['xh'=2,'xl'=2,'yh'=4,'core'=2,'section'=8,'cfg'=2] {'xl','core'}, dimensions={0}, use_global_device_ids=true | all-gather | bytes 245760 | tf_op jit(solution)/shard_map/all_gather | solution.py:270
  166.4 6.0 %all-gather.6 = bf16[128,384]{1,0:T(8,128)(2,1)S(1)} all-gather(bf16[64,384]{1,0:T(8,128)(2,1)S(1)} %get-tuple-element.52), channel_id=8, replica_groups={{2,4},{6,8},{10,12},{14,0},{3,5},{7,9},{11,13},{15,1},{18,20},{22,24},{..., dimensions={0}, use_global_device_ids=true | all-gather | bytes 147456 | tf_op jit(solution)/shard_map/all_gather | solution.py:269
  172.4 5.6 %all-gather.15 = bf16[256,384]{1,0:T(8,128)(2,1)S(1)} all-gather(bf16[64,384]{1,0:T(8,128)(2,1)S(1)} %slice.65), channel_id=17, replica_groups=mesh['xh'=2,'xl'=2,'yh'=4,'core'=2,'section'=8,'cfg'=2] {'xl','core'}, dimensions={0}, use_global_device_ids=true | all-gather | bytes 245760 | tf_op jit(solution)/shard_map/all_gather | solution.py:270
  179.9 4.8 %all-gather.7 = bf16[128,384]{1,0:T(8,128)(2,1)S(1)} all-gather(bf16[64,384]{1,0:T(8,128)(2,1)S(1)} %get-tuple-element.54), channel_id=9, replica_groups={{0,2},{4,6},{8,10},{12,14},{1,3},{5,7},{9,11},{13,15},{16,18},{20,22},{..., dimensions={0}, use_global_device_ids=true | all-gather | bytes 147456 | tf_op jit(solution)/shard_map/all_gather | solution.py:269
  184.7 5.6 %all-gather.16 = bf16[256,384]{1,0:T(8,128)(2,1)S(1)} all-gather(bf16[64,384]{1,0:T(8,128)(2,1)S(1)} %slice.66), channel_id=18, replica_groups=mesh['xh'=2,'xl'=2,'yh'=4,'core'=2,'section'=8,'cfg'=2] {'xl','core'}, dimensions={0}, use_global_device_ids=true | all-gather | bytes 245760 | tf_op jit(solution)/shard_map/all_gather | solution.py:270
  192.2 5.6 %all-gather.8 = bf16[256,384]{1,0:T(8,128)(2,1)S(1)} all-gather(bf16[64,384]{1,0:T(8,128)(2,1)S(1)} %get-tuple-element.56), channel_id=10, replica_groups=mesh['xh'=2,'xl'=2,'yh'=4,'core'=2,'section'=8,'cfg'=2] {'xl','core'}, dimensions={0}, use_global_device_ids=true | all-gather | bytes 245760 | tf_op jit(solution)/shard_map/all_gather | solution.py:272
  198.5 7.1 %all-to-all-start.1 = ((bf16[16,2,768]{2,1,0:T(2,128)(2,1)}), bf16[16,2,768]{2,1,0:T(2,128)(2,1)S(1)}, u32[]{:S(2)}, u32[]{:S(2)}) async-start(bf16[16,2,768]{2,1,0:T(2,128)(2,1)} %bitcast.24), calls=%async_computation.1 | async-start | bytes 98304 | tf_op jit(solution)/shard_map/all_to_all | solution.py:276
  205.6 6.3 %all-gather.9 = bf16[256,768]{1,0:T(8,128)(2,1)S(1)} all-gather(bf16[64,768]{1,0:T(8,128)(2,1)S(1)} %get-tuple-element.57), channel_id=11, replica_groups=mesh['xh'=2,'xl'=2,'yh'=4,'core'=2,'section'=8,'cfg'=2] {'xl','core'}, dimensions={0}, use_global_device_ids=true | all-gather | bytes 491520 | tf_op jit(solution)/shard_map/all_gather | solution.py:277
  211.9 2.4 %all-to-all-done.1 = bf16[16,2,768]{2,1,0:T(2,128)(2,1)S(1)} async-done(((bf16[16,2,768]{2,1,0:T(2,128)(2,1)}), bf16[16,2,768]{2,1,0:T(2,128)(2,1)S(1)}, u32[]{:S(2)}, u32[]{:S(2)}) %all-to-all-start.1) | async-done | bytes 49184 | tf_op jit(solution)/shard_map/all_to_all | solution.py:276
  (65 shorter events, 34.2 us)
Async XLA Ops:
  0.6 72.3 %copy-start = (f32[1,1,28,4608]{3,1,2,0:T(1,128)S(1)}, f32[1,1,28,4608]{3,1,2,0:T(1,128)}, u32[]{:S(2)}) copy-start(f32[1,1,28,4608]{3,1,2,0:T(1,128)} %param.9) | copy-start | bytes 1548292
  0.6 51.6 %copy-start.3 = (s32[64]{0:T(128)S(1)}, s32[64]{0:T(128)}, u32[]{:S(2)}) copy-start(s32[64]{0:T(128)} %param.8) | copy-start | bytes 772
  0.7 1.0 copy-start.1
  1.8 0.9 copy-start.2
  2.7 50.4 %copy-start.4 = (bf16[1,16,1536]{2,1,0:T(8,128)(2,1)S(1)}, bf16[1,16,1536]{2,1,0:T(8,128)(2,1)}, u32[]{:S(2)}) copy-start(bf16[1,16,1536]{2,1,0:T(8,128)(2,1)} %param.6) | copy-start | bytes 147460
  4.0 27.6 %all-to-all-start = ((bf16[16,16,768]{2,1,0:T(8,128)(2,1)}), bf16[16,16,768]{2,1,0:T(8,128)(2,1)S(1)}, u32[]{:S(2)}, u32[]{:S(2)}) async-start(bf16[16,16,768]{2,1,0:T(8,128)(2,1)} %get-tuple-element.34), calls=%async_computation | async-start | bytes 786432 | tf_op jit(solution)/shard_map/all_to_all | solution.py:230
  28.2 3.4 %collective-permute-start = (bf16[144,768]{1,0:T(8,128)(2,1)S(1)}, bf16[144,768]{1,0:T(8,128)(2,1)S(1)}, u32[]{:S(2)}, u32[]{:S(2)}) collective-permute-start(bf16[144,768]{1,0:T(8,128)(2,1)S(1)} %get-tuple-element.33), channel_id=1, source_target_pairs={{0,16},{2,18},{4,20},{6,22},{8,24},{10,26},{12,28},{14,30},{16,0},... | collective-permute-start | bytes 663560 | tf_op jit(solution)/shard_map/ppermute | solution.py:235
  31.6 13.2 %collective-permute-start.3 = (bf16[288,768]{1,0:T(8,128)(2,1)S(1)}, bf16[288,768]{1,0:T(8,128)(2,1)S(1)}, u32[]{:S(2)}, u32[]{:S(2)}) collective-permute-start(bf16[288,768]{1,0:T(8,128)(2,1)S(1)} %pad_maximum_fusion.own), channel_id=1, source_target_pairs={{0,1},{2,3},{4,5},{6,7},{8,9},{10,11},{12,13},{14,15},{16,113},{18... | collective-permute-start | bytes 1327112 | tf_op jit(solution)/shard_map/ppermute | solution.py:237
  34.7 14.9 %collective-permute-start.1 = (bf16[288,768]{1,0:T(8,128)(2,1)S(1)}, bf16[288,768]{1,0:T(8,128)(2,1)S(1)}, u32[]{:S(2)}, u32[]{:S(2)}) collective-permute-start(bf16[288,768]{1,0:T(8,128)(2,1)S(1)} %pad_maximum_fusion.own), channel_id=1, source_target_pairs={{0,97},{2,99},{4,101},{6,103},{8,105},{10,107},{12,109},{14,111},{... | collective-permute-start | bytes 1327112 | tf_op jit(solution)/shard_map/ppermute | solution.py:237
  44.8 18.8 %collective-permute-start.4 = (bf16[288,768]{1,0:T(8,128)(2,1)S(1)}, bf16[288,768]{1,0:T(8,128)(2,1)}, u32[]{:S(2)}, u32[]{:S(2)}) collective-permute-start(bf16[288,768]{1,0:T(8,128)(2,1)S(1)} %collective-permute-done.3.up1), channel_id=1, source_target_pairs={{0,1},{2,3},{4,5},{6,7},{8,9},{10,11},{12,13},{14,15},{16,113},{18... | collective-permute-start | bytes 1327112 | tf_op jit(solution)/shard_map/ppermute | solution.py:241
  49.6 12.0 %collective-permute-start.2 = (bf16[288,768]{1,0:T(8,128)(2,1)S(1)}, bf16[288,768]{1,0:T(8,128)(2,1)}, u32[]{:S(2)}, u32[]{:S(2)}) collective-permute-start(bf16[288,768]{1,0:T(8,128)(2,1)S(1)} %collective-permute-done.1.down1), channel_id=1, source_target_pairs={{0,97},{2,99},{4,101},{6,103},{8,105},{10,107},{12,109},{14,111},{... | collective-permute-start | bytes 1327112 | tf_op jit(solution)/shard_map/ppermute | solution.py:241
  61.6 19.8 %collective-permute-start.6 = (bf16[288,768]{1,0:T(8,128)(2,1)}, bf16[288,768]{1,0:T(8,128)(2,1)S(1)}, u32[]{:S(2)}, u32[]{:S(2)}) collective-permute-start(bf16[288,768]{1,0:T(8,128)(2,1)} %collective-permute-done.2.down2), channel_id=1, source_target_pairs={{0,97},{2,99},{4,101},{6,103},{8,105},{10,107},{12,109},{14,111},{... | collective-permute-start | bytes 1327112 | tf_op jit(solution)/shard_map/ppermute | solution.py:243
  63.6 12.1 %collective-permute-start.5 = (bf16[288,768]{1,0:T(8,128)(2,1)}, bf16[288,768]{1,0:T(8,128)(2,1)S(1)}, u32[]{:S(2)}, u32[]{:S(2)}) collective-permute-start(bf16[288,768]{1,0:T(8,128)(2,1)} %collective-permute-done.4.up2), channel_id=1, source_target_pairs={{0,1},{2,3},{4,5},{6,7},{8,9},{10,11},{12,13},{14,15},{16,113},{18... | collective-permute-start | bytes 1327112 | tf_op jit(solution)/shard_map/ppermute | solution.py:243
  69.5 25.2 %collective-permute-start.9 = (bf16[256,768]{1,0:T(8,128)(2,1)S(1)}, bf16[256,768]{1,0:T(8,128)(2,1)S(1)}, u32[]{:S(2)}, u32[]{:S(2)}) collective-permute-start(bf16[256,768]{1,0:T(8,128)(2,1)S(1)} %bitcast.46), channel_id=1, source_target_pairs={{0,256},{1,257},{2,258},{3,259},{4,260},{5,261},{6,262},{7,263},{8... | collective-permute-start | bytes 1179656 | tf_op jit(solution)/shard_map/ppermute | solution.py:239
  75.7 9.6 %collective-permute-start.7 = (bf16[144,768]{1,0:T(8,128)(2,1)S(1)}, bf16[144,768]{1,0:T(8,128)(2,1)S(1)}, u32[]{:S(2)}, u32[]{:S(2)}) collective-permute-start(bf16[144,768]{1,0:T(8,128)(2,1)S(1)} %slice.58), channel_id=1, source_target_pairs={{0,1},{2,3},{4,5},{6,7},{8,9},{10,11},{12,13},{14,15},{16,113},{18... | collective-permute-start | bytes 663560 | tf_op jit(solution)/shard_map/ppermute | solution.py:244
  81.5 9.4 %collective-permute-start.8 = (bf16[144,768]{1,0:T(8,128)(2,1)S(1)}, bf16[144,768]{1,0:T(8,128)(2,1)S(1)}, u32[]{:S(2)}, u32[]{:S(2)}) collective-permute-start(bf16[144,768]{1,0:T(8,128)(2,1)S(1)} %slice.59), channel_id=1, source_target_pairs={{0,97},{2,99},{4,101},{6,103},{8,105},{10,107},{12,109},{14,111},{... | collective-permute-start | bytes 663560 | tf_op jit(solution)/shard_map/ppermute | solution.py:245
  198.5 15.8 %all-to-all-start.1 = ((bf16[16,2,768]{2,1,0:T(2,128)(2,1)}), bf16[16,2,768]{2,1,0:T(2,128)(2,1)S(1)}, u32[]{:S(2)}, u32[]{:S(2)}) async-start(bf16[16,2,768]{2,1,0:T(2,128)(2,1)} %bitcast.24), calls=%async_computation.1 | async-start | bytes 98304 | tf_op jit(solution)/shard_map/all_to_all | solution.py:276

commit v5 on v4

--- a/solution.py
+++ b/solution.py
@@ -49,20 +49,42 @@
 UP = route(lambda x, y, core: (x, (y + 1 - 2 * core) % 8, core))
 DOWN = route(lambda x, y, core: (x, (y - 1 + 2 * core) % 8, core))
 ACROSS = [(i, (i + 256) % 512) for i in range(512)]
-PAIRS = (
-    [[s, s + 1] for s in range(0, SECTIONS, 2)],
-    [[s, (s + 1) % SECTIONS] for s in range(1, SECTIONS, 2)],
-)
+
+
+def onward(section, flip):
+    def number(x, y, core, s):
+        return (((x * 4 + y // 2) * 2 + core) * 8 + s) * 2 + y % 2
+
+    return [
+        (number(x, y, core, section), number(x ^ flip, y, core, section + 1))
+        for x in range(4)
+        for y in range(8)
+        for core in range(2)
+    ]
 
 
 def nt_dot(a, b):
     return lax.dot_general(a, b, (((1,), (1,)), ((), ())), preferred_element_type=jnp.float32)
 
 
-def block_kernel(tick, who, x_ref, w_ref, kv_ref, other_ref, mod_ref, gate_ref, cos_ref, sin_ref, block_ref, old_ref, state_ref, fresh_ref):
-    member = who[0]
+def block_kernel(tick, who, near_ref, far_ref, w_ref, kv_ref, other_ref, mod_ref, gate_ref, cos_ref, sin_ref, block_ref, old_ref, state_ref, fresh_ref):
     active = who[1] == tick
-    xs = [x_ref[i].astype(jnp.float32) for i in range(MEMBERS)]
+
+    @pl.when(jnp.logical_not(active))
+    def _():
+        fresh_ref[...] = old_ref[...]
+
+    @pl.when(active)
+    def _():
+        active_block(who[0], near_ref, far_ref, w_ref, kv_ref, other_ref, mod_ref, gate_ref, cos_ref, sin_ref, block_ref, state_ref, fresh_ref)
+
+
+def active_block(member, near_ref, far_ref, w_ref, kv_ref, other_ref, mod_ref, gate_ref, cos_ref, sin_ref, block_ref, state_ref, fresh_ref):
+    near = [near_ref[core].astype(jnp.float32) for core in range(2)]
+    far = [far_ref[core].astype(jnp.float32) for core in range(2)]
+    low = member < 2
+    xs = [jnp.where(low, near[core], far[core]) for core in range(2)]
+    xs += [jnp.where(low, far[core], near[core]) for core in range(2)]
     center = sum(jnp.sum(x, axis=-1, keepdims=True) for x in xs) / D
     xs = [x - center for x in xs]
     spread = sum(jnp.sum(x * x, axis=-1, keepdims=True) for x in xs) / D
@@ -115,13 +137,13 @@
         for h in heads
     ]
     for h in heads:
-        state = x_ref[member, :, cols[h]].astype(jnp.float32) + gate_ref[0:1, cols[h]] * (attended[h] / total[h])
+        state = near_ref[member % 2, :, cols[h]].astype(jnp.float32) + gate_ref[0:1, cols[h]] * (attended[h] / total[h])
         state_ref[:, cols[h]] = state.astype(jnp.bfloat16)
-        fresh_ref[:, cols[h]] = jnp.where(active, key[h], old_ref[:, cols[h]])
-        fresh_ref[:, vcols[h]] = jnp.where(active, value[h], old_ref[:, vcols[h]])
-
-
-def run_block(tick, who, x, weight, kv, other, mod, gate, cosine, sine, blocks, old):
+        fresh_ref[:, cols[h]] = key[h]
+        fresh_ref[:, vcols[h]] = value[h]
+
+
+def run_block(tick, who, near, far, weight, kv, other, mod, gate, cosine, sine, blocks, old):
     vmem = pl.BlockSpec(memory_space=pltpu.VMEM)
     weight = pltpu.with_memory_space_constraint(weight, pltpu.VMEM)
     return pl.pallas_call(
@@ -130,11 +152,11 @@
             jax.ShapeDtypeStruct((GROUP, PART), jnp.bfloat16),
             jax.ShapeDtypeStruct((GROUP, 2 * PART), jnp.bfloat16),
         ),
-        in_specs=[pl.BlockSpec(memory_space=pltpu.SMEM)] + [vmem] * 10,
+        in_specs=[pl.BlockSpec(memory_space=pltpu.SMEM)] + [vmem] * 11,
         out_specs=(vmem, vmem),
-        compiler_params=pltpu.CompilerParams(vmem_limit_bytes=24 * 1024 * 1024),
+        compiler_params=pltpu.CompilerParams(vmem_limit_bytes=8 * 1024 * 1024),
         name="block_step",
-    )(who, x, weight, kv, other, mod, gate, cosine, sine, blocks, old)
+    )(who, near, far, weight, kv, other, mod, gate, cosine, sine, blocks, old)
 
 
 def prepare_kernel(where, stale_ref, columns_ref, out_ref, half_ref):
@@ -195,7 +217,7 @@
         in_specs=[pl.BlockSpec(memory_space=pltpu.SMEM)] + [pl.BlockSpec(memory_space=pl.ANY)] * len(blocks),
         out_specs=pl.BlockSpec(memory_space=pltpu.VMEM),
         scratch_shapes=[pltpu.VMEM((3 * PART, D), jnp.bfloat16), pltpu.SemaphoreType.DMA],
-        compiler_params=pltpu.CompilerParams(vmem_limit_bytes=12 * 1024 * 1024),
+        compiler_params=pltpu.CompilerParams(vmem_limit_bytes=8 * 1024 * 1024),
         name="place_weight",
     )(where, *blocks)
 
@@ -207,7 +229,7 @@
         out_shape=[jax.ShapeDtypeStruct(shape, jnp.bfloat16) for shape in outs],
         in_specs=[pl.BlockSpec(memory_space=pltpu.SMEM)] + [vmem] * len(arrays),
         out_specs=[vmem] * len(outs),
-        compiler_params=pltpu.CompilerParams(vmem_limit_bytes=24 * 1024 * 1024),
+        compiler_params=pltpu.CompilerParams(vmem_limit_bytes=8 * 1024 * 1024),
         name=kernel.__name__,
     )(where, *arrays)
 
@@ -245,6 +267,8 @@
     down4 = lax.ppermute(down3[COLUMNS:], AXES, DOWN)
     weight = place(where, [own, up1, up2, up3, down1, down2, down3, up4, down4])
     x = jnp.transpose(x.reshape(GROUP, MEMBERS, PART), (1, 0, 2))
+    near = lax.dynamic_slice_in_dim(x, index["xl"] * 2, 2, 0)
+    far = lax.dynamic_slice_in_dim(x, 2 - index["xl"] * 2, 2, 0)
 
     row = lax.dynamic_index_in_dim(modulation[0, 0], timestep[0], 0, keepdims=False)
     mod = row[: 2 * D].reshape(2, D)
@@ -264,10 +288,12 @@
 
     fresh = jnp.zeros((GROUP, 2 * PART), jnp.bfloat16)
     for tick in range(SECTIONS):
-        state, fresh = run_block(tick, who, x, weight, kv, kv_other, mod, gate, cosine, sine, blocks[:, None], fresh)
+        state, fresh = run_block(tick, who, near, far, weight, kv, kv_other, mod, gate, cosine, sine, blocks[:, None], fresh)
         if tick + 1 < SECTIONS:
-            state = lax.all_gather(state, "section", axis=0, tiled=False, axis_index_groups=PAIRS[tick % 2])[0]
-            x = lax.all_gather(state, ("xl", "core"), axis=0, tiled=False)
+            near = lax.ppermute(state, AXES, onward(tick, 0))
+            far = lax.ppermute(state, AXES, onward(tick, 1))
+            near = lax.all_gather(near, "core", axis=0, tiled=False)
+            far = lax.all_gather(far, "core", axis=0, tiled=False)
 
     ends = lax.all_gather(state, ("xl", "core"), axis=0, tiled=False)
     finals = lax.dynamic_slice_in_dim(ends, member * LOCAL, LOCAL, 1)

time: 217 us -> 196 us (0.903)
  blocking collectives: 115 us -> 58.7 us
  starting transfers between devices: 48.7 us -> 89.5 us
  Pallas kernels: 20.9 us -> 11.8 us
  local copies, waits for them, and re-layouts: 5.35 us -> 9.38 us
    all_gather x14, blocking collectives: 82.2 us -> 26.2 us  [the longest x7 13.1 us: body(): near = lax.all_gather(near, 'core', axis=0, tiled=False)]
    all_to_all x1, starting transfers between devices: 7.11 us -> 35.3 us  [body(): lax.all_to_all(finals, ('section', 'cfg'), split_axis=0, concat_axis=0, t...]
    ppermute x0 -> x14, starting transfers between devices: none -> 12.5 us  [the longest x7 6.82 us: body(): near = lax.ppermute(state, AXES, onward(tick, 0))]
    pallas_call x8, Pallas kernels: 15.1 us -> 5.98 us  [run_block(): pl.pallas_call(functools.partial(block_kernel, tick), out_shape=(jax.Shap...]
    unnamed x11 -> x19, local copies, waits for them, and re-layouts: 1.94 us -> 5.74 us
  transfers between devices with their start and end apart: 12 -> 26, of which waited for: 6 -> 7; matrix products, arithmetic and copies ran while one was open for 2% -> 1% of each run, Pallas kernels for 2% -> 2%
where the time goes in v5:
time: 196 us; the launch traced here: 195 us
  starting transfers between devices  89.5 us (46%)
  blocking collectives  58.7 us (30%)
  waiting for transfers between devices  22.1 us (11%)
  Pallas kernels  11.8 us (6%)
  local copies, waits for them, and re-layouts  9.38 us (5%)
    all_to_all x1, starting transfers between devices, body(): lax.all_to_all(finals, ('section', 'cfg'), split_axis=0, concat_axis=0, t...  35.3 us
    all_gather x1, blocking collectives, body(): columns = lax.all_gather(columns, ('xh', 'xl'), axis=0, tiled=False)  14.6 us
    all_gather x7, blocking collectives, body(): near = lax.all_gather(near, 'core', axis=0, tiled=False)  13.1 us
    all_gather x7, blocking collectives, body(): far = lax.all_gather(far, 'core', axis=0, tiled=False)  13.1 us
    all_to_all x1, starting transfers between devices, body(): lax.all_to_all(outgoing, ('xl', 'yh', 'core'), split_axis=0, concat_axis=...  9.06 us
    ppermute x2, starting transfers between devices, body(): up3, down3 = (lax.ppermute(up2, AXES, UP), lax.ppermute(down2, AXES, DOWN))  7.04 us
    ppermute x7, starting transfers between devices, body(): near = lax.ppermute(state, AXES, onward(tick, 0))  6.82 us
    ppermute x2, starting transfers between devices, body(): up2, down2 = (lax.ppermute(up1, AXES, UP), lax.ppermute(down1, AXES, DOWN))  6.77 us
  transfers between devices with their start and end apart: 26, of which 7 were waited for; matrix products, arithmetic and copies ran while one was open for 1% of the time, Pallas kernels for 2%

profile of v5, /device:TPU:16, one launch (start us, length us, event | category | flops | bytes accessed | tf_op | source)
XLA Modules:
  0.0 194.5 jit_solution(10745586112374887418)
XLA Ops:
  4.0 9.1 %all-to-all-start = ((bf16[16,16,768]{2,1,0:T(8,128)(2,1)}), bf16[16,16,768]{2,1,0:T(8,128)(2,1)S(1)}, u32[]{:S(2)}, u32[]{:S(2)}) async-start(bf16[16,16,768]{2,1,0:T(8,128)(2,1)} %get-tuple-element.34), calls=%async_computation | async-start | bytes 786432 | tf_op jit(solution)/shard_map/all_to_all | solution.py:252
  13.0 14.6 %all-gather = bf16[576,768]{1,0:T(8,128)(2,1)S(1)} all-gather(bf16[144,768]{1,0:T(8,128)(2,1)S(1)} %get-tuple-element.31), channel_id=2, replica_groups=mesh['xh'=2,'xl'=2,'yh'=4,'core'=2,'section'=8,'cfg'=2] {'xh','xl'}, dimensions={0}, use_global_device_ids=true | all-gather | bytes 1105920 | tf_op jit(solution)/shard_map/all_gather | solution.py:255
  28.2 1.9 collective-permute-start
  31.6 3.1 %collective-permute-start.3 = (bf16[288,768]{1,0:T(8,128)(2,1)S(1)}, bf16[288,768]{1,0:T(8,128)(2,1)S(1)}, u32[]{:S(2)}, u32[]{:S(2)}) collective-permute-start(bf16[288,768]{1,0:T(8,128)(2,1)S(1)} %pad_maximum_fusion.own), channel_id=1, source_target_pairs={{0,1},{2,3},{4,5},{6,7},{8,9},{10,11},{12,13},{14,15},{16,113},{18... | collective-permute-start | bytes 1327112 | tf_op jit(solution)/shard_map/ppermute | solution.py:259
  34.7 2.8 %collective-permute-start.1 = (bf16[288,768]{1,0:T(8,128)(2,1)S(1)}, bf16[288,768]{1,0:T(8,128)(2,1)S(1)}, u32[]{:S(2)}, u32[]{:S(2)}) collective-permute-start(bf16[288,768]{1,0:T(8,128)(2,1)S(1)} %pad_maximum_fusion.own), channel_id=1, source_target_pairs={{0,97},{2,99},{4,101},{6,103},{8,105},{10,107},{12,109},{14,111},{... | collective-permute-start | bytes 1327112 | tf_op jit(solution)/shard_map/ppermute | solution.py:259
  38.4 6.4 %collective-permute-done.3.up1 = bf16[288,768]{1,0:T(8,128)(2,1)S(1)} collective-permute-done((bf16[288,768]{1,0:T(8,128)(2,1)S(1)}, bf16[288,768]{1,0:T(8,128)(2,1)S(1)}, u32[]{:S(2)}, u32[]{:S(2)}) %collective-permute-start.3) | collective-permute-done | bytes 442400 | tf_op jit(solution)/shard_map/ppermute | solution.py:259
  44.8 4.8 %collective-permute-start.4 = (bf16[288,768]{1,0:T(8,128)(2,1)S(1)}, bf16[288,768]{1,0:T(8,128)(2,1)}, u32[]{:S(2)}, u32[]{:S(2)}) collective-permute-start(bf16[288,768]{1,0:T(8,128)(2,1)S(1)} %collective-permute-done.3.up1), channel_id=1, source_target_pairs={{0,1},{2,3},{4,5},{6,7},{8,9},{10,11},{12,13},{14,15},{16,113},{18... | collective-permute-start | bytes 1327112 | tf_op jit(solution)/shard_map/ppermute | solution.py:263
  49.6 1.9 collective-permute-start.2
  53.3 6.1 %all_gather.107 = bf16[64,1536]{1,0:T(8,128)(2,1)} all-gather(bf16[16,1536]{1,0:T(8,128)(2,1)S(1)} %bitcast.81), channel_id=1, replica_groups=mesh['xh'=2,'xl'=2,'yh'=4,'core'=2,'section'=8,'cfg'=2] {'xl','core'}, dimensions={0}, use_global_device_ids=true | all-gather | bytes 245760 | tf_op jit(solution)/shard_map/all_gather | solution.py:262
  59.3 2.3 %collective-permute-done.2.down2 = bf16[288,768]{1,0:T(8,128)(2,1)} collective-permute-done((bf16[288,768]{1,0:T(8,128)(2,1)S(1)}, bf16[288,768]{1,0:T(8,128)(2,1)}, u32[]{:S(2)}, u32[]{:S(2)}) %collective-permute-start.2) | collective-permute-done | bytes 442400 | tf_op jit(solution)/shard_map/ppermute | solution.py:263
  61.6 1.9 collective-permute-start.6
  63.6 5.1 %collective-permute-start.5 = (bf16[288,768]{1,0:T(8,128)(2,1)}, bf16[288,768]{1,0:T(8,128)(2,1)S(1)}, u32[]{:S(2)}, u32[]{:S(2)}) collective-permute-start(bf16[288,768]{1,0:T(8,128)(2,1)} %collective-permute-done.4.up2), channel_id=1, source_target_pairs={{0,1},{2,3},{4,5},{6,7},{8,9},{10,11},{12,13},{14,15},{16,113},{18... | collective-permute-start | bytes 1327112 | tf_op jit(solution)/shard_map/ppermute | solution.py:265
  68.9 3.4 %collective-permute-start.9 = (bf16[256,768]{1,0:T(8,128)(2,1)S(1)}, bf16[256,768]{1,0:T(8,128)(2,1)S(1)}, u32[]{:S(2)}, u32[]{:S(2)}) collective-permute-start(bf16[256,768]{1,0:T(8,128)(2,1)S(1)} %bitcast.50), channel_id=1, source_target_pairs={{0,256},{1,257},{2,258},{3,259},{4,260},{5,261},{6,262},{7,263},{8... | collective-permute-start | bytes 1179656 | tf_op jit(solution)/shard_map/ppermute | solution.py:261
  73.6 2.1 %collective-permute-done.5.up3 = bf16[288,768]{1,0:T(8,128)(2,1)S(1)} collective-permute-done((bf16[288,768]{1,0:T(8,128)(2,1)}, bf16[288,768]{1,0:T(8,128)(2,1)S(1)}, u32[]{:S(2)}, u32[]{:S(2)}) %collective-permute-start.5) | collective-permute-done | bytes 442400 | tf_op jit(solution)/shard_map/ppermute | solution.py:265
  75.7 5.7 %collective-permute-start.7 = (bf16[144,768]{1,0:T(8,128)(2,1)S(1)}, bf16[144,768]{1,0:T(8,128)(2,1)S(1)}, u32[]{:S(2)}, u32[]{:S(2)}) collective-permute-start(bf16[144,768]{1,0:T(8,128)(2,1)S(1)} %slice.23), channel_id=1, source_target_pairs={{0,1},{2,3},{4,5},{6,7},{8,9},{10,11},{12,13},{14,15},{16,113},{18... | collective-permute-start | bytes 663560 | tf_op jit(solution)/shard_map/ppermute | solution.py:266
  81.5 1.9 collective-permute-start.8
  84.9 6.0 %collective-permute-done.8.down4 = bf16[144,768]{1,0:T(8,128)(2,1)S(1)} collective-permute-done((bf16[144,768]{1,0:T(8,128)(2,1)S(1)}, bf16[144,768]{1,0:T(8,128)(2,1)S(1)}, u32[]{:S(2)}, u32[]{:S(2)}) %collective-permute-start.8) | collective-permute-done | bytes 221216 | tf_op jit(solution)/shard_map/ppermute | solution.py:267
  91.9 3.9 %place_weight.1.w_ref = bf16[1536,1152]{1,0:T(8,128)(2,1)S(1)} custom-call(s32[4]{0:T(128)S(1)} %pad_add_fusion.1.where, bf16[288,768]{1,0:T(8,128)(2,1)S(1)} %pad_maximum_fusion.own, bf16[288,768]{1,0:T(8,128)(2,1)S(1)} %collective-permute-done.3.up1, bf16[288,768]{1,0:T(8,128)(2,1)} %collective-permute-done.4.up2, ...), custom_call_target="tpu_custom_call" | custom-call | tf_op jit(solution)/shard_map/place_weight/pallas_call | solution.py:214
  95.8 1.9 block_step.8
  97.7 2.8 %collective-permute-start.10 = (bf16[64,384]{1,0:T(8,128)(2,1)S(1)}, bf16[64,384]{1,0:T(8,128)(2,1)S(1)}, u32[]{:S(2)}, u32[]{:S(2)}) collective-permute-start(bf16[64,384]{1,0:T(8,128)(2,1)S(1)} %get-tuple-element.42), channel_id=1, source_target_pairs={{0,2},{16,18},{1,3},{17,19},{32,34},{48,50},{33,35},{49,51},{64,66... | collective-permute-start | bytes 147464 | tf_op jit(solution)/shard_map/ppermute | solution.py:293
  104.2 1.9 all-gather.2
  107.9 1.9 all-gather.3
  113.6 1.9 all-gather.5
  119.3 1.9 all-gather.7
  124.9 1.9 all-gather.9
  130.8 1.9 all-gather.11
  136.4 1.9 all-gather.13
  140.2 2.0 %copy-done.2 = bf16[1536,1152]{1,0:T(8,128)(2,1)S(1)} copy-done((bf16[1536,1152]{1,0:T(8,128)(2,1)S(1)}, bf16[1536,1152]{1,0:T(8,128)(2,1)}, u32[]{:S(2)}) %copy-start.2) | copy-done | bytes 3538968
  142.7 5.6 %all-gather.15 = bf16[256,384]{1,0:T(8,128)(2,1)S(1)} all-gather(bf16[64,384]{1,0:T(8,128)(2,1)S(1)} %get-tuple-element.56), channel_id=17, replica_groups=mesh['xh'=2,'xl'=2,'yh'=4,'core'=2,'section'=8,'cfg'=2] {'xl','core'}, dimensions={0}, use_global_device_ids=true | all-gather | bytes 245760 | tf_op jit(solution)/shard_map/all_gather | solution.py:298
  149.1 35.3 %all-to-all-start.1 = ((bf16[16,2,768]{2,1,0:T(2,128)(2,1)}), bf16[16,2,768]{2,1,0:T(2,128)(2,1)S(1)}, u32[]{:S(2)}, u32[]{:S(2)}) async-start(bf16[16,2,768]{2,1,0:T(2,128)(2,1)} %bitcast.32), calls=%async_computation.1 | async-start | bytes 98304 | tf_op jit(solution)/shard_map/all_to_all | solution.py:302
  184.4 6.3 %all-gather.16 = bf16[256,768]{1,0:T(8,128)(2,1)S(1)} all-gather(bf16[64,768]{1,0:T(8,128)(2,1)S(1)} %get-tuple-element.57), channel_id=18, replica_groups=mesh['xh'=2,'xl'=2,'yh'=4,'core'=2,'section'=8,'cfg'=2] {'xl','core'}, dimensions={0}, use_global_device_ids=true | all-gather | bytes 491520 | tf_op jit(solution)/shard_map/all_gather | solution.py:303
  190.7 2.4 %all-to-all-done.1 = bf16[16,2,768]{2,1,0:T(2,128)(2,1)S(1)} async-done(((bf16[16,2,768]{2,1,0:T(2,128)(2,1)}), bf16[16,2,768]{2,1,0:T(2,128)(2,1)S(1)}, u32[]{:S(2)}, u32[]{:S(2)}) %all-to-all-start.1) | async-done | bytes 49184 | tf_op jit(solution)/shard_map/all_to_all | solution.py:302
  (96 shorter events, 40.3 us)
Async XLA Ops:
  0.6 68.1 %copy-start = (f32[1,1,28,4608]{3,1,2,0:T(1,128)S(1)}, f32[1,1,28,4608]{3,1,2,0:T(1,128)}, u32[]{:S(2)}) copy-start(f32[1,1,28,4608]{3,1,2,0:T(1,128)} %param.9) | copy-start | bytes 1548292
  0.6 37.0 %copy-start.7 = (s32[64]{0:T(128)S(1)}, s32[64]{0:T(128)}, u32[]{:S(2)}) copy-start(s32[64]{0:T(128)} %param.8) | copy-start | bytes 772
  0.7 1.0 copy-start.5
  2.7 50.6 %copy-start.8 = (bf16[1,16,1536]{2,1,0:T(8,128)(2,1)S(1)}, bf16[1,16,1536]{2,1,0:T(8,128)(2,1)}, u32[]{:S(2)}) copy-start(bf16[1,16,1536]{2,1,0:T(8,128)(2,1)} %param.6) | copy-start | bytes 147460
  4.0 27.6 %all-to-all-start = ((bf16[16,16,768]{2,1,0:T(8,128)(2,1)}), bf16[16,16,768]{2,1,0:T(8,128)(2,1)S(1)}, u32[]{:S(2)}, u32[]{:S(2)}) async-start(bf16[16,16,768]{2,1,0:T(8,128)(2,1)} %get-tuple-element.34), calls=%async_computation | async-start | bytes 786432 | tf_op jit(solution)/shard_map/all_to_all | solution.py:252
  28.2 3.4 %collective-permute-start = (bf16[144,768]{1,0:T(8,128)(2,1)S(1)}, bf16[144,768]{1,0:T(8,128)(2,1)S(1)}, u32[]{:S(2)}, u32[]{:S(2)}) collective-permute-start(bf16[144,768]{1,0:T(8,128)(2,1)S(1)} %get-tuple-element.33), channel_id=1, source_target_pairs={{0,16},{2,18},{4,20},{6,22},{8,24},{10,26},{12,28},{14,30},{16,0},... | collective-permute-start | bytes 663560 | tf_op jit(solution)/shard_map/ppermute | solution.py:257
  31.6 13.2 %collective-permute-start.3 = (bf16[288,768]{1,0:T(8,128)(2,1)S(1)}, bf16[288,768]{1,0:T(8,128)(2,1)S(1)}, u32[]{:S(2)}, u32[]{:S(2)}) collective-permute-start(bf16[288,768]{1,0:T(8,128)(2,1)S(1)} %pad_maximum_fusion.own), channel_id=1, source_target_pairs={{0,1},{2,3},{4,5},{6,7},{8,9},{10,11},{12,13},{14,15},{16,113},{18... | collective-permute-start | bytes 1327112 | tf_op jit(solution)/shard_map/ppermute | solution.py:259
  34.7 14.9 %collective-permute-start.1 = (bf16[288,768]{1,0:T(8,128)(2,1)S(1)}, bf16[288,768]{1,0:T(8,128)(2,1)S(1)}, u32[]{:S(2)}, u32[]{:S(2)}) collective-permute-start(bf16[288,768]{1,0:T(8,128)(2,1)S(1)} %pad_maximum_fusion.own), channel_id=1, source_target_pairs={{0,97},{2,99},{4,101},{6,103},{8,105},{10,107},{12,109},{14,111},{... | collective-permute-start | bytes 1327112 | tf_op jit(solution)/shard_map/ppermute | solution.py:259
  44.8 18.8 %collective-permute-start.4 = (bf16[288,768]{1,0:T(8,128)(2,1)S(1)}, bf16[288,768]{1,0:T(8,128)(2,1)}, u32[]{:S(2)}, u32[]{:S(2)}) collective-permute-start(bf16[288,768]{1,0:T(8,128)(2,1)S(1)} %collective-permute-done.3.up1), channel_id=1, source_target_pairs={{0,1},{2,3},{4,5},{6,7},{8,9},{10,11},{12,13},{14,15},{16,113},{18... | collective-permute-start | bytes 1327112 | tf_op jit(solution)/shard_map/ppermute | solution.py:263
  49.6 12.0 %collective-permute-start.2 = (bf16[288,768]{1,0:T(8,128)(2,1)S(1)}, bf16[288,768]{1,0:T(8,128)(2,1)}, u32[]{:S(2)}, u32[]{:S(2)}) collective-permute-start(bf16[288,768]{1,0:T(8,128)(2,1)S(1)} %collective-permute-done.1.down1), channel_id=1, source_target_pairs={{0,97},{2,99},{4,101},{6,103},{8,105},{10,107},{12,109},{14,111},{... | collective-permute-start | bytes 1327112 | tf_op jit(solution)/shard_map/ppermute | solution.py:263
  61.6 19.8 %collective-permute-start.6 = (bf16[288,768]{1,0:T(8,128)(2,1)}, bf16[288,768]{1,0:T(8,128)(2,1)S(1)}, u32[]{:S(2)}, u32[]{:S(2)}) collective-permute-start(bf16[288,768]{1,0:T(8,128)(2,1)} %collective-permute-done.2.down2), channel_id=1, source_target_pairs={{0,97},{2,99},{4,101},{6,103},{8,105},{10,107},{12,109},{14,111},{... | collective-permute-start | bytes 1327112 | tf_op jit(solution)/shard_map/ppermute | solution.py:265
  63.6 12.1 %collective-permute-start.5 = (bf16[288,768]{1,0:T(8,128)(2,1)}, bf16[288,768]{1,0:T(8,128)(2,1)S(1)}, u32[]{:S(2)}, u32[]{:S(2)}) collective-permute-start(bf16[288,768]{1,0:T(8,128)(2,1)} %collective-permute-done.4.up2), channel_id=1, source_target_pairs={{0,1},{2,3},{4,5},{6,7},{8,9},{10,11},{12,13},{14,15},{16,113},{18... | collective-permute-start | bytes 1327112 | tf_op jit(solution)/shard_map/ppermute | solution.py:265
  68.9 26.9 %collective-permute-start.9 = (bf16[256,768]{1,0:T(8,128)(2,1)S(1)}, bf16[256,768]{1,0:T(8,128)(2,1)S(1)}, u32[]{:S(2)}, u32[]{:S(2)}) collective-permute-start(bf16[256,768]{1,0:T(8,128)(2,1)S(1)} %bitcast.50), channel_id=1, source_target_pairs={{0,256},{1,257},{2,258},{3,259},{4,260},{5,261},{6,262},{7,263},{8... | collective-permute-start | bytes 1179656 | tf_op jit(solution)/shard_map/ppermute | solution.py:261
  75.7 9.1 %collective-permute-start.7 = (bf16[144,768]{1,0:T(8,128)(2,1)S(1)}, bf16[144,768]{1,0:T(8,128)(2,1)S(1)}, u32[]{:S(2)}, u32[]{:S(2)}) collective-permute-start(bf16[144,768]{1,0:T(8,128)(2,1)S(1)} %slice.23), channel_id=1, source_target_pairs={{0,1},{2,3},{4,5},{6,7},{8,9},{10,11},{12,13},{14,15},{16,113},{18... | collective-permute-start | bytes 663560 | tf_op jit(solution)/shard_map/ppermute | solution.py:266
  81.5 9.4 %collective-permute-start.8 = (bf16[144,768]{1,0:T(8,128)(2,1)S(1)}, bf16[144,768]{1,0:T(8,128)(2,1)S(1)}, u32[]{:S(2)}, u32[]{:S(2)}) collective-permute-start(bf16[144,768]{1,0:T(8,128)(2,1)S(1)} %slice.24), channel_id=1, source_target_pairs={{0,97},{2,99},{4,101},{6,103},{8,105},{10,107},{12,109},{14,111},{... | collective-permute-start | bytes 663560 | tf_op jit(solution)/shard_map/ppermute | solution.py:267
  95.8 38.8 %copy-start.1 = (bf16[1536,1152]{1,0:T(8,128)(2,1)}, bf16[1536,1152]{1,0:T(8,128)(2,1)S(1)}, u32[]{:S(2)}) copy-start(bf16[1536,1152]{1,0:T(8,128)(2,1)S(1)} %place_weight.1.w_ref) | copy-start | bytes 10616836
  97.7 4.6 %collective-permute-start.10 = (bf16[64,384]{1,0:T(8,128)(2,1)S(1)}, bf16[64,384]{1,0:T(8,128)(2,1)S(1)}, u32[]{:S(2)}, u32[]{:S(2)}) collective-permute-start(bf16[64,384]{1,0:T(8,128)(2,1)S(1)} %get-tuple-element.42), channel_id=1, source_target_pairs={{0,2},{16,18},{1,3},{17,19},{32,34},{48,50},{33,35},{49,51},{64,66... | collective-permute-start | bytes 147464 | tf_op jit(solution)/shard_map/ppermute | solution.py:293
  100.6 3.6 %collective-permute-start.11 = (bf16[64,384]{1,0:T(8,128)(2,1)S(1)}, bf16[64,384]{1,0:T(8,128)(2,1)S(1)}, u32[]{:S(2)}, u32[]{:S(2)}) collective-permute-start(bf16[64,384]{1,0:T(8,128)(2,1)S(1)} %get-tuple-element.42), channel_id=1, source_target_pairs={{0,130},{16,146},{1,131},{17,147},{32,162},{48,178},{33,163},{49,1... | collective-permute-start | bytes 147464 | tf_op jit(solution)/shard_map/ppermute | solution.py:294
  106.6 1.3 collective-permute-start.12
  107.3 2.6 %collective-permute-start.13 = (bf16[64,384]{1,0:T(8,128)(2,1)S(1)}, bf16[64,384]{1,0:T(8,128)(2,1)S(1)}, u32[]{:S(2)}, u32[]{:S(2)}) collective-permute-start(bf16[64,384]{1,0:T(8,128)(2,1)S(1)} %get-tuple-element.44), channel_id=1, source_target_pairs={{2,132},{18,148},{3,133},{19,149},{34,164},{50,180},{35,165},{51,1... | collective-permute-start | bytes 147464 | tf_op jit(solution)/shard_map/ppermute | solution.py:294
  112.2 1.3 collective-permute-start.14
  112.9 2.6 %collective-permute-start.15 = (bf16[64,384]{1,0:T(8,128)(2,1)S(1)}, bf16[64,384]{1,0:T(8,128)(2,1)S(1)}, u32[]{:S(2)}, u32[]{:S(2)}) collective-permute-start(bf16[64,384]{1,0:T(8,128)(2,1)S(1)} %get-tuple-element.46), channel_id=1, source_target_pairs={{4,134},{20,150},{5,135},{21,151},{36,166},{52,182},{37,167},{53,1... | collective-permute-start | bytes 147464 | tf_op jit(solution)/shard_map/ppermute | solution.py:294
  117.9 1.3 collective-permute-start.16
  118.6 2.6 %collective-permute-start.17 = (bf16[64,384]{1,0:T(8,128)(2,1)S(1)}, bf16[64,384]{1,0:T(8,128)(2,1)S(1)}, u32[]{:S(2)}, u32[]{:S(2)}) collective-permute-start(bf16[64,384]{1,0:T(8,128)(2,1)S(1)} %get-tuple-element.48), channel_id=1, source_target_pairs={{6,136},{22,152},{7,137},{23,153},{38,168},{54,184},{39,169},{55,1... | collective-permute-start | bytes 147464 | tf_op jit(solution)/shard_map/ppermute | solution.py:294
  123.6 1.3 collective-permute-start.18
  124.2 2.6 %collective-permute-start.19 = (bf16[64,384]{1,0:T(8,128)(2,1)S(1)}, bf16[64,384]{1,0:T(8,128)(2,1)S(1)}, u32[]{:S(2)}, u32[]{:S(2)}) collective-permute-start(bf16[64,384]{1,0:T(8,128)(2,1)S(1)} %get-tuple-element.50), channel_id=1, source_target_pairs={{8,138},{24,154},{9,139},{25,155},{40,170},{56,186},{41,171},{57,1... | collective-permute-start | bytes 147464 | tf_op jit(solution)/shard_map/ppermute | solution.py:294
  129.4 1.3 collective-permute-start.20
  130.1 2.6 %collective-permute-start.21 = (bf16[64,384]{1,0:T(8,128)(2,1)S(1)}, bf16[64,384]{1,0:T(8,128)(2,1)S(1)}, u32[]{:S(2)}, u32[]{:S(2)}) collective-permute-start(bf16[64,384]{1,0:T(8,128)(2,1)S(1)} %get-tuple-element.52), channel_id=1, source_target_pairs={{10,140},{26,156},{11,141},{27,157},{42,172},{58,188},{43,173},{59... | collective-permute-start | bytes 147464 | tf_op jit(solution)/shard_map/ppermute | solution.py:294
  135.1 1.3 collective-permute-start.22
  135.8 2.6 %collective-permute-start.23 = (bf16[64,384]{1,0:T(8,128)(2,1)S(1)}, bf16[64,384]{1,0:T(8,128)(2,1)S(1)}, u32[]{:S(2)}, u32[]{:S(2)}) collective-permute-start(bf16[64,384]{1,0:T(8,128)(2,1)S(1)} %get-tuple-element.54), channel_id=1, source_target_pairs={{12,142},{28,158},{13,143},{29,159},{44,174},{60,190},{45,175},{61... | collective-permute-start | bytes 147464 | tf_op jit(solution)/shard_map/ppermute | solution.py:294
  140.2 2.0 %copy-start.2 = (bf16[1536,1152]{1,0:T(8,128)(2,1)S(1)}, bf16[1536,1152]{1,0:T(8,128)(2,1)}, u32[]{:S(2)}) copy-start(bf16[1536,1152]{1,0:T(8,128)(2,1)} %copy-done.1) | copy-start | bytes 10616836
  149.1 44.0 %all-to-all-start.1 = ((bf16[16,2,768]{2,1,0:T(2,128)(2,1)}), bf16[16,2,768]{2,1,0:T(2,128)(2,1)S(1)}, u32[]{:S(2)}, u32[]{:S(2)}) async-start(bf16[16,2,768]{2,1,0:T(2,128)(2,1)} %bitcast.32), calls=%async_computation.1 | async-start | bytes 98304 | tf_op jit(solution)/shard_map/all_to_all | solution.py:302
  (3 other events, 2.7 us)

commit v6 on v5

--- a/solution.py
+++ b/solution.py
@@ -45,18 +45,41 @@
     ]
 
 
-SWAP = route(lambda x, y, core: (x, y, 1 - core))
+def member_at(x, y, core, row):
+    return (((y // 2 * 2 + core) * COLUMNS + row) // PART - x) % 4
+
+
+def spread(copy, row):
+    def step(x, y, core):
+        member = member_at(x, y, core, row(y, core))
+        return (copy(core) * 2 + member // 2, y, member % 2)
+
+    return route(step)
+
+
+def cut(y, core):
+    if (y // 2, core) == (1, 0):
+        return 1, 2 * UNIT, 0
+    if (y // 2, core) == (2, 1):
+        return 1, 0, UNIT
+    return 0, 0, 0
+
+
+MAIN = [spread(lambda core, k=k: core ^ k, lambda y, core: cut(y, core)[2]) for k in range(2)]
+TURN = [spread(lambda core, k=k: k, lambda y, core: cut(y, core)[1]) for k in range(2)]
+_CUTS = {n for n in range(512) if cut(n // 16 // 2 % 4 * 2 + n % 2, n // 16 % 2)[0]}
+TURN = [[edge for edge in edges if edge[0] in _CUTS] for edges in TURN]
 UP = route(lambda x, y, core: (x, (y + 1 - 2 * core) % 8, core))
 DOWN = route(lambda x, y, core: (x, (y - 1 + 2 * core) % 8, core))
 ACROSS = [(i, (i + 256) % 512) for i in range(512)]
 
 
-def onward(section, flip):
+def onward(section, flip, turn):
     def number(x, y, core, s):
         return (((x * 4 + y // 2) * 2 + core) * 8 + s) * 2 + y % 2
 
     return [
-        (number(x, y, core, section), number(x ^ flip, y, core, section + 1))
+        (number(x, y, core, section), number(x ^ flip, y, core ^ turn, section + 1))
         for x in range(4)
         for y in range(8)
         for core in range(2)
@@ -67,7 +90,7 @@
     return lax.dot_general(a, b, (((1,), (1,)), ((), ())), preferred_element_type=jnp.float32)
 
 
-def block_kernel(tick, who, near_ref, far_ref, w_ref, kv_ref, other_ref, mod_ref, gate_ref, cos_ref, sin_ref, block_ref, old_ref, state_ref, fresh_ref):
+def block_kernel(tick, who, near_ref, cross_ref, far_ref, w_ref, kv_ref, other_ref, mod_ref, gate_ref, cos_ref, sin_ref, block_ref, old_ref, state_ref, fresh_ref):
     active = who[1] == tick
 
     @pl.when(jnp.logical_not(active))
@@ -76,11 +99,13 @@
 
     @pl.when(active)
     def _():
-        active_block(who[0], near_ref, far_ref, w_ref, kv_ref, other_ref, mod_ref, gate_ref, cos_ref, sin_ref, block_ref, state_ref, fresh_ref)
-
-
-def active_block(member, near_ref, far_ref, w_ref, kv_ref, other_ref, mod_ref, gate_ref, cos_ref, sin_ref, block_ref, state_ref, fresh_ref):
-    near = [near_ref[core].astype(jnp.float32) for core in range(2)]
+        active_block(who[0], near_ref, cross_ref, far_ref, w_ref, kv_ref, other_ref, mod_ref, gate_ref, cos_ref, sin_ref, block_ref, state_ref, fresh_ref)
+
+
+def active_block(member, near_ref, cross_ref, far_ref, w_ref, kv_ref, other_ref, mod_ref, gate_ref, cos_ref, sin_ref, block_ref, state_ref, fresh_ref):
+    near, cross = near_ref[...].astype(jnp.float32), cross_ref[...].astype(jnp.float32)
+    first = member % 2 == 0
+    near = [jnp.where(first, near, cross), jnp.where(first, cross, near)]
     far = [far_ref[core].astype(jnp.float32) for core in range(2)]
     low = member < 2
     xs = [jnp.where(low, near[core], far[core]) for core in range(2)]
@@ -137,13 +162,13 @@
         for h in heads
     ]
     for h in heads:
-        state = near_ref[member % 2, :, cols[h]].astype(jnp.float32) + gate_ref[0:1, cols[h]] * (attended[h] / total[h])
+        state = near_ref[:, cols[h]].astype(jnp.float32) + gate_ref[0:1, cols[h]] * (attended[h] / total[h])
         state_ref[:, cols[h]] = state.astype(jnp.bfloat16)
         fresh_ref[:, cols[h]] = key[h]
         fresh_ref[:, vcols[h]] = value[h]
 
 
-def run_block(tick, who, near, far, weight, kv, other, mod, gate, cosine, sine, blocks, old):
+def run_block(tick, who, near, cross, far, weight, kv, other, mod, gate, cosine, sine, blocks, old):
     vmem = pl.BlockSpec(memory_space=pltpu.VMEM)
     weight = pltpu.with_memory_space_constraint(weight, pltpu.VMEM)
     return pl.pallas_call(
@@ -152,31 +177,64 @@
             jax.ShapeDtypeStruct((GROUP, PART), jnp.bfloat16),
             jax.ShapeDtypeStruct((GROUP, 2 * PART), jnp.bfloat16),
         ),
-        in_specs=[pl.BlockSpec(memory_space=pltpu.SMEM)] + [vmem] * 11,
+        in_specs=[pl.BlockSpec(memory_space=pltpu.SMEM)] + [vmem] * 12,
         out_specs=(vmem, vmem),
         compiler_params=pltpu.CompilerParams(vmem_limit_bytes=8 * 1024 * 1024),
         name="block_step",
-    )(who, near, far, weight, kv, other, mod, gate, cosine, sine, blocks, old)
-
-
-def prepare_kernel(where, stale_ref, columns_ref, out_ref, half_ref):
+    )(who, near, cross, far, weight, kv, other, mod, gate, cosine, sine, blocks, old)
+
+
+def half_kernel(where, columns_ref, half_ref, turn_ref, sems):
+    first = jnp.where(where[2] == 0, 2 * UNIT, 0)
+    col = pl.ds(pl.multiple_of(where[3] % 2 * HALF, 128), HALF)
+    whole = pltpu.make_async_copy(columns_ref.at[:, col], half_ref, sems.at[0])
+    turn = pltpu.make_async_copy(
+        columns_ref.at[pl.ds(pl.multiple_of(first, 16), UNIT), col], turn_ref, sems.at[1]
+    )
+    whole.start()
+    turn.start()
+    whole.wait()
+    turn.wait()
+
+
+def stale_kernel(where, stale_ref, out_ref, sem):
+    copies = []
     for slot in range(2 * 4 * 2):
         m = slot // 8 * 2 + slot % 2
-        out_ref[slot, :, :PART] = stale_ref[:, m * PART : (m + 1) * PART]
-        out_ref[slot, :, PART:] = stale_ref[:, D + m * PART : D + (m + 1) * PART]
-    half_ref[...] = columns_ref[:, pl.ds(pl.multiple_of(where[3] % 2 * HALF, 128), HALF)]
-
-
-def pick_kernel(where, x_ref, keep_ref, send_ref):
-    member, first, core = where[0], where[1], where[2]
-    peer = member + 1 - 2 * core
-    for j in range(UNITS):
-        third = (first + j * UNIT) // PART
-        keep_ref[j * UNIT : (j + 1) * UNIT, :] = x_ref[(third - member + 4) % 4, j * UNIT : (j + 1) * UNIT, :]
-        send_ref[j * UNIT : (j + 1) * UNIT, :] = x_ref[(third - peer + 4) % 4, j * UNIT : (j + 1) * UNIT, :]
-
-
-def place_kernel(where, own, up1, up2, up3, down1, down2, down3, up4, down4, out_ref, rows, sem):
+        for part in range(2):
+            copies.append(
+                pltpu.make_async_copy(
+                    stale_ref.at[:, part * D + m * PART : part * D + (m + 1) * PART],
+                    out_ref.at[slot, :, part * PART : (part + 1) * PART],
+                    sem,
+                )
+            )
+            copies[-1].start()
+    for copy in copies:
+        copy.wait()
+
+
+def join_kernel(where, first_ref, second_ref, turn0_ref, turn1_ref, own_ref):
+    half, y = where[1], where[3]
+
+    def pick(one, two):
+        return jnp.where(half == 0, one[...], two[...])
+
+    own_ref[:COLUMNS, :] = pick(first_ref, second_ref)
+    own_ref[COLUMNS:, :] = pick(second_ref, first_ref)
+
+    @pl.when(y // 2 == 1)
+    def _():
+        own_ref[2 * UNIT : COLUMNS, :] = pick(turn0_ref, turn1_ref)
+
+    @pl.when(y // 2 == 2)
+    def _():
+        own_ref[COLUMNS : COLUMNS + UNIT, :] = pick(turn0_ref, turn1_ref)
+
+
+def place_kernel(sources, last, where, *refs):
+    blocks, refs = refs[: len(sources)], refs[len(sources) :]
+    rows, sem = (refs[1], refs[3]) if last else (refs[0], refs[1])
     member, core, y = where[0], where[2], where[3]
     sign = 1 - 2 * core
     copies = []
@@ -186,49 +244,51 @@
         part = (COLUMNS * 8 * ((third - member + 4) % 4) + PART * third) // D
         return part * PART + unit % 8 * UNIT
 
-    def put(source, part, ref, begin):
+    for (source, parts), ref in zip(sources, blocks):
         at = (y + sign * source + 8) % 8
-        first = (at // 2 * 2 + (core + part) % 2) * UNITS
-        for j in range(UNITS):
-            unit = first + j
-            row = pl.multiple_of(home(unit), 16)
-            col = pl.multiple_of(at % 2 * HALF, 128)
-            copy = pltpu.make_async_copy(
-                ref.at[pl.ds(begin + j * UNIT, UNIT)], rows.at[pl.ds(row, UNIT), pl.ds(col, HALF)], sem
-            )
-            copy.start()
-            copies.append(copy)
-
-    for source, ref in ((0, own), (-1, up1), (-2, up2), (-3, up3), (1, down1), (2, down2), (3, down3)):
-        put(source, 0, ref, 0)
-        put(source, 1, ref, COLUMNS)
-    put(4, 0, up4, 0)
-    put(4, 1, down4, 0)
+        col = pl.ds(pl.multiple_of(at % 2 * HALF, 128), HALF)
+        for n, part in enumerate(parts):
+            for j in range(UNITS):
+                row = pl.multiple_of(home((at // 2 * 2 + part) * UNITS + j), 16)
+                copy = pltpu.make_async_copy(
+                    ref.at[pl.ds(n * COLUMNS + j * UNIT, UNIT)], rows.at[pl.ds(row, UNIT), col], sem
+                )
+                copy.start()
+                copies.append(copy)
     for copy in copies:
         copy.wait()
-    for c in range(0, D, HDIM):
-        out_ref[c : c + HDIM, :] = jnp.transpose(rows[:, c : c + HDIM])
-
-
-def place(where, blocks):
+    if last:
+        for c in range(0, D, HDIM):
+            refs[2][c : c + HDIM, :] = jnp.transpose(rows[:, c : c + HDIM])
+
+
+def place(sources, where, blocks, rows=None):
+    last = rows is not None
+    held = pl.BlockSpec(memory_space=pl.ANY)
+    vmem = pl.BlockSpec(memory_space=pltpu.VMEM)
+    whole = jax.ShapeDtypeStruct((3 * PART, D), jnp.bfloat16)
+    turned = jax.ShapeDtypeStruct((D, 3 * PART), jnp.bfloat16)
     return pl.pallas_call(
-        place_kernel,
-        out_shape=jax.ShapeDtypeStruct((D, 3 * PART), jnp.bfloat16),
-        in_specs=[pl.BlockSpec(memory_space=pltpu.SMEM)] + [pl.BlockSpec(memory_space=pl.ANY)] * len(blocks),
-        out_specs=pl.BlockSpec(memory_space=pltpu.VMEM),
-        scratch_shapes=[pltpu.VMEM((3 * PART, D), jnp.bfloat16), pltpu.SemaphoreType.DMA],
-        compiler_params=pltpu.CompilerParams(vmem_limit_bytes=8 * 1024 * 1024),
-        name="place_weight",
-    )(where, *blocks)
-
-
-def whole_call(kernel, where, arrays, outs):
+        functools.partial(place_kernel, sources, last),
+        out_shape=(whole, turned) if last else whole,
+        in_specs=[pl.BlockSpec(memory_space=pltpu.SMEM)] + [held] * len(blocks) + [vmem] * last,
+        out_specs=(vmem, vmem) if last else vmem,
+        input_output_aliases={len(blocks) + 1: 0} if last else {},
+        scratch_shapes=[pltpu.SemaphoreType.DMA],
+        compiler_params=pltpu.CompilerParams(vmem_limit_bytes=12 * 1024 * 1024),
+        name="place_last" if last else "place_first",
+    )(where, *blocks, *([rows] if last else []))
+
+
+def whole_call(kernel, where, arrays, outs, sems=()):
     vmem = pl.BlockSpec(memory_space=pltpu.VMEM)
+    held = pl.BlockSpec(memory_space=pl.ANY) if sems else vmem
     return pl.pallas_call(
         kernel,
         out_shape=[jax.ShapeDtypeStruct(shape, jnp.bfloat16) for shape in outs],
-        in_specs=[pl.BlockSpec(memory_space=pltpu.SMEM)] + [vmem] * len(arrays),
+        in_specs=[pl.BlockSpec(memory_space=pltpu.SMEM)] + [held] * len(arrays),
         out_specs=[vmem] * len(outs),
+        scratch_shapes=list(sems),
         compiler_params=pltpu.CompilerParams(vmem_limit_bytes=8 * 1024 * 1024),
         name=kernel.__name__,
     )(where, *arrays)
@@ -239,23 +299,24 @@
     section = index["section"]
     member = index["xl"] * 2 + index["core"]
     y = index["yh"] * 2 + index["cfg"]
-    first = (index["yh"] * 2 + index["core"]) * COLUMNS
-    where = jnp.stack([member, first, index["core"], y]).astype(jnp.int32)
+    where = jnp.stack([member, index["xh"], index["core"], y]).astype(jnp.int32)
     who = jnp.stack([member, section]).astype(jnp.int32)
 
-    outgoing, columns = whole_call(
-        prepare_kernel,
+    half, turn = whole_call(
+        half_kernel,
         where,
-        [stale_kv[0, 0], jnp.transpose(qkv_weight[0])],
-        [(2 * 4 * 2, LOCAL, 2 * PART), (COLUMNS, HALF)],
+        [jnp.transpose(qkv_weight[0])],
+        [(COLUMNS, HALF), (UNIT, HALF)],
+        [pltpu.SemaphoreType.DMA((2,))],
+    )
+    moved = [lax.ppermute(half, AXES, edges) for edges in MAIN]
+    turned = [lax.ppermute(turn, AXES, edges) for edges in TURN]
+    (outgoing,) = whole_call(
+        stale_kernel, where, [stale_kv[0, 0]], [(2 * 4 * 2, LOCAL, 2 * PART)], [pltpu.SemaphoreType.DMA]
     )
     kv = lax.all_to_all(outgoing, ("xl", "yh", "core"), split_axis=0, concat_axis=0, tiled=True)
     kv = kv.reshape(TOKENS // 2, 2 * PART)
-
-    columns = lax.all_gather(columns, ("xh", "xl"), axis=0, tiled=False)
-    keep, send = whole_call(pick_kernel, where, [columns], [(COLUMNS, HALF)] * 2)
-    own = jnp.concatenate([keep, lax.ppermute(send, AXES, SWAP)])
-    own, kv = lax.optimization_barrier((own, kv))
+    (own,) = whole_call(join_kernel, where, [*moved, *turned], [(BLOCK, HALF)])
     up1, down1 = lax.ppermute(own, AXES, UP), lax.ppermute(own, AXES, DOWN)
     up1, entering, kv = lax.optimization_barrier((up1, hidden[0], kv))
     kv_other = lax.ppermute(kv, AXES, ACROSS)
@@ -265,9 +326,14 @@
     up3, down3 = lax.ppermute(up2, AXES, UP), lax.ppermute(down2, AXES, DOWN)
     up4 = lax.ppermute(up3[:COLUMNS], AXES, UP)
     down4 = lax.ppermute(down3[COLUMNS:], AXES, DOWN)
-    weight = place(where, [own, up1, up2, up3, down1, down2, down3, up4, down4])
+    both = (0, 1)
+    rows = place(
+        ((0, both), (-1, both), (1, both), (-2, both), (2, both)), where, [own, up1, down1, up2, down2]
+    )
+    _, weight = place(((-3, both), (3, both), (4, (0,)), (4, (1,))), where, [up3, down3, up4, down4], rows)
     x = jnp.transpose(x.reshape(GROUP, MEMBERS, PART), (1, 0, 2))
-    near = lax.dynamic_slice_in_dim(x, index["xl"] * 2, 2, 0)
+    near = lax.dynamic_index_in_dim(x, member, 0, keepdims=False)
+    cross = lax.dynamic_index_in_dim(x, member + 1 - 2 * index["core"], 0, keepdims=False)
     far = lax.dynamic_slice_in_dim(x, 2 - index["xl"] * 2, 2, 0)
 
     row = lax.dynamic_index_in_dim(modulation[0, 0], timestep[0], 0, keepdims=False)
@@ -288,11 +354,11 @@
 
     fresh = jnp.zeros((GROUP, 2 * PART), jnp.bfloat16)
     for tick in range(SECTIONS):
-        state, fresh = run_block(tick, who, near, far, weight, kv, kv_other, mod, gate, cosine, sine, blocks[:, None], fresh)
+        state, fresh = run_block(tick, who, near, cross, far, weight, kv, kv_other, mod, gate, cosine, sine, blocks[:, None], fresh)
         if tick + 1 < SECTIONS:
-            near = lax.ppermute(state, AXES, onward(tick, 0))
-            far = lax.ppermute(state, AXES, onward(tick, 1))
-            near = lax.all_gather(near, "core", axis=0, tiled=False)
+            far = lax.ppermute(state, AXES, onward(tick, 1, 0))
+            near = lax.ppermute(state, AXES, onward(tick, 0, 0))
+            cross = lax.ppermute(state, AXES, onward(tick, 0, 1))
             far = lax.all_gather(far, "core", axis=0, tiled=False)
 
     ends = lax.all_gather(state, ("xl", "core"), axis=0, tiled=False)

time: 196 us -> 178 us (0.908)
  the two profiles are of different devices: /device:TPU:16 before, /device:TPU:1 now
where the time goes in v6:
time: 178 us; the launch traced here: 177 us
  starting transfers between devices  101 us (57%)
  blocking collectives  34 us (19%)
  waiting for transfers between devices  15.6 us (9%)
  Pallas kernels  13.7 us (8%)
  local copies, waits for them, and re-layouts  9.41 us (5%)
  between operations  2.01 us (1%)
    all_to_all x1, starting transfers between devices, body(): lax.all_to_all(finals, ('section', 'cfg'), split_axis=0, concat_axis=0, t...  30.8 us
    all_gather x7, blocking collectives, body(): far = lax.all_gather(far, 'core', axis=0, tiled=False)  13.2 us
    ppermute x7, starting transfers between devices, body(): cross = lax.ppermute(state, AXES, onward(tick, 0, 1))  11.5 us
    all_to_all x1, starting transfers between devices, body(): lax.all_to_all(outgoing, ('xl', 'yh', 'core'), split_axis=0, concat_axis=...  10.2 us
    all_gather x1, blocking collectives, body(): x = lax.all_gather(entering, ('xl', 'core'), axis=0, tiled=True)  8.45 us
    ppermute x7, starting transfers between devices, body(): far = lax.ppermute(state, AXES, onward(tick, 1, 0))  7.02 us
    ppermute x2, starting transfers between devices, body(): up2, down2 = (lax.ppermute(up1, AXES, UP), lax.ppermute(down1, AXES, DOWN))  6.92 us
    ppermute x2, starting transfers between devices, body(): up3, down3 = (lax.ppermute(up2, AXES, UP), lax.ppermute(down2, AXES, DOWN))  6.76 us
  transfers between devices with their start and end apart: 36, of which 7 were waited for; matrix products, arithmetic and copies ran while one was open for 2% of the time, Pallas kernels for 4%

profile of v6, /device:TPU:1, one launch (start us, length us, event | category | flops | bytes accessed | tf_op | source)
XLA Modules:
  0.0 176.8 jit_solution(3435958664896216493)
XLA Ops:
  3.2 10.2 %all-to-all-start = ((bf16[16,16,768]{2,1,0:T(8,128)(2,1)}), bf16[16,16,768]{2,1,0:T(8,128)(2,1)S(1)}, u32[]{:S(2)}, u32[]{:S(2)}) async-start(bf16[16,16,768]{2,1,0:T(8,128)(2,1)} %stale_kernel.1), calls=%async_computation | async-start | bytes 786432 | tf_op jit(solution)/shard_map/all_to_all | solution.py:317
  15.0 3.7 %collective-permute-start = (bf16[144,768]{1,0:T(8,128)(2,1)S(1)}, bf16[144,768]{1,0:T(8,128)(2,1)S(1)}, u32[]{:S(2)}, u32[]{:S(2)}) collective-permute-start(bf16[144,768]{1,0:T(8,128)(2,1)S(1)} %get-tuple-element.28), channel_id=1, source_target_pairs={{0,0},{2,2},{4,4},{6,6},{8,8},{10,10},{12,12},{14,14},{16,256},{18... | collective-permute-start | bytes 663560 | tf_op jit(solution)/shard_map/ppermute | solution.py:312
  18.7 1.9 %collective-permute-start.1 = (bf16[144,768]{1,0:T(8,128)(2,1)S(1)}, bf16[144,768]{1,0:T(8,128)(2,1)S(1)}, u32[]{:S(2)}, u32[]{:S(2)}) collective-permute-start(bf16[144,768]{1,0:T(8,128)(2,1)S(1)} %get-tuple-element.28), channel_id=1, source_target_pairs={{0,256},{2,258},{4,260},{6,262},{8,264},{10,266},{12,268},{14,270}... | collective-permute-start | bytes 663560 | tf_op jit(solution)/shard_map/ppermute | solution.py:312
  23.8 3.1 %collective-permute-done.1.second_ref = bf16[144,768]{1,0:T(8,128)(2,1)S(1)} collective-permute-done((bf16[144,768]{1,0:T(8,128)(2,1)S(1)}, bf16[144,768]{1,0:T(8,128)(2,1)S(1)}, u32[]{:S(2)}, u32[]{:S(2)}) %collective-permute-start.1) | collective-permute-done | bytes 221216 | tf_op jit(solution)/shard_map/ppermute | solution.py:312
  27.5 2.0 %collective-permute-start.4 = (bf16[288,768]{1,0:T(8,128)(2,1)S(1)}, bf16[288,768]{1,0:T(8,128)(2,1)S(1)}, u32[]{:S(2)}, u32[]{:S(2)}) collective-permute-start(bf16[288,768]{1,0:T(8,128)(2,1)S(1)} %join_kernel.1.refs_0_), channel_id=1, source_target_pairs={{0,97},{2,99},{4,101},{6,103},{8,105},{10,107},{12,109},{14,111},{... | collective-permute-start | bytes 1327112 | tf_op jit(solution)/shard_map/ppermute | solution.py:320
  29.5 4.5 %collective-permute-start.6 = (bf16[288,768]{1,0:T(8,128)(2,1)S(1)}, bf16[288,768]{1,0:T(8,128)(2,1)S(1)}, u32[]{:S(2)}, u32[]{:S(2)}) collective-permute-start(bf16[288,768]{1,0:T(8,128)(2,1)S(1)} %join_kernel.1.refs_0_), channel_id=1, source_target_pairs={{0,1},{2,3},{4,5},{6,7},{8,9},{10,11},{12,13},{14,15},{16,113},{18... | collective-permute-start | bytes 1327112 | tf_op jit(solution)/shard_map/ppermute | solution.py:320
  35.5 2.2 %collective-permute-done.4.refs_2_ = bf16[288,768]{1,0:T(8,128)(2,1)S(1)} collective-permute-done((bf16[288,768]{1,0:T(8,128)(2,1)S(1)}, bf16[288,768]{1,0:T(8,128)(2,1)S(1)}, u32[]{:S(2)}, u32[]{:S(2)}) %collective-permute-start.4) | collective-permute-done | bytes 442400 | tf_op jit(solution)/shard_map/ppermute | solution.py:320
  37.7 1.9 %collective-permute-start.5 = (bf16[288,768]{1,0:T(8,128)(2,1)S(1)}, bf16[288,768]{1,0:T(8,128)(2,1)}, u32[]{:S(2)}, u32[]{:S(2)}) collective-permute-start(bf16[288,768]{1,0:T(8,128)(2,1)S(1)} %collective-permute-done.4.refs_2_), channel_id=1, source_target_pairs={{0,97},{2,99},{4,101},{6,103},{8,105},{10,107},{12,109},{14,111},{... | collective-permute-start | bytes 1327112 | tf_op jit(solution)/shard_map/ppermute | solution.py:324
  39.7 3.9 %collective-permute-done.6.refs_1_ = bf16[288,768]{1,0:T(8,128)(2,1)S(1)} collective-permute-done((bf16[288,768]{1,0:T(8,128)(2,1)S(1)}, bf16[288,768]{1,0:T(8,128)(2,1)S(1)}, u32[]{:S(2)}, u32[]{:S(2)}) %collective-permute-start.6) | collective-permute-done | bytes 442400 | tf_op jit(solution)/shard_map/ppermute | solution.py:320
  43.5 5.0 %collective-permute-start.7 = (bf16[288,768]{1,0:T(8,128)(2,1)S(1)}, bf16[288,768]{1,0:T(8,128)(2,1)}, u32[]{:S(2)}, u32[]{:S(2)}) collective-permute-start(bf16[288,768]{1,0:T(8,128)(2,1)S(1)} %collective-permute-done.6.refs_1_), channel_id=1, source_target_pairs={{0,1},{2,3},{4,5},{6,7},{8,9},{10,11},{12,13},{14,15},{16,113},{18... | collective-permute-start | bytes 1327112 | tf_op jit(solution)/shard_map/ppermute | solution.py:324
  48.9 8.4 %all_gather.57 = bf16[64,1536]{1,0:T(8,128)(2,1)} all-gather(bf16[16,1536]{1,0:T(8,128)(2,1)S(1)} %bitcast.69), channel_id=1, replica_groups=mesh['xh'=2,'xl'=2,'yh'=4,'core'=2,'section'=8,'cfg'=2] {'xl','core'}, dimensions={0}, use_global_device_ids=true | all-gather | bytes 245760 | tf_op jit(solution)/shard_map/all_gather | solution.py:323
  57.3 2.5 %collective-permute-start.9 = (bf16[288,768]{1,0:T(8,128)(2,1)}, bf16[288,768]{1,0:T(8,128)(2,1)S(1)}, u32[]{:S(2)}, u32[]{:S(2)}) collective-permute-start(bf16[288,768]{1,0:T(8,128)(2,1)} %collective-permute-done.5.refs_4_), channel_id=1, source_target_pairs={{0,97},{2,99},{4,101},{6,103},{8,105},{10,107},{12,109},{14,111},{... | collective-permute-start | bytes 1327112 | tf_op jit(solution)/shard_map/ppermute | solution.py:326
  59.9 4.3 %collective-permute-start.8 = (bf16[288,768]{1,0:T(8,128)(2,1)}, bf16[288,768]{1,0:T(8,128)(2,1)S(1)}, u32[]{:S(2)}, u32[]{:S(2)}) collective-permute-start(bf16[288,768]{1,0:T(8,128)(2,1)} %collective-permute-done.7.refs_3_), channel_id=1, source_target_pairs={{0,1},{2,3},{4,5},{6,7},{8,9},{10,11},{12,13},{14,15},{16,113},{18... | collective-permute-start | bytes 1327112 | tf_op jit(solution)/shard_map/ppermute | solution.py:326
  64.3 1.9 %collective-permute-start.12 = (bf16[256,768]{1,0:T(8,128)(2,1)S(1)}, bf16[256,768]{1,0:T(8,128)(2,1)S(1)}, u32[]{:S(2)}, u32[]{:S(2)}) collective-permute-start(bf16[256,768]{1,0:T(8,128)(2,1)S(1)} %bitcast.45), channel_id=1, source_target_pairs={{0,256},{1,257},{2,258},{3,259},{4,260},{5,261},{6,262},{7,263},{8... | collective-permute-start | bytes 1179656 | tf_op jit(solution)/shard_map/ppermute | solution.py:322
  68.1 1.9 %collective-permute-start.11 = (bf16[144,768]{1,0:T(8,128)(2,1)S(1)}, bf16[144,768]{1,0:T(8,128)(2,1)S(1)}, u32[]{:S(2)}, u32[]{:S(2)}) collective-permute-start(bf16[144,768]{1,0:T(8,128)(2,1)S(1)} %slice.24), channel_id=1, source_target_pairs={{0,97},{2,99},{4,101},{6,103},{8,105},{10,107},{12,109},{14,111},{... | collective-permute-start | bytes 663560 | tf_op jit(solution)/shard_map/ppermute | solution.py:328
  70.0 3.8 %collective-permute-done.8.refs_0_ = bf16[288,768]{1,0:T(8,128)(2,1)S(1)} collective-permute-done((bf16[288,768]{1,0:T(8,128)(2,1)}, bf16[288,768]{1,0:T(8,128)(2,1)S(1)}, u32[]{:S(2)}, u32[]{:S(2)}) %collective-permute-start.8) | collective-permute-done | bytes 442400 | tf_op jit(solution)/shard_map/ppermute | solution.py:326
  73.9 5.2 %collective-permute-start.10 = (bf16[144,768]{1,0:T(8,128)(2,1)S(1)}, bf16[144,768]{1,0:T(8,128)(2,1)S(1)}, u32[]{:S(2)}, u32[]{:S(2)}) collective-permute-start(bf16[144,768]{1,0:T(8,128)(2,1)S(1)} %slice.23), channel_id=1, source_target_pairs={{0,1},{2,3},{4,5},{6,7},{8,9},{10,11},{12,13},{14,15},{16,113},{18... | collective-permute-start | bytes 663560 | tf_op jit(solution)/shard_map/ppermute | solution.py:327
  80.1 2.7 %place_first.1.refs_4_ = bf16[1152,1536]{1,0:T(8,128)(2,1)S(1)} custom-call(s32[4]{0:T(128)S(1)} %pad_add_fusion.1.where, bf16[288,768]{1,0:T(8,128)(2,1)S(1)} %join_kernel.1.refs_0_, bf16[288,768]{1,0:T(8,128)(2,1)S(1)} %copy-done.4, bf16[288,768]{1,0:T(8,128)(2,1)S(1)} %collective-permute-done.4.refs_2_, bf16[288,768]{1,0:T(8,128)(2,1)} %collective-permute-done.7.refs_3_, ...), custom_call_target="tpu_custom_call" | custom-call | tf_op jit(solution)/shard_map/place_first/pallas_call | solution.py:271
  82.8 2.3 %place_last.1 = (bf16[1152,1536]{1,0:T(8,128)(2,1)S(1)}, bf16[1536,1152]{1,0:T(8,128)(2,1)S(1)}) custom-call(s32[4]{0:T(128)S(1)} %pad_add_fusion.1.where, bf16[288,768]{1,0:T(8,128)(2,1)S(1)} %collective-permute-done.8.refs_0_, bf16[288,768]{1,0:T(8,128)(2,1)S(1)} %collective-permute-done.9.refs_1_, ...), custom_call_target="tpu_custom_call", output_to_operand_aliasing={{0}: (5, {})} | custom-call | tf_op jit(solution)/shard_map/place_last/pallas_call | solution.py:271
  85.2 1.9 %block_step.8 = (bf16[64,384]{1,0:T(8,128)(2,1)S(1)}, bf16[64,768]{1,0:T(8,128)(2,1)S(1)}) custom-call(s32[2]{0:T(128)S(1)} %pad_add_fusion.who, bf16[64,384]{1,0:T(8,128)(2,1)S(1)} %get-tuple-element.60.near_ref, bf16[64,384]{1,0:T(8,128)(2,1)S(1)} %get-tuple-element.59.cross_ref, bf16[2,64,384]{2,1,0:T(8,128)(2,1)S(1)} %bitcast.55, ...), custom_call_target="tpu_custom_call" | custom-call | tf_op jit(solution)/shard_map/block_step/pallas_call | solution.py:174
  87.2 3.0 %collective-permute-start.15 = (bf16[64,384]{1,0:T(8,128)(2,1)S(1)}, bf16[64,384]{1,0:T(8,128)(2,1)S(1)}, u32[]{:S(2)}, u32[]{:S(2)}) collective-permute-start(bf16[64,384]{1,0:T(8,128)(2,1)S(1)} %get-tuple-element.36), channel_id=1, source_target_pairs={{0,130},{16,146},{1,131},{17,147},{32,162},{48,178},{33,163},{49,1... | collective-permute-start | bytes 147464 | tf_op jit(solution)/shard_map/ppermute | solution.py:359
  91.5 7.5 %collective-permute-start.14 = (bf16[64,384]{1,0:T(8,128)(2,1)S(1)}, bf16[64,384]{1,0:T(8,128)(2,1)S(1)}, u32[]{:S(2)}, u32[]{:S(2)}) collective-permute-start(bf16[64,384]{1,0:T(8,128)(2,1)S(1)} %get-tuple-element.36), channel_id=1, source_target_pairs={{0,18},{16,2},{1,19},{17,3},{32,50},{48,34},{33,51},{49,35},{64,82... | collective-permute-start | bytes 147464 | tf_op jit(solution)/shard_map/ppermute | solution.py:361
  99.0 1.9 %all-gather = bf16[128,384]{1,0:T(8,128)(2,1)S(1)} all-gather(bf16[64,384]{1,0:T(8,128)(2,1)S(1)} %collective-permute-done.15), channel_id=2, replica_groups=mesh['xh'=2,'xl'=2,'yh'=4,'core'=2,'section'=8,'cfg'=2] {'core'}, dimensions={0}, use_global_device_ids=true | all-gather | bytes 147456 | tf_op jit(solution)/shard_map/all_gather | solution.py:362
  103.5 1.9 %all-gather.1 = bf16[128,384]{1,0:T(8,128)(2,1)S(1)} all-gather(bf16[64,384]{1,0:T(8,128)(2,1)S(1)} %collective-permute-done.18), channel_id=3, replica_groups=mesh['xh'=2,'xl'=2,'yh'=4,'core'=2,'section'=8,'cfg'=2] {'core'}, dimensions={0}, use_global_device_ids=true | all-gather | bytes 147456 | tf_op jit(solution)/shard_map/all_gather | solution.py:362
  108.0 1.9 %all-gather.2 = bf16[128,384]{1,0:T(8,128)(2,1)S(1)} all-gather(bf16[64,384]{1,0:T(8,128)(2,1)S(1)} %collective-permute-done.21), channel_id=4, replica_groups=mesh['xh'=2,'xl'=2,'yh'=4,'core'=2,'section'=8,'cfg'=2] {'core'}, dimensions={0}, use_global_device_ids=true | all-gather | bytes 147456 | tf_op jit(solution)/shard_map/all_gather | solution.py:362
  112.5 1.9 %all-gather.3 = bf16[128,384]{1,0:T(8,128)(2,1)S(1)} all-gather(bf16[64,384]{1,0:T(8,128)(2,1)S(1)} %collective-permute-done.24), channel_id=5, replica_groups=mesh['xh'=2,'xl'=2,'yh'=4,'core'=2,'section'=8,'cfg'=2] {'core'}, dimensions={0}, use_global_device_ids=true | all-gather | bytes 147456 | tf_op jit(solution)/shard_map/all_gather | solution.py:362
  117.1 1.9 %all-gather.4 = bf16[128,384]{1,0:T(8,128)(2,1)S(1)} all-gather(bf16[64,384]{1,0:T(8,128)(2,1)S(1)} %collective-permute-done.27), channel_id=6, replica_groups=mesh['xh'=2,'xl'=2,'yh'=4,'core'=2,'section'=8,'cfg'=2] {'core'}, dimensions={0}, use_global_device_ids=true | all-gather | bytes 147456 | tf_op jit(solution)/shard_map/all_gather | solution.py:362
  121.6 1.9 %all-gather.5 = bf16[128,384]{1,0:T(8,128)(2,1)S(1)} all-gather(bf16[64,384]{1,0:T(8,128)(2,1)S(1)} %collective-permute-done.30), channel_id=7, replica_groups=mesh['xh'=2,'xl'=2,'yh'=4,'core'=2,'section'=8,'cfg'=2] {'core'}, dimensions={0}, use_global_device_ids=true | all-gather | bytes 147456 | tf_op jit(solution)/shard_map/all_gather | solution.py:362
  128.0 2.0 %copy-done.2 = bf16[1536,1152]{1,0:T(8,128)(2,1)S(1)} copy-done((bf16[1536,1152]{1,0:T(8,128)(2,1)S(1)}, bf16[1536,1152]{1,0:T(8,128)(2,1)}, u32[]{:S(2)}) %copy-start.2) | copy-done | bytes 3538968
  130.5 5.8 %all-gather.7 = bf16[256,384]{1,0:T(8,128)(2,1)S(1)} all-gather(bf16[64,384]{1,0:T(8,128)(2,1)S(1)} %get-tuple-element.50), channel_id=9, replica_groups=mesh['xh'=2,'xl'=2,'yh'=4,'core'=2,'section'=8,'cfg'=2] {'xl','core'}, dimensions={0}, use_global_device_ids=true | all-gather | bytes 245760 | tf_op jit(solution)/shard_map/all_gather | solution.py:364
  137.1 30.8 %all-to-all-start.1 = ((bf16[16,2,768]{2,1,0:T(2,128)(2,1)}), bf16[16,2,768]{2,1,0:T(2,128)(2,1)S(1)}, u32[]{:S(2)}, u32[]{:S(2)}) async-start(bf16[16,2,768]{2,1,0:T(2,128)(2,1)} %bitcast.23), calls=%async_computation.1 | async-start | bytes 98304 | tf_op jit(solution)/shard_map/all_to_all | solution.py:368
  167.8 6.6 %all-gather.8 = bf16[256,768]{1,0:T(8,128)(2,1)S(1)} all-gather(bf16[64,768]{1,0:T(8,128)(2,1)S(1)} %get-tuple-element.51), channel_id=10, replica_groups=mesh['xh'=2,'xl'=2,'yh'=4,'core'=2,'section'=8,'cfg'=2] {'xl','core'}, dimensions={0}, use_global_device_ids=true | all-gather | bytes 491520 | tf_op jit(solution)/shard_map/all_gather | solution.py:369
  (109 shorter events, 34.4 us)
Async XLA Ops:
  3.2 40.3 %all-to-all-start = ((bf16[16,16,768]{2,1,0:T(8,128)(2,1)}), bf16[16,16,768]{2,1,0:T(8,128)(2,1)S(1)}, u32[]{:S(2)}, u32[]{:S(2)}) async-start(bf16[16,16,768]{2,1,0:T(8,128)(2,1)} %stale_kernel.1), calls=%async_computation | async-start | bytes 786432 | tf_op jit(solution)/shard_map/all_to_all | solution.py:317
  15.0 8.8 %collective-permute-start = (bf16[144,768]{1,0:T(8,128)(2,1)S(1)}, bf16[144,768]{1,0:T(8,128)(2,1)S(1)}, u32[]{:S(2)}, u32[]{:S(2)}) collective-permute-start(bf16[144,768]{1,0:T(8,128)(2,1)S(1)} %get-tuple-element.28), channel_id=1, source_target_pairs={{0,0},{2,2},{4,4},{6,6},{8,8},{10,10},{12,12},{14,14},{16,256},{18... | collective-permute-start | bytes 663560 | tf_op jit(solution)/shard_map/ppermute | solution.py:312
  18.7 8.2 %collective-permute-start.1 = (bf16[144,768]{1,0:T(8,128)(2,1)S(1)}, bf16[144,768]{1,0:T(8,128)(2,1)S(1)}, u32[]{:S(2)}, u32[]{:S(2)}) collective-permute-start(bf16[144,768]{1,0:T(8,128)(2,1)S(1)} %get-tuple-element.28), channel_id=1, source_target_pairs={{0,256},{2,258},{4,260},{6,262},{8,264},{10,266},{12,268},{14,270}... | collective-permute-start | bytes 663560 | tf_op jit(solution)/shard_map/ppermute | solution.py:312
  20.6 2.1 %collective-permute-start.2 = (bf16[48,768]{1,0:T(8,128)(2,1)S(1)}, bf16[48,768]{1,0:T(8,128)(2,1)S(1)}, u32[]{:S(2)}, u32[]{:S(2)}) collective-permute-start(bf16[48,768]{1,0:T(8,128)(2,1)S(1)} %get-tuple-element.29), channel_id=1, source_target_pairs={{32,48},{34,50},{36,52},{38,54},{40,56},{42,58},{44,60},{46,62},{3... | collective-permute-start | bytes 221192 | tf_op jit(solution)/shard_map/ppermute | solution.py:313
  27.5 10.3 %collective-permute-start.4 = (bf16[288,768]{1,0:T(8,128)(2,1)S(1)}, bf16[288,768]{1,0:T(8,128)(2,1)S(1)}, u32[]{:S(2)}, u32[]{:S(2)}) collective-permute-start(bf16[288,768]{1,0:T(8,128)(2,1)S(1)} %join_kernel.1.refs_0_), channel_id=1, source_target_pairs={{0,97},{2,99},{4,101},{6,103},{8,105},{10,107},{12,109},{14,111},{... | collective-permute-start | bytes 1327112 | tf_op jit(solution)/shard_map/ppermute | solution.py:320
  29.5 14.0 %collective-permute-start.6 = (bf16[288,768]{1,0:T(8,128)(2,1)S(1)}, bf16[288,768]{1,0:T(8,128)(2,1)S(1)}, u32[]{:S(2)}, u32[]{:S(2)}) collective-permute-start(bf16[288,768]{1,0:T(8,128)(2,1)S(1)} %join_kernel.1.refs_0_), channel_id=1, source_target_pairs={{0,1},{2,3},{4,5},{6,7},{8,9},{10,11},{12,13},{14,15},{16,113},{18... | collective-permute-start | bytes 1327112 | tf_op jit(solution)/shard_map/ppermute | solution.py:320
  37.7 19.6 %collective-permute-start.5 = (bf16[288,768]{1,0:T(8,128)(2,1)S(1)}, bf16[288,768]{1,0:T(8,128)(2,1)}, u32[]{:S(2)}, u32[]{:S(2)}) collective-permute-start(bf16[288,768]{1,0:T(8,128)(2,1)S(1)} %collective-permute-done.4.refs_2_), channel_id=1, source_target_pairs={{0,97},{2,99},{4,101},{6,103},{8,105},{10,107},{12,109},{14,111},{... | collective-permute-start | bytes 1327112 | tf_op jit(solution)/shard_map/ppermute | solution.py:324
  43.5 16.3 %collective-permute-start.7 = (bf16[288,768]{1,0:T(8,128)(2,1)S(1)}, bf16[288,768]{1,0:T(8,128)(2,1)}, u32[]{:S(2)}, u32[]{:S(2)}) collective-permute-start(bf16[288,768]{1,0:T(8,128)(2,1)S(1)} %collective-permute-done.6.refs_1_), channel_id=1, source_target_pairs={{0,1},{2,3},{4,5},{6,7},{8,9},{10,11},{12,13},{14,15},{16,113},{18... | collective-permute-start | bytes 1327112 | tf_op jit(solution)/shard_map/ppermute | solution.py:324
  57.3 10.7 %collective-permute-start.9 = (bf16[288,768]{1,0:T(8,128)(2,1)}, bf16[288,768]{1,0:T(8,128)(2,1)S(1)}, u32[]{:S(2)}, u32[]{:S(2)}) collective-permute-start(bf16[288,768]{1,0:T(8,128)(2,1)} %collective-permute-done.5.refs_4_), channel_id=1, source_target_pairs={{0,97},{2,99},{4,101},{6,103},{8,105},{10,107},{12,109},{14,111},{... | collective-permute-start | bytes 1327112 | tf_op jit(solution)/shard_map/ppermute | solution.py:326
  59.9 14.0 %collective-permute-start.8 = (bf16[288,768]{1,0:T(8,128)(2,1)}, bf16[288,768]{1,0:T(8,128)(2,1)S(1)}, u32[]{:S(2)}, u32[]{:S(2)}) collective-permute-start(bf16[288,768]{1,0:T(8,128)(2,1)} %collective-permute-done.7.refs_3_), channel_id=1, source_target_pairs={{0,1},{2,3},{4,5},{6,7},{8,9},{10,11},{12,13},{14,15},{16,113},{18... | collective-permute-start | bytes 1327112 | tf_op jit(solution)/shard_map/ppermute | solution.py:326
  64.3 20.9 %collective-permute-start.12 = (bf16[256,768]{1,0:T(8,128)(2,1)S(1)}, bf16[256,768]{1,0:T(8,128)(2,1)S(1)}, u32[]{:S(2)}, u32[]{:S(2)}) collective-permute-start(bf16[256,768]{1,0:T(8,128)(2,1)S(1)} %bitcast.45), channel_id=1, source_target_pairs={{0,256},{1,257},{2,258},{3,259},{4,260},{5,261},{6,262},{7,263},{8... | collective-permute-start | bytes 1179656 | tf_op jit(solution)/shard_map/ppermute | solution.py:322
  68.1 14.7 %collective-permute-start.11 = (bf16[144,768]{1,0:T(8,128)(2,1)S(1)}, bf16[144,768]{1,0:T(8,128)(2,1)S(1)}, u32[]{:S(2)}, u32[]{:S(2)}) collective-permute-start(bf16[144,768]{1,0:T(8,128)(2,1)S(1)} %slice.24), channel_id=1, source_target_pairs={{0,97},{2,99},{4,101},{6,103},{8,105},{10,107},{12,109},{14,111},{... | collective-permute-start | bytes 663560 | tf_op jit(solution)/shard_map/ppermute | solution.py:328
  73.9 9.0 %collective-permute-start.10 = (bf16[144,768]{1,0:T(8,128)(2,1)S(1)}, bf16[144,768]{1,0:T(8,128)(2,1)S(1)}, u32[]{:S(2)}, u32[]{:S(2)}) collective-permute-start(bf16[144,768]{1,0:T(8,128)(2,1)S(1)} %slice.23), channel_id=1, source_target_pairs={{0,1},{2,3},{4,5},{6,7},{8,9},{10,11},{12,13},{14,15},{16,113},{18... | collective-permute-start | bytes 663560 | tf_op jit(solution)/shard_map/ppermute | solution.py:327
  87.2 11.8 %collective-permute-start.15 = (bf16[64,384]{1,0:T(8,128)(2,1)S(1)}, bf16[64,384]{1,0:T(8,128)(2,1)S(1)}, u32[]{:S(2)}, u32[]{:S(2)}) collective-permute-start(bf16[64,384]{1,0:T(8,128)(2,1)S(1)} %get-tuple-element.36), channel_id=1, source_target_pairs={{0,130},{16,146},{1,131},{17,147},{32,162},{48,178},{33,163},{49,1... | collective-permute-start | bytes 147464 | tf_op jit(solution)/shard_map/ppermute | solution.py:359
  90.2 10.7 %collective-permute-start.13 = (bf16[64,384]{1,0:T(8,128)(2,1)S(1)}, bf16[64,384]{1,0:T(8,128)(2,1)S(1)}, u32[]{:S(2)}, u32[]{:S(2)}) collective-permute-start(bf16[64,384]{1,0:T(8,128)(2,1)S(1)} %get-tuple-element.36), channel_id=1, source_target_pairs={{0,2},{16,18},{1,3},{17,19},{32,34},{48,50},{33,35},{49,51},{64,66... | collective-permute-start | bytes 147464 | tf_op jit(solution)/shard_map/ppermute | solution.py:360
  91.5 9.4 %collective-permute-start.14 = (bf16[64,384]{1,0:T(8,128)(2,1)S(1)}, bf16[64,384]{1,0:T(8,128)(2,1)S(1)}, u32[]{:S(2)}, u32[]{:S(2)}) collective-permute-start(bf16[64,384]{1,0:T(8,128)(2,1)S(1)} %get-tuple-element.36), channel_id=1, source_target_pairs={{0,18},{16,2},{1,19},{17,3},{32,50},{48,34},{33,51},{49,35},{64,82... | collective-permute-start | bytes 147464 | tf_op jit(solution)/shard_map/ppermute | solution.py:361
  101.5 2.0 %collective-permute-start.18 = (bf16[64,384]{1,0:T(8,128)(2,1)S(1)}, bf16[64,384]{1,0:T(8,128)(2,1)S(1)}, u32[]{:S(2)}, u32[]{:S(2)}) collective-permute-start(bf16[64,384]{1,0:T(8,128)(2,1)S(1)} %get-tuple-element.38), channel_id=1, source_target_pairs={{2,132},{18,148},{3,133},{19,149},{34,164},{50,180},{35,165},{51,1... | collective-permute-start | bytes 147464 | tf_op jit(solution)/shard_map/ppermute | solution.py:359
  102.2 3.2 %collective-permute-start.16 = (bf16[64,384]{1,0:T(8,128)(2,1)S(1)}, bf16[64,384]{1,0:T(8,128)(2,1)S(1)}, u32[]{:S(2)}, u32[]{:S(2)}) collective-permute-start(bf16[64,384]{1,0:T(8,128)(2,1)S(1)} %get-tuple-element.38), channel_id=1, source_target_pairs={{2,4},{18,20},{3,5},{19,21},{34,36},{50,52},{35,37},{51,53},{66,68... | collective-permute-start | bytes 147464 | tf_op jit(solution)/shard_map/ppermute | solution.py:360
  102.8 2.6 %collective-permute-start.17 = (bf16[64,384]{1,0:T(8,128)(2,1)S(1)}, bf16[64,384]{1,0:T(8,128)(2,1)S(1)}, u32[]{:S(2)}, u32[]{:S(2)}) collective-permute-start(bf16[64,384]{1,0:T(8,128)(2,1)S(1)} %get-tuple-element.38), channel_id=1, source_target_pairs={{2,20},{18,4},{3,21},{19,5},{34,52},{50,36},{35,53},{51,37},{66,84... | collective-permute-start | bytes 147464 | tf_op jit(solution)/shard_map/ppermute | solution.py:361
  106.0 2.0 %collective-permute-start.21 = (bf16[64,384]{1,0:T(8,128)(2,1)S(1)}, bf16[64,384]{1,0:T(8,128)(2,1)S(1)}, u32[]{:S(2)}, u32[]{:S(2)}) collective-permute-start(bf16[64,384]{1,0:T(8,128)(2,1)S(1)} %get-tuple-element.40), channel_id=1, source_target_pairs={{4,134},{20,150},{5,135},{21,151},{36,166},{52,182},{37,167},{53,1... | collective-permute-start | bytes 147464 | tf_op jit(solution)/shard_map/ppermute | solution.py:359
  106.6 3.2 %collective-permute-start.19 = (bf16[64,384]{1,0:T(8,128)(2,1)S(1)}, bf16[64,384]{1,0:T(8,128)(2,1)S(1)}, u32[]{:S(2)}, u32[]{:S(2)}) collective-permute-start(bf16[64,384]{1,0:T(8,128)(2,1)S(1)} %get-tuple-element.40), channel_id=1, source_target_pairs={{4,6},{20,22},{5,7},{21,23},{36,38},{52,54},{37,39},{53,55},{68,70... | collective-permute-start | bytes 147464 | tf_op jit(solution)/shard_map/ppermute | solution.py:360
  107.3 2.6 %collective-permute-start.20 = (bf16[64,384]{1,0:T(8,128)(2,1)S(1)}, bf16[64,384]{1,0:T(8,128)(2,1)S(1)}, u32[]{:S(2)}, u32[]{:S(2)}) collective-permute-start(bf16[64,384]{1,0:T(8,128)(2,1)S(1)} %get-tuple-element.40), channel_id=1, source_target_pairs={{4,22},{20,6},{5,23},{21,7},{36,54},{52,38},{37,55},{53,39},{68,86... | collective-permute-start | bytes 147464 | tf_op jit(solution)/shard_map/ppermute | solution.py:361
  110.4 2.0 %collective-permute-start.24 = (bf16[64,384]{1,0:T(8,128)(2,1)S(1)}, bf16[64,384]{1,0:T(8,128)(2,1)S(1)}, u32[]{:S(2)}, u32[]{:S(2)}) collective-permute-start(bf16[64,384]{1,0:T(8,128)(2,1)S(1)} %get-tuple-element.42), channel_id=1, source_target_pairs={{6,136},{22,152},{7,137},{23,153},{38,168},{54,184},{39,169},{55,1... | collective-permute-start | bytes 147464 | tf_op jit(solution)/shard_map/ppermute | solution.py:359
  111.1 3.2 %collective-permute-start.22 = (bf16[64,384]{1,0:T(8,128)(2,1)S(1)}, bf16[64,384]{1,0:T(8,128)(2,1)S(1)}, u32[]{:S(2)}, u32[]{:S(2)}) collective-permute-start(bf16[64,384]{1,0:T(8,128)(2,1)S(1)} %get-tuple-element.42), channel_id=1, source_target_pairs={{6,8},{22,24},{7,9},{23,25},{38,40},{54,56},{39,41},{55,57},{70,72... | collective-permute-start | bytes 147464 | tf_op jit(solution)/shard_map/ppermute | solution.py:360
  111.8 2.6 %collective-permute-start.23 = (bf16[64,384]{1,0:T(8,128)(2,1)S(1)}, bf16[64,384]{1,0:T(8,128)(2,1)S(1)}, u32[]{:S(2)}, u32[]{:S(2)}) collective-permute-start(bf16[64,384]{1,0:T(8,128)(2,1)S(1)} %get-tuple-element.42), channel_id=1, source_target_pairs={{6,24},{22,8},{7,25},{23,9},{38,56},{54,40},{39,57},{55,41},{70,88... | collective-permute-start | bytes 147464 | tf_op jit(solution)/shard_map/ppermute | solution.py:361
  115.8 3.2 %collective-permute-start.25 = (bf16[64,384]{1,0:T(8,128)(2,1)S(1)}, bf16[64,384]{1,0:T(8,128)(2,1)S(1)}, u32[]{:S(2)}, u32[]{:S(2)}) collective-permute-start(bf16[64,384]{1,0:T(8,128)(2,1)S(1)} %get-tuple-element.44), channel_id=1, source_target_pairs={{8,10},{24,26},{9,11},{25,27},{40,42},{56,58},{41,43},{57,59},{72,... | collective-permute-start | bytes 147464 | tf_op jit(solution)/shard_map/ppermute | solution.py:360
  116.4 2.6 %collective-permute-start.26 = (bf16[64,384]{1,0:T(8,128)(2,1)S(1)}, bf16[64,384]{1,0:T(8,128)(2,1)S(1)}, u32[]{:S(2)}, u32[]{:S(2)}) collective-permute-start(bf16[64,384]{1,0:T(8,128)(2,1)S(1)} %get-tuple-element.44), channel_id=1, source_target_pairs={{8,26},{24,10},{9,27},{25,11},{40,58},{56,42},{41,59},{57,43},{72,... | collective-permute-start | bytes 147464 | tf_op jit(solution)/shard_map/ppermute | solution.py:361
  120.2 3.2 %collective-permute-start.28 = (bf16[64,384]{1,0:T(8,128)(2,1)S(1)}, bf16[64,384]{1,0:T(8,128)(2,1)S(1)}, u32[]{:S(2)}, u32[]{:S(2)}) collective-permute-start(bf16[64,384]{1,0:T(8,128)(2,1)S(1)} %get-tuple-element.46), channel_id=1, source_target_pairs={{10,12},{26,28},{11,13},{27,29},{42,44},{58,60},{43,45},{59,61},{7... | collective-permute-start | bytes 147464 | tf_op jit(solution)/shard_map/ppermute | solution.py:360
  120.9 2.6 %collective-permute-start.29 = (bf16[64,384]{1,0:T(8,128)(2,1)S(1)}, bf16[64,384]{1,0:T(8,128)(2,1)S(1)}, u32[]{:S(2)}, u32[]{:S(2)}) collective-permute-start(bf16[64,384]{1,0:T(8,128)(2,1)S(1)} %get-tuple-element.46), channel_id=1, source_target_pairs={{10,28},{26,12},{11,29},{27,13},{42,60},{58,44},{43,61},{59,45},{7... | collective-permute-start | bytes 147464 | tf_op jit(solution)/shard_map/ppermute | solution.py:361
  124.7 3.2 %collective-permute-start.31 = (bf16[64,384]{1,0:T(8,128)(2,1)S(1)}, bf16[64,384]{1,0:T(8,128)(2,1)S(1)}, u32[]{:S(2)}, u32[]{:S(2)}) collective-permute-start(bf16[64,384]{1,0:T(8,128)(2,1)S(1)} %get-tuple-element.48), channel_id=1, source_target_pairs={{12,14},{28,30},{13,15},{29,31},{44,46},{60,62},{45,47},{61,63},{7... | collective-permute-start | bytes 147464 | tf_op jit(solution)/shard_map/ppermute | solution.py:360
  125.4 2.6 %collective-permute-start.32 = (bf16[64,384]{1,0:T(8,128)(2,1)S(1)}, bf16[64,384]{1,0:T(8,128)(2,1)S(1)}, u32[]{:S(2)}, u32[]{:S(2)}) collective-permute-start(bf16[64,384]{1,0:T(8,128)(2,1)S(1)} %get-tuple-element.48), channel_id=1, source_target_pairs={{12,30},{28,14},{13,31},{29,15},{44,62},{60,46},{45,63},{61,47},{7... | collective-permute-start | bytes 147464 | tf_op jit(solution)/shard_map/ppermute | solution.py:361
  137.1 38.4 %all-to-all-start.1 = ((bf16[16,2,768]{2,1,0:T(2,128)(2,1)}), bf16[16,2,768]{2,1,0:T(2,128)(2,1)S(1)}, u32[]{:S(2)}, u32[]{:S(2)}) async-start(bf16[16,2,768]{2,1,0:T(2,128)(2,1)} %bitcast.23), calls=%async_computation.1 | async-start | bytes 98304 | tf_op jit(solution)/shard_map/all_to_all | solution.py:368
  (12 other events, 149.1 us)

commit v7 on v6

--- a/solution.py
+++ b/solution.py
@@ -74,15 +74,19 @@
 ACROSS = [(i, (i + 256) % 512) for i in range(512)]
 
 
-def onward(section, flip, turn):
-    def number(x, y, core, s):
-        return (((x * 4 + y // 2) * 2 + core) * 8 + s) * 2 + y % 2
-
+def place_of(x, y, core, section):
+    return (((x * 4 + y // 2) * 2 + core) * 8 + section) * 2 + y % 2
+
+
+PLANE = [(x, y, core) for x in range(4) for y in range(8) for core in range(2)]
+LAST = SECTIONS - 1
+
+
+def onward(tick, flip, turn):
     return [
-        (number(x, y, core, section), number(x ^ flip, y, core ^ turn, section + 1))
-        for x in range(4)
-        for y in range(8)
-        for core in range(2)
+        (place_of(x, y, core, section), place_of(x ^ flip, y, core ^ turn, section + 1))
+        for section in range(tick % 4, LAST, 4)
+        for x, y, core in PLANE
     ]
 
 
@@ -232,52 +236,58 @@
         own_ref[COLUMNS : COLUMNS + UNIT, :] = pick(turn0_ref, turn1_ref)
 
 
-def place_kernel(sources, last, where, *refs):
+def place_kernel(sources, kind, where, *refs):
     blocks, refs = refs[: len(sources)], refs[len(sources) :]
-    rows, sem = (refs[1], refs[3]) if last else (refs[0], refs[1])
-    member, core, y = where[0], where[2], where[3]
+    rows = refs[{"first": 0, "last": 1, "rest": 2}[kind]]
+    sem = refs[-1]
+    member, core, y, later = where[0], where[2], where[3], where[4]
     sign = 1 - 2 * core
-    copies = []
 
     def home(unit):
         third = unit // 8
         part = (COLUMNS * 8 * ((third - member + 4) % 4) + PART * third) // D
         return part * PART + unit % 8 * UNIT
 
-    for (source, parts), ref in zip(sources, blocks):
-        at = (y + sign * source + 8) % 8
-        col = pl.ds(pl.multiple_of(at % 2 * HALF, 128), HALF)
-        for n, part in enumerate(parts):
-            for j in range(UNITS):
-                row = pl.multiple_of(home((at // 2 * 2 + part) * UNITS + j), 16)
-                copy = pltpu.make_async_copy(
-                    ref.at[pl.ds(n * COLUMNS + j * UNIT, UNIT)], rows.at[pl.ds(row, UNIT), col], sem
-                )
-                copy.start()
-                copies.append(copy)
-    for copy in copies:
-        copy.wait()
-    if last:
-        for c in range(0, D, HDIM):
-            refs[2][c : c + HDIM, :] = jnp.transpose(rows[:, c : c + HDIM])
-
-
-def place(sources, where, blocks, rows=None):
-    last = rows is not None
-    held = pl.BlockSpec(memory_space=pl.ANY)
+    @pl.when(later == (1 if kind == "rest" else 0))
+    def _():
+        copies = []
+        for (source, parts), ref in zip(sources, blocks):
+            at = (y + sign * source + 8) % 8
+            col = pl.ds(pl.multiple_of(at % 2 * HALF, 128), HALF)
+            for n, part in enumerate(parts):
+                for j in range(UNITS):
+                    row = pl.multiple_of(home((at // 2 * 2 + part) * UNITS + j), 16)
+                    copy = pltpu.make_async_copy(
+                        ref.at[pl.ds(n * COLUMNS + j * UNIT, UNIT)], rows.at[pl.ds(row, UNIT), col], sem
+                    )
+                    copy.start()
+                    copies.append(copy)
+        for copy in copies:
+            copy.wait()
+        if kind != "first":
+            out_ref = refs[2 if kind == "last" else 1]
+            for c in range(0, D, HDIM):
+                out_ref[c : c + HDIM, :] = jnp.transpose(rows[:, c : c + HDIM])
+
+
+def place(sources, kind, where, blocks, held=()):
+    any_space = pl.BlockSpec(memory_space=pl.ANY)
     vmem = pl.BlockSpec(memory_space=pltpu.VMEM)
     whole = jax.ShapeDtypeStruct((3 * PART, D), jnp.bfloat16)
     turned = jax.ShapeDtypeStruct((D, 3 * PART), jnp.bfloat16)
+    scratch = [pltpu.SemaphoreType.DMA]
+    if kind == "rest":
+        scratch = [pltpu.VMEM((3 * PART, D), jnp.bfloat16), *scratch]
     return pl.pallas_call(
-        functools.partial(place_kernel, sources, last),
-        out_shape=(whole, turned) if last else whole,
-        in_specs=[pl.BlockSpec(memory_space=pltpu.SMEM)] + [held] * len(blocks) + [vmem] * last,
-        out_specs=(vmem, vmem) if last else vmem,
-        input_output_aliases={len(blocks) + 1: 0} if last else {},
-        scratch_shapes=[pltpu.SemaphoreType.DMA],
+        functools.partial(place_kernel, sources, kind),
+        out_shape={"first": whole, "last": (whole, turned), "rest": turned}[kind],
+        in_specs=[pl.BlockSpec(memory_space=pltpu.SMEM)] + [any_space] * len(blocks) + [vmem] * len(held),
+        out_specs=(vmem, vmem) if kind == "last" else vmem,
+        input_output_aliases={len(blocks) + 1: 0} if held else {},
+        scratch_shapes=scratch,
         compiler_params=pltpu.CompilerParams(vmem_limit_bytes=12 * 1024 * 1024),
-        name="place_last" if last else "place_first",
-    )(where, *blocks, *([rows] if last else []))
+        name="place_" + kind,
+    )(where, *blocks, *held)
 
 
 def whole_call(kernel, where, arrays, outs, sems=()):
@@ -299,7 +309,7 @@
     section = index["section"]
     member = index["xl"] * 2 + index["core"]
     y = index["yh"] * 2 + index["cfg"]
-    where = jnp.stack([member, index["xh"], index["core"], y]).astype(jnp.int32)
+    where = jnp.stack([member, index["xh"], index["core"], y, jnp.minimum(section, 1)]).astype(jnp.int32)
     who = jnp.stack([member, section]).astype(jnp.int32)
 
     half, turn = whole_call(
@@ -327,10 +337,10 @@
     up4 = lax.ppermute(up3[:COLUMNS], AXES, UP)
     down4 = lax.ppermute(down3[COLUMNS:], AXES, DOWN)
     both = (0, 1)
-    rows = place(
-        ((0, both), (-1, both), (1, both), (-2, both), (2, both)), where, [own, up1, down1, up2, down2]
-    )
-    _, weight = place(((-3, both), (3, both), (4, (0,)), (4, (1,))), where, [up3, down3, up4, down4], rows)
+    early = ((0, both), (-1, both), (1, both), (-2, both), (2, both)), [own, up1, down1, up2, down2]
+    late = ((-3, both), (3, both), (4, (0,)), (4, (1,))), [up3, down3, up4, down4]
+    rows = place(early[0], "first", where, early[1])
+    _, weight = place(late[0], "last", where, late[1], [rows])
     x = jnp.transpose(x.reshape(GROUP, MEMBERS, PART), (1, 0, 2))
     near = lax.dynamic_index_in_dim(x, member, 0, keepdims=False)
     cross = lax.dynamic_index_in_dim(x, member + 1 - 2 * index["core"], 0, keepdims=False)
@@ -355,6 +365,9 @@
     fresh = jnp.zeros((GROUP, 2 * PART), jnp.bfloat16)
     for tick in range(SECTIONS):
         state, fresh = run_block(tick, who, near, cross, far, weight, kv, kv_other, mod, gate, cosine, sine, blocks[:, None], fresh)
+        if tick == 0:
+            moved, state = lax.optimization_barrier((early[1] + late[1], state))
+            weight = place(early[0] + late[0], "rest", where, moved, [weight])
         if tick + 1 < SECTIONS:
             far = lax.ppermute(state, AXES, onward(tick, 1, 0))
             near = lax.ppermute(state, AXES, onward(tick, 0, 0))
@@ -367,9 +380,9 @@
     finals = jnp.transpose(finals, (0, 2, 1, 3)).reshape(SECTIONS * 2, LOCAL // SECTIONS, D // 2)
     spread = lax.all_to_all(finals, ("section", "cfg"), split_axis=0, concat_axis=0, tiled=True)
     kept = lax.all_gather(fresh, ("xl", "core"), axis=0, tiled=False)
-    spread, kept = lax.optimization_barrier((spread, kept))
     kept = lax.dynamic_slice_in_dim(kept, member * LOCAL, LOCAL, 1)
     kept = jnp.transpose(kept.reshape(MEMBERS, LOCAL, 2, PART), (1, 2, 0, 3)).reshape(LOCAL, 2 * D)
+    spread, kept = lax.optimization_barrier((spread, kept))
     uncond = spread[2 * SECTIONS - 2].astype(jnp.float32)
     conditioned = spread[2 * SECTIONS - 1].astype(jnp.float32)
     guided = (uncond + guide_weight * (conditioned - uncond)).astype(jnp.bfloat16)

time: 178 us -> 176 us (0.989)
  starting transfers between devices: 101 us -> 98.1 us
    all_to_all x1, starting transfers between devices: 30.8 us -> 22.5 us  [body(): lax.all_to_all(finals, ('section', 'cfg'), split_axis=0, concat_axis=0, t...]
    ppermute x7, starting transfers between devices: 7.02 us -> 13.8 us  [body(): far = lax.ppermute(state, AXES, onward(tick, 1, 0))]
    all_gather x7, blocking collectives: 13.2 us -> 17.6 us  [body(): far = lax.all_gather(far, 'core', axis=0, tiled=False)]
    ppermute x2, waiting for transfers between devices: 4.31 us -> 0.01 us  [body(): up3, down3 = (lax.ppermute(up2, AXES, UP), lax.ppermute(down2, AXES, DOWN))]
    ppermute x7, starting transfers between devices: 11.5 us -> 7.39 us  [body(): cross = lax.ppermute(state, AXES, onward(tick, 0, 1))]
    ppermute x1, starting transfers between devices: 1.92 us -> 5.11 us  [body(): kv_other = lax.ppermute(kv, AXES, ACROSS)]
    ppermute x2, waiting for transfers between devices: 6.06 us -> 9.06 us  [body(): up1, down1 = (lax.ppermute(own, AXES, UP), lax.ppermute(own, AXES, DOWN))]
    all_gather x1, blocking collectives: 8.45 us -> 5.48 us  [body(): x = lax.all_gather(entering, ('xl', 'core'), axis=0, tiled=True)]
  transfers between devices with their start and end apart: 36 -> 36, of which waited for: 7 -> 5; matrix products, arithmetic and copies ran while one was open for 2% -> 2% of each run, Pallas kernels for 4% -> 4%
where the time goes in v7:
time: 176 us; the launch traced here: 175 us
  starting transfers between devices  98.1 us (56%)
  blocking collectives  35.4 us (20%)
  waiting for transfers between devices  14.4 us (8%)
  Pallas kernels  14.1 us (8%)
  local copies, waits for them, and re-layouts  9.5 us (5%)
  between operations  2.06 us (1%)
    all_to_all x1, starting transfers between devices, body(): lax.all_to_all(finals, ('section', 'cfg'), split_axis=0, concat_axis=0, t...  22.5 us
    all_gather x7, blocking collectives, body(): far = lax.all_gather(far, 'core', axis=0, tiled=False)  17.6 us
    ppermute x7, starting transfers between devices, body(): far = lax.ppermute(state, AXES, onward(tick, 1, 0))  13.8 us
    all_to_all x1, starting transfers between devices, body(): lax.all_to_all(outgoing, ('xl', 'yh', 'core'), split_axis=0, concat_axis=...  10.2 us
    ppermute x2, waiting for transfers between devices, body(): up1, down1 = (lax.ppermute(own, AXES, UP), lax.ppermute(own, AXES, DOWN))  9.06 us
    ppermute x7, starting transfers between devices, body(): cross = lax.ppermute(state, AXES, onward(tick, 0, 1))  7.39 us
    ppermute x2, starting transfers between devices, body(): up3, down3 = (lax.ppermute(up2, AXES, UP), lax.ppermute(down2, AXES, DOWN))  6.7 us
    all_gather x1, blocking collectives, body(): kept = lax.all_gather(fresh, ('xl', 'core'), axis=0, tiled=False)  6.58 us
  transfers between devices with their start and end apart: 36, of which 5 were waited for; matrix products, arithmetic and copies ran while one was open for 2% of the time, Pallas kernels for 4%

profile of v7, /device:TPU:1, one launch (start us, length us, event | category | flops | bytes accessed | tf_op | source)
XLA Modules:
  0.0 174.7 jit_solution(12862645960324005842)
XLA Ops:
  3.2 10.2 %all-to-all-start = ((bf16[16,16,768]{2,1,0:T(8,128)(2,1)}), bf16[16,16,768]{2,1,0:T(8,128)(2,1)S(1)}, u32[]{:S(2)}, u32[]{:S(2)}) async-start(bf16[16,16,768]{2,1,0:T(8,128)(2,1)} %stale_kernel.1), calls=%async_computation | async-start | bytes 786432 | tf_op jit(solution)/shard_map/all_to_all | solution.py:327
  15.0 3.7 %collective-permute-start = (bf16[144,768]{1,0:T(8,128)(2,1)S(1)}, bf16[144,768]{1,0:T(8,128)(2,1)S(1)}, u32[]{:S(2)}, u32[]{:S(2)}) collective-permute-start(bf16[144,768]{1,0:T(8,128)(2,1)S(1)} %get-tuple-element.38), channel_id=1, source_target_pairs={{0,0},{2,2},{4,4},{6,6},{8,8},{10,10},{12,12},{14,14},{16,256},{18... | collective-permute-start | bytes 663560 | tf_op jit(solution)/shard_map/ppermute | solution.py:322
  18.7 1.9 %collective-permute-start.1 = (bf16[144,768]{1,0:T(8,128)(2,1)S(1)}, bf16[144,768]{1,0:T(8,128)(2,1)S(1)}, u32[]{:S(2)}, u32[]{:S(2)}) collective-permute-start(bf16[144,768]{1,0:T(8,128)(2,1)S(1)} %get-tuple-element.38), channel_id=1, source_target_pairs={{0,256},{2,258},{4,260},{6,262},{8,264},{10,266},{12,268},{14,270}... | collective-permute-start | bytes 663560 | tf_op jit(solution)/shard_map/ppermute | solution.py:322
  23.8 3.1 %collective-permute-done.1.second_ref = bf16[144,768]{1,0:T(8,128)(2,1)S(1)} collective-permute-done((bf16[144,768]{1,0:T(8,128)(2,1)S(1)}, bf16[144,768]{1,0:T(8,128)(2,1)S(1)}, u32[]{:S(2)}, u32[]{:S(2)}) %collective-permute-start.1) | collective-permute-done | bytes 221216 | tf_op jit(solution)/shard_map/ppermute | solution.py:322
  27.5 3.7 %collective-permute-start.4 = (bf16[288,768]{1,0:T(8,128)(2,1)S(1)}, bf16[288,768]{1,0:T(8,128)(2,1)S(1)}, u32[]{:S(2)}, u32[]{:S(2)}) collective-permute-start(bf16[288,768]{1,0:T(8,128)(2,1)S(1)} %join_kernel.1.refs_0_), channel_id=1, source_target_pairs={{0,1},{2,3},{4,5},{6,7},{8,9},{10,11},{12,13},{14,15},{16,113},{18... | collective-permute-start | bytes 1327112 | tf_op jit(solution)/shard_map/ppermute | solution.py:330
  31.2 1.9 %collective-permute-start.5 = (bf16[288,768]{1,0:T(8,128)(2,1)S(1)}, bf16[288,768]{1,0:T(8,128)(2,1)S(1)}, u32[]{:S(2)}, u32[]{:S(2)}) collective-permute-start(bf16[288,768]{1,0:T(8,128)(2,1)S(1)} %join_kernel.1.refs_0_), channel_id=1, source_target_pairs={{0,97},{2,99},{4,101},{6,103},{8,105},{10,107},{12,109},{14,111},{... | collective-permute-start | bytes 1327112 | tf_op jit(solution)/shard_map/ppermute | solution.py:330
  34.6 9.1 %collective-permute-done.5.refs_2_ = bf16[288,768]{1,0:T(8,128)(2,1)S(1)} collective-permute-done((bf16[288,768]{1,0:T(8,128)(2,1)S(1)}, bf16[288,768]{1,0:T(8,128)(2,1)S(1)}, u32[]{:S(2)}, u32[]{:S(2)}) %collective-permute-start.5) | collective-permute-done | bytes 442400 | tf_op jit(solution)/shard_map/ppermute | solution.py:330
  43.7 1.9 %collective-permute-start.7 = (bf16[288,768]{1,0:T(8,128)(2,1)S(1)}, bf16[288,768]{1,0:T(8,128)(2,1)}, u32[]{:S(2)}, u32[]{:S(2)}) collective-permute-start(bf16[288,768]{1,0:T(8,128)(2,1)S(1)} %collective-permute-done.5.refs_2_), channel_id=1, source_target_pairs={{0,97},{2,99},{4,101},{6,103},{8,105},{10,107},{12,109},{14,111},{... | collective-permute-start | bytes 1327112 | tf_op jit(solution)/shard_map/ppermute | solution.py:334
  45.6 4.6 %collective-permute-start.6 = (bf16[288,768]{1,0:T(8,128)(2,1)S(1)}, bf16[288,768]{1,0:T(8,128)(2,1)}, u32[]{:S(2)}, u32[]{:S(2)}) collective-permute-start(bf16[288,768]{1,0:T(8,128)(2,1)S(1)} %collective-permute-done.4.refs_1_), channel_id=1, source_target_pairs={{0,1},{2,3},{4,5},{6,7},{8,9},{10,11},{12,13},{14,15},{16,113},{18... | collective-permute-start | bytes 1327112 | tf_op jit(solution)/shard_map/ppermute | solution.py:334
  50.5 5.5 %all_gather.57 = bf16[64,1536]{1,0:T(8,128)(2,1)} all-gather(bf16[16,1536]{1,0:T(8,128)(2,1)S(1)} %bitcast.72), channel_id=1, replica_groups=mesh['xh'=2,'xl'=2,'yh'=4,'core'=2,'section'=8,'cfg'=2] {'xl','core'}, dimensions={0}, use_global_device_ids=true | all-gather | bytes 245760 | tf_op jit(solution)/shard_map/all_gather | solution.py:333
  56.0 3.5 %collective-permute-start.9 = (bf16[288,768]{1,0:T(8,128)(2,1)}, bf16[288,768]{1,0:T(8,128)(2,1)S(1)}, u32[]{:S(2)}, u32[]{:S(2)}) collective-permute-start(bf16[288,768]{1,0:T(8,128)(2,1)} %collective-permute-done.7.refs_4_), channel_id=1, source_target_pairs={{0,97},{2,99},{4,101},{6,103},{8,105},{10,107},{12,109},{14,111},{... | collective-permute-start | bytes 1327112 | tf_op jit(solution)/shard_map/ppermute | solution.py:336
  59.6 3.2 %collective-permute-start.8 = (bf16[288,768]{1,0:T(8,128)(2,1)}, bf16[288,768]{1,0:T(8,128)(2,1)S(1)}, u32[]{:S(2)}, u32[]{:S(2)}) collective-permute-start(bf16[288,768]{1,0:T(8,128)(2,1)} %collective-permute-done.6.refs_3_), channel_id=1, source_target_pairs={{0,1},{2,3},{4,5},{6,7},{8,9},{10,11},{12,13},{14,15},{16,113},{18... | collective-permute-start | bytes 1327112 | tf_op jit(solution)/shard_map/ppermute | solution.py:336
  62.9 5.1 %collective-permute-start.12 = (bf16[256,768]{1,0:T(8,128)(2,1)S(1)}, bf16[256,768]{1,0:T(8,128)(2,1)S(1)}, u32[]{:S(2)}, u32[]{:S(2)}) collective-permute-start(bf16[256,768]{1,0:T(8,128)(2,1)S(1)} %bitcast.47), channel_id=1, source_target_pairs={{0,256},{1,257},{2,258},{3,259},{4,260},{5,261},{6,262},{7,263},{8... | collective-permute-start | bytes 1179656 | tf_op jit(solution)/shard_map/ppermute | solution.py:332
  69.4 2.6 %collective-permute-start.11 = (bf16[144,768]{1,0:T(8,128)(2,1)S(1)}, bf16[144,768]{1,0:T(8,128)(2,1)S(1)}, u32[]{:S(2)}, u32[]{:S(2)}) collective-permute-start(bf16[144,768]{1,0:T(8,128)(2,1)S(1)} %slice.24), channel_id=1, source_target_pairs={{0,97},{2,99},{4,101},{6,103},{8,105},{10,107},{12,109},{14,111},{... | collective-permute-start | bytes 663560 | tf_op jit(solution)/shard_map/ppermute | solution.py:338
  72.1 4.9 %collective-permute-start.10 = (bf16[144,768]{1,0:T(8,128)(2,1)S(1)}, bf16[144,768]{1,0:T(8,128)(2,1)S(1)}, u32[]{:S(2)}, u32[]{:S(2)}) collective-permute-start(bf16[144,768]{1,0:T(8,128)(2,1)S(1)} %slice.23), channel_id=1, source_target_pairs={{0,1},{2,3},{4,5},{6,7},{8,9},{10,11},{12,13},{14,15},{16,113},{18... | collective-permute-start | bytes 663560 | tf_op jit(solution)/shard_map/ppermute | solution.py:337
  78.0 2.7 %place_first.1.refs_4_ = bf16[1152,1536]{1,0:T(8,128)(2,1)S(1)} custom-call(s32[5]{0:T(128)S(1)} %stack.32.where, bf16[288,768]{1,0:T(8,128)(2,1)S(1)} %join_kernel.1.refs_0_, bf16[288,768]{1,0:T(8,128)(2,1)S(1)} %collective-permute-done.4.refs_1_, bf16[288,768]{1,0:T(8,128)(2,1)S(1)} %copy-done.4, bf16[288,768]{1,0:T(8,128)(2,1)} %collective-permute-done.6.refs_3_, ...), custom_call_target="tpu_custom_call" | custom-call | tf_op jit(solution)/shard_map/place_first/pallas_call | solution.py:281
  81.7 2.3 %place_last.1 = (bf16[1152,1536]{1,0:T(8,128)(2,1)S(1)}, bf16[1536,1152]{1,0:T(8,128)(2,1)S(1)}) custom-call(s32[5]{0:T(128)S(1)} %stack.32.where, bf16[288,768]{1,0:T(8,128)(2,1)S(1)} %collective-permute-done.8.refs_0_.refs_5_, bf16[288,768]{1,0:T(8,128)(2,1)S(1)} %collective-permute-done.9.refs_1_.refs_6_, ...), custom_call_target="tpu_custom_call", output_to_operand_aliasing={{0}: (5, {})} | custom-call | tf_op jit(solution)/shard_map/place_last/pallas_call | solution.py:281
  84.1 1.9 %block_step.8 = (bf16[64,384]{1,0:T(8,128)(2,1)S(1)}, bf16[64,768]{1,0:T(8,128)(2,1)S(1)}) custom-call(s32[2]{0:T(128)S(1)} %pad_add_fusion.who, bf16[64,384]{1,0:T(8,128)(2,1)S(1)} %get-tuple-element.80.near_ref, bf16[64,384]{1,0:T(8,128)(2,1)S(1)} %get-tuple-element.79.cross_ref, bf16[2,64,384]{2,1,0:T(8,128)(2,1)S(1)} %bitcast.57, ...), custom_call_target="tpu_custom_call" | custom-call | tf_op jit(solution)/shard_map/block_step/pallas_call | solution.py:178
  86.0 3.1 %collective-permute-start.15 = (bf16[64,384]{1,0:T(8,128)(2,1)S(1)}, bf16[64,384]{1,0:T(8,128)(2,1)S(1)}, u32[]{:S(2)}, u32[]{:S(2)}) collective-permute-start(bf16[64,384]{1,0:T(8,128)(2,1)S(1)} %get-tuple-element.47), channel_id=1, source_target_pairs={{0,130},{16,146},{1,131},{17,147},{32,162},{48,178},{33,163},{49,1... | collective-permute-start | bytes 147464 | tf_op jit(solution)/shard_map/ppermute | solution.py:372
  90.4 2.6 %collective-permute-start.14 = (bf16[64,384]{1,0:T(8,128)(2,1)S(1)}, bf16[64,384]{1,0:T(8,128)(2,1)S(1)}, u32[]{:S(2)}, u32[]{:S(2)}) collective-permute-start(bf16[64,384]{1,0:T(8,128)(2,1)S(1)} %get-tuple-element.47), channel_id=1, source_target_pairs={{0,18},{16,2},{1,19},{17,3},{32,50},{48,34},{33,51},{49,35},{64,82... | collective-permute-start | bytes 147464 | tf_op jit(solution)/shard_map/ppermute | solution.py:374
  93.6 6.0 %all-gather = bf16[128,384]{1,0:T(8,128)(2,1)S(1)} all-gather(bf16[64,384]{1,0:T(8,128)(2,1)S(1)} %collective-permute-done.15), channel_id=2, replica_groups=mesh['xh'=2,'xl'=2,'yh'=4,'core'=2,'section'=8,'cfg'=2] {'core'}, dimensions={0}, use_global_device_ids=true | all-gather | bytes 147456 | tf_op jit(solution)/shard_map/all_gather | solution.py:375
  102.2 1.9 %all-gather.1 = bf16[128,384]{1,0:T(8,128)(2,1)S(1)} all-gather(bf16[64,384]{1,0:T(8,128)(2,1)S(1)} %collective-permute-done.18), channel_id=3, replica_groups=mesh['xh'=2,'xl'=2,'yh'=4,'core'=2,'section'=8,'cfg'=2] {'core'}, dimensions={0}, use_global_device_ids=true | all-gather | bytes 147456 | tf_op jit(solution)/shard_map/all_gather | solution.py:375
  106.9 1.9 %all-gather.2 = bf16[128,384]{1,0:T(8,128)(2,1)S(1)} all-gather(bf16[64,384]{1,0:T(8,128)(2,1)S(1)} %collective-permute-done.21), channel_id=4, replica_groups=mesh['xh'=2,'xl'=2,'yh'=4,'core'=2,'section'=8,'cfg'=2] {'core'}, dimensions={0}, use_global_device_ids=true | all-gather | bytes 147456 | tf_op jit(solution)/shard_map/all_gather | solution.py:375
  111.4 1.9 %all-gather.3 = bf16[128,384]{1,0:T(8,128)(2,1)S(1)} all-gather(bf16[64,384]{1,0:T(8,128)(2,1)S(1)} %collective-permute-done.24), channel_id=5, replica_groups=mesh['xh'=2,'xl'=2,'yh'=4,'core'=2,'section'=8,'cfg'=2] {'core'}, dimensions={0}, use_global_device_ids=true | all-gather | bytes 147456 | tf_op jit(solution)/shard_map/all_gather | solution.py:375
  113.8 7.4 %collective-permute-start.27 = (bf16[64,384]{1,0:T(8,128)(2,1)S(1)}, bf16[64,384]{1,0:T(8,128)(2,1)S(1)}, u32[]{:S(2)}, u32[]{:S(2)}) collective-permute-start(bf16[64,384]{1,0:T(8,128)(2,1)S(1)} %get-tuple-element.64), channel_id=1, source_target_pairs={{0,130},{16,146},{1,131},{17,147},{32,162},{48,178},{33,163},{49,1... | collective-permute-start | bytes 147464 | tf_op jit(solution)/shard_map/ppermute | solution.py:372
  123.8 2.2 %all-gather.4 = bf16[128,384]{1,0:T(8,128)(2,1)S(1)} all-gather(bf16[64,384]{1,0:T(8,128)(2,1)S(1)} %collective-permute-done.27), channel_id=6, replica_groups=mesh['xh'=2,'xl'=2,'yh'=4,'core'=2,'section'=8,'cfg'=2] {'core'}, dimensions={0}, use_global_device_ids=true | all-gather | bytes 147456 | tf_op jit(solution)/shard_map/all_gather | solution.py:375
  128.6 1.9 %all-gather.5 = bf16[128,384]{1,0:T(8,128)(2,1)S(1)} all-gather(bf16[64,384]{1,0:T(8,128)(2,1)S(1)} %collective-permute-done.30), channel_id=7, replica_groups=mesh['xh'=2,'xl'=2,'yh'=4,'core'=2,'section'=8,'cfg'=2] {'core'}, dimensions={0}, use_global_device_ids=true | all-gather | bytes 147456 | tf_op jit(solution)/shard_map/all_gather | solution.py:375
  133.0 1.9 %all-gather.6 = bf16[128,384]{1,0:T(8,128)(2,1)S(1)} all-gather(bf16[64,384]{1,0:T(8,128)(2,1)S(1)} %collective-permute-done.33), channel_id=8, replica_groups=mesh['xh'=2,'xl'=2,'yh'=4,'core'=2,'section'=8,'cfg'=2] {'core'}, dimensions={0}, use_global_device_ids=true | all-gather | bytes 147456 | tf_op jit(solution)/shard_map/all_gather | solution.py:375
  134.9 2.0 %copy-done.2 = bf16[1536,1152]{1,0:T(8,128)(2,1)S(1)} copy-done((bf16[1536,1152]{1,0:T(8,128)(2,1)S(1)}, bf16[1536,1152]{1,0:T(8,128)(2,1)}, u32[]{:S(2)}) %copy-start.2) | copy-done | bytes 3538968
  137.5 5.8 %all-gather.7 = bf16[256,384]{1,0:T(8,128)(2,1)S(1)} all-gather(bf16[64,384]{1,0:T(8,128)(2,1)S(1)} %get-tuple-element.70), channel_id=9, replica_groups=mesh['xh'=2,'xl'=2,'yh'=4,'core'=2,'section'=8,'cfg'=2] {'xl','core'}, dimensions={0}, use_global_device_ids=true | all-gather | bytes 245760 | tf_op jit(solution)/shard_map/all_gather | solution.py:377
  144.0 22.5 %all-to-all-start.1 = ((bf16[16,2,768]{2,1,0:T(2,128)(2,1)}), bf16[16,2,768]{2,1,0:T(2,128)(2,1)S(1)}, u32[]{:S(2)}, u32[]{:S(2)}) async-start(bf16[16,2,768]{2,1,0:T(2,128)(2,1)} %bitcast.24), calls=%async_computation.1 | async-start | bytes 98304 | tf_op jit(solution)/shard_map/all_to_all | solution.py:381
  166.5 6.6 %all-gather.8 = bf16[256,768]{1,0:T(8,128)(2,1)S(1)} all-gather(bf16[64,768]{1,0:T(8,128)(2,1)S(1)} %get-tuple-element.71), channel_id=10, replica_groups=mesh['xh'=2,'xl'=2,'yh'=4,'core'=2,'section'=8,'cfg'=2] {'xl','core'}, dimensions={0}, use_global_device_ids=true | all-gather | bytes 491520 | tf_op jit(solution)/shard_map/all_gather | solution.py:382
  (112 shorter events, 33.4 us)
Async XLA Ops:
  3.2 42.4 %all-to-all-start = ((bf16[16,16,768]{2,1,0:T(8,128)(2,1)}), bf16[16,16,768]{2,1,0:T(8,128)(2,1)S(1)}, u32[]{:S(2)}, u32[]{:S(2)}) async-start(bf16[16,16,768]{2,1,0:T(8,128)(2,1)} %stale_kernel.1), calls=%async_computation | async-start | bytes 786432 | tf_op jit(solution)/shard_map/all_to_all | solution.py:327
  15.0 8.8 %collective-permute-start = (bf16[144,768]{1,0:T(8,128)(2,1)S(1)}, bf16[144,768]{1,0:T(8,128)(2,1)S(1)}, u32[]{:S(2)}, u32[]{:S(2)}) collective-permute-start(bf16[144,768]{1,0:T(8,128)(2,1)S(1)} %get-tuple-element.38), channel_id=1, source_target_pairs={{0,0},{2,2},{4,4},{6,6},{8,8},{10,10},{12,12},{14,14},{16,256},{18... | collective-permute-start | bytes 663560 | tf_op jit(solution)/shard_map/ppermute | solution.py:322
  18.7 8.2 %collective-permute-start.1 = (bf16[144,768]{1,0:T(8,128)(2,1)S(1)}, bf16[144,768]{1,0:T(8,128)(2,1)S(1)}, u32[]{:S(2)}, u32[]{:S(2)}) collective-permute-start(bf16[144,768]{1,0:T(8,128)(2,1)S(1)} %get-tuple-element.38), channel_id=1, source_target_pairs={{0,256},{2,258},{4,260},{6,262},{8,264},{10,266},{12,268},{14,270}... | collective-permute-start | bytes 663560 | tf_op jit(solution)/shard_map/ppermute | solution.py:322
  20.6 2.1 %collective-permute-start.2 = (bf16[48,768]{1,0:T(8,128)(2,1)S(1)}, bf16[48,768]{1,0:T(8,128)(2,1)S(1)}, u32[]{:S(2)}, u32[]{:S(2)}) collective-permute-start(bf16[48,768]{1,0:T(8,128)(2,1)S(1)} %get-tuple-element.39), channel_id=1, source_target_pairs={{32,48},{34,50},{36,52},{38,54},{40,56},{42,58},{44,60},{46,62},{3... | collective-permute-start | bytes 221192 | tf_op jit(solution)/shard_map/ppermute | solution.py:323
  27.5 18.1 %collective-permute-start.4 = (bf16[288,768]{1,0:T(8,128)(2,1)S(1)}, bf16[288,768]{1,0:T(8,128)(2,1)S(1)}, u32[]{:S(2)}, u32[]{:S(2)}) collective-permute-start(bf16[288,768]{1,0:T(8,128)(2,1)S(1)} %join_kernel.1.refs_0_), channel_id=1, source_target_pairs={{0,1},{2,3},{4,5},{6,7},{8,9},{10,11},{12,13},{14,15},{16,113},{18... | collective-permute-start | bytes 1327112 | tf_op jit(solution)/shard_map/ppermute | solution.py:330
  31.2 12.5 %collective-permute-start.5 = (bf16[288,768]{1,0:T(8,128)(2,1)S(1)}, bf16[288,768]{1,0:T(8,128)(2,1)S(1)}, u32[]{:S(2)}, u32[]{:S(2)}) collective-permute-start(bf16[288,768]{1,0:T(8,128)(2,1)S(1)} %join_kernel.1.refs_0_), channel_id=1, source_target_pairs={{0,97},{2,99},{4,101},{6,103},{8,105},{10,107},{12,109},{14,111},{... | collective-permute-start | bytes 1327112 | tf_op jit(solution)/shard_map/ppermute | solution.py:330
  43.7 12.3 %collective-permute-start.7 = (bf16[288,768]{1,0:T(8,128)(2,1)S(1)}, bf16[288,768]{1,0:T(8,128)(2,1)}, u32[]{:S(2)}, u32[]{:S(2)}) collective-permute-start(bf16[288,768]{1,0:T(8,128)(2,1)S(1)} %collective-permute-done.5.refs_2_), channel_id=1, source_target_pairs={{0,97},{2,99},{4,101},{6,103},{8,105},{10,107},{12,109},{14,111},{... | collective-permute-start | bytes 1327112 | tf_op jit(solution)/shard_map/ppermute | solution.py:334
  45.6 13.9 %collective-permute-start.6 = (bf16[288,768]{1,0:T(8,128)(2,1)S(1)}, bf16[288,768]{1,0:T(8,128)(2,1)}, u32[]{:S(2)}, u32[]{:S(2)}) collective-permute-start(bf16[288,768]{1,0:T(8,128)(2,1)S(1)} %collective-permute-done.4.refs_1_), channel_id=1, source_target_pairs={{0,1},{2,3},{4,5},{6,7},{8,9},{10,11},{12,13},{14,15},{16,113},{18... | collective-permute-start | bytes 1327112 | tf_op jit(solution)/shard_map/ppermute | solution.py:334
  56.0 13.4 %collective-permute-start.9 = (bf16[288,768]{1,0:T(8,128)(2,1)}, bf16[288,768]{1,0:T(8,128)(2,1)S(1)}, u32[]{:S(2)}, u32[]{:S(2)}) collective-permute-start(bf16[288,768]{1,0:T(8,128)(2,1)} %collective-permute-done.7.refs_4_), channel_id=1, source_target_pairs={{0,97},{2,99},{4,101},{6,103},{8,105},{10,107},{12,109},{14,111},{... | collective-permute-start | bytes 1327112 | tf_op jit(solution)/shard_map/ppermute | solution.py:336
  59.6 12.5 %collective-permute-start.8 = (bf16[288,768]{1,0:T(8,128)(2,1)}, bf16[288,768]{1,0:T(8,128)(2,1)S(1)}, u32[]{:S(2)}, u32[]{:S(2)}) collective-permute-start(bf16[288,768]{1,0:T(8,128)(2,1)} %collective-permute-done.6.refs_3_), channel_id=1, source_target_pairs={{0,1},{2,3},{4,5},{6,7},{8,9},{10,11},{12,13},{14,15},{16,113},{18... | collective-permute-start | bytes 1327112 | tf_op jit(solution)/shard_map/ppermute | solution.py:336
  62.9 21.1 %collective-permute-start.12 = (bf16[256,768]{1,0:T(8,128)(2,1)S(1)}, bf16[256,768]{1,0:T(8,128)(2,1)S(1)}, u32[]{:S(2)}, u32[]{:S(2)}) collective-permute-start(bf16[256,768]{1,0:T(8,128)(2,1)S(1)} %bitcast.47), channel_id=1, source_target_pairs={{0,256},{1,257},{2,258},{3,259},{4,260},{5,261},{6,262},{7,263},{8... | collective-permute-start | bytes 1179656 | tf_op jit(solution)/shard_map/ppermute | solution.py:332
  69.4 11.3 %collective-permute-start.11 = (bf16[144,768]{1,0:T(8,128)(2,1)S(1)}, bf16[144,768]{1,0:T(8,128)(2,1)S(1)}, u32[]{:S(2)}, u32[]{:S(2)}) collective-permute-start(bf16[144,768]{1,0:T(8,128)(2,1)S(1)} %slice.24), channel_id=1, source_target_pairs={{0,97},{2,99},{4,101},{6,103},{8,105},{10,107},{12,109},{14,111},{... | collective-permute-start | bytes 663560 | tf_op jit(solution)/shard_map/ppermute | solution.py:338
  72.1 9.6 %collective-permute-start.10 = (bf16[144,768]{1,0:T(8,128)(2,1)S(1)}, bf16[144,768]{1,0:T(8,128)(2,1)S(1)}, u32[]{:S(2)}, u32[]{:S(2)}) collective-permute-start(bf16[144,768]{1,0:T(8,128)(2,1)S(1)} %slice.23), channel_id=1, source_target_pairs={{0,1},{2,3},{4,5},{6,7},{8,9},{10,11},{12,13},{14,15},{16,113},{18... | collective-permute-start | bytes 663560 | tf_op jit(solution)/shard_map/ppermute | solution.py:337
  86.0 7.6 %collective-permute-start.15 = (bf16[64,384]{1,0:T(8,128)(2,1)S(1)}, bf16[64,384]{1,0:T(8,128)(2,1)S(1)}, u32[]{:S(2)}, u32[]{:S(2)}) collective-permute-start(bf16[64,384]{1,0:T(8,128)(2,1)S(1)} %get-tuple-element.47), channel_id=1, source_target_pairs={{0,130},{16,146},{1,131},{17,147},{32,162},{48,178},{33,163},{49,1... | collective-permute-start | bytes 147464 | tf_op jit(solution)/shard_map/ppermute | solution.py:372
  89.1 10.6 %collective-permute-start.13 = (bf16[64,384]{1,0:T(8,128)(2,1)S(1)}, bf16[64,384]{1,0:T(8,128)(2,1)S(1)}, u32[]{:S(2)}, u32[]{:S(2)}) collective-permute-start(bf16[64,384]{1,0:T(8,128)(2,1)S(1)} %get-tuple-element.47), channel_id=1, source_target_pairs={{0,2},{16,18},{1,3},{17,19},{32,34},{48,50},{33,35},{49,51},{64,66... | collective-permute-start | bytes 147464 | tf_op jit(solution)/shard_map/ppermute | solution.py:373
  90.4 9.3 %collective-permute-start.14 = (bf16[64,384]{1,0:T(8,128)(2,1)S(1)}, bf16[64,384]{1,0:T(8,128)(2,1)S(1)}, u32[]{:S(2)}, u32[]{:S(2)}) collective-permute-start(bf16[64,384]{1,0:T(8,128)(2,1)S(1)} %get-tuple-element.47), channel_id=1, source_target_pairs={{0,18},{16,2},{1,19},{17,3},{32,50},{48,34},{33,51},{49,35},{64,82... | collective-permute-start | bytes 147464 | tf_op jit(solution)/shard_map/ppermute | solution.py:374
  100.9 3.2 %collective-permute-start.16 = (bf16[64,384]{1,0:T(8,128)(2,1)S(1)}, bf16[64,384]{1,0:T(8,128)(2,1)S(1)}, u32[]{:S(2)}, u32[]{:S(2)}) collective-permute-start(bf16[64,384]{1,0:T(8,128)(2,1)S(1)} %get-tuple-element.58), channel_id=1, source_target_pairs={{2,4},{18,20},{3,5},{19,21},{34,36},{50,52},{35,37},{51,53},{66,68... | collective-permute-start | bytes 147464 | tf_op jit(solution)/shard_map/ppermute | solution.py:373
  101.6 2.6 %collective-permute-start.17 = (bf16[64,384]{1,0:T(8,128)(2,1)S(1)}, bf16[64,384]{1,0:T(8,128)(2,1)S(1)}, u32[]{:S(2)}, u32[]{:S(2)}) collective-permute-start(bf16[64,384]{1,0:T(8,128)(2,1)S(1)} %get-tuple-element.58), channel_id=1, source_target_pairs={{2,20},{18,4},{3,21},{19,5},{34,52},{50,36},{35,53},{51,37},{66,84... | collective-permute-start | bytes 147464 | tf_op jit(solution)/shard_map/ppermute | solution.py:374
  104.7 2.2 %collective-permute-start.21 = (bf16[64,384]{1,0:T(8,128)(2,1)S(1)}, bf16[64,384]{1,0:T(8,128)(2,1)S(1)}, u32[]{:S(2)}, u32[]{:S(2)}) collective-permute-start(bf16[64,384]{1,0:T(8,128)(2,1)S(1)} %get-tuple-element.60), channel_id=1, source_target_pairs={{4,134},{20,150},{5,135},{21,151},{36,166},{52,182},{37,167},{53,1... | collective-permute-start | bytes 147464 | tf_op jit(solution)/shard_map/ppermute | solution.py:372
  105.4 3.4 %collective-permute-start.19 = (bf16[64,384]{1,0:T(8,128)(2,1)S(1)}, bf16[64,384]{1,0:T(8,128)(2,1)S(1)}, u32[]{:S(2)}, u32[]{:S(2)}) collective-permute-start(bf16[64,384]{1,0:T(8,128)(2,1)S(1)} %get-tuple-element.60), channel_id=1, source_target_pairs={{4,6},{20,22},{5,7},{21,23},{36,38},{52,54},{37,39},{53,55},{68,70... | collective-permute-start | bytes 147464 | tf_op jit(solution)/shard_map/ppermute | solution.py:373
  106.0 2.7 %collective-permute-start.20 = (bf16[64,384]{1,0:T(8,128)(2,1)S(1)}, bf16[64,384]{1,0:T(8,128)(2,1)S(1)}, u32[]{:S(2)}, u32[]{:S(2)}) collective-permute-start(bf16[64,384]{1,0:T(8,128)(2,1)S(1)} %get-tuple-element.60), channel_id=1, source_target_pairs={{4,22},{20,6},{5,23},{21,7},{36,54},{52,38},{37,55},{53,39},{68,86... | collective-permute-start | bytes 147464 | tf_op jit(solution)/shard_map/ppermute | solution.py:374
  109.4 2.0 %collective-permute-start.24 = (bf16[64,384]{1,0:T(8,128)(2,1)S(1)}, bf16[64,384]{1,0:T(8,128)(2,1)S(1)}, u32[]{:S(2)}, u32[]{:S(2)}) collective-permute-start(bf16[64,384]{1,0:T(8,128)(2,1)S(1)} %get-tuple-element.62), channel_id=1, source_target_pairs={{6,136},{22,152},{7,137},{23,153},{38,168},{54,184},{39,169},{55,1... | collective-permute-start | bytes 147464 | tf_op jit(solution)/shard_map/ppermute | solution.py:372
  110.0 3.2 %collective-permute-start.22 = (bf16[64,384]{1,0:T(8,128)(2,1)S(1)}, bf16[64,384]{1,0:T(8,128)(2,1)S(1)}, u32[]{:S(2)}, u32[]{:S(2)}) collective-permute-start(bf16[64,384]{1,0:T(8,128)(2,1)S(1)} %get-tuple-element.62), channel_id=1, source_target_pairs={{6,8},{22,24},{7,9},{23,25},{38,40},{54,56},{39,41},{55,57},{70,72... | collective-permute-start | bytes 147464 | tf_op jit(solution)/shard_map/ppermute | solution.py:373
  110.7 2.6 %collective-permute-start.23 = (bf16[64,384]{1,0:T(8,128)(2,1)S(1)}, bf16[64,384]{1,0:T(8,128)(2,1)S(1)}, u32[]{:S(2)}, u32[]{:S(2)}) collective-permute-start(bf16[64,384]{1,0:T(8,128)(2,1)S(1)} %get-tuple-element.62), channel_id=1, source_target_pairs={{6,24},{22,8},{7,25},{23,9},{38,56},{54,40},{39,57},{55,41},{70,88... | collective-permute-start | bytes 147464 | tf_op jit(solution)/shard_map/ppermute | solution.py:374
  113.8 10.0 %collective-permute-start.27 = (bf16[64,384]{1,0:T(8,128)(2,1)S(1)}, bf16[64,384]{1,0:T(8,128)(2,1)S(1)}, u32[]{:S(2)}, u32[]{:S(2)}) collective-permute-start(bf16[64,384]{1,0:T(8,128)(2,1)S(1)} %get-tuple-element.64), channel_id=1, source_target_pairs={{0,130},{16,146},{1,131},{17,147},{32,162},{48,178},{33,163},{49,1... | collective-permute-start | bytes 147464 | tf_op jit(solution)/shard_map/ppermute | solution.py:372
  121.2 4.8 %collective-permute-start.25 = (bf16[64,384]{1,0:T(8,128)(2,1)S(1)}, bf16[64,384]{1,0:T(8,128)(2,1)S(1)}, u32[]{:S(2)}, u32[]{:S(2)}) collective-permute-start(bf16[64,384]{1,0:T(8,128)(2,1)S(1)} %get-tuple-element.64), channel_id=1, source_target_pairs={{0,2},{16,18},{1,3},{17,19},{32,34},{48,50},{33,35},{49,51},{64,66... | collective-permute-start | bytes 147464 | tf_op jit(solution)/shard_map/ppermute | solution.py:373
  122.5 3.5 %collective-permute-start.26 = (bf16[64,384]{1,0:T(8,128)(2,1)S(1)}, bf16[64,384]{1,0:T(8,128)(2,1)S(1)}, u32[]{:S(2)}, u32[]{:S(2)}) collective-permute-start(bf16[64,384]{1,0:T(8,128)(2,1)S(1)} %get-tuple-element.64), channel_id=1, source_target_pairs={{0,18},{16,2},{1,19},{17,3},{32,50},{48,34},{33,51},{49,35},{64,82... | collective-permute-start | bytes 147464 | tf_op jit(solution)/shard_map/ppermute | solution.py:374
  127.2 3.2 %collective-permute-start.28 = (bf16[64,384]{1,0:T(8,128)(2,1)S(1)}, bf16[64,384]{1,0:T(8,128)(2,1)S(1)}, u32[]{:S(2)}, u32[]{:S(2)}) collective-permute-start(bf16[64,384]{1,0:T(8,128)(2,1)S(1)} %get-tuple-element.66), channel_id=1, source_target_pairs={{2,4},{18,20},{3,5},{19,21},{34,36},{50,52},{35,37},{51,53},{66,68... | collective-permute-start | bytes 147464 | tf_op jit(solution)/shard_map/ppermute | solution.py:373
  127.9 2.6 %collective-permute-start.29 = (bf16[64,384]{1,0:T(8,128)(2,1)S(1)}, bf16[64,384]{1,0:T(8,128)(2,1)S(1)}, u32[]{:S(2)}, u32[]{:S(2)}) collective-permute-start(bf16[64,384]{1,0:T(8,128)(2,1)S(1)} %get-tuple-element.66), channel_id=1, source_target_pairs={{2,20},{18,4},{3,21},{19,5},{34,52},{50,36},{35,53},{51,37},{66,84... | collective-permute-start | bytes 147464 | tf_op jit(solution)/shard_map/ppermute | solution.py:374
  131.7 3.2 %collective-permute-start.31 = (bf16[64,384]{1,0:T(8,128)(2,1)S(1)}, bf16[64,384]{1,0:T(8,128)(2,1)S(1)}, u32[]{:S(2)}, u32[]{:S(2)}) collective-permute-start(bf16[64,384]{1,0:T(8,128)(2,1)S(1)} %get-tuple-element.68), channel_id=1, source_target_pairs={{4,6},{20,22},{5,7},{21,23},{36,38},{52,54},{37,39},{53,55},{68,70... | collective-permute-start | bytes 147464 | tf_op jit(solution)/shard_map/ppermute | solution.py:373
  132.4 2.6 %collective-permute-start.32 = (bf16[64,384]{1,0:T(8,128)(2,1)S(1)}, bf16[64,384]{1,0:T(8,128)(2,1)S(1)}, u32[]{:S(2)}, u32[]{:S(2)}) collective-permute-start(bf16[64,384]{1,0:T(8,128)(2,1)S(1)} %get-tuple-element.68), channel_id=1, source_target_pairs={{4,22},{20,6},{5,23},{21,7},{36,54},{52,38},{37,55},{53,39},{68,86... | collective-permute-start | bytes 147464 | tf_op jit(solution)/shard_map/ppermute | solution.py:374
  144.0 30.1 %all-to-all-start.1 = ((bf16[16,2,768]{2,1,0:T(2,128)(2,1)}), bf16[16,2,768]{2,1,0:T(2,128)(2,1)S(1)}, u32[]{:S(2)}, u32[]{:S(2)}) async-start(bf16[16,2,768]{2,1,0:T(2,128)(2,1)} %bitcast.24), calls=%async_computation.1 | async-start | bytes 98304 | tf_op jit(solution)/shard_map/all_to_all | solution.py:381
  (13 other events, 154.5 us)

commit v8 on v7

--- a/solution.py
+++ b/solution.py
@@ -290,6 +290,25 @@
     )(where, *blocks, *held)
 
 
+def renew_kernel(weight_ref, out_ref, sem):
+    copy = pltpu.make_async_copy(weight_ref, out_ref, sem)
+    copy.start()
+    copy.wait()
+
+
+def renew(weight):
+    vmem = pl.BlockSpec(memory_space=pltpu.VMEM)
+    return pl.pallas_call(
+        renew_kernel,
+        out_shape=jax.ShapeDtypeStruct(weight.shape, weight.dtype),
+        in_specs=[vmem],
+        out_specs=vmem,
+        scratch_shapes=[pltpu.SemaphoreType.DMA],
+        compiler_params=pltpu.CompilerParams(vmem_limit_bytes=8 * 1024 * 1024),
+        name="renew_weight",
+    )(pltpu.with_memory_space_constraint(weight, pltpu.VMEM))
+
+
 def whole_call(kernel, where, arrays, outs, sems=()):
     vmem = pl.BlockSpec(memory_space=pltpu.VMEM)
     held = pl.BlockSpec(memory_space=pl.ANY) if sems else vmem
@@ -368,6 +387,9 @@
         if tick == 0:
             moved, state = lax.optimization_barrier((early[1] + late[1], state))
             weight = place(early[0] + late[0], "rest", where, moved, [weight])
+        if tick == SECTIONS - 2:
+            state, weight = lax.optimization_barrier((state, weight))
+            weight = renew(weight)
         if tick + 1 < SECTIONS:
             far = lax.ppermute(state, AXES, onward(tick, 1, 0))
             near = lax.ppermute(state, AXES, onward(tick, 0, 0))

time: 176 us -> 175 us (level)
  starting transfers between devices: 98.1 us -> 96.3 us
where the time goes in v8:
time: 175 us; the launch traced here: 173 us
  starting transfers between devices  96.3 us (55%)
  blocking collectives  35.4 us (20%)
  Pallas kernels  14.5 us (8%)
  waiting for transfers between devices  14.4 us (8%)
  local copies, waits for them, and re-layouts  9.49 us (5%)
  between operations  2.07 us (1%)
    all_to_all x1, starting transfers between devices, body(): lax.all_to_all(finals, ('section', 'cfg'), split_axis=0, concat_axis=0, t...  20.7 us
    all_gather x7, blocking collectives, body(): far = lax.all_gather(far, 'core', axis=0, tiled=False)  17.6 us
    ppermute x7, starting transfers between devices, body(): far = lax.ppermute(state, AXES, onward(tick, 1, 0))  13.8 us
    all_to_all x1, starting transfers between devices, body(): lax.all_to_all(outgoing, ('xl', 'yh', 'core'), split_axis=0, concat_axis=...  10.2 us
    ppermute x2, waiting for transfers between devices, body(): up1, down1 = (lax.ppermute(own, AXES, UP), lax.ppermute(own, AXES, DOWN))  9.06 us
    ppermute x7, starting transfers between devices, body(): cross = lax.ppermute(state, AXES, onward(tick, 0, 1))  7.39 us
    ppermute x2, starting transfers between devices, body(): up3, down3 = (lax.ppermute(up2, AXES, UP), lax.ppermute(down2, AXES, DOWN))  6.7 us
    all_gather x1, blocking collectives, body(): kept = lax.all_gather(fresh, ('xl', 'core'), axis=0, tiled=False)  6.58 us
  transfers between devices with their start and end apart: 36, of which 5 were waited for; matrix products, arithmetic and copies ran while one was open for 2% of the time, Pallas kernels for 4%

profile of v8, /device:TPU:1, one launch (start us, length us, event | category | flops | bytes accessed | tf_op | source)
XLA Modules:
  0.0 173.3 jit_solution(13236869431758236038)
XLA Ops:
  3.2 10.2 %all-to-all-start = ((bf16[16,16,768]{2,1,0:T(8,128)(2,1)}), bf16[16,16,768]{2,1,0:T(8,128)(2,1)S(1)}, u32[]{:S(2)}, u32[]{:S(2)}) async-start(bf16[16,16,768]{2,1,0:T(8,128)(2,1)} %stale_kernel.1), calls=%async_computation | async-start | bytes 786432 | tf_op jit(solution)/shard_map/all_to_all | solution.py:346
  15.0 3.7 %collective-permute-start = (bf16[144,768]{1,0:T(8,128)(2,1)S(1)}, bf16[144,768]{1,0:T(8,128)(2,1)S(1)}, u32[]{:S(2)}, u32[]{:S(2)}) collective-permute-start(bf16[144,768]{1,0:T(8,128)(2,1)S(1)} %get-tuple-element.40), channel_id=1, source_target_pairs={{0,0},{2,2},{4,4},{6,6},{8,8},{10,10},{12,12},{14,14},{16,256},{18... | collective-permute-start | bytes 663560 | tf_op jit(solution)/shard_map/ppermute | solution.py:341
  18.7 1.9 %collective-permute-start.1 = (bf16[144,768]{1,0:T(8,128)(2,1)S(1)}, bf16[144,768]{1,0:T(8,128)(2,1)S(1)}, u32[]{:S(2)}, u32[]{:S(2)}) collective-permute-start(bf16[144,768]{1,0:T(8,128)(2,1)S(1)} %get-tuple-element.40), channel_id=1, source_target_pairs={{0,256},{2,258},{4,260},{6,262},{8,264},{10,266},{12,268},{14,270}... | collective-permute-start | bytes 663560 | tf_op jit(solution)/shard_map/ppermute | solution.py:341
  23.8 3.1 %collective-permute-done.1.second_ref = bf16[144,768]{1,0:T(8,128)(2,1)S(1)} collective-permute-done((bf16[144,768]{1,0:T(8,128)(2,1)S(1)}, bf16[144,768]{1,0:T(8,128)(2,1)S(1)}, u32[]{:S(2)}, u32[]{:S(2)}) %collective-permute-start.1) | collective-permute-done | bytes 221216 | tf_op jit(solution)/shard_map/ppermute | solution.py:341
  27.5 3.7 %collective-permute-start.4 = (bf16[288,768]{1,0:T(8,128)(2,1)S(1)}, bf16[288,768]{1,0:T(8,128)(2,1)S(1)}, u32[]{:S(2)}, u32[]{:S(2)}) collective-permute-start(bf16[288,768]{1,0:T(8,128)(2,1)S(1)} %join_kernel.1.refs_0_), channel_id=1, source_target_pairs={{0,1},{2,3},{4,5},{6,7},{8,9},{10,11},{12,13},{14,15},{16,113},{18... | collective-permute-start | bytes 1327112 | tf_op jit(solution)/shard_map/ppermute | solution.py:349
  31.2 1.9 %collective-permute-start.5 = (bf16[288,768]{1,0:T(8,128)(2,1)S(1)}, bf16[288,768]{1,0:T(8,128)(2,1)S(1)}, u32[]{:S(2)}, u32[]{:S(2)}) collective-permute-start(bf16[288,768]{1,0:T(8,128)(2,1)S(1)} %join_kernel.1.refs_0_), channel_id=1, source_target_pairs={{0,97},{2,99},{4,101},{6,103},{8,105},{10,107},{12,109},{14,111},{... | collective-permute-start | bytes 1327112 | tf_op jit(solution)/shard_map/ppermute | solution.py:349
  34.6 9.1 %collective-permute-done.5.refs_2_ = bf16[288,768]{1,0:T(8,128)(2,1)S(1)} collective-permute-done((bf16[288,768]{1,0:T(8,128)(2,1)S(1)}, bf16[288,768]{1,0:T(8,128)(2,1)S(1)}, u32[]{:S(2)}, u32[]{:S(2)}) %collective-permute-start.5) | collective-permute-done | bytes 442400 | tf_op jit(solution)/shard_map/ppermute | solution.py:349
  43.7 1.9 %collective-permute-start.7 = (bf16[288,768]{1,0:T(8,128)(2,1)S(1)}, bf16[288,768]{1,0:T(8,128)(2,1)}, u32[]{:S(2)}, u32[]{:S(2)}) collective-permute-start(bf16[288,768]{1,0:T(8,128)(2,1)S(1)} %collective-permute-done.5.refs_2_), channel_id=1, source_target_pairs={{0,97},{2,99},{4,101},{6,103},{8,105},{10,107},{12,109},{14,111},{... | collective-permute-start | bytes 1327112 | tf_op jit(solution)/shard_map/ppermute | solution.py:353
  45.6 4.6 %collective-permute-start.6 = (bf16[288,768]{1,0:T(8,128)(2,1)S(1)}, bf16[288,768]{1,0:T(8,128)(2,1)}, u32[]{:S(2)}, u32[]{:S(2)}) collective-permute-start(bf16[288,768]{1,0:T(8,128)(2,1)S(1)} %collective-permute-done.4.refs_1_), channel_id=1, source_target_pairs={{0,1},{2,3},{4,5},{6,7},{8,9},{10,11},{12,13},{14,15},{16,113},{18... | collective-permute-start | bytes 1327112 | tf_op jit(solution)/shard_map/ppermute | solution.py:353
  50.5 5.5 %all_gather.57 = bf16[64,1536]{1,0:T(8,128)(2,1)} all-gather(bf16[16,1536]{1,0:T(8,128)(2,1)S(1)} %bitcast.72), channel_id=1, replica_groups=mesh['xh'=2,'xl'=2,'yh'=4,'core'=2,'section'=8,'cfg'=2] {'xl','core'}, dimensions={0}, use_global_device_ids=true | all-gather | bytes 245760 | tf_op jit(solution)/shard_map/all_gather | solution.py:352
  56.0 3.5 %collective-permute-start.9 = (bf16[288,768]{1,0:T(8,128)(2,1)}, bf16[288,768]{1,0:T(8,128)(2,1)S(1)}, u32[]{:S(2)}, u32[]{:S(2)}) collective-permute-start(bf16[288,768]{1,0:T(8,128)(2,1)} %collective-permute-done.7.refs_4_), channel_id=1, source_target_pairs={{0,97},{2,99},{4,101},{6,103},{8,105},{10,107},{12,109},{14,111},{... | collective-permute-start | bytes 1327112 | tf_op jit(solution)/shard_map/ppermute | solution.py:355
  59.6 3.2 %collective-permute-start.8 = (bf16[288,768]{1,0:T(8,128)(2,1)}, bf16[288,768]{1,0:T(8,128)(2,1)S(1)}, u32[]{:S(2)}, u32[]{:S(2)}) collective-permute-start(bf16[288,768]{1,0:T(8,128)(2,1)} %collective-permute-done.6.refs_3_), channel_id=1, source_target_pairs={{0,1},{2,3},{4,5},{6,7},{8,9},{10,11},{12,13},{14,15},{16,113},{18... | collective-permute-start | bytes 1327112 | tf_op jit(solution)/shard_map/ppermute | solution.py:355
  62.9 5.1 %collective-permute-start.12 = (bf16[256,768]{1,0:T(8,128)(2,1)S(1)}, bf16[256,768]{1,0:T(8,128)(2,1)S(1)}, u32[]{:S(2)}, u32[]{:S(2)}) collective-permute-start(bf16[256,768]{1,0:T(8,128)(2,1)S(1)} %bitcast.47), channel_id=1, source_target_pairs={{0,256},{1,257},{2,258},{3,259},{4,260},{5,261},{6,262},{7,263},{8... | collective-permute-start | bytes 1179656 | tf_op jit(solution)/shard_map/ppermute | solution.py:351
  69.4 2.6 %collective-permute-start.11 = (bf16[144,768]{1,0:T(8,128)(2,1)S(1)}, bf16[144,768]{1,0:T(8,128)(2,1)S(1)}, u32[]{:S(2)}, u32[]{:S(2)}) collective-permute-start(bf16[144,768]{1,0:T(8,128)(2,1)S(1)} %slice.24), channel_id=1, source_target_pairs={{0,97},{2,99},{4,101},{6,103},{8,105},{10,107},{12,109},{14,111},{... | collective-permute-start | bytes 663560 | tf_op jit(solution)/shard_map/ppermute | solution.py:357
  72.1 4.9 %collective-permute-start.10 = (bf16[144,768]{1,0:T(8,128)(2,1)S(1)}, bf16[144,768]{1,0:T(8,128)(2,1)S(1)}, u32[]{:S(2)}, u32[]{:S(2)}) collective-permute-start(bf16[144,768]{1,0:T(8,128)(2,1)S(1)} %slice.23), channel_id=1, source_target_pairs={{0,1},{2,3},{4,5},{6,7},{8,9},{10,11},{12,13},{14,15},{16,113},{18... | collective-permute-start | bytes 663560 | tf_op jit(solution)/shard_map/ppermute | solution.py:356
  78.0 2.7 %place_first.1.refs_4_ = bf16[1152,1536]{1,0:T(8,128)(2,1)S(1)} custom-call(s32[5]{0:T(128)S(1)} %stack.32.where, bf16[288,768]{1,0:T(8,128)(2,1)S(1)} %join_kernel.1.refs_0_, bf16[288,768]{1,0:T(8,128)(2,1)S(1)} %collective-permute-done.4.refs_1_, bf16[288,768]{1,0:T(8,128)(2,1)S(1)} %copy-done.4, bf16[288,768]{1,0:T(8,128)(2,1)} %collective-permute-done.6.refs_3_, ...), custom_call_target="tpu_custom_call" | custom-call | tf_op jit(solution)/shard_map/place_first/pallas_call | solution.py:281
  81.7 2.3 %place_last.1 = (bf16[1152,1536]{1,0:T(8,128)(2,1)S(1)}, bf16[1536,1152]{1,0:T(8,128)(2,1)S(1)}) custom-call(s32[5]{0:T(128)S(1)} %stack.32.where, bf16[288,768]{1,0:T(8,128)(2,1)S(1)} %collective-permute-done.8.refs_0_.refs_5_, bf16[288,768]{1,0:T(8,128)(2,1)S(1)} %collective-permute-done.9.refs_1_.refs_6_, ...), custom_call_target="tpu_custom_call", output_to_operand_aliasing={{0}: (5, {})} | custom-call | tf_op jit(solution)/shard_map/place_last/pallas_call | solution.py:281
  84.1 1.9 %block_step.8 = (bf16[64,384]{1,0:T(8,128)(2,1)S(1)}, bf16[64,768]{1,0:T(8,128)(2,1)S(1)}) custom-call(s32[2]{0:T(128)S(1)} %pad_add_fusion.who, bf16[64,384]{1,0:T(8,128)(2,1)S(1)} %get-tuple-element.84.near_ref, bf16[64,384]{1,0:T(8,128)(2,1)S(1)} %get-tuple-element.83.cross_ref, bf16[2,64,384]{2,1,0:T(8,128)(2,1)S(1)} %bitcast.57, ...), custom_call_target="tpu_custom_call" | custom-call | tf_op jit(solution)/shard_map/block_step/pallas_call | solution.py:178
  86.0 3.1 %collective-permute-start.15 = (bf16[64,384]{1,0:T(8,128)(2,1)S(1)}, bf16[64,384]{1,0:T(8,128)(2,1)S(1)}, u32[]{:S(2)}, u32[]{:S(2)}) collective-permute-start(bf16[64,384]{1,0:T(8,128)(2,1)S(1)} %get-tuple-element.49), channel_id=1, source_target_pairs={{0,130},{16,146},{1,131},{17,147},{32,162},{48,178},{33,163},{49,1... | collective-permute-start | bytes 147464 | tf_op jit(solution)/shard_map/ppermute | solution.py:394
  90.4 2.6 %collective-permute-start.14 = (bf16[64,384]{1,0:T(8,128)(2,1)S(1)}, bf16[64,384]{1,0:T(8,128)(2,1)S(1)}, u32[]{:S(2)}, u32[]{:S(2)}) collective-permute-start(bf16[64,384]{1,0:T(8,128)(2,1)S(1)} %get-tuple-element.49), channel_id=1, source_target_pairs={{0,18},{16,2},{1,19},{17,3},{32,50},{48,34},{33,51},{49,35},{64,82... | collective-permute-start | bytes 147464 | tf_op jit(solution)/shard_map/ppermute | solution.py:396
  93.6 6.0 %all-gather = bf16[128,384]{1,0:T(8,128)(2,1)S(1)} all-gather(bf16[64,384]{1,0:T(8,128)(2,1)S(1)} %collective-permute-done.15), channel_id=2, replica_groups=mesh['xh'=2,'xl'=2,'yh'=4,'core'=2,'section'=8,'cfg'=2] {'core'}, dimensions={0}, use_global_device_ids=true | all-gather | bytes 147456 | tf_op jit(solution)/shard_map/all_gather | solution.py:397
  102.2 1.9 %all-gather.1 = bf16[128,384]{1,0:T(8,128)(2,1)S(1)} all-gather(bf16[64,384]{1,0:T(8,128)(2,1)S(1)} %collective-permute-done.18), channel_id=3, replica_groups=mesh['xh'=2,'xl'=2,'yh'=4,'core'=2,'section'=8,'cfg'=2] {'core'}, dimensions={0}, use_global_device_ids=true | all-gather | bytes 147456 | tf_op jit(solution)/shard_map/all_gather | solution.py:397
  106.9 1.9 %all-gather.2 = bf16[128,384]{1,0:T(8,128)(2,1)S(1)} all-gather(bf16[64,384]{1,0:T(8,128)(2,1)S(1)} %collective-permute-done.21), channel_id=4, replica_groups=mesh['xh'=2,'xl'=2,'yh'=4,'core'=2,'section'=8,'cfg'=2] {'core'}, dimensions={0}, use_global_device_ids=true | all-gather | bytes 147456 | tf_op jit(solution)/shard_map/all_gather | solution.py:397
  111.4 1.9 %all-gather.3 = bf16[128,384]{1,0:T(8,128)(2,1)S(1)} all-gather(bf16[64,384]{1,0:T(8,128)(2,1)S(1)} %collective-permute-done.24), channel_id=5, replica_groups=mesh['xh'=2,'xl'=2,'yh'=4,'core'=2,'section'=8,'cfg'=2] {'core'}, dimensions={0}, use_global_device_ids=true | all-gather | bytes 147456 | tf_op jit(solution)/shard_map/all_gather | solution.py:397
  113.8 7.4 %collective-permute-start.27 = (bf16[64,384]{1,0:T(8,128)(2,1)S(1)}, bf16[64,384]{1,0:T(8,128)(2,1)S(1)}, u32[]{:S(2)}, u32[]{:S(2)}) collective-permute-start(bf16[64,384]{1,0:T(8,128)(2,1)S(1)} %get-tuple-element.66), channel_id=1, source_target_pairs={{0,130},{16,146},{1,131},{17,147},{32,162},{48,178},{33,163},{49,1... | collective-permute-start | bytes 147464 | tf_op jit(solution)/shard_map/ppermute | solution.py:394
  123.8 2.2 %all-gather.4 = bf16[128,384]{1,0:T(8,128)(2,1)S(1)} all-gather(bf16[64,384]{1,0:T(8,128)(2,1)S(1)} %collective-permute-done.27), channel_id=6, replica_groups=mesh['xh'=2,'xl'=2,'yh'=4,'core'=2,'section'=8,'cfg'=2] {'core'}, dimensions={0}, use_global_device_ids=true | all-gather | bytes 147456 | tf_op jit(solution)/shard_map/all_gather | solution.py:397
  128.6 1.9 %all-gather.5 = bf16[128,384]{1,0:T(8,128)(2,1)S(1)} all-gather(bf16[64,384]{1,0:T(8,128)(2,1)S(1)} %collective-permute-done.30), channel_id=7, replica_groups=mesh['xh'=2,'xl'=2,'yh'=4,'core'=2,'section'=8,'cfg'=2] {'core'}, dimensions={0}, use_global_device_ids=true | all-gather | bytes 147456 | tf_op jit(solution)/shard_map/all_gather | solution.py:397
  133.0 2.0 %copy-done.2 = bf16[1536,1152]{1,0:T(8,128)(2,1)S(1)} copy-done((bf16[1536,1152]{1,0:T(8,128)(2,1)S(1)}, bf16[1536,1152]{1,0:T(8,128)(2,1)}, u32[]{:S(2)}) %copy-start.2) | copy-done | bytes 3538968
  135.4 1.9 %all-gather.6 = bf16[128,384]{1,0:T(8,128)(2,1)S(1)} all-gather(bf16[64,384]{1,0:T(8,128)(2,1)S(1)} %collective-permute-done.33), channel_id=8, replica_groups=mesh['xh'=2,'xl'=2,'yh'=4,'core'=2,'section'=8,'cfg'=2] {'core'}, dimensions={0}, use_global_device_ids=true | all-gather | bytes 147456 | tf_op jit(solution)/shard_map/all_gather | solution.py:397
  137.9 5.8 %all-gather.7 = bf16[256,384]{1,0:T(8,128)(2,1)S(1)} all-gather(bf16[64,384]{1,0:T(8,128)(2,1)S(1)} %get-tuple-element.74), channel_id=9, replica_groups=mesh['xh'=2,'xl'=2,'yh'=4,'core'=2,'section'=8,'cfg'=2] {'xl','core'}, dimensions={0}, use_global_device_ids=true | all-gather | bytes 245760 | tf_op jit(solution)/shard_map/all_gather | solution.py:399
  144.4 20.7 %all-to-all-start.1 = ((bf16[16,2,768]{2,1,0:T(2,128)(2,1)}), bf16[16,2,768]{2,1,0:T(2,128)(2,1)S(1)}, u32[]{:S(2)}, u32[]{:S(2)}) async-start(bf16[16,2,768]{2,1,0:T(2,128)(2,1)} %bitcast.24), calls=%async_computation.1 | async-start | bytes 98304 | tf_op jit(solution)/shard_map/all_to_all | solution.py:403
  165.2 6.6 %all-gather.8 = bf16[256,768]{1,0:T(8,128)(2,1)S(1)} all-gather(bf16[64,768]{1,0:T(8,128)(2,1)S(1)} %get-tuple-element.75), channel_id=10, replica_groups=mesh['xh'=2,'xl'=2,'yh'=4,'core'=2,'section'=8,'cfg'=2] {'xl','core'}, dimensions={0}, use_global_device_ids=true | all-gather | bytes 491520 | tf_op jit(solution)/shard_map/all_gather | solution.py:404
  (113 shorter events, 33.8 us)
Async XLA Ops:
  3.2 42.4 %all-to-all-start = ((bf16[16,16,768]{2,1,0:T(8,128)(2,1)}), bf16[16,16,768]{2,1,0:T(8,128)(2,1)S(1)}, u32[]{:S(2)}, u32[]{:S(2)}) async-start(bf16[16,16,768]{2,1,0:T(8,128)(2,1)} %stale_kernel.1), calls=%async_computation | async-start | bytes 786432 | tf_op jit(solution)/shard_map/all_to_all | solution.py:346
  15.0 8.8 %collective-permute-start = (bf16[144,768]{1,0:T(8,128)(2,1)S(1)}, bf16[144,768]{1,0:T(8,128)(2,1)S(1)}, u32[]{:S(2)}, u32[]{:S(2)}) collective-permute-start(bf16[144,768]{1,0:T(8,128)(2,1)S(1)} %get-tuple-element.40), channel_id=1, source_target_pairs={{0,0},{2,2},{4,4},{6,6},{8,8},{10,10},{12,12},{14,14},{16,256},{18... | collective-permute-start | bytes 663560 | tf_op jit(solution)/shard_map/ppermute | solution.py:341
  18.7 8.2 %collective-permute-start.1 = (bf16[144,768]{1,0:T(8,128)(2,1)S(1)}, bf16[144,768]{1,0:T(8,128)(2,1)S(1)}, u32[]{:S(2)}, u32[]{:S(2)}) collective-permute-start(bf16[144,768]{1,0:T(8,128)(2,1)S(1)} %get-tuple-element.40), channel_id=1, source_target_pairs={{0,256},{2,258},{4,260},{6,262},{8,264},{10,266},{12,268},{14,270}... | collective-permute-start | bytes 663560 | tf_op jit(solution)/shard_map/ppermute | solution.py:341
  20.6 2.1 %collective-permute-start.2 = (bf16[48,768]{1,0:T(8,128)(2,1)S(1)}, bf16[48,768]{1,0:T(8,128)(2,1)S(1)}, u32[]{:S(2)}, u32[]{:S(2)}) collective-permute-start(bf16[48,768]{1,0:T(8,128)(2,1)S(1)} %get-tuple-element.41), channel_id=1, source_target_pairs={{32,48},{34,50},{36,52},{38,54},{40,56},{42,58},{44,60},{46,62},{3... | collective-permute-start | bytes 221192 | tf_op jit(solution)/shard_map/ppermute | solution.py:342
  27.5 18.1 %collective-permute-start.4 = (bf16[288,768]{1,0:T(8,128)(2,1)S(1)}, bf16[288,768]{1,0:T(8,128)(2,1)S(1)}, u32[]{:S(2)}, u32[]{:S(2)}) collective-permute-start(bf16[288,768]{1,0:T(8,128)(2,1)S(1)} %join_kernel.1.refs_0_), channel_id=1, source_target_pairs={{0,1},{2,3},{4,5},{6,7},{8,9},{10,11},{12,13},{14,15},{16,113},{18... | collective-permute-start | bytes 1327112 | tf_op jit(solution)/shard_map/ppermute | solution.py:349
  31.2 12.5 %collective-permute-start.5 = (bf16[288,768]{1,0:T(8,128)(2,1)S(1)}, bf16[288,768]{1,0:T(8,128)(2,1)S(1)}, u32[]{:S(2)}, u32[]{:S(2)}) collective-permute-start(bf16[288,768]{1,0:T(8,128)(2,1)S(1)} %join_kernel.1.refs_0_), channel_id=1, source_target_pairs={{0,97},{2,99},{4,101},{6,103},{8,105},{10,107},{12,109},{14,111},{... | collective-permute-start | bytes 1327112 | tf_op jit(solution)/shard_map/ppermute | solution.py:349
  43.7 12.3 %collective-permute-start.7 = (bf16[288,768]{1,0:T(8,128)(2,1)S(1)}, bf16[288,768]{1,0:T(8,128)(2,1)}, u32[]{:S(2)}, u32[]{:S(2)}) collective-permute-start(bf16[288,768]{1,0:T(8,128)(2,1)S(1)} %collective-permute-done.5.refs_2_), channel_id=1, source_target_pairs={{0,97},{2,99},{4,101},{6,103},{8,105},{10,107},{12,109},{14,111},{... | collective-permute-start | bytes 1327112 | tf_op jit(solution)/shard_map/ppermute | solution.py:353
  45.6 13.9 %collective-permute-start.6 = (bf16[288,768]{1,0:T(8,128)(2,1)S(1)}, bf16[288,768]{1,0:T(8,128)(2,1)}, u32[]{:S(2)}, u32[]{:S(2)}) collective-permute-start(bf16[288,768]{1,0:T(8,128)(2,1)S(1)} %collective-permute-done.4.refs_1_), channel_id=1, source_target_pairs={{0,1},{2,3},{4,5},{6,7},{8,9},{10,11},{12,13},{14,15},{16,113},{18... | collective-permute-start | bytes 1327112 | tf_op jit(solution)/shard_map/ppermute | solution.py:353
  56.0 13.4 %collective-permute-start.9 = (bf16[288,768]{1,0:T(8,128)(2,1)}, bf16[288,768]{1,0:T(8,128)(2,1)S(1)}, u32[]{:S(2)}, u32[]{:S(2)}) collective-permute-start(bf16[288,768]{1,0:T(8,128)(2,1)} %collective-permute-done.7.refs_4_), channel_id=1, source_target_pairs={{0,97},{2,99},{4,101},{6,103},{8,105},{10,107},{12,109},{14,111},{... | collective-permute-start | bytes 1327112 | tf_op jit(solution)/shard_map/ppermute | solution.py:355
  59.6 12.5 %collective-permute-start.8 = (bf16[288,768]{1,0:T(8,128)(2,1)}, bf16[288,768]{1,0:T(8,128)(2,1)S(1)}, u32[]{:S(2)}, u32[]{:S(2)}) collective-permute-start(bf16[288,768]{1,0:T(8,128)(2,1)} %collective-permute-done.6.refs_3_), channel_id=1, source_target_pairs={{0,1},{2,3},{4,5},{6,7},{8,9},{10,11},{12,13},{14,15},{16,113},{18... | collective-permute-start | bytes 1327112 | tf_op jit(solution)/shard_map/ppermute | solution.py:355
  62.9 21.1 %collective-permute-start.12 = (bf16[256,768]{1,0:T(8,128)(2,1)S(1)}, bf16[256,768]{1,0:T(8,128)(2,1)S(1)}, u32[]{:S(2)}, u32[]{:S(2)}) collective-permute-start(bf16[256,768]{1,0:T(8,128)(2,1)S(1)} %bitcast.47), channel_id=1, source_target_pairs={{0,256},{1,257},{2,258},{3,259},{4,260},{5,261},{6,262},{7,263},{8... | collective-permute-start | bytes 1179656 | tf_op jit(solution)/shard_map/ppermute | solution.py:351
  69.4 11.3 %collective-permute-start.11 = (bf16[144,768]{1,0:T(8,128)(2,1)S(1)}, bf16[144,768]{1,0:T(8,128)(2,1)S(1)}, u32[]{:S(2)}, u32[]{:S(2)}) collective-permute-start(bf16[144,768]{1,0:T(8,128)(2,1)S(1)} %slice.24), channel_id=1, source_target_pairs={{0,97},{2,99},{4,101},{6,103},{8,105},{10,107},{12,109},{14,111},{... | collective-permute-start | bytes 663560 | tf_op jit(solution)/shard_map/ppermute | solution.py:357
  72.1 9.6 %collective-permute-start.10 = (bf16[144,768]{1,0:T(8,128)(2,1)S(1)}, bf16[144,768]{1,0:T(8,128)(2,1)S(1)}, u32[]{:S(2)}, u32[]{:S(2)}) collective-permute-start(bf16[144,768]{1,0:T(8,128)(2,1)S(1)} %slice.23), channel_id=1, source_target_pairs={{0,1},{2,3},{4,5},{6,7},{8,9},{10,11},{12,13},{14,15},{16,113},{18... | collective-permute-start | bytes 663560 | tf_op jit(solution)/shard_map/ppermute | solution.py:356
  86.0 7.6 %collective-permute-start.15 = (bf16[64,384]{1,0:T(8,128)(2,1)S(1)}, bf16[64,384]{1,0:T(8,128)(2,1)S(1)}, u32[]{:S(2)}, u32[]{:S(2)}) collective-permute-start(bf16[64,384]{1,0:T(8,128)(2,1)S(1)} %get-tuple-element.49), channel_id=1, source_target_pairs={{0,130},{16,146},{1,131},{17,147},{32,162},{48,178},{33,163},{49,1... | collective-permute-start | bytes 147464 | tf_op jit(solution)/shard_map/ppermute | solution.py:394
  89.1 10.6 %collective-permute-start.13 = (bf16[64,384]{1,0:T(8,128)(2,1)S(1)}, bf16[64,384]{1,0:T(8,128)(2,1)S(1)}, u32[]{:S(2)}, u32[]{:S(2)}) collective-permute-start(bf16[64,384]{1,0:T(8,128)(2,1)S(1)} %get-tuple-element.49), channel_id=1, source_target_pairs={{0,2},{16,18},{1,3},{17,19},{32,34},{48,50},{33,35},{49,51},{64,66... | collective-permute-start | bytes 147464 | tf_op jit(solution)/shard_map/ppermute | solution.py:395
  90.4 9.3 %collective-permute-start.14 = (bf16[64,384]{1,0:T(8,128)(2,1)S(1)}, bf16[64,384]{1,0:T(8,128)(2,1)S(1)}, u32[]{:S(2)}, u32[]{:S(2)}) collective-permute-start(bf16[64,384]{1,0:T(8,128)(2,1)S(1)} %get-tuple-element.49), channel_id=1, source_target_pairs={{0,18},{16,2},{1,19},{17,3},{32,50},{48,34},{33,51},{49,35},{64,82... | collective-permute-start | bytes 147464 | tf_op jit(solution)/shard_map/ppermute | solution.py:396
  100.9 3.2 %collective-permute-start.16 = (bf16[64,384]{1,0:T(8,128)(2,1)S(1)}, bf16[64,384]{1,0:T(8,128)(2,1)S(1)}, u32[]{:S(2)}, u32[]{:S(2)}) collective-permute-start(bf16[64,384]{1,0:T(8,128)(2,1)S(1)} %get-tuple-element.60), channel_id=1, source_target_pairs={{2,4},{18,20},{3,5},{19,21},{34,36},{50,52},{35,37},{51,53},{66,68... | collective-permute-start | bytes 147464 | tf_op jit(solution)/shard_map/ppermute | solution.py:395
  101.6 2.6 %collective-permute-start.17 = (bf16[64,384]{1,0:T(8,128)(2,1)S(1)}, bf16[64,384]{1,0:T(8,128)(2,1)S(1)}, u32[]{:S(2)}, u32[]{:S(2)}) collective-permute-start(bf16[64,384]{1,0:T(8,128)(2,1)S(1)} %get-tuple-element.60), channel_id=1, source_target_pairs={{2,20},{18,4},{3,21},{19,5},{34,52},{50,36},{35,53},{51,37},{66,84... | collective-permute-start | bytes 147464 | tf_op jit(solution)/shard_map/ppermute | solution.py:396
  104.7 2.2 %collective-permute-start.21 = (bf16[64,384]{1,0:T(8,128)(2,1)S(1)}, bf16[64,384]{1,0:T(8,128)(2,1)S(1)}, u32[]{:S(2)}, u32[]{:S(2)}) collective-permute-start(bf16[64,384]{1,0:T(8,128)(2,1)S(1)} %get-tuple-element.62), channel_id=1, source_target_pairs={{4,134},{20,150},{5,135},{21,151},{36,166},{52,182},{37,167},{53,1... | collective-permute-start | bytes 147464 | tf_op jit(solution)/shard_map/ppermute | solution.py:394
  105.4 3.4 %collective-permute-start.19 = (bf16[64,384]{1,0:T(8,128)(2,1)S(1)}, bf16[64,384]{1,0:T(8,128)(2,1)S(1)}, u32[]{:S(2)}, u32[]{:S(2)}) collective-permute-start(bf16[64,384]{1,0:T(8,128)(2,1)S(1)} %get-tuple-element.62), channel_id=1, source_target_pairs={{4,6},{20,22},{5,7},{21,23},{36,38},{52,54},{37,39},{53,55},{68,70... | collective-permute-start | bytes 147464 | tf_op jit(solution)/shard_map/ppermute | solution.py:395
  106.0 2.7 %collective-permute-start.20 = (bf16[64,384]{1,0:T(8,128)(2,1)S(1)}, bf16[64,384]{1,0:T(8,128)(2,1)S(1)}, u32[]{:S(2)}, u32[]{:S(2)}) collective-permute-start(bf16[64,384]{1,0:T(8,128)(2,1)S(1)} %get-tuple-element.62), channel_id=1, source_target_pairs={{4,22},{20,6},{5,23},{21,7},{36,54},{52,38},{37,55},{53,39},{68,86... | collective-permute-start | bytes 147464 | tf_op jit(solution)/shard_map/ppermute | solution.py:396
  110.0 3.2 %collective-permute-start.22 = (bf16[64,384]{1,0:T(8,128)(2,1)S(1)}, bf16[64,384]{1,0:T(8,128)(2,1)S(1)}, u32[]{:S(2)}, u32[]{:S(2)}) collective-permute-start(bf16[64,384]{1,0:T(8,128)(2,1)S(1)} %get-tuple-element.64), channel_id=1, source_target_pairs={{6,8},{22,24},{7,9},{23,25},{38,40},{54,56},{39,41},{55,57},{70,72... | collective-permute-start | bytes 147464 | tf_op jit(solution)/shard_map/ppermute | solution.py:395
  110.7 2.6 %collective-permute-start.23 = (bf16[64,384]{1,0:T(8,128)(2,1)S(1)}, bf16[64,384]{1,0:T(8,128)(2,1)S(1)}, u32[]{:S(2)}, u32[]{:S(2)}) collective-permute-start(bf16[64,384]{1,0:T(8,128)(2,1)S(1)} %get-tuple-element.64), channel_id=1, source_target_pairs={{6,24},{22,8},{7,25},{23,9},{38,56},{54,40},{39,57},{55,41},{70,88... | collective-permute-start | bytes 147464 | tf_op jit(solution)/shard_map/ppermute | solution.py:396
  113.8 10.0 %collective-permute-start.27 = (bf16[64,384]{1,0:T(8,128)(2,1)S(1)}, bf16[64,384]{1,0:T(8,128)(2,1)S(1)}, u32[]{:S(2)}, u32[]{:S(2)}) collective-permute-start(bf16[64,384]{1,0:T(8,128)(2,1)S(1)} %get-tuple-element.66), channel_id=1, source_target_pairs={{0,130},{16,146},{1,131},{17,147},{32,162},{48,178},{33,163},{49,1... | collective-permute-start | bytes 147464 | tf_op jit(solution)/shard_map/ppermute | solution.py:394
  121.2 4.8 %collective-permute-start.25 = (bf16[64,384]{1,0:T(8,128)(2,1)S(1)}, bf16[64,384]{1,0:T(8,128)(2,1)S(1)}, u32[]{:S(2)}, u32[]{:S(2)}) collective-permute-start(bf16[64,384]{1,0:T(8,128)(2,1)S(1)} %get-tuple-element.66), channel_id=1, source_target_pairs={{0,2},{16,18},{1,3},{17,19},{32,34},{48,50},{33,35},{49,51},{64,66... | collective-permute-start | bytes 147464 | tf_op jit(solution)/shard_map/ppermute | solution.py:395
  122.5 3.5 %collective-permute-start.26 = (bf16[64,384]{1,0:T(8,128)(2,1)S(1)}, bf16[64,384]{1,0:T(8,128)(2,1)S(1)}, u32[]{:S(2)}, u32[]{:S(2)}) collective-permute-start(bf16[64,384]{1,0:T(8,128)(2,1)S(1)} %get-tuple-element.66), channel_id=1, source_target_pairs={{0,18},{16,2},{1,19},{17,3},{32,50},{48,34},{33,51},{49,35},{64,82... | collective-permute-start | bytes 147464 | tf_op jit(solution)/shard_map/ppermute | solution.py:396
  127.2 3.2 %collective-permute-start.28 = (bf16[64,384]{1,0:T(8,128)(2,1)S(1)}, bf16[64,384]{1,0:T(8,128)(2,1)S(1)}, u32[]{:S(2)}, u32[]{:S(2)}) collective-permute-start(bf16[64,384]{1,0:T(8,128)(2,1)S(1)} %get-tuple-element.68), channel_id=1, source_target_pairs={{2,4},{18,20},{3,5},{19,21},{34,36},{50,52},{35,37},{51,53},{66,68... | collective-permute-start | bytes 147464 | tf_op jit(solution)/shard_map/ppermute | solution.py:395
  127.9 2.6 %collective-permute-start.29 = (bf16[64,384]{1,0:T(8,128)(2,1)S(1)}, bf16[64,384]{1,0:T(8,128)(2,1)S(1)}, u32[]{:S(2)}, u32[]{:S(2)}) collective-permute-start(bf16[64,384]{1,0:T(8,128)(2,1)S(1)} %get-tuple-element.68), channel_id=1, source_target_pairs={{2,20},{18,4},{3,21},{19,5},{34,52},{50,36},{35,53},{51,37},{66,84... | collective-permute-start | bytes 147464 | tf_op jit(solution)/shard_map/ppermute | solution.py:396
  131.0 4.4 %collective-permute-start.33 = (bf16[64,384]{1,0:T(8,128)(2,1)S(1)}, bf16[64,384]{1,0:T(8,128)(2,1)S(1)}, u32[]{:S(2)}, u32[]{:S(2)}) collective-permute-start(bf16[64,384]{1,0:T(8,128)(2,1)S(1)} %get-tuple-element.71), channel_id=1, source_target_pairs={{4,134},{20,150},{5,135},{21,151},{36,166},{52,182},{37,167},{53,1... | collective-permute-start | bytes 147464 | tf_op jit(solution)/shard_map/ppermute | solution.py:394
  131.7 5.7 %collective-permute-start.31 = (bf16[64,384]{1,0:T(8,128)(2,1)S(1)}, bf16[64,384]{1,0:T(8,128)(2,1)S(1)}, u32[]{:S(2)}, u32[]{:S(2)}) collective-permute-start(bf16[64,384]{1,0:T(8,128)(2,1)S(1)} %get-tuple-element.71), channel_id=1, source_target_pairs={{4,6},{20,22},{5,7},{21,23},{36,38},{52,54},{37,39},{53,55},{68,70... | collective-permute-start | bytes 147464 | tf_op jit(solution)/shard_map/ppermute | solution.py:395
  132.4 5.0 %collective-permute-start.32 = (bf16[64,384]{1,0:T(8,128)(2,1)S(1)}, bf16[64,384]{1,0:T(8,128)(2,1)S(1)}, u32[]{:S(2)}, u32[]{:S(2)}) collective-permute-start(bf16[64,384]{1,0:T(8,128)(2,1)S(1)} %get-tuple-element.71), channel_id=1, source_target_pairs={{4,22},{20,6},{5,23},{21,7},{36,54},{52,38},{37,55},{53,39},{68,86... | collective-permute-start | bytes 147464 | tf_op jit(solution)/shard_map/ppermute | solution.py:396
  144.4 28.3 %all-to-all-start.1 = ((bf16[16,2,768]{2,1,0:T(2,128)(2,1)}), bf16[16,2,768]{2,1,0:T(2,128)(2,1)S(1)}, u32[]{:S(2)}, u32[]{:S(2)}) async-start(bf16[16,2,768]{2,1,0:T(2,128)(2,1)} %bitcast.24), calls=%async_computation.1 | async-start | bytes 98304 | tf_op jit(solution)/shard_map/all_to_all | solution.py:403
  (13 other events, 154.5 us)

commit v9 on v8

--- a/solution.py
+++ b/solution.py
@@ -94,8 +94,9 @@
     return lax.dot_general(a, b, (((1,), (1,)), ((), ())), preferred_element_type=jnp.float32)
 
 
-def block_kernel(tick, who, near_ref, cross_ref, far_ref, w_ref, kv_ref, other_ref, mod_ref, gate_ref, cos_ref, sin_ref, block_ref, old_ref, state_ref, fresh_ref):
-    active = who[1] == tick
+def block_kernel(tick, near_ref, cross_ref, far_ref, w_ref, kv_ref, other_ref, mod_ref, gate_ref, cos_ref, sin_ref, block_ref, old_ref, state_ref, fresh_ref):
+    active = lax.axis_index("section") == tick
+    member = lax.axis_index("xl") * 2 + lax.axis_index("core")
 
     @pl.when(jnp.logical_not(active))
     def _():
@@ -103,7 +104,7 @@
 
     @pl.when(active)
     def _():
-        active_block(who[0], near_ref, cross_ref, far_ref, w_ref, kv_ref, other_ref, mod_ref, gate_ref, cos_ref, sin_ref, block_ref, state_ref, fresh_ref)
+        active_block(member, near_ref, cross_ref, far_ref, w_ref, kv_ref, other_ref, mod_ref, gate_ref, cos_ref, sin_ref, block_ref, state_ref, fresh_ref)
 
 
 def active_block(member, near_ref, cross_ref, far_ref, w_ref, kv_ref, other_ref, mod_ref, gate_ref, cos_ref, sin_ref, block_ref, state_ref, fresh_ref):
@@ -172,7 +173,7 @@
         fresh_ref[:, vcols[h]] = value[h]
 
 
-def run_block(tick, who, near, cross, far, weight, kv, other, mod, gate, cosine, sine, blocks, old):
+def run_block(tick, near, cross, far, weight, kv, other, mod, gate, cosine, sine, blocks, old):
     vmem = pl.BlockSpec(memory_space=pltpu.VMEM)
     weight = pltpu.with_memory_space_constraint(weight, pltpu.VMEM)
     return pl.pallas_call(
@@ -181,16 +182,24 @@
             jax.ShapeDtypeStruct((GROUP, PART), jnp.bfloat16),
             jax.ShapeDtypeStruct((GROUP, 2 * PART), jnp.bfloat16),
         ),
-        in_specs=[pl.BlockSpec(memory_space=pltpu.SMEM)] + [vmem] * 12,
+        in_specs=[vmem] * 12,
         out_specs=(vmem, vmem),
         compiler_params=pltpu.CompilerParams(vmem_limit_bytes=8 * 1024 * 1024),
         name="block_step",
-    )(who, near, cross, far, weight, kv, other, mod, gate, cosine, sine, blocks, old)
-
-
-def half_kernel(where, columns_ref, half_ref, turn_ref, sems):
-    first = jnp.where(where[2] == 0, 2 * UNIT, 0)
-    col = pl.ds(pl.multiple_of(where[3] % 2 * HALF, 128), HALF)
+    )(near, cross, far, weight, kv, other, mod, gate, cosine, sine, blocks, old)
+
+
+def seat():
+    y = lax.axis_index("yh") * 2 + lax.axis_index("cfg")
+    core = lax.axis_index("core")
+    later = jnp.minimum(lax.axis_index("section"), 1)
+    return lax.axis_index("xl") * 2 + core, lax.axis_index("xh"), core, y, later
+
+
+def half_kernel(columns_ref, half_ref, turn_ref, sems):
+    _, _, core, y, _ = seat()
+    first = (1 - core) * (2 * UNIT)
+    col = pl.ds(pl.multiple_of(y % 2 * HALF, 128), HALF)
     whole = pltpu.make_async_copy(columns_ref.at[:, col], half_ref, sems.at[0])
     turn = pltpu.make_async_copy(
         columns_ref.at[pl.ds(pl.multiple_of(first, 16), UNIT), col], turn_ref, sems.at[1]
@@ -201,7 +210,7 @@
     turn.wait()
 
 
-def stale_kernel(where, stale_ref, out_ref, sem):
+def stale_kernel(stale_ref, out_ref, sem):
     copies = []
     for slot in range(2 * 4 * 2):
         m = slot // 8 * 2 + slot % 2
@@ -218,8 +227,8 @@
         copy.wait()
 
 
-def join_kernel(where, first_ref, second_ref, turn0_ref, turn1_ref, own_ref):
-    half, y = where[1], where[3]
+def join_kernel(first_ref, second_ref, turn0_ref, turn1_ref, own_ref):
+    _, half, _, y, _ = seat()
 
     def pick(one, two):
         return jnp.where(half == 0, one[...], two[...])
@@ -236,11 +245,11 @@
         own_ref[COLUMNS : COLUMNS + UNIT, :] = pick(turn0_ref, turn1_ref)
 
 
-def place_kernel(sources, kind, where, *refs):
+def place_kernel(sources, kind, *refs):
     blocks, refs = refs[: len(sources)], refs[len(sources) :]
     rows = refs[{"first": 0, "last": 1, "rest": 2}[kind]]
     sem = refs[-1]
-    member, core, y, later = where[0], where[2], where[3], where[4]
+    member, _, core, y, later = seat()
     sign = 1 - 2 * core
 
     def home(unit):
@@ -270,7 +279,7 @@
                 out_ref[c : c + HDIM, :] = jnp.transpose(rows[:, c : c + HDIM])
 
 
-def place(sources, kind, where, blocks, held=()):
+def place(sources, kind, blocks, held=()):
     any_space = pl.BlockSpec(memory_space=pl.ANY)
     vmem = pl.BlockSpec(memory_space=pltpu.VMEM)
     whole = jax.ShapeDtypeStruct((3 * PART, D), jnp.bfloat16)
@@ -281,13 +290,13 @@
     return pl.pallas_call(
         functools.partial(place_kernel, sources, kind),
         out_shape={"first": whole, "last": (whole, turned), "rest": turned}[kind],
-        in_specs=[pl.BlockSpec(memory_space=pltpu.SMEM)] + [any_space] * len(blocks) + [vmem] * len(held),
+        in_specs=[any_space] * len(blocks) + [vmem] * len(held),
         out_specs=(vmem, vmem) if kind == "last" else vmem,
-        input_output_aliases={len(blocks) + 1: 0} if held else {},
+        input_output_aliases={len(blocks): 0} if held else {},
         scratch_shapes=scratch,
         compiler_params=pltpu.CompilerParams(vmem_limit_bytes=12 * 1024 * 1024),
         name="place_" + kind,
-    )(where, *blocks, *held)
+    )(*blocks, *held)
 
 
 def renew_kernel(weight_ref, out_ref, sem):
@@ -309,31 +318,27 @@
     )(pltpu.with_memory_space_constraint(weight, pltpu.VMEM))
 
 
-def whole_call(kernel, where, arrays, outs, sems=()):
+def whole_call(kernel, arrays, outs, sems=()):
     vmem = pl.BlockSpec(memory_space=pltpu.VMEM)
     held = pl.BlockSpec(memory_space=pl.ANY) if sems else vmem
     return pl.pallas_call(
         kernel,
         out_shape=[jax.ShapeDtypeStruct(shape, jnp.bfloat16) for shape in outs],
-        in_specs=[pl.BlockSpec(memory_space=pltpu.SMEM)] + [held] * len(arrays),
+        in_specs=[held] * len(arrays),
         out_specs=[vmem] * len(outs),
         scratch_shapes=list(sems),
         compiler_params=pltpu.CompilerParams(vmem_limit_bytes=8 * 1024 * 1024),
         name=kernel.__name__,
-    )(where, *arrays)
+    )(*arrays)
 
 
 def body(hidden, timestep, patch_order, modulation, qkv_weight, stale_kv):
     index = {a: lax.axis_index(a) for a in AXES}
     section = index["section"]
     member = index["xl"] * 2 + index["core"]
-    y = index["yh"] * 2 + index["cfg"]
-    where = jnp.stack([member, index["xh"], index["core"], y, jnp.minimum(section, 1)]).astype(jnp.int32)
-    who = jnp.stack([member, section]).astype(jnp.int32)
 
     half, turn = whole_call(
         half_kernel,
-        where,
         [jnp.transpose(qkv_weight[0])],
         [(COLUMNS, HALF), (UNIT, HALF)],
         [pltpu.SemaphoreType.DMA((2,))],
@@ -341,11 +346,11 @@
     moved = [lax.ppermute(half, AXES, edges) for edges in MAIN]
     turned = [lax.ppermute(turn, AXES, edges) for edges in TURN]
     (outgoing,) = whole_call(
-        stale_kernel, where, [stale_kv[0, 0]], [(2 * 4 * 2, LOCAL, 2 * PART)], [pltpu.SemaphoreType.DMA]
+        stale_kernel, [stale_kv[0, 0]], [(2 * 4 * 2, LOCAL, 2 * PART)], [pltpu.SemaphoreType.DMA]
     )
     kv = lax.all_to_all(outgoing, ("xl", "yh", "core"), split_axis=0, concat_axis=0, tiled=True)
     kv = kv.reshape(TOKENS // 2, 2 * PART)
-    (own,) = whole_call(join_kernel, where, [*moved, *turned], [(BLOCK, HALF)])
+    (own,) = whole_call(join_kernel, [*moved, *turned], [(BLOCK, HALF)])
     up1, down1 = lax.ppermute(own, AXES, UP), lax.ppermute(own, AXES, DOWN)
     up1, entering, kv = lax.optimization_barrier((up1, hidden[0], kv))
     kv_other = lax.ppermute(kv, AXES, ACROSS)
@@ -358,8 +363,8 @@
     both = (0, 1)
     early = ((0, both), (-1, both), (1, both), (-2, both), (2, both)), [own, up1, down1, up2, down2]
     late = ((-3, both), (3, both), (4, (0,)), (4, (1,))), [up3, down3, up4, down4]
-    rows = place(early[0], "first", where, early[1])
-    _, weight = place(late[0], "last", where, late[1], [rows])
+    rows = place(early[0], "first", early[1])
+    _, weight = place(late[0], "last", late[1], [rows])
     x = jnp.transpose(x.reshape(GROUP, MEMBERS, PART), (1, 0, 2))
     near = lax.dynamic_index_in_dim(x, member, 0, keepdims=False)
     cross = lax.dynamic_index_in_dim(x, member + 1 - 2 * index["core"], 0, keepdims=False)
@@ -383,10 +388,10 @@
 
     fresh = jnp.zeros((GROUP, 2 * PART), jnp.bfloat16)
     for tick in range(SECTIONS):
-        state, fresh = run_block(tick, who, near, cross, far, weight, kv, kv_other, mod, gate, cosine, sine, blocks[:, None], fresh)
+        state, fresh = run_block(tick, near, cross, far, weight, kv, kv_other, mod, gate, cosine, sine, blocks[:, None], fresh)
         if tick == 0:
             moved, state = lax.optimization_barrier((early[1] + late[1], state))
-            weight = place(early[0] + late[0], "rest", where, moved, [weight])
+            weight = place(early[0] + late[0], "rest", moved, [weight])
         if tick == SECTIONS - 2:
             state, weight = lax.optimization_barrier((state, weight))
             weight = renew(weight)

time: 175 us -> 169 us (0.966)
  Pallas kernels: 14.5 us -> 6.77 us
  waiting for transfers between devices: 14.4 us -> 17.5 us
    ppermute x2, waiting for transfers between devices: 0.01 us -> 4.81 us  [body(): up3, down3 = (lax.ppermute(up2, AXES, UP), lax.ppermute(down2, AXES, DOWN))]
    pallas_call x8, Pallas kernels: 5.82 us -> 1.49 us  [run_block(): pl.pallas_call(functools.partial(block_kernel, tick), out_shape=(jax.Shap...]
    all_gather x7, blocking collectives: 17.6 us -> 13.6 us  [body(): far = lax.all_gather(far, 'core', axis=0, tiled=False)]
    ppermute x7, starting transfers between devices: 7.39 us -> 10.7 us  [body(): cross = lax.ppermute(state, AXES, onward(tick, 0, 1))]
    ppermute x1, starting transfers between devices: 5.11 us -> 1.92 us  [body(): kv_other = lax.ppermute(kv, AXES, ACROSS)]
    all_gather x1, blocking collectives: 5.48 us -> 8.52 us  [body(): x = lax.all_gather(entering, ('xl', 'core'), axis=0, tiled=True)]
    ppermute x2, waiting for transfers between devices: 9.06 us -> 6.42 us  [body(): up1, down1 = (lax.ppermute(own, AXES, UP), lax.ppermute(own, AXES, DOWN))]
    pallas_call x3, Pallas kernels: 5.6 us -> 3.82 us  [place(): pl.pallas_call(functools.partial(place_kernel, sources, kind), out_shape=...]
  transfers between devices with their start and end apart: 36 -> 36, of which waited for: 5 -> 8; matrix products, arithmetic and copies ran while one was open for 2% -> 2% of each run, Pallas kernels for 4% -> 3%
where the time goes in v9:
time: 169 us; the launch traced here: 167 us
  starting transfers between devices  96.1 us (57%)
  blocking collectives  34.5 us (20%)
  waiting for transfers between devices  17.5 us (10%)
  local copies, waits for them, and re-layouts  9.4 us (6%)
  Pallas kernels  6.77 us (4%)
  between operations  2.04 us (1%)
    all_to_all x1, starting transfers between devices, body(): lax.all_to_all(finals, ('section', 'cfg'), split_axis=0, concat_axis=0, t...  20.5 us
    all_gather x7, blocking collectives, body(): far = lax.all_gather(far, 'core', axis=0, tiled=False)  13.6 us
    ppermute x7, starting transfers between devices, body(): far = lax.ppermute(state, AXES, onward(tick, 1, 0))  12.5 us
    ppermute x7, starting transfers between devices, body(): cross = lax.ppermute(state, AXES, onward(tick, 0, 1))  10.7 us
    all_to_all x1, starting transfers between devices, body(): lax.all_to_all(outgoing, ('xl', 'yh', 'core'), split_axis=0, concat_axis=...  10.2 us
    all_gather x1, blocking collectives, body(): x = lax.all_gather(entering, ('xl', 'core'), axis=0, tiled=True)  8.52 us
    ppermute x2, starting transfers between devices, body(): up2, down2 = (lax.ppermute(up1, AXES, UP), lax.ppermute(down1, AXES, DOWN))  7.02 us
    ppermute x2, starting transfers between devices, body(): up3, down3 = (lax.ppermute(up2, AXES, UP), lax.ppermute(down2, AXES, DOWN))  6.76 us
  transfers between devices with their start and end apart: 36, of which 8 were waited for; matrix products, arithmetic and copies ran while one was open for 2% of the time, Pallas kernels for 3%

profile of v9, /device:TPU:1, one launch (start us, length us, event | category | flops | bytes accessed | tf_op | source)
XLA Modules:
  0.0 167.4 jit_solution(8448969618683059147)
XLA Ops:
  2.6 10.2 %all-to-all-start = ((bf16[16,16,768]{2,1,0:T(8,128)(2,1)}), bf16[16,16,768]{2,1,0:T(8,128)(2,1)S(1)}, u32[]{:S(2)}, u32[]{:S(2)}) async-start(bf16[16,16,768]{2,1,0:T(8,128)(2,1)} %stale_kernel.1), calls=%async_computation | async-start | bytes 786432 | tf_op jit(solution)/shard_map/all_to_all | solution.py:351
  13.9 3.7 %collective-permute-start = (bf16[144,768]{1,0:T(8,128)(2,1)S(1)}, bf16[144,768]{1,0:T(8,128)(2,1)S(1)}, u32[]{:S(2)}, u32[]{:S(2)}) collective-permute-start(bf16[144,768]{1,0:T(8,128)(2,1)S(1)} %get-tuple-element.40), channel_id=1, source_target_pairs={{0,0},{2,2},{4,4},{6,6},{8,8},{10,10},{12,12},{14,14},{16,256},{18... | collective-permute-start | bytes 663560 | tf_op jit(solution)/shard_map/ppermute | solution.py:346
  17.5 1.9 %collective-permute-start.1 = (bf16[144,768]{1,0:T(8,128)(2,1)S(1)}, bf16[144,768]{1,0:T(8,128)(2,1)S(1)}, u32[]{:S(2)}, u32[]{:S(2)}) collective-permute-start(bf16[144,768]{1,0:T(8,128)(2,1)S(1)} %get-tuple-element.40), channel_id=1, source_target_pairs={{0,256},{2,258},{4,260},{6,262},{8,264},{10,266},{12,268},{14,270}... | collective-permute-start | bytes 663560 | tf_op jit(solution)/shard_map/ppermute | solution.py:346
  20.8 1.8 %collective-permute-done.first_ref = bf16[144,768]{1,0:T(8,128)(2,1)S(1)} collective-permute-done((bf16[144,768]{1,0:T(8,128)(2,1)S(1)}, bf16[144,768]{1,0:T(8,128)(2,1)S(1)}, u32[]{:S(2)}, u32[]{:S(2)}) %collective-permute-start) | collective-permute-done | bytes 221216 | tf_op jit(solution)/shard_map/ppermute | solution.py:346
  22.6 2.8 %collective-permute-done.1.second_ref = bf16[144,768]{1,0:T(8,128)(2,1)S(1)} collective-permute-done((bf16[144,768]{1,0:T(8,128)(2,1)S(1)}, bf16[144,768]{1,0:T(8,128)(2,1)S(1)}, u32[]{:S(2)}, u32[]{:S(2)}) %collective-permute-start.1) | collective-permute-done | bytes 221216 | tf_op jit(solution)/shard_map/ppermute | solution.py:346
  25.5 2.3 %collective-permute-start.5 = (bf16[288,768]{1,0:T(8,128)(2,1)S(1)}, bf16[288,768]{1,0:T(8,128)(2,1)S(1)}, u32[]{:S(2)}, u32[]{:S(2)}) collective-permute-start(bf16[288,768]{1,0:T(8,128)(2,1)S(1)} %join_kernel.1.refs_0_), channel_id=1, source_target_pairs={{0,97},{2,99},{4,101},{6,103},{8,105},{10,107},{12,109},{14,111},{... | collective-permute-start | bytes 1327112 | tf_op jit(solution)/shard_map/ppermute | solution.py:354
  27.8 4.2 %collective-permute-start.4 = (bf16[288,768]{1,0:T(8,128)(2,1)S(1)}, bf16[288,768]{1,0:T(8,128)(2,1)S(1)}, u32[]{:S(2)}, u32[]{:S(2)}) collective-permute-start(bf16[288,768]{1,0:T(8,128)(2,1)S(1)} %join_kernel.1.refs_0_), channel_id=1, source_target_pairs={{0,1},{2,3},{4,5},{6,7},{8,9},{10,11},{12,13},{14,15},{16,113},{18... | collective-permute-start | bytes 1327112 | tf_op jit(solution)/shard_map/ppermute | solution.py:354
  33.6 2.2 %collective-permute-done.5.refs_2_ = bf16[288,768]{1,0:T(8,128)(2,1)S(1)} collective-permute-done((bf16[288,768]{1,0:T(8,128)(2,1)S(1)}, bf16[288,768]{1,0:T(8,128)(2,1)S(1)}, u32[]{:S(2)}, u32[]{:S(2)}) %collective-permute-start.5) | collective-permute-done | bytes 442400 | tf_op jit(solution)/shard_map/ppermute | solution.py:354
  35.8 1.9 %collective-permute-start.7 = (bf16[288,768]{1,0:T(8,128)(2,1)S(1)}, bf16[288,768]{1,0:T(8,128)(2,1)}, u32[]{:S(2)}, u32[]{:S(2)}) collective-permute-start(bf16[288,768]{1,0:T(8,128)(2,1)S(1)} %collective-permute-done.5.refs_2_), channel_id=1, source_target_pairs={{0,97},{2,99},{4,101},{6,103},{8,105},{10,107},{12,109},{14,111},{... | collective-permute-start | bytes 1327112 | tf_op jit(solution)/shard_map/ppermute | solution.py:358
  37.7 4.3 %collective-permute-done.4.refs_1_ = bf16[288,768]{1,0:T(8,128)(2,1)S(1)} collective-permute-done((bf16[288,768]{1,0:T(8,128)(2,1)S(1)}, bf16[288,768]{1,0:T(8,128)(2,1)S(1)}, u32[]{:S(2)}, u32[]{:S(2)}) %collective-permute-start.4) | collective-permute-done | bytes 442400 | tf_op jit(solution)/shard_map/ppermute | solution.py:354
  41.9 5.1 %collective-permute-start.6 = (bf16[288,768]{1,0:T(8,128)(2,1)S(1)}, bf16[288,768]{1,0:T(8,128)(2,1)}, u32[]{:S(2)}, u32[]{:S(2)}) collective-permute-start(bf16[288,768]{1,0:T(8,128)(2,1)S(1)} %collective-permute-done.4.refs_1_), channel_id=1, source_target_pairs={{0,1},{2,3},{4,5},{6,7},{8,9},{10,11},{12,13},{14,15},{16,113},{18... | collective-permute-start | bytes 1327112 | tf_op jit(solution)/shard_map/ppermute | solution.py:358
  48.1 8.5 %all_gather.57 = bf16[64,1536]{1,0:T(8,128)(2,1)} all-gather(bf16[16,1536]{1,0:T(8,128)(2,1)S(1)} %bitcast.66), channel_id=1, replica_groups=mesh['xh'=2,'xl'=2,'yh'=4,'core'=2,'section'=8,'cfg'=2] {'xl','core'}, dimensions={0}, use_global_device_ids=true | all-gather | bytes 245760 | tf_op jit(solution)/shard_map/all_gather | solution.py:357
  56.6 2.3 %collective-permute-start.9 = (bf16[288,768]{1,0:T(8,128)(2,1)}, bf16[288,768]{1,0:T(8,128)(2,1)S(1)}, u32[]{:S(2)}, u32[]{:S(2)}) collective-permute-start(bf16[288,768]{1,0:T(8,128)(2,1)} %collective-permute-done.7.refs_4_), channel_id=1, source_target_pairs={{0,97},{2,99},{4,101},{6,103},{8,105},{10,107},{12,109},{14,111},{... | collective-permute-start | bytes 1327112 | tf_op jit(solution)/shard_map/ppermute | solution.py:360
  59.0 4.4 %collective-permute-start.8 = (bf16[288,768]{1,0:T(8,128)(2,1)}, bf16[288,768]{1,0:T(8,128)(2,1)S(1)}, u32[]{:S(2)}, u32[]{:S(2)}) collective-permute-start(bf16[288,768]{1,0:T(8,128)(2,1)} %collective-permute-done.6.refs_3_), channel_id=1, source_target_pairs={{0,1},{2,3},{4,5},{6,7},{8,9},{10,11},{12,13},{14,15},{16,113},{18... | collective-permute-start | bytes 1327112 | tf_op jit(solution)/shard_map/ppermute | solution.py:360
  63.6 1.9 %collective-permute-start.12 = (bf16[256,768]{1,0:T(8,128)(2,1)S(1)}, bf16[256,768]{1,0:T(8,128)(2,1)S(1)}, u32[]{:S(2)}, u32[]{:S(2)}) collective-permute-start(bf16[256,768]{1,0:T(8,128)(2,1)S(1)} %bitcast.41), channel_id=1, source_target_pairs={{0,256},{1,257},{2,258},{3,259},{4,260},{5,261},{6,262},{7,263},{8... | collective-permute-start | bytes 1179656 | tf_op jit(solution)/shard_map/ppermute | solution.py:356
  67.4 1.9 %collective-permute-start.11 = (bf16[144,768]{1,0:T(8,128)(2,1)S(1)}, bf16[144,768]{1,0:T(8,128)(2,1)S(1)}, u32[]{:S(2)}, u32[]{:S(2)}) collective-permute-start(bf16[144,768]{1,0:T(8,128)(2,1)S(1)} %slice.24), channel_id=1, source_target_pairs={{0,97},{2,99},{4,101},{6,103},{8,105},{10,107},{12,109},{14,111},{... | collective-permute-start | bytes 663560 | tf_op jit(solution)/shard_map/ppermute | solution.py:362
  69.3 4.3 %collective-permute-done.8.refs_0_.refs_5_ = bf16[288,768]{1,0:T(8,128)(2,1)S(1)} collective-permute-done((bf16[288,768]{1,0:T(8,128)(2,1)}, bf16[288,768]{1,0:T(8,128)(2,1)S(1)}, u32[]{:S(2)}, u32[]{:S(2)}) %collective-permute-start.8) | collective-permute-done | bytes 442400 | tf_op jit(solution)/shard_map/ppermute | solution.py:360
  73.6 5.2 %collective-permute-start.10 = (bf16[144,768]{1,0:T(8,128)(2,1)S(1)}, bf16[144,768]{1,0:T(8,128)(2,1)S(1)}, u32[]{:S(2)}, u32[]{:S(2)}) collective-permute-start(bf16[144,768]{1,0:T(8,128)(2,1)S(1)} %slice.23), channel_id=1, source_target_pairs={{0,1},{2,3},{4,5},{6,7},{8,9},{10,11},{12,13},{14,15},{16,113},{18... | collective-permute-start | bytes 663560 | tf_op jit(solution)/shard_map/ppermute | solution.py:361
  79.9 2.1 %place_first.1.refs_4_ = bf16[1152,1536]{1,0:T(8,128)(2,1)S(1)} custom-call(bf16[288,768]{1,0:T(8,128)(2,1)S(1)} %join_kernel.1.refs_0_, bf16[288,768]{1,0:T(8,128)(2,1)S(1)} %copy-done.4, bf16[288,768]{1,0:T(8,128)(2,1)S(1)} %collective-permute-done.5.refs_2_, bf16[288,768]{1,0:T(8,128)(2,1)} %collective-permute-done.6.refs_3_, ...), custom_call_target="tpu_custom_call" | custom-call | tf_op jit(solution)/shard_map/place_first/pallas_call | solution.py:290
  89.1 5.9 %collective-permute-start.14 = (bf16[64,384]{1,0:T(8,128)(2,1)S(1)}, bf16[64,384]{1,0:T(8,128)(2,1)S(1)}, u32[]{:S(2)}, u32[]{:S(2)}) collective-permute-start(bf16[64,384]{1,0:T(8,128)(2,1)S(1)} %get-tuple-element.49), channel_id=1, source_target_pairs={{0,18},{16,2},{1,19},{17,3},{32,50},{48,34},{33,51},{49,35},{64,82... | collective-permute-start | bytes 147464 | tf_op jit(solution)/shard_map/ppermute | solution.py:401
  95.1 2.0 %all-gather = bf16[128,384]{1,0:T(8,128)(2,1)S(1)} all-gather(bf16[64,384]{1,0:T(8,128)(2,1)S(1)} %collective-permute-done.15), channel_id=2, replica_groups=mesh['xh'=2,'xl'=2,'yh'=4,'core'=2,'section'=8,'cfg'=2] {'core'}, dimensions={0}, use_global_device_ids=true | all-gather | bytes 147456 | tf_op jit(solution)/shard_map/all_gather | solution.py:402
  99.2 1.9 %all-gather.1 = bf16[128,384]{1,0:T(8,128)(2,1)S(1)} all-gather(bf16[64,384]{1,0:T(8,128)(2,1)S(1)} %collective-permute-done.18), channel_id=3, replica_groups=mesh['xh'=2,'xl'=2,'yh'=4,'core'=2,'section'=8,'cfg'=2] {'core'}, dimensions={0}, use_global_device_ids=true | all-gather | bytes 147456 | tf_op jit(solution)/shard_map/all_gather | solution.py:402
  103.3 1.9 %all-gather.2 = bf16[128,384]{1,0:T(8,128)(2,1)S(1)} all-gather(bf16[64,384]{1,0:T(8,128)(2,1)S(1)} %collective-permute-done.21), channel_id=4, replica_groups=mesh['xh'=2,'xl'=2,'yh'=4,'core'=2,'section'=8,'cfg'=2] {'core'}, dimensions={0}, use_global_device_ids=true | all-gather | bytes 147456 | tf_op jit(solution)/shard_map/all_gather | solution.py:402
  107.2 1.9 %all-gather.3 = bf16[128,384]{1,0:T(8,128)(2,1)S(1)} all-gather(bf16[64,384]{1,0:T(8,128)(2,1)S(1)} %collective-permute-done.24), channel_id=5, replica_groups=mesh['xh'=2,'xl'=2,'yh'=4,'core'=2,'section'=8,'cfg'=2] {'core'}, dimensions={0}, use_global_device_ids=true | all-gather | bytes 147456 | tf_op jit(solution)/shard_map/all_gather | solution.py:402
  109.1 7.9 %collective-permute-start.27 = (bf16[64,384]{1,0:T(8,128)(2,1)S(1)}, bf16[64,384]{1,0:T(8,128)(2,1)S(1)}, u32[]{:S(2)}, u32[]{:S(2)}) collective-permute-start(bf16[64,384]{1,0:T(8,128)(2,1)S(1)} %get-tuple-element.66), channel_id=1, source_target_pairs={{0,130},{16,146},{1,131},{17,147},{32,162},{48,178},{33,163},{49,1... | collective-permute-start | bytes 147464 | tf_op jit(solution)/shard_map/ppermute | solution.py:399
  119.7 2.2 %all-gather.4 = bf16[128,384]{1,0:T(8,128)(2,1)S(1)} all-gather(bf16[64,384]{1,0:T(8,128)(2,1)S(1)} %collective-permute-done.27), channel_id=6, replica_groups=mesh['xh'=2,'xl'=2,'yh'=4,'core'=2,'section'=8,'cfg'=2] {'core'}, dimensions={0}, use_global_device_ids=true | all-gather | bytes 147456 | tf_op jit(solution)/shard_map/all_gather | solution.py:402
  123.9 1.9 %all-gather.5 = bf16[128,384]{1,0:T(8,128)(2,1)S(1)} all-gather(bf16[64,384]{1,0:T(8,128)(2,1)S(1)} %collective-permute-done.30), channel_id=7, replica_groups=mesh['xh'=2,'xl'=2,'yh'=4,'core'=2,'section'=8,'cfg'=2] {'core'}, dimensions={0}, use_global_device_ids=true | all-gather | bytes 147456 | tf_op jit(solution)/shard_map/all_gather | solution.py:402
  127.8 2.0 %copy-done.2 = bf16[1536,1152]{1,0:T(8,128)(2,1)S(1)} copy-done((bf16[1536,1152]{1,0:T(8,128)(2,1)S(1)}, bf16[1536,1152]{1,0:T(8,128)(2,1)}, u32[]{:S(2)}) %copy-start.2) | copy-done | bytes 3538968
  130.3 1.9 %all-gather.6 = bf16[128,384]{1,0:T(8,128)(2,1)S(1)} all-gather(bf16[64,384]{1,0:T(8,128)(2,1)S(1)} %collective-permute-done.33), channel_id=8, replica_groups=mesh['xh'=2,'xl'=2,'yh'=4,'core'=2,'section'=8,'cfg'=2] {'core'}, dimensions={0}, use_global_device_ids=true | all-gather | bytes 147456 | tf_op jit(solution)/shard_map/all_gather | solution.py:402
  132.2 5.8 %all-gather.7 = bf16[256,384]{1,0:T(8,128)(2,1)S(1)} all-gather(bf16[64,384]{1,0:T(8,128)(2,1)S(1)} %get-tuple-element.74), channel_id=9, replica_groups=mesh['xh'=2,'xl'=2,'yh'=4,'core'=2,'section'=8,'cfg'=2] {'xl','core'}, dimensions={0}, use_global_device_ids=true | all-gather | bytes 245760 | tf_op jit(solution)/shard_map/all_gather | solution.py:404
  138.7 20.5 %all-to-all-start.1 = ((bf16[16,2,768]{2,1,0:T(2,128)(2,1)}), bf16[16,2,768]{2,1,0:T(2,128)(2,1)S(1)}, u32[]{:S(2)}, u32[]{:S(2)}) async-start(bf16[16,2,768]{2,1,0:T(2,128)(2,1)} %bitcast.18), calls=%async_computation.1 | async-start | bytes 98304 | tf_op jit(solution)/shard_map/all_to_all | solution.py:408
  159.2 6.6 %all-gather.8 = bf16[256,768]{1,0:T(8,128)(2,1)S(1)} all-gather(bf16[64,768]{1,0:T(8,128)(2,1)S(1)} %get-tuple-element.75), channel_id=10, replica_groups=mesh['xh'=2,'xl'=2,'yh'=4,'core'=2,'section'=8,'cfg'=2] {'xl','core'}, dimensions={0}, use_global_device_ids=true | all-gather | bytes 491520 | tf_op jit(solution)/shard_map/all_gather | solution.py:409
  (111 shorter events, 32.0 us)
Async XLA Ops:
  2.6 39.4 %all-to-all-start = ((bf16[16,16,768]{2,1,0:T(8,128)(2,1)}), bf16[16,16,768]{2,1,0:T(8,128)(2,1)S(1)}, u32[]{:S(2)}, u32[]{:S(2)}) async-start(bf16[16,16,768]{2,1,0:T(8,128)(2,1)} %stale_kernel.1), calls=%async_computation | async-start | bytes 786432 | tf_op jit(solution)/shard_map/all_to_all | solution.py:351
  13.9 8.8 %collective-permute-start = (bf16[144,768]{1,0:T(8,128)(2,1)S(1)}, bf16[144,768]{1,0:T(8,128)(2,1)S(1)}, u32[]{:S(2)}, u32[]{:S(2)}) collective-permute-start(bf16[144,768]{1,0:T(8,128)(2,1)S(1)} %get-tuple-element.40), channel_id=1, source_target_pairs={{0,0},{2,2},{4,4},{6,6},{8,8},{10,10},{12,12},{14,14},{16,256},{18... | collective-permute-start | bytes 663560 | tf_op jit(solution)/shard_map/ppermute | solution.py:346
  17.5 7.9 %collective-permute-start.1 = (bf16[144,768]{1,0:T(8,128)(2,1)S(1)}, bf16[144,768]{1,0:T(8,128)(2,1)S(1)}, u32[]{:S(2)}, u32[]{:S(2)}) collective-permute-start(bf16[144,768]{1,0:T(8,128)(2,1)S(1)} %get-tuple-element.40), channel_id=1, source_target_pairs={{0,256},{2,258},{4,260},{6,262},{8,264},{10,266},{12,268},{14,270}... | collective-permute-start | bytes 663560 | tf_op jit(solution)/shard_map/ppermute | solution.py:346
  25.5 10.3 %collective-permute-start.5 = (bf16[288,768]{1,0:T(8,128)(2,1)S(1)}, bf16[288,768]{1,0:T(8,128)(2,1)S(1)}, u32[]{:S(2)}, u32[]{:S(2)}) collective-permute-start(bf16[288,768]{1,0:T(8,128)(2,1)S(1)} %join_kernel.1.refs_0_), channel_id=1, source_target_pairs={{0,97},{2,99},{4,101},{6,103},{8,105},{10,107},{12,109},{14,111},{... | collective-permute-start | bytes 1327112 | tf_op jit(solution)/shard_map/ppermute | solution.py:354
  27.8 14.1 %collective-permute-start.4 = (bf16[288,768]{1,0:T(8,128)(2,1)S(1)}, bf16[288,768]{1,0:T(8,128)(2,1)S(1)}, u32[]{:S(2)}, u32[]{:S(2)}) collective-permute-start(bf16[288,768]{1,0:T(8,128)(2,1)S(1)} %join_kernel.1.refs_0_), channel_id=1, source_target_pairs={{0,1},{2,3},{4,5},{6,7},{8,9},{10,11},{12,13},{14,15},{16,113},{18... | collective-permute-start | bytes 1327112 | tf_op jit(solution)/shard_map/ppermute | solution.py:354
  35.8 20.8 %collective-permute-start.7 = (bf16[288,768]{1,0:T(8,128)(2,1)S(1)}, bf16[288,768]{1,0:T(8,128)(2,1)}, u32[]{:S(2)}, u32[]{:S(2)}) collective-permute-start(bf16[288,768]{1,0:T(8,128)(2,1)S(1)} %collective-permute-done.5.refs_2_), channel_id=1, source_target_pairs={{0,97},{2,99},{4,101},{6,103},{8,105},{10,107},{12,109},{14,111},{... | collective-permute-start | bytes 1327112 | tf_op jit(solution)/shard_map/ppermute | solution.py:358
  41.9 17.0 %collective-permute-start.6 = (bf16[288,768]{1,0:T(8,128)(2,1)S(1)}, bf16[288,768]{1,0:T(8,128)(2,1)}, u32[]{:S(2)}, u32[]{:S(2)}) collective-permute-start(bf16[288,768]{1,0:T(8,128)(2,1)S(1)} %collective-permute-done.4.refs_1_), channel_id=1, source_target_pairs={{0,1},{2,3},{4,5},{6,7},{8,9},{10,11},{12,13},{14,15},{16,113},{18... | collective-permute-start | bytes 1327112 | tf_op jit(solution)/shard_map/ppermute | solution.py:358
  56.6 10.7 %collective-permute-start.9 = (bf16[288,768]{1,0:T(8,128)(2,1)}, bf16[288,768]{1,0:T(8,128)(2,1)S(1)}, u32[]{:S(2)}, u32[]{:S(2)}) collective-permute-start(bf16[288,768]{1,0:T(8,128)(2,1)} %collective-permute-done.7.refs_4_), channel_id=1, source_target_pairs={{0,97},{2,99},{4,101},{6,103},{8,105},{10,107},{12,109},{14,111},{... | collective-permute-start | bytes 1327112 | tf_op jit(solution)/shard_map/ppermute | solution.py:360
  59.0 14.6 %collective-permute-start.8 = (bf16[288,768]{1,0:T(8,128)(2,1)}, bf16[288,768]{1,0:T(8,128)(2,1)S(1)}, u32[]{:S(2)}, u32[]{:S(2)}) collective-permute-start(bf16[288,768]{1,0:T(8,128)(2,1)} %collective-permute-done.6.refs_3_), channel_id=1, source_target_pairs={{0,1},{2,3},{4,5},{6,7},{8,9},{10,11},{12,13},{14,15},{16,113},{18... | collective-permute-start | bytes 1327112 | tf_op jit(solution)/shard_map/ppermute | solution.py:360
  63.6 21.5 %collective-permute-start.12 = (bf16[256,768]{1,0:T(8,128)(2,1)S(1)}, bf16[256,768]{1,0:T(8,128)(2,1)S(1)}, u32[]{:S(2)}, u32[]{:S(2)}) collective-permute-start(bf16[256,768]{1,0:T(8,128)(2,1)S(1)} %bitcast.41), channel_id=1, source_target_pairs={{0,256},{1,257},{2,258},{3,259},{4,260},{5,261},{6,262},{7,263},{8... | collective-permute-start | bytes 1179656 | tf_op jit(solution)/shard_map/ppermute | solution.py:356
  67.4 14.6 %collective-permute-start.11 = (bf16[144,768]{1,0:T(8,128)(2,1)S(1)}, bf16[144,768]{1,0:T(8,128)(2,1)S(1)}, u32[]{:S(2)}, u32[]{:S(2)}) collective-permute-start(bf16[144,768]{1,0:T(8,128)(2,1)S(1)} %slice.24), channel_id=1, source_target_pairs={{0,97},{2,99},{4,101},{6,103},{8,105},{10,107},{12,109},{14,111},{... | collective-permute-start | bytes 663560 | tf_op jit(solution)/shard_map/ppermute | solution.py:362
  73.6 9.7 %collective-permute-start.10 = (bf16[144,768]{1,0:T(8,128)(2,1)S(1)}, bf16[144,768]{1,0:T(8,128)(2,1)S(1)}, u32[]{:S(2)}, u32[]{:S(2)}) collective-permute-start(bf16[144,768]{1,0:T(8,128)(2,1)S(1)} %slice.23), channel_id=1, source_target_pairs={{0,1},{2,3},{4,5},{6,7},{8,9},{10,11},{12,13},{14,15},{16,113},{18... | collective-permute-start | bytes 663560 | tf_op jit(solution)/shard_map/ppermute | solution.py:361
  86.5 8.6 %collective-permute-start.15 = (bf16[64,384]{1,0:T(8,128)(2,1)S(1)}, bf16[64,384]{1,0:T(8,128)(2,1)S(1)}, u32[]{:S(2)}, u32[]{:S(2)}) collective-permute-start(bf16[64,384]{1,0:T(8,128)(2,1)S(1)} %get-tuple-element.49), channel_id=1, source_target_pairs={{0,130},{16,146},{1,131},{17,147},{32,162},{48,178},{33,163},{49,1... | collective-permute-start | bytes 147464 | tf_op jit(solution)/shard_map/ppermute | solution.py:399
  87.8 9.3 %collective-permute-start.13 = (bf16[64,384]{1,0:T(8,128)(2,1)S(1)}, bf16[64,384]{1,0:T(8,128)(2,1)S(1)}, u32[]{:S(2)}, u32[]{:S(2)}) collective-permute-start(bf16[64,384]{1,0:T(8,128)(2,1)S(1)} %get-tuple-element.49), channel_id=1, source_target_pairs={{0,2},{16,18},{1,3},{17,19},{32,34},{48,50},{33,35},{49,51},{64,66... | collective-permute-start | bytes 147464 | tf_op jit(solution)/shard_map/ppermute | solution.py:400
  89.1 8.0 %collective-permute-start.14 = (bf16[64,384]{1,0:T(8,128)(2,1)S(1)}, bf16[64,384]{1,0:T(8,128)(2,1)S(1)}, u32[]{:S(2)}, u32[]{:S(2)}) collective-permute-start(bf16[64,384]{1,0:T(8,128)(2,1)S(1)} %get-tuple-element.49), channel_id=1, source_target_pairs={{0,18},{16,2},{1,19},{17,3},{32,50},{48,34},{33,51},{49,35},{64,82... | collective-permute-start | bytes 147464 | tf_op jit(solution)/shard_map/ppermute | solution.py:401
  97.2 2.0 %collective-permute-start.18 = (bf16[64,384]{1,0:T(8,128)(2,1)S(1)}, bf16[64,384]{1,0:T(8,128)(2,1)S(1)}, u32[]{:S(2)}, u32[]{:S(2)}) collective-permute-start(bf16[64,384]{1,0:T(8,128)(2,1)S(1)} %get-tuple-element.60), channel_id=1, source_target_pairs={{2,132},{18,148},{3,133},{19,149},{34,164},{50,180},{35,165},{51,1... | collective-permute-start | bytes 147464 | tf_op jit(solution)/shard_map/ppermute | solution.py:399
  97.8 3.2 %collective-permute-start.16 = (bf16[64,384]{1,0:T(8,128)(2,1)S(1)}, bf16[64,384]{1,0:T(8,128)(2,1)S(1)}, u32[]{:S(2)}, u32[]{:S(2)}) collective-permute-start(bf16[64,384]{1,0:T(8,128)(2,1)S(1)} %get-tuple-element.60), channel_id=1, source_target_pairs={{2,4},{18,20},{3,5},{19,21},{34,36},{50,52},{35,37},{51,53},{66,68... | collective-permute-start | bytes 147464 | tf_op jit(solution)/shard_map/ppermute | solution.py:400
  98.5 2.6 %collective-permute-start.17 = (bf16[64,384]{1,0:T(8,128)(2,1)S(1)}, bf16[64,384]{1,0:T(8,128)(2,1)S(1)}, u32[]{:S(2)}, u32[]{:S(2)}) collective-permute-start(bf16[64,384]{1,0:T(8,128)(2,1)S(1)} %get-tuple-element.60), channel_id=1, source_target_pairs={{2,20},{18,4},{3,21},{19,5},{34,52},{50,36},{35,53},{51,37},{66,84... | collective-permute-start | bytes 147464 | tf_op jit(solution)/shard_map/ppermute | solution.py:401
  101.1 2.2 %collective-permute-start.21 = (bf16[64,384]{1,0:T(8,128)(2,1)S(1)}, bf16[64,384]{1,0:T(8,128)(2,1)S(1)}, u32[]{:S(2)}, u32[]{:S(2)}) collective-permute-start(bf16[64,384]{1,0:T(8,128)(2,1)S(1)} %get-tuple-element.62), channel_id=1, source_target_pairs={{4,134},{20,150},{5,135},{21,151},{36,166},{52,182},{37,167},{53,1... | collective-permute-start | bytes 147464 | tf_op jit(solution)/shard_map/ppermute | solution.py:399
  101.8 3.4 %collective-permute-start.19 = (bf16[64,384]{1,0:T(8,128)(2,1)S(1)}, bf16[64,384]{1,0:T(8,128)(2,1)S(1)}, u32[]{:S(2)}, u32[]{:S(2)}) collective-permute-start(bf16[64,384]{1,0:T(8,128)(2,1)S(1)} %get-tuple-element.62), channel_id=1, source_target_pairs={{4,6},{20,22},{5,7},{21,23},{36,38},{52,54},{37,39},{53,55},{68,70... | collective-permute-start | bytes 147464 | tf_op jit(solution)/shard_map/ppermute | solution.py:400
  102.4 2.8 %collective-permute-start.20 = (bf16[64,384]{1,0:T(8,128)(2,1)S(1)}, bf16[64,384]{1,0:T(8,128)(2,1)S(1)}, u32[]{:S(2)}, u32[]{:S(2)}) collective-permute-start(bf16[64,384]{1,0:T(8,128)(2,1)S(1)} %get-tuple-element.62), channel_id=1, source_target_pairs={{4,22},{20,6},{5,23},{21,7},{36,54},{52,38},{37,55},{53,39},{68,86... | collective-permute-start | bytes 147464 | tf_op jit(solution)/shard_map/ppermute | solution.py:401
  105.9 3.2 %collective-permute-start.22 = (bf16[64,384]{1,0:T(8,128)(2,1)S(1)}, bf16[64,384]{1,0:T(8,128)(2,1)S(1)}, u32[]{:S(2)}, u32[]{:S(2)}) collective-permute-start(bf16[64,384]{1,0:T(8,128)(2,1)S(1)} %get-tuple-element.64), channel_id=1, source_target_pairs={{6,8},{22,24},{7,9},{23,25},{38,40},{54,56},{39,41},{55,57},{70,72... | collective-permute-start | bytes 147464 | tf_op jit(solution)/shard_map/ppermute | solution.py:400
  106.6 2.6 %collective-permute-start.23 = (bf16[64,384]{1,0:T(8,128)(2,1)S(1)}, bf16[64,384]{1,0:T(8,128)(2,1)S(1)}, u32[]{:S(2)}, u32[]{:S(2)}) collective-permute-start(bf16[64,384]{1,0:T(8,128)(2,1)S(1)} %get-tuple-element.64), channel_id=1, source_target_pairs={{6,24},{22,8},{7,25},{23,9},{38,56},{54,40},{39,57},{55,41},{70,88... | collective-permute-start | bytes 147464 | tf_op jit(solution)/shard_map/ppermute | solution.py:401
  109.1 10.5 %collective-permute-start.27 = (bf16[64,384]{1,0:T(8,128)(2,1)S(1)}, bf16[64,384]{1,0:T(8,128)(2,1)S(1)}, u32[]{:S(2)}, u32[]{:S(2)}) collective-permute-start(bf16[64,384]{1,0:T(8,128)(2,1)S(1)} %get-tuple-element.66), channel_id=1, source_target_pairs={{0,130},{16,146},{1,131},{17,147},{32,162},{48,178},{33,163},{49,1... | collective-permute-start | bytes 147464 | tf_op jit(solution)/shard_map/ppermute | solution.py:399
  117.0 4.8 %collective-permute-start.25 = (bf16[64,384]{1,0:T(8,128)(2,1)S(1)}, bf16[64,384]{1,0:T(8,128)(2,1)S(1)}, u32[]{:S(2)}, u32[]{:S(2)}) collective-permute-start(bf16[64,384]{1,0:T(8,128)(2,1)S(1)} %get-tuple-element.66), channel_id=1, source_target_pairs={{0,2},{16,18},{1,3},{17,19},{32,34},{48,50},{33,35},{49,51},{64,66... | collective-permute-start | bytes 147464 | tf_op jit(solution)/shard_map/ppermute | solution.py:400
  118.3 3.5 %collective-permute-start.26 = (bf16[64,384]{1,0:T(8,128)(2,1)S(1)}, bf16[64,384]{1,0:T(8,128)(2,1)S(1)}, u32[]{:S(2)}, u32[]{:S(2)}) collective-permute-start(bf16[64,384]{1,0:T(8,128)(2,1)S(1)} %get-tuple-element.66), channel_id=1, source_target_pairs={{0,18},{16,2},{1,19},{17,3},{32,50},{48,34},{33,51},{49,35},{64,82... | collective-permute-start | bytes 147464 | tf_op jit(solution)/shard_map/ppermute | solution.py:401
  122.5 3.2 %collective-permute-start.28 = (bf16[64,384]{1,0:T(8,128)(2,1)S(1)}, bf16[64,384]{1,0:T(8,128)(2,1)S(1)}, u32[]{:S(2)}, u32[]{:S(2)}) collective-permute-start(bf16[64,384]{1,0:T(8,128)(2,1)S(1)} %get-tuple-element.68), channel_id=1, source_target_pairs={{2,4},{18,20},{3,5},{19,21},{34,36},{50,52},{35,37},{51,53},{66,68... | collective-permute-start | bytes 147464 | tf_op jit(solution)/shard_map/ppermute | solution.py:400
  123.2 2.6 %collective-permute-start.29 = (bf16[64,384]{1,0:T(8,128)(2,1)S(1)}, bf16[64,384]{1,0:T(8,128)(2,1)S(1)}, u32[]{:S(2)}, u32[]{:S(2)}) collective-permute-start(bf16[64,384]{1,0:T(8,128)(2,1)S(1)} %get-tuple-element.68), channel_id=1, source_target_pairs={{2,20},{18,4},{3,21},{19,5},{34,52},{50,36},{35,53},{51,37},{66,84... | collective-permute-start | bytes 147464 | tf_op jit(solution)/shard_map/ppermute | solution.py:401
  125.8 4.4 %collective-permute-start.33 = (bf16[64,384]{1,0:T(8,128)(2,1)S(1)}, bf16[64,384]{1,0:T(8,128)(2,1)S(1)}, u32[]{:S(2)}, u32[]{:S(2)}) collective-permute-start(bf16[64,384]{1,0:T(8,128)(2,1)S(1)} %get-tuple-element.71), channel_id=1, source_target_pairs={{4,134},{20,150},{5,135},{21,151},{36,166},{52,182},{37,167},{53,1... | collective-permute-start | bytes 147464 | tf_op jit(solution)/shard_map/ppermute | solution.py:399
  126.5 5.7 %collective-permute-start.31 = (bf16[64,384]{1,0:T(8,128)(2,1)S(1)}, bf16[64,384]{1,0:T(8,128)(2,1)S(1)}, u32[]{:S(2)}, u32[]{:S(2)}) collective-permute-start(bf16[64,384]{1,0:T(8,128)(2,1)S(1)} %get-tuple-element.71), channel_id=1, source_target_pairs={{4,6},{20,22},{5,7},{21,23},{36,38},{52,54},{37,39},{53,55},{68,70... | collective-permute-start | bytes 147464 | tf_op jit(solution)/shard_map/ppermute | solution.py:400
  127.2 5.0 %collective-permute-start.32 = (bf16[64,384]{1,0:T(8,128)(2,1)S(1)}, bf16[64,384]{1,0:T(8,128)(2,1)S(1)}, u32[]{:S(2)}, u32[]{:S(2)}) collective-permute-start(bf16[64,384]{1,0:T(8,128)(2,1)S(1)} %get-tuple-element.71), channel_id=1, source_target_pairs={{4,22},{20,6},{5,23},{21,7},{36,54},{52,38},{37,55},{53,39},{68,86... | collective-permute-start | bytes 147464 | tf_op jit(solution)/shard_map/ppermute | solution.py:401
  138.7 28.1 %all-to-all-start.1 = ((bf16[16,2,768]{2,1,0:T(2,128)(2,1)}), bf16[16,2,768]{2,1,0:T(2,128)(2,1)S(1)}, u32[]{:S(2)}, u32[]{:S(2)}) async-start(bf16[16,2,768]{2,1,0:T(2,128)(2,1)} %bitcast.18), calls=%async_computation.1 | async-start | bytes 98304 | tf_op jit(solution)/shard_map/all_to_all | solution.py:408
  (13 other events, 162.3 us)

commit v10 on v9

--- a/solution.py
+++ b/solution.py
@@ -210,21 +210,11 @@
     turn.wait()
 
 
-def stale_kernel(stale_ref, out_ref, sem):
-    copies = []
+def stale_kernel(stale_ref, out_ref):
     for slot in range(2 * 4 * 2):
         m = slot // 8 * 2 + slot % 2
-        for part in range(2):
-            copies.append(
-                pltpu.make_async_copy(
-                    stale_ref.at[:, part * D + m * PART : part * D + (m + 1) * PART],
-                    out_ref.at[slot, :, part * PART : (part + 1) * PART],
-                    sem,
-                )
-            )
-            copies[-1].start()
-    for copy in copies:
-        copy.wait()
+        out_ref[slot, :, :PART] = stale_ref[:, m * PART : (m + 1) * PART]
+        out_ref[slot, :, PART:] = stale_ref[:, D + m * PART : D + (m + 1) * PART]
 
 
 def join_kernel(first_ref, second_ref, turn0_ref, turn1_ref, own_ref):
@@ -346,7 +336,7 @@
     moved = [lax.ppermute(half, AXES, edges) for edges in MAIN]
     turned = [lax.ppermute(turn, AXES, edges) for edges in TURN]
     (outgoing,) = whole_call(
-        stale_kernel, [stale_kv[0, 0]], [(2 * 4 * 2, LOCAL, 2 * PART)], [pltpu.SemaphoreType.DMA]
+        stale_kernel, [stale_kv[0, 0]], [(2 * 4 * 2, LOCAL, 2 * PART)]
     )
     kv = lax.all_to_all(outgoing, ("xl", "yh", "core"), split_axis=0, concat_axis=0, tiled=True)
     kv = kv.reshape(TOKENS // 2, 2 * PART)

time: 169 us -> 169 us (level)
  no operation moved by 1% of the time
where the time goes in v10:
time: 169 us; the launch traced here: 167 us
  starting transfers between devices  96 us (57%)
  blocking collectives  34.5 us (20%)
  waiting for transfers between devices  17.5 us (10%)
  local copies, waits for them, and re-layouts  9.4 us (6%)
  Pallas kernels  6.81 us (4%)
  between operations  2.03 us (1%)
    all_to_all x1, starting transfers between devices, body(): lax.all_to_all(finals, ('section', 'cfg'), split_axis=0, concat_axis=0, t...  20.6 us
    all_gather x7, blocking collectives, body(): far = lax.all_gather(far, 'core', axis=0, tiled=False)  13.6 us
    ppermute x7, starting transfers between devices, body(): far = lax.ppermute(state, AXES, onward(tick, 1, 0))  12.5 us
    ppermute x7, starting transfers between devices, body(): cross = lax.ppermute(state, AXES, onward(tick, 0, 1))  10.6 us
    all_to_all x1, starting transfers between devices, body(): lax.all_to_all(outgoing, ('xl', 'yh', 'core'), split_axis=0, concat_axis=...  10.2 us
    all_gather x1, blocking collectives, body(): x = lax.all_gather(entering, ('xl', 'core'), axis=0, tiled=True)  8.52 us
    ppermute x2, starting transfers between devices, body(): up2, down2 = (lax.ppermute(up1, AXES, UP), lax.ppermute(down1, AXES, DOWN))  7.02 us
    ppermute x2, starting transfers between devices, body(): up3, down3 = (lax.ppermute(up2, AXES, UP), lax.ppermute(down2, AXES, DOWN))  6.76 us
  transfers between devices with their start and end apart: 36, of which 8 were waited for; matrix products, arithmetic and copies ran while one was open for 2% of the time, Pallas kernels for 3%

profile of v10, /device:TPU:1, one launch (start us, length us, event | category | flops | bytes accessed | tf_op | source)
XLA Modules:
  0.0 167.3 jit_solution(12778168148499717804)
XLA Ops:
  2.4 10.2 %all-to-all-start = ((bf16[16,16,768]{2,1,0:T(8,128)(2,1)}), bf16[16,16,768]{2,1,0:T(8,128)(2,1)S(1)}, u32[]{:S(2)}, u32[]{:S(2)}) async-start(bf16[16,16,768]{2,1,0:T(8,128)(2,1)} %stale_kernel.1), calls=%async_computation | async-start | bytes 786432 | tf_op jit(solution)/shard_map/all_to_all | solution.py:341
  13.7 3.7 %collective-permute-start = (bf16[144,768]{1,0:T(8,128)(2,1)S(1)}, bf16[144,768]{1,0:T(8,128)(2,1)S(1)}, u32[]{:S(2)}, u32[]{:S(2)}) collective-permute-start(bf16[144,768]{1,0:T(8,128)(2,1)S(1)} %get-tuple-element.40), channel_id=1, source_target_pairs={{0,0},{2,2},{4,4},{6,6},{8,8},{10,10},{12,12},{14,14},{16,256},{18... | collective-permute-start | bytes 663560 | tf_op jit(solution)/shard_map/ppermute | solution.py:336
  17.4 1.9 %collective-permute-start.1 = (bf16[144,768]{1,0:T(8,128)(2,1)S(1)}, bf16[144,768]{1,0:T(8,128)(2,1)S(1)}, u32[]{:S(2)}, u32[]{:S(2)}) collective-permute-start(bf16[144,768]{1,0:T(8,128)(2,1)S(1)} %get-tuple-element.40), channel_id=1, source_target_pairs={{0,256},{2,258},{4,260},{6,262},{8,264},{10,266},{12,268},{14,270}... | collective-permute-start | bytes 663560 | tf_op jit(solution)/shard_map/ppermute | solution.py:336
  20.7 1.8 %collective-permute-done.first_ref = bf16[144,768]{1,0:T(8,128)(2,1)S(1)} collective-permute-done((bf16[144,768]{1,0:T(8,128)(2,1)S(1)}, bf16[144,768]{1,0:T(8,128)(2,1)S(1)}, u32[]{:S(2)}, u32[]{:S(2)}) %collective-permute-start) | collective-permute-done | bytes 221216 | tf_op jit(solution)/shard_map/ppermute | solution.py:336
  22.5 2.8 %collective-permute-done.1.second_ref = bf16[144,768]{1,0:T(8,128)(2,1)S(1)} collective-permute-done((bf16[144,768]{1,0:T(8,128)(2,1)S(1)}, bf16[144,768]{1,0:T(8,128)(2,1)S(1)}, u32[]{:S(2)}, u32[]{:S(2)}) %collective-permute-start.1) | collective-permute-done | bytes 221216 | tf_op jit(solution)/shard_map/ppermute | solution.py:336
  25.3 2.3 %collective-permute-start.5 = (bf16[288,768]{1,0:T(8,128)(2,1)S(1)}, bf16[288,768]{1,0:T(8,128)(2,1)S(1)}, u32[]{:S(2)}, u32[]{:S(2)}) collective-permute-start(bf16[288,768]{1,0:T(8,128)(2,1)S(1)} %join_kernel.1.refs_0_), channel_id=1, source_target_pairs={{0,97},{2,99},{4,101},{6,103},{8,105},{10,107},{12,109},{14,111},{... | collective-permute-start | bytes 1327112 | tf_op jit(solution)/shard_map/ppermute | solution.py:344
  27.6 4.2 %collective-permute-start.4 = (bf16[288,768]{1,0:T(8,128)(2,1)S(1)}, bf16[288,768]{1,0:T(8,128)(2,1)S(1)}, u32[]{:S(2)}, u32[]{:S(2)}) collective-permute-start(bf16[288,768]{1,0:T(8,128)(2,1)S(1)} %join_kernel.1.refs_0_), channel_id=1, source_target_pairs={{0,1},{2,3},{4,5},{6,7},{8,9},{10,11},{12,13},{14,15},{16,113},{18... | collective-permute-start | bytes 1327112 | tf_op jit(solution)/shard_map/ppermute | solution.py:344
  33.4 2.2 %collective-permute-done.5.refs_2_ = bf16[288,768]{1,0:T(8,128)(2,1)S(1)} collective-permute-done((bf16[288,768]{1,0:T(8,128)(2,1)S(1)}, bf16[288,768]{1,0:T(8,128)(2,1)S(1)}, u32[]{:S(2)}, u32[]{:S(2)}) %collective-permute-start.5) | collective-permute-done | bytes 442400 | tf_op jit(solution)/shard_map/ppermute | solution.py:344
  35.6 1.9 %collective-permute-start.7 = (bf16[288,768]{1,0:T(8,128)(2,1)S(1)}, bf16[288,768]{1,0:T(8,128)(2,1)}, u32[]{:S(2)}, u32[]{:S(2)}) collective-permute-start(bf16[288,768]{1,0:T(8,128)(2,1)S(1)} %collective-permute-done.5.refs_2_), channel_id=1, source_target_pairs={{0,97},{2,99},{4,101},{6,103},{8,105},{10,107},{12,109},{14,111},{... | collective-permute-start | bytes 1327112 | tf_op jit(solution)/shard_map/ppermute | solution.py:348
  37.5 4.3 %collective-permute-done.4.refs_1_ = bf16[288,768]{1,0:T(8,128)(2,1)S(1)} collective-permute-done((bf16[288,768]{1,0:T(8,128)(2,1)S(1)}, bf16[288,768]{1,0:T(8,128)(2,1)S(1)}, u32[]{:S(2)}, u32[]{:S(2)}) %collective-permute-start.4) | collective-permute-done | bytes 442400 | tf_op jit(solution)/shard_map/ppermute | solution.py:344
  41.8 5.1 %collective-permute-start.6 = (bf16[288,768]{1,0:T(8,128)(2,1)S(1)}, bf16[288,768]{1,0:T(8,128)(2,1)}, u32[]{:S(2)}, u32[]{:S(2)}) collective-permute-start(bf16[288,768]{1,0:T(8,128)(2,1)S(1)} %collective-permute-done.4.refs_1_), channel_id=1, source_target_pairs={{0,1},{2,3},{4,5},{6,7},{8,9},{10,11},{12,13},{14,15},{16,113},{18... | collective-permute-start | bytes 1327112 | tf_op jit(solution)/shard_map/ppermute | solution.py:348
  47.9 8.5 %all_gather.57 = bf16[64,1536]{1,0:T(8,128)(2,1)} all-gather(bf16[16,1536]{1,0:T(8,128)(2,1)S(1)} %bitcast.66), channel_id=1, replica_groups=mesh['xh'=2,'xl'=2,'yh'=4,'core'=2,'section'=8,'cfg'=2] {'xl','core'}, dimensions={0}, use_global_device_ids=true | all-gather | bytes 245760 | tf_op jit(solution)/shard_map/all_gather | solution.py:347
  56.4 2.3 %collective-permute-start.9 = (bf16[288,768]{1,0:T(8,128)(2,1)}, bf16[288,768]{1,0:T(8,128)(2,1)S(1)}, u32[]{:S(2)}, u32[]{:S(2)}) collective-permute-start(bf16[288,768]{1,0:T(8,128)(2,1)} %collective-permute-done.7.refs_4_), channel_id=1, source_target_pairs={{0,97},{2,99},{4,101},{6,103},{8,105},{10,107},{12,109},{14,111},{... | collective-permute-start | bytes 1327112 | tf_op jit(solution)/shard_map/ppermute | solution.py:350
  58.8 4.4 %collective-permute-start.8 = (bf16[288,768]{1,0:T(8,128)(2,1)}, bf16[288,768]{1,0:T(8,128)(2,1)S(1)}, u32[]{:S(2)}, u32[]{:S(2)}) collective-permute-start(bf16[288,768]{1,0:T(8,128)(2,1)} %collective-permute-done.6.refs_3_), channel_id=1, source_target_pairs={{0,1},{2,3},{4,5},{6,7},{8,9},{10,11},{12,13},{14,15},{16,113},{18... | collective-permute-start | bytes 1327112 | tf_op jit(solution)/shard_map/ppermute | solution.py:350
  63.4 1.9 %collective-permute-start.12 = (bf16[256,768]{1,0:T(8,128)(2,1)S(1)}, bf16[256,768]{1,0:T(8,128)(2,1)S(1)}, u32[]{:S(2)}, u32[]{:S(2)}) collective-permute-start(bf16[256,768]{1,0:T(8,128)(2,1)S(1)} %bitcast.41), channel_id=1, source_target_pairs={{0,256},{1,257},{2,258},{3,259},{4,260},{5,261},{6,262},{7,263},{8... | collective-permute-start | bytes 1179656 | tf_op jit(solution)/shard_map/ppermute | solution.py:346
  67.2 1.9 %collective-permute-start.11 = (bf16[144,768]{1,0:T(8,128)(2,1)S(1)}, bf16[144,768]{1,0:T(8,128)(2,1)S(1)}, u32[]{:S(2)}, u32[]{:S(2)}) collective-permute-start(bf16[144,768]{1,0:T(8,128)(2,1)S(1)} %slice.24), channel_id=1, source_target_pairs={{0,97},{2,99},{4,101},{6,103},{8,105},{10,107},{12,109},{14,111},{... | collective-permute-start | bytes 663560 | tf_op jit(solution)/shard_map/ppermute | solution.py:352
  69.1 4.3 %collective-permute-done.8.refs_0_.refs_5_ = bf16[288,768]{1,0:T(8,128)(2,1)S(1)} collective-permute-done((bf16[288,768]{1,0:T(8,128)(2,1)}, bf16[288,768]{1,0:T(8,128)(2,1)S(1)}, u32[]{:S(2)}, u32[]{:S(2)}) %collective-permute-start.8) | collective-permute-done | bytes 442400 | tf_op jit(solution)/shard_map/ppermute | solution.py:350
  73.5 5.2 %collective-permute-start.10 = (bf16[144,768]{1,0:T(8,128)(2,1)S(1)}, bf16[144,768]{1,0:T(8,128)(2,1)S(1)}, u32[]{:S(2)}, u32[]{:S(2)}) collective-permute-start(bf16[144,768]{1,0:T(8,128)(2,1)S(1)} %slice.23), channel_id=1, source_target_pairs={{0,1},{2,3},{4,5},{6,7},{8,9},{10,11},{12,13},{14,15},{16,113},{18... | collective-permute-start | bytes 663560 | tf_op jit(solution)/shard_map/ppermute | solution.py:351
  79.7 2.1 %place_first.1.refs_4_ = bf16[1152,1536]{1,0:T(8,128)(2,1)S(1)} custom-call(bf16[288,768]{1,0:T(8,128)(2,1)S(1)} %join_kernel.1.refs_0_, bf16[288,768]{1,0:T(8,128)(2,1)S(1)} %copy-done.4, bf16[288,768]{1,0:T(8,128)(2,1)S(1)} %collective-permute-done.5.refs_2_, bf16[288,768]{1,0:T(8,128)(2,1)} %collective-permute-done.6.refs_3_, ...), custom_call_target="tpu_custom_call" | custom-call | tf_op jit(solution)/shard_map/place_first/pallas_call | solution.py:280
  88.9 5.9 %collective-permute-start.14 = (bf16[64,384]{1,0:T(8,128)(2,1)S(1)}, bf16[64,384]{1,0:T(8,128)(2,1)S(1)}, u32[]{:S(2)}, u32[]{:S(2)}) collective-permute-start(bf16[64,384]{1,0:T(8,128)(2,1)S(1)} %get-tuple-element.49), channel_id=1, source_target_pairs={{0,18},{16,2},{1,19},{17,3},{32,50},{48,34},{33,51},{49,35},{64,82... | collective-permute-start | bytes 147464 | tf_op jit(solution)/shard_map/ppermute | solution.py:391
  95.0 2.0 %all-gather = bf16[128,384]{1,0:T(8,128)(2,1)S(1)} all-gather(bf16[64,384]{1,0:T(8,128)(2,1)S(1)} %collective-permute-done.15), channel_id=2, replica_groups=mesh['xh'=2,'xl'=2,'yh'=4,'core'=2,'section'=8,'cfg'=2] {'core'}, dimensions={0}, use_global_device_ids=true | all-gather | bytes 147456 | tf_op jit(solution)/shard_map/all_gather | solution.py:392
  99.0 1.9 %all-gather.1 = bf16[128,384]{1,0:T(8,128)(2,1)S(1)} all-gather(bf16[64,384]{1,0:T(8,128)(2,1)S(1)} %collective-permute-done.18), channel_id=3, replica_groups=mesh['xh'=2,'xl'=2,'yh'=4,'core'=2,'section'=8,'cfg'=2] {'core'}, dimensions={0}, use_global_device_ids=true | all-gather | bytes 147456 | tf_op jit(solution)/shard_map/all_gather | solution.py:392
  103.0 1.9 %all-gather.2 = bf16[128,384]{1,0:T(8,128)(2,1)S(1)} all-gather(bf16[64,384]{1,0:T(8,128)(2,1)S(1)} %collective-permute-done.21), channel_id=4, replica_groups=mesh['xh'=2,'xl'=2,'yh'=4,'core'=2,'section'=8,'cfg'=2] {'core'}, dimensions={0}, use_global_device_ids=true | all-gather | bytes 147456 | tf_op jit(solution)/shard_map/all_gather | solution.py:392
  107.1 1.9 %all-gather.3 = bf16[128,384]{1,0:T(8,128)(2,1)S(1)} all-gather(bf16[64,384]{1,0:T(8,128)(2,1)S(1)} %collective-permute-done.24), channel_id=5, replica_groups=mesh['xh'=2,'xl'=2,'yh'=4,'core'=2,'section'=8,'cfg'=2] {'core'}, dimensions={0}, use_global_device_ids=true | all-gather | bytes 147456 | tf_op jit(solution)/shard_map/all_gather | solution.py:392
  109.0 7.9 %collective-permute-start.27 = (bf16[64,384]{1,0:T(8,128)(2,1)S(1)}, bf16[64,384]{1,0:T(8,128)(2,1)S(1)}, u32[]{:S(2)}, u32[]{:S(2)}) collective-permute-start(bf16[64,384]{1,0:T(8,128)(2,1)S(1)} %get-tuple-element.66), channel_id=1, source_target_pairs={{0,130},{16,146},{1,131},{17,147},{32,162},{48,178},{33,163},{49,1... | collective-permute-start | bytes 147464 | tf_op jit(solution)/shard_map/ppermute | solution.py:389
  119.5 2.2 %all-gather.4 = bf16[128,384]{1,0:T(8,128)(2,1)S(1)} all-gather(bf16[64,384]{1,0:T(8,128)(2,1)S(1)} %collective-permute-done.27), channel_id=6, replica_groups=mesh['xh'=2,'xl'=2,'yh'=4,'core'=2,'section'=8,'cfg'=2] {'core'}, dimensions={0}, use_global_device_ids=true | all-gather | bytes 147456 | tf_op jit(solution)/shard_map/all_gather | solution.py:392
  123.7 1.9 %all-gather.5 = bf16[128,384]{1,0:T(8,128)(2,1)S(1)} all-gather(bf16[64,384]{1,0:T(8,128)(2,1)S(1)} %collective-permute-done.30), channel_id=7, replica_groups=mesh['xh'=2,'xl'=2,'yh'=4,'core'=2,'section'=8,'cfg'=2] {'core'}, dimensions={0}, use_global_device_ids=true | all-gather | bytes 147456 | tf_op jit(solution)/shard_map/all_gather | solution.py:392
  127.7 2.0 %copy-done.2 = bf16[1536,1152]{1,0:T(8,128)(2,1)S(1)} copy-done((bf16[1536,1152]{1,0:T(8,128)(2,1)S(1)}, bf16[1536,1152]{1,0:T(8,128)(2,1)}, u32[]{:S(2)}) %copy-start.2) | copy-done | bytes 3538968
  130.1 1.9 %all-gather.6 = bf16[128,384]{1,0:T(8,128)(2,1)S(1)} all-gather(bf16[64,384]{1,0:T(8,128)(2,1)S(1)} %collective-permute-done.33), channel_id=8, replica_groups=mesh['xh'=2,'xl'=2,'yh'=4,'core'=2,'section'=8,'cfg'=2] {'core'}, dimensions={0}, use_global_device_ids=true | all-gather | bytes 147456 | tf_op jit(solution)/shard_map/all_gather | solution.py:392
  132.0 5.8 %all-gather.7 = bf16[256,384]{1,0:T(8,128)(2,1)S(1)} all-gather(bf16[64,384]{1,0:T(8,128)(2,1)S(1)} %get-tuple-element.74), channel_id=9, replica_groups=mesh['xh'=2,'xl'=2,'yh'=4,'core'=2,'section'=8,'cfg'=2] {'xl','core'}, dimensions={0}, use_global_device_ids=true | all-gather | bytes 245760 | tf_op jit(solution)/shard_map/all_gather | solution.py:394
  138.5 20.6 %all-to-all-start.1 = ((bf16[16,2,768]{2,1,0:T(2,128)(2,1)}), bf16[16,2,768]{2,1,0:T(2,128)(2,1)S(1)}, u32[]{:S(2)}, u32[]{:S(2)}) async-start(bf16[16,2,768]{2,1,0:T(2,128)(2,1)} %bitcast.18), calls=%async_computation.1 | async-start | bytes 98304 | tf_op jit(solution)/shard_map/all_to_all | solution.py:398
  159.1 6.6 %all-gather.8 = bf16[256,768]{1,0:T(8,128)(2,1)S(1)} all-gather(bf16[64,768]{1,0:T(8,128)(2,1)S(1)} %get-tuple-element.75), channel_id=10, replica_groups=mesh['xh'=2,'xl'=2,'yh'=4,'core'=2,'section'=8,'cfg'=2] {'xl','core'}, dimensions={0}, use_global_device_ids=true | all-gather | bytes 491520 | tf_op jit(solution)/shard_map/all_gather | solution.py:399
  (111 shorter events, 31.8 us)
Async XLA Ops:
  2.4 39.4 %all-to-all-start = ((bf16[16,16,768]{2,1,0:T(8,128)(2,1)}), bf16[16,16,768]{2,1,0:T(8,128)(2,1)S(1)}, u32[]{:S(2)}, u32[]{:S(2)}) async-start(bf16[16,16,768]{2,1,0:T(8,128)(2,1)} %stale_kernel.1), calls=%async_computation | async-start | bytes 786432 | tf_op jit(solution)/shard_map/all_to_all | solution.py:341
  13.7 8.8 %collective-permute-start = (bf16[144,768]{1,0:T(8,128)(2,1)S(1)}, bf16[144,768]{1,0:T(8,128)(2,1)S(1)}, u32[]{:S(2)}, u32[]{:S(2)}) collective-permute-start(bf16[144,768]{1,0:T(8,128)(2,1)S(1)} %get-tuple-element.40), channel_id=1, source_target_pairs={{0,0},{2,2},{4,4},{6,6},{8,8},{10,10},{12,12},{14,14},{16,256},{18... | collective-permute-start | bytes 663560 | tf_op jit(solution)/shard_map/ppermute | solution.py:336
  17.4 7.9 %collective-permute-start.1 = (bf16[144,768]{1,0:T(8,128)(2,1)S(1)}, bf16[144,768]{1,0:T(8,128)(2,1)S(1)}, u32[]{:S(2)}, u32[]{:S(2)}) collective-permute-start(bf16[144,768]{1,0:T(8,128)(2,1)S(1)} %get-tuple-element.40), channel_id=1, source_target_pairs={{0,256},{2,258},{4,260},{6,262},{8,264},{10,266},{12,268},{14,270}... | collective-permute-start | bytes 663560 | tf_op jit(solution)/shard_map/ppermute | solution.py:336
  25.3 10.3 %collective-permute-start.5 = (bf16[288,768]{1,0:T(8,128)(2,1)S(1)}, bf16[288,768]{1,0:T(8,128)(2,1)S(1)}, u32[]{:S(2)}, u32[]{:S(2)}) collective-permute-start(bf16[288,768]{1,0:T(8,128)(2,1)S(1)} %join_kernel.1.refs_0_), channel_id=1, source_target_pairs={{0,97},{2,99},{4,101},{6,103},{8,105},{10,107},{12,109},{14,111},{... | collective-permute-start | bytes 1327112 | tf_op jit(solution)/shard_map/ppermute | solution.py:344
  27.6 14.1 %collective-permute-start.4 = (bf16[288,768]{1,0:T(8,128)(2,1)S(1)}, bf16[288,768]{1,0:T(8,128)(2,1)S(1)}, u32[]{:S(2)}, u32[]{:S(2)}) collective-permute-start(bf16[288,768]{1,0:T(8,128)(2,1)S(1)} %join_kernel.1.refs_0_), channel_id=1, source_target_pairs={{0,1},{2,3},{4,5},{6,7},{8,9},{10,11},{12,13},{14,15},{16,113},{18... | collective-permute-start | bytes 1327112 | tf_op jit(solution)/shard_map/ppermute | solution.py:344
  35.6 20.8 %collective-permute-start.7 = (bf16[288,768]{1,0:T(8,128)(2,1)S(1)}, bf16[288,768]{1,0:T(8,128)(2,1)}, u32[]{:S(2)}, u32[]{:S(2)}) collective-permute-start(bf16[288,768]{1,0:T(8,128)(2,1)S(1)} %collective-permute-done.5.refs_2_), channel_id=1, source_target_pairs={{0,97},{2,99},{4,101},{6,103},{8,105},{10,107},{12,109},{14,111},{... | collective-permute-start | bytes 1327112 | tf_op jit(solution)/shard_map/ppermute | solution.py:348
  41.8 17.0 %collective-permute-start.6 = (bf16[288,768]{1,0:T(8,128)(2,1)S(1)}, bf16[288,768]{1,0:T(8,128)(2,1)}, u32[]{:S(2)}, u32[]{:S(2)}) collective-permute-start(bf16[288,768]{1,0:T(8,128)(2,1)S(1)} %collective-permute-done.4.refs_1_), channel_id=1, source_target_pairs={{0,1},{2,3},{4,5},{6,7},{8,9},{10,11},{12,13},{14,15},{16,113},{18... | collective-permute-start | bytes 1327112 | tf_op jit(solution)/shard_map/ppermute | solution.py:348
  56.4 10.7 %collective-permute-start.9 = (bf16[288,768]{1,0:T(8,128)(2,1)}, bf16[288,768]{1,0:T(8,128)(2,1)S(1)}, u32[]{:S(2)}, u32[]{:S(2)}) collective-permute-start(bf16[288,768]{1,0:T(8,128)(2,1)} %collective-permute-done.7.refs_4_), channel_id=1, source_target_pairs={{0,97},{2,99},{4,101},{6,103},{8,105},{10,107},{12,109},{14,111},{... | collective-permute-start | bytes 1327112 | tf_op jit(solution)/shard_map/ppermute | solution.py:350
  58.8 14.6 %collective-permute-start.8 = (bf16[288,768]{1,0:T(8,128)(2,1)}, bf16[288,768]{1,0:T(8,128)(2,1)S(1)}, u32[]{:S(2)}, u32[]{:S(2)}) collective-permute-start(bf16[288,768]{1,0:T(8,128)(2,1)} %collective-permute-done.6.refs_3_), channel_id=1, source_target_pairs={{0,1},{2,3},{4,5},{6,7},{8,9},{10,11},{12,13},{14,15},{16,113},{18... | collective-permute-start | bytes 1327112 | tf_op jit(solution)/shard_map/ppermute | solution.py:350
  63.4 21.5 %collective-permute-start.12 = (bf16[256,768]{1,0:T(8,128)(2,1)S(1)}, bf16[256,768]{1,0:T(8,128)(2,1)S(1)}, u32[]{:S(2)}, u32[]{:S(2)}) collective-permute-start(bf16[256,768]{1,0:T(8,128)(2,1)S(1)} %bitcast.41), channel_id=1, source_target_pairs={{0,256},{1,257},{2,258},{3,259},{4,260},{5,261},{6,262},{7,263},{8... | collective-permute-start | bytes 1179656 | tf_op jit(solution)/shard_map/ppermute | solution.py:346
  67.2 14.6 %collective-permute-start.11 = (bf16[144,768]{1,0:T(8,128)(2,1)S(1)}, bf16[144,768]{1,0:T(8,128)(2,1)S(1)}, u32[]{:S(2)}, u32[]{:S(2)}) collective-permute-start(bf16[144,768]{1,0:T(8,128)(2,1)S(1)} %slice.24), channel_id=1, source_target_pairs={{0,97},{2,99},{4,101},{6,103},{8,105},{10,107},{12,109},{14,111},{... | collective-permute-start | bytes 663560 | tf_op jit(solution)/shard_map/ppermute | solution.py:352
  73.5 9.7 %collective-permute-start.10 = (bf16[144,768]{1,0:T(8,128)(2,1)S(1)}, bf16[144,768]{1,0:T(8,128)(2,1)S(1)}, u32[]{:S(2)}, u32[]{:S(2)}) collective-permute-start(bf16[144,768]{1,0:T(8,128)(2,1)S(1)} %slice.23), channel_id=1, source_target_pairs={{0,1},{2,3},{4,5},{6,7},{8,9},{10,11},{12,13},{14,15},{16,113},{18... | collective-permute-start | bytes 663560 | tf_op jit(solution)/shard_map/ppermute | solution.py:351
  86.3 8.6 %collective-permute-start.15 = (bf16[64,384]{1,0:T(8,128)(2,1)S(1)}, bf16[64,384]{1,0:T(8,128)(2,1)S(1)}, u32[]{:S(2)}, u32[]{:S(2)}) collective-permute-start(bf16[64,384]{1,0:T(8,128)(2,1)S(1)} %get-tuple-element.49), channel_id=1, source_target_pairs={{0,130},{16,146},{1,131},{17,147},{32,162},{48,178},{33,163},{49,1... | collective-permute-start | bytes 147464 | tf_op jit(solution)/shard_map/ppermute | solution.py:389
  87.6 9.3 %collective-permute-start.13 = (bf16[64,384]{1,0:T(8,128)(2,1)S(1)}, bf16[64,384]{1,0:T(8,128)(2,1)S(1)}, u32[]{:S(2)}, u32[]{:S(2)}) collective-permute-start(bf16[64,384]{1,0:T(8,128)(2,1)S(1)} %get-tuple-element.49), channel_id=1, source_target_pairs={{0,2},{16,18},{1,3},{17,19},{32,34},{48,50},{33,35},{49,51},{64,66... | collective-permute-start | bytes 147464 | tf_op jit(solution)/shard_map/ppermute | solution.py:390
  88.9 8.0 %collective-permute-start.14 = (bf16[64,384]{1,0:T(8,128)(2,1)S(1)}, bf16[64,384]{1,0:T(8,128)(2,1)S(1)}, u32[]{:S(2)}, u32[]{:S(2)}) collective-permute-start(bf16[64,384]{1,0:T(8,128)(2,1)S(1)} %get-tuple-element.49), channel_id=1, source_target_pairs={{0,18},{16,2},{1,19},{17,3},{32,50},{48,34},{33,51},{49,35},{64,82... | collective-permute-start | bytes 147464 | tf_op jit(solution)/shard_map/ppermute | solution.py:391
  97.0 2.0 %collective-permute-start.18 = (bf16[64,384]{1,0:T(8,128)(2,1)S(1)}, bf16[64,384]{1,0:T(8,128)(2,1)S(1)}, u32[]{:S(2)}, u32[]{:S(2)}) collective-permute-start(bf16[64,384]{1,0:T(8,128)(2,1)S(1)} %get-tuple-element.60), channel_id=1, source_target_pairs={{2,132},{18,148},{3,133},{19,149},{34,164},{50,180},{35,165},{51,1... | collective-permute-start | bytes 147464 | tf_op jit(solution)/shard_map/ppermute | solution.py:389
  97.7 3.2 %collective-permute-start.16 = (bf16[64,384]{1,0:T(8,128)(2,1)S(1)}, bf16[64,384]{1,0:T(8,128)(2,1)S(1)}, u32[]{:S(2)}, u32[]{:S(2)}) collective-permute-start(bf16[64,384]{1,0:T(8,128)(2,1)S(1)} %get-tuple-element.60), channel_id=1, source_target_pairs={{2,4},{18,20},{3,5},{19,21},{34,36},{50,52},{35,37},{51,53},{66,68... | collective-permute-start | bytes 147464 | tf_op jit(solution)/shard_map/ppermute | solution.py:390
  98.3 2.6 %collective-permute-start.17 = (bf16[64,384]{1,0:T(8,128)(2,1)S(1)}, bf16[64,384]{1,0:T(8,128)(2,1)S(1)}, u32[]{:S(2)}, u32[]{:S(2)}) collective-permute-start(bf16[64,384]{1,0:T(8,128)(2,1)S(1)} %get-tuple-element.60), channel_id=1, source_target_pairs={{2,20},{18,4},{3,21},{19,5},{34,52},{50,36},{35,53},{51,37},{66,84... | collective-permute-start | bytes 147464 | tf_op jit(solution)/shard_map/ppermute | solution.py:391
  101.6 3.2 %collective-permute-start.19 = (bf16[64,384]{1,0:T(8,128)(2,1)S(1)}, bf16[64,384]{1,0:T(8,128)(2,1)S(1)}, u32[]{:S(2)}, u32[]{:S(2)}) collective-permute-start(bf16[64,384]{1,0:T(8,128)(2,1)S(1)} %get-tuple-element.62), channel_id=1, source_target_pairs={{4,6},{20,22},{5,7},{21,23},{36,38},{52,54},{37,39},{53,55},{68,70... | collective-permute-start | bytes 147464 | tf_op jit(solution)/shard_map/ppermute | solution.py:390
  102.3 2.6 %collective-permute-start.20 = (bf16[64,384]{1,0:T(8,128)(2,1)S(1)}, bf16[64,384]{1,0:T(8,128)(2,1)S(1)}, u32[]{:S(2)}, u32[]{:S(2)}) collective-permute-start(bf16[64,384]{1,0:T(8,128)(2,1)S(1)} %get-tuple-element.62), channel_id=1, source_target_pairs={{4,22},{20,6},{5,23},{21,7},{36,54},{52,38},{37,55},{53,39},{68,86... | collective-permute-start | bytes 147464 | tf_op jit(solution)/shard_map/ppermute | solution.py:391
  105.0 2.0 %collective-permute-start.24 = (bf16[64,384]{1,0:T(8,128)(2,1)S(1)}, bf16[64,384]{1,0:T(8,128)(2,1)S(1)}, u32[]{:S(2)}, u32[]{:S(2)}) collective-permute-start(bf16[64,384]{1,0:T(8,128)(2,1)S(1)} %get-tuple-element.64), channel_id=1, source_target_pairs={{6,136},{22,152},{7,137},{23,153},{38,168},{54,184},{39,169},{55,1... | collective-permute-start | bytes 147464 | tf_op jit(solution)/shard_map/ppermute | solution.py:389
  105.7 3.2 %collective-permute-start.22 = (bf16[64,384]{1,0:T(8,128)(2,1)S(1)}, bf16[64,384]{1,0:T(8,128)(2,1)S(1)}, u32[]{:S(2)}, u32[]{:S(2)}) collective-permute-start(bf16[64,384]{1,0:T(8,128)(2,1)S(1)} %get-tuple-element.64), channel_id=1, source_target_pairs={{6,8},{22,24},{7,9},{23,25},{38,40},{54,56},{39,41},{55,57},{70,72... | collective-permute-start | bytes 147464 | tf_op jit(solution)/shard_map/ppermute | solution.py:390
  106.4 2.6 %collective-permute-start.23 = (bf16[64,384]{1,0:T(8,128)(2,1)S(1)}, bf16[64,384]{1,0:T(8,128)(2,1)S(1)}, u32[]{:S(2)}, u32[]{:S(2)}) collective-permute-start(bf16[64,384]{1,0:T(8,128)(2,1)S(1)} %get-tuple-element.64), channel_id=1, source_target_pairs={{6,24},{22,8},{7,25},{23,9},{38,56},{54,40},{39,57},{55,41},{70,88... | collective-permute-start | bytes 147464 | tf_op jit(solution)/shard_map/ppermute | solution.py:391
  109.0 10.5 %collective-permute-start.27 = (bf16[64,384]{1,0:T(8,128)(2,1)S(1)}, bf16[64,384]{1,0:T(8,128)(2,1)S(1)}, u32[]{:S(2)}, u32[]{:S(2)}) collective-permute-start(bf16[64,384]{1,0:T(8,128)(2,1)S(1)} %get-tuple-element.66), channel_id=1, source_target_pairs={{0,130},{16,146},{1,131},{17,147},{32,162},{48,178},{33,163},{49,1... | collective-permute-start | bytes 147464 | tf_op jit(solution)/shard_map/ppermute | solution.py:389
  116.9 4.8 %collective-permute-start.25 = (bf16[64,384]{1,0:T(8,128)(2,1)S(1)}, bf16[64,384]{1,0:T(8,128)(2,1)S(1)}, u32[]{:S(2)}, u32[]{:S(2)}) collective-permute-start(bf16[64,384]{1,0:T(8,128)(2,1)S(1)} %get-tuple-element.66), channel_id=1, source_target_pairs={{0,2},{16,18},{1,3},{17,19},{32,34},{48,50},{33,35},{49,51},{64,66... | collective-permute-start | bytes 147464 | tf_op jit(solution)/shard_map/ppermute | solution.py:390
  118.2 3.5 %collective-permute-start.26 = (bf16[64,384]{1,0:T(8,128)(2,1)S(1)}, bf16[64,384]{1,0:T(8,128)(2,1)S(1)}, u32[]{:S(2)}, u32[]{:S(2)}) collective-permute-start(bf16[64,384]{1,0:T(8,128)(2,1)S(1)} %get-tuple-element.66), channel_id=1, source_target_pairs={{0,18},{16,2},{1,19},{17,3},{32,50},{48,34},{33,51},{49,35},{64,82... | collective-permute-start | bytes 147464 | tf_op jit(solution)/shard_map/ppermute | solution.py:391
  122.4 3.2 %collective-permute-start.28 = (bf16[64,384]{1,0:T(8,128)(2,1)S(1)}, bf16[64,384]{1,0:T(8,128)(2,1)S(1)}, u32[]{:S(2)}, u32[]{:S(2)}) collective-permute-start(bf16[64,384]{1,0:T(8,128)(2,1)S(1)} %get-tuple-element.68), channel_id=1, source_target_pairs={{2,4},{18,20},{3,5},{19,21},{34,36},{50,52},{35,37},{51,53},{66,68... | collective-permute-start | bytes 147464 | tf_op jit(solution)/shard_map/ppermute | solution.py:390
  123.0 2.6 %collective-permute-start.29 = (bf16[64,384]{1,0:T(8,128)(2,1)S(1)}, bf16[64,384]{1,0:T(8,128)(2,1)S(1)}, u32[]{:S(2)}, u32[]{:S(2)}) collective-permute-start(bf16[64,384]{1,0:T(8,128)(2,1)S(1)} %get-tuple-element.68), channel_id=1, source_target_pairs={{2,20},{18,4},{3,21},{19,5},{34,52},{50,36},{35,53},{51,37},{66,84... | collective-permute-start | bytes 147464 | tf_op jit(solution)/shard_map/ppermute | solution.py:391
  125.7 4.4 %collective-permute-start.33 = (bf16[64,384]{1,0:T(8,128)(2,1)S(1)}, bf16[64,384]{1,0:T(8,128)(2,1)S(1)}, u32[]{:S(2)}, u32[]{:S(2)}) collective-permute-start(bf16[64,384]{1,0:T(8,128)(2,1)S(1)} %get-tuple-element.71), channel_id=1, source_target_pairs={{4,134},{20,150},{5,135},{21,151},{36,166},{52,182},{37,167},{53,1... | collective-permute-start | bytes 147464 | tf_op jit(solution)/shard_map/ppermute | solution.py:389
  126.3 5.7 %collective-permute-start.31 = (bf16[64,384]{1,0:T(8,128)(2,1)S(1)}, bf16[64,384]{1,0:T(8,128)(2,1)S(1)}, u32[]{:S(2)}, u32[]{:S(2)}) collective-permute-start(bf16[64,384]{1,0:T(8,128)(2,1)S(1)} %get-tuple-element.71), channel_id=1, source_target_pairs={{4,6},{20,22},{5,7},{21,23},{36,38},{52,54},{37,39},{53,55},{68,70... | collective-permute-start | bytes 147464 | tf_op jit(solution)/shard_map/ppermute | solution.py:390
  127.0 5.0 %collective-permute-start.32 = (bf16[64,384]{1,0:T(8,128)(2,1)S(1)}, bf16[64,384]{1,0:T(8,128)(2,1)S(1)}, u32[]{:S(2)}, u32[]{:S(2)}) collective-permute-start(bf16[64,384]{1,0:T(8,128)(2,1)S(1)} %get-tuple-element.71), channel_id=1, source_target_pairs={{4,22},{20,6},{5,23},{21,7},{36,54},{52,38},{37,55},{53,39},{68,86... | collective-permute-start | bytes 147464 | tf_op jit(solution)/shard_map/ppermute | solution.py:391
  138.5 28.2 %all-to-all-start.1 = ((bf16[16,2,768]{2,1,0:T(2,128)(2,1)}), bf16[16,2,768]{2,1,0:T(2,128)(2,1)S(1)}, u32[]{:S(2)}, u32[]{:S(2)}) async-start(bf16[16,2,768]{2,1,0:T(2,128)(2,1)} %bitcast.18), calls=%async_computation.1 | async-start | bytes 98304 | tf_op jit(solution)/shard_map/all_to_all | solution.py:398
  (13 other events, 162.0 us)

commit v11 on v9

--- a/solution.py
+++ b/solution.py
@@ -146,16 +146,16 @@
     heads = range(PART // HDIM)
     cols = [slice(h * HDIM, (h + 1) * HDIM) for h in heads]
     vcols = [slice(PART + h * HDIM, PART + (h + 1) * HDIM) for h in heads]
-    scale = 1.0 / math.sqrt(HDIM)
+    scale = math.log2(math.e) / math.sqrt(HDIM)
     query = [turned(projected[:, cols[h]]) for h in heads]
     key = [turned(projected[:, vcols[h]]) for h in heads]
     value = [projected[:, 2 * PART + h * HDIM : 2 * PART + (h + 1) * HDIM] for h in heads]
     scores = [nt_dot(query[h], kv_ref[:, cols[h]]) for h in heads]
     other_scores = [nt_dot(query[h], other_ref[:, cols[h]]) for h in heads]
     own_scores = [nt_dot(query[h], key[h]) for h in heads]
-    weights = [jnp.where(stale_mask, 0.0, jnp.exp(scores[h] * scale)) for h in heads]
-    others = [jnp.exp(other_scores[h] * scale) for h in heads]
-    own = [jnp.where(own_mask, jnp.exp(own_scores[h] * scale), 0.0) for h in heads]
+    weights = [jnp.where(stale_mask, 0.0, jnp.exp2(scores[h] * scale)) for h in heads]
+    others = [jnp.exp2(other_scores[h] * scale) for h in heads]
+    own = [jnp.where(own_mask, jnp.exp2(own_scores[h] * scale), 0.0) for h in heads]
     total = [
         jnp.sum(weights[h] + others[h], axis=-1, keepdims=True) + jnp.sum(own[h], axis=-1, keepdims=True)
         for h in heads

time: 169 us -> 169 us (level)
  no operation moved by 1% of the time
where the time goes in v11:
time: 169 us; the launch traced here: 167 us
  starting transfers between devices  96 us (57%)
  blocking collectives  34.7 us (21%)
  waiting for transfers between devices  17.5 us (10%)
  local copies, waits for them, and re-layouts  9.4 us (6%)
  Pallas kernels  6.77 us (4%)
  between operations  2.03 us (1%)
    all_to_all x1, starting transfers between devices, body(): lax.all_to_all(finals, ('section', 'cfg'), split_axis=0, concat_axis=0, t...  20.6 us
    all_gather x7, blocking collectives, body(): far = lax.all_gather(far, 'core', axis=0, tiled=False)  13.8 us
    ppermute x7, starting transfers between devices, body(): far = lax.ppermute(state, AXES, onward(tick, 1, 0))  12.5 us
    ppermute x7, starting transfers between devices, body(): cross = lax.ppermute(state, AXES, onward(tick, 0, 1))  10.6 us
    all_to_all x1, starting transfers between devices, body(): lax.all_to_all(outgoing, ('xl', 'yh', 'core'), split_axis=0, concat_axis=...  10.2 us
    all_gather x1, blocking collectives, body(): x = lax.all_gather(entering, ('xl', 'core'), axis=0, tiled=True)  8.52 us
    ppermute x2, starting transfers between devices, body(): up2, down2 = (lax.ppermute(up1, AXES, UP), lax.ppermute(down1, AXES, DOWN))  7.02 us
    ppermute x2, starting transfers between devices, body(): up3, down3 = (lax.ppermute(up2, AXES, UP), lax.ppermute(down2, AXES, DOWN))  6.76 us
  transfers between devices with their start and end apart: 36, of which 8 were waited for; matrix products, arithmetic and copies ran while one was open for 2% of the time, Pallas kernels for 3%

profile of v11, /device:TPU:1, one launch (start us, length us, event | category | flops | bytes accessed | tf_op | source)
XLA Modules:
  0.0 167.4 jit_solution(9375473652911694870)
XLA Ops:
  2.6 10.2 %all-to-all-start = ((bf16[16,16,768]{2,1,0:T(8,128)(2,1)}), bf16[16,16,768]{2,1,0:T(8,128)(2,1)S(1)}, u32[]{:S(2)}, u32[]{:S(2)}) async-start(bf16[16,16,768]{2,1,0:T(8,128)(2,1)} %stale_kernel.1), calls=%async_computation | async-start | bytes 786432 | tf_op jit(solution)/shard_map/all_to_all | solution.py:351
  13.9 3.7 %collective-permute-start = (bf16[144,768]{1,0:T(8,128)(2,1)S(1)}, bf16[144,768]{1,0:T(8,128)(2,1)S(1)}, u32[]{:S(2)}, u32[]{:S(2)}) collective-permute-start(bf16[144,768]{1,0:T(8,128)(2,1)S(1)} %get-tuple-element.40), channel_id=1, source_target_pairs={{0,0},{2,2},{4,4},{6,6},{8,8},{10,10},{12,12},{14,14},{16,256},{18... | collective-permute-start | bytes 663560 | tf_op jit(solution)/shard_map/ppermute | solution.py:346
  17.5 1.9 %collective-permute-start.1 = (bf16[144,768]{1,0:T(8,128)(2,1)S(1)}, bf16[144,768]{1,0:T(8,128)(2,1)S(1)}, u32[]{:S(2)}, u32[]{:S(2)}) collective-permute-start(bf16[144,768]{1,0:T(8,128)(2,1)S(1)} %get-tuple-element.40), channel_id=1, source_target_pairs={{0,256},{2,258},{4,260},{6,262},{8,264},{10,266},{12,268},{14,270}... | collective-permute-start | bytes 663560 | tf_op jit(solution)/shard_map/ppermute | solution.py:346
  20.8 1.8 %collective-permute-done.first_ref = bf16[144,768]{1,0:T(8,128)(2,1)S(1)} collective-permute-done((bf16[144,768]{1,0:T(8,128)(2,1)S(1)}, bf16[144,768]{1,0:T(8,128)(2,1)S(1)}, u32[]{:S(2)}, u32[]{:S(2)}) %collective-permute-start) | collective-permute-done | bytes 221216 | tf_op jit(solution)/shard_map/ppermute | solution.py:346
  22.6 2.8 %collective-permute-done.1.second_ref = bf16[144,768]{1,0:T(8,128)(2,1)S(1)} collective-permute-done((bf16[144,768]{1,0:T(8,128)(2,1)S(1)}, bf16[144,768]{1,0:T(8,128)(2,1)S(1)}, u32[]{:S(2)}, u32[]{:S(2)}) %collective-permute-start.1) | collective-permute-done | bytes 221216 | tf_op jit(solution)/shard_map/ppermute | solution.py:346
  25.5 2.3 %collective-permute-start.5 = (bf16[288,768]{1,0:T(8,128)(2,1)S(1)}, bf16[288,768]{1,0:T(8,128)(2,1)S(1)}, u32[]{:S(2)}, u32[]{:S(2)}) collective-permute-start(bf16[288,768]{1,0:T(8,128)(2,1)S(1)} %join_kernel.1.refs_0_), channel_id=1, source_target_pairs={{0,97},{2,99},{4,101},{6,103},{8,105},{10,107},{12,109},{14,111},{... | collective-permute-start | bytes 1327112 | tf_op jit(solution)/shard_map/ppermute | solution.py:354
  27.8 4.2 %collective-permute-start.4 = (bf16[288,768]{1,0:T(8,128)(2,1)S(1)}, bf16[288,768]{1,0:T(8,128)(2,1)S(1)}, u32[]{:S(2)}, u32[]{:S(2)}) collective-permute-start(bf16[288,768]{1,0:T(8,128)(2,1)S(1)} %join_kernel.1.refs_0_), channel_id=1, source_target_pairs={{0,1},{2,3},{4,5},{6,7},{8,9},{10,11},{12,13},{14,15},{16,113},{18... | collective-permute-start | bytes 1327112 | tf_op jit(solution)/shard_map/ppermute | solution.py:354
  33.6 2.2 %collective-permute-done.5.refs_2_ = bf16[288,768]{1,0:T(8,128)(2,1)S(1)} collective-permute-done((bf16[288,768]{1,0:T(8,128)(2,1)S(1)}, bf16[288,768]{1,0:T(8,128)(2,1)S(1)}, u32[]{:S(2)}, u32[]{:S(2)}) %collective-permute-start.5) | collective-permute-done | bytes 442400 | tf_op jit(solution)/shard_map/ppermute | solution.py:354
  35.8 1.9 %collective-permute-start.7 = (bf16[288,768]{1,0:T(8,128)(2,1)S(1)}, bf16[288,768]{1,0:T(8,128)(2,1)}, u32[]{:S(2)}, u32[]{:S(2)}) collective-permute-start(bf16[288,768]{1,0:T(8,128)(2,1)S(1)} %collective-permute-done.5.refs_2_), channel_id=1, source_target_pairs={{0,97},{2,99},{4,101},{6,103},{8,105},{10,107},{12,109},{14,111},{... | collective-permute-start | bytes 1327112 | tf_op jit(solution)/shard_map/ppermute | solution.py:358
  37.7 4.3 %collective-permute-done.4.refs_1_ = bf16[288,768]{1,0:T(8,128)(2,1)S(1)} collective-permute-done((bf16[288,768]{1,0:T(8,128)(2,1)S(1)}, bf16[288,768]{1,0:T(8,128)(2,1)S(1)}, u32[]{:S(2)}, u32[]{:S(2)}) %collective-permute-start.4) | collective-permute-done | bytes 442400 | tf_op jit(solution)/shard_map/ppermute | solution.py:354
  41.9 5.1 %collective-permute-start.6 = (bf16[288,768]{1,0:T(8,128)(2,1)S(1)}, bf16[288,768]{1,0:T(8,128)(2,1)}, u32[]{:S(2)}, u32[]{:S(2)}) collective-permute-start(bf16[288,768]{1,0:T(8,128)(2,1)S(1)} %collective-permute-done.4.refs_1_), channel_id=1, source_target_pairs={{0,1},{2,3},{4,5},{6,7},{8,9},{10,11},{12,13},{14,15},{16,113},{18... | collective-permute-start | bytes 1327112 | tf_op jit(solution)/shard_map/ppermute | solution.py:358
  48.1 8.5 %all_gather.57 = bf16[64,1536]{1,0:T(8,128)(2,1)} all-gather(bf16[16,1536]{1,0:T(8,128)(2,1)S(1)} %bitcast.66), channel_id=1, replica_groups=mesh['xh'=2,'xl'=2,'yh'=4,'core'=2,'section'=8,'cfg'=2] {'xl','core'}, dimensions={0}, use_global_device_ids=true | all-gather | bytes 245760 | tf_op jit(solution)/shard_map/all_gather | solution.py:357
  56.6 2.3 %collective-permute-start.9 = (bf16[288,768]{1,0:T(8,128)(2,1)}, bf16[288,768]{1,0:T(8,128)(2,1)S(1)}, u32[]{:S(2)}, u32[]{:S(2)}) collective-permute-start(bf16[288,768]{1,0:T(8,128)(2,1)} %collective-permute-done.7.refs_4_), channel_id=1, source_target_pairs={{0,97},{2,99},{4,101},{6,103},{8,105},{10,107},{12,109},{14,111},{... | collective-permute-start | bytes 1327112 | tf_op jit(solution)/shard_map/ppermute | solution.py:360
  59.0 4.4 %collective-permute-start.8 = (bf16[288,768]{1,0:T(8,128)(2,1)}, bf16[288,768]{1,0:T(8,128)(2,1)S(1)}, u32[]{:S(2)}, u32[]{:S(2)}) collective-permute-start(bf16[288,768]{1,0:T(8,128)(2,1)} %collective-permute-done.6.refs_3_), channel_id=1, source_target_pairs={{0,1},{2,3},{4,5},{6,7},{8,9},{10,11},{12,13},{14,15},{16,113},{18... | collective-permute-start | bytes 1327112 | tf_op jit(solution)/shard_map/ppermute | solution.py:360
  63.6 1.9 %collective-permute-start.12 = (bf16[256,768]{1,0:T(8,128)(2,1)S(1)}, bf16[256,768]{1,0:T(8,128)(2,1)S(1)}, u32[]{:S(2)}, u32[]{:S(2)}) collective-permute-start(bf16[256,768]{1,0:T(8,128)(2,1)S(1)} %bitcast.41), channel_id=1, source_target_pairs={{0,256},{1,257},{2,258},{3,259},{4,260},{5,261},{6,262},{7,263},{8... | collective-permute-start | bytes 1179656 | tf_op jit(solution)/shard_map/ppermute | solution.py:356
  67.4 1.9 %collective-permute-start.11 = (bf16[144,768]{1,0:T(8,128)(2,1)S(1)}, bf16[144,768]{1,0:T(8,128)(2,1)S(1)}, u32[]{:S(2)}, u32[]{:S(2)}) collective-permute-start(bf16[144,768]{1,0:T(8,128)(2,1)S(1)} %slice.24), channel_id=1, source_target_pairs={{0,97},{2,99},{4,101},{6,103},{8,105},{10,107},{12,109},{14,111},{... | collective-permute-start | bytes 663560 | tf_op jit(solution)/shard_map/ppermute | solution.py:362
  69.3 4.3 %collective-permute-done.8.refs_0_.refs_5_ = bf16[288,768]{1,0:T(8,128)(2,1)S(1)} collective-permute-done((bf16[288,768]{1,0:T(8,128)(2,1)}, bf16[288,768]{1,0:T(8,128)(2,1)S(1)}, u32[]{:S(2)}, u32[]{:S(2)}) %collective-permute-start.8) | collective-permute-done | bytes 442400 | tf_op jit(solution)/shard_map/ppermute | solution.py:360
  73.6 5.2 %collective-permute-start.10 = (bf16[144,768]{1,0:T(8,128)(2,1)S(1)}, bf16[144,768]{1,0:T(8,128)(2,1)S(1)}, u32[]{:S(2)}, u32[]{:S(2)}) collective-permute-start(bf16[144,768]{1,0:T(8,128)(2,1)S(1)} %slice.23), channel_id=1, source_target_pairs={{0,1},{2,3},{4,5},{6,7},{8,9},{10,11},{12,13},{14,15},{16,113},{18... | collective-permute-start | bytes 663560 | tf_op jit(solution)/shard_map/ppermute | solution.py:361
  79.9 2.1 %place_first.1.refs_4_ = bf16[1152,1536]{1,0:T(8,128)(2,1)S(1)} custom-call(bf16[288,768]{1,0:T(8,128)(2,1)S(1)} %join_kernel.1.refs_0_, bf16[288,768]{1,0:T(8,128)(2,1)S(1)} %copy-done.4, bf16[288,768]{1,0:T(8,128)(2,1)S(1)} %collective-permute-done.5.refs_2_, bf16[288,768]{1,0:T(8,128)(2,1)} %collective-permute-done.6.refs_3_, ...), custom_call_target="tpu_custom_call" | custom-call | tf_op jit(solution)/shard_map/place_first/pallas_call | solution.py:290
  89.1 5.9 %collective-permute-start.14 = (bf16[64,384]{1,0:T(8,128)(2,1)S(1)}, bf16[64,384]{1,0:T(8,128)(2,1)S(1)}, u32[]{:S(2)}, u32[]{:S(2)}) collective-permute-start(bf16[64,384]{1,0:T(8,128)(2,1)S(1)} %get-tuple-element.49), channel_id=1, source_target_pairs={{0,18},{16,2},{1,19},{17,3},{32,50},{48,34},{33,51},{49,35},{64,82... | collective-permute-start | bytes 147464 | tf_op jit(solution)/shard_map/ppermute | solution.py:401
  95.1 2.0 %all-gather = bf16[128,384]{1,0:T(8,128)(2,1)S(1)} all-gather(bf16[64,384]{1,0:T(8,128)(2,1)S(1)} %collective-permute-done.15), channel_id=2, replica_groups=mesh['xh'=2,'xl'=2,'yh'=4,'core'=2,'section'=8,'cfg'=2] {'core'}, dimensions={0}, use_global_device_ids=true | all-gather | bytes 147456 | tf_op jit(solution)/shard_map/all_gather | solution.py:402
  99.2 1.9 %all-gather.1 = bf16[128,384]{1,0:T(8,128)(2,1)S(1)} all-gather(bf16[64,384]{1,0:T(8,128)(2,1)S(1)} %collective-permute-done.18), channel_id=3, replica_groups=mesh['xh'=2,'xl'=2,'yh'=4,'core'=2,'section'=8,'cfg'=2] {'core'}, dimensions={0}, use_global_device_ids=true | all-gather | bytes 147456 | tf_op jit(solution)/shard_map/all_gather | solution.py:402
  103.1 2.1 %all-gather.2 = bf16[128,384]{1,0:T(8,128)(2,1)S(1)} all-gather(bf16[64,384]{1,0:T(8,128)(2,1)S(1)} %collective-permute-done.21), channel_id=4, replica_groups=mesh['xh'=2,'xl'=2,'yh'=4,'core'=2,'section'=8,'cfg'=2] {'core'}, dimensions={0}, use_global_device_ids=true | all-gather | bytes 147456 | tf_op jit(solution)/shard_map/all_gather | solution.py:402
  107.2 1.9 %all-gather.3 = bf16[128,384]{1,0:T(8,128)(2,1)S(1)} all-gather(bf16[64,384]{1,0:T(8,128)(2,1)S(1)} %collective-permute-done.24), channel_id=5, replica_groups=mesh['xh'=2,'xl'=2,'yh'=4,'core'=2,'section'=8,'cfg'=2] {'core'}, dimensions={0}, use_global_device_ids=true | all-gather | bytes 147456 | tf_op jit(solution)/shard_map/all_gather | solution.py:402
  109.1 7.9 %collective-permute-start.27 = (bf16[64,384]{1,0:T(8,128)(2,1)S(1)}, bf16[64,384]{1,0:T(8,128)(2,1)S(1)}, u32[]{:S(2)}, u32[]{:S(2)}) collective-permute-start(bf16[64,384]{1,0:T(8,128)(2,1)S(1)} %get-tuple-element.66), channel_id=1, source_target_pairs={{0,130},{16,146},{1,131},{17,147},{32,162},{48,178},{33,163},{49,1... | collective-permute-start | bytes 147464 | tf_op jit(solution)/shard_map/ppermute | solution.py:399
  119.7 2.2 %all-gather.4 = bf16[128,384]{1,0:T(8,128)(2,1)S(1)} all-gather(bf16[64,384]{1,0:T(8,128)(2,1)S(1)} %collective-permute-done.27), channel_id=6, replica_groups=mesh['xh'=2,'xl'=2,'yh'=4,'core'=2,'section'=8,'cfg'=2] {'core'}, dimensions={0}, use_global_device_ids=true | all-gather | bytes 147456 | tf_op jit(solution)/shard_map/all_gather | solution.py:402
  123.9 1.9 %all-gather.5 = bf16[128,384]{1,0:T(8,128)(2,1)S(1)} all-gather(bf16[64,384]{1,0:T(8,128)(2,1)S(1)} %collective-permute-done.30), channel_id=7, replica_groups=mesh['xh'=2,'xl'=2,'yh'=4,'core'=2,'section'=8,'cfg'=2] {'core'}, dimensions={0}, use_global_device_ids=true | all-gather | bytes 147456 | tf_op jit(solution)/shard_map/all_gather | solution.py:402
  127.8 2.0 %copy-done.2 = bf16[1536,1152]{1,0:T(8,128)(2,1)S(1)} copy-done((bf16[1536,1152]{1,0:T(8,128)(2,1)S(1)}, bf16[1536,1152]{1,0:T(8,128)(2,1)}, u32[]{:S(2)}) %copy-start.2) | copy-done | bytes 3538968
  130.3 1.9 %all-gather.6 = bf16[128,384]{1,0:T(8,128)(2,1)S(1)} all-gather(bf16[64,384]{1,0:T(8,128)(2,1)S(1)} %collective-permute-done.33), channel_id=8, replica_groups=mesh['xh'=2,'xl'=2,'yh'=4,'core'=2,'section'=8,'cfg'=2] {'core'}, dimensions={0}, use_global_device_ids=true | all-gather | bytes 147456 | tf_op jit(solution)/shard_map/all_gather | solution.py:402
  132.2 5.8 %all-gather.7 = bf16[256,384]{1,0:T(8,128)(2,1)S(1)} all-gather(bf16[64,384]{1,0:T(8,128)(2,1)S(1)} %get-tuple-element.74), channel_id=9, replica_groups=mesh['xh'=2,'xl'=2,'yh'=4,'core'=2,'section'=8,'cfg'=2] {'xl','core'}, dimensions={0}, use_global_device_ids=true | all-gather | bytes 245760 | tf_op jit(solution)/shard_map/all_gather | solution.py:404
  138.7 20.6 %all-to-all-start.1 = ((bf16[16,2,768]{2,1,0:T(2,128)(2,1)}), bf16[16,2,768]{2,1,0:T(2,128)(2,1)S(1)}, u32[]{:S(2)}, u32[]{:S(2)}) async-start(bf16[16,2,768]{2,1,0:T(2,128)(2,1)} %bitcast.18), calls=%async_computation.1 | async-start | bytes 98304 | tf_op jit(solution)/shard_map/all_to_all | solution.py:408
  159.3 6.6 %all-gather.8 = bf16[256,768]{1,0:T(8,128)(2,1)S(1)} all-gather(bf16[64,768]{1,0:T(8,128)(2,1)S(1)} %get-tuple-element.75), channel_id=10, replica_groups=mesh['xh'=2,'xl'=2,'yh'=4,'core'=2,'section'=8,'cfg'=2] {'xl','core'}, dimensions={0}, use_global_device_ids=true | all-gather | bytes 491520 | tf_op jit(solution)/shard_map/all_gather | solution.py:409
  (111 shorter events, 31.8 us)
Async XLA Ops:
  2.6 39.4 %all-to-all-start = ((bf16[16,16,768]{2,1,0:T(8,128)(2,1)}), bf16[16,16,768]{2,1,0:T(8,128)(2,1)S(1)}, u32[]{:S(2)}, u32[]{:S(2)}) async-start(bf16[16,16,768]{2,1,0:T(8,128)(2,1)} %stale_kernel.1), calls=%async_computation | async-start | bytes 786432 | tf_op jit(solution)/shard_map/all_to_all | solution.py:351
  13.9 8.8 %collective-permute-start = (bf16[144,768]{1,0:T(8,128)(2,1)S(1)}, bf16[144,768]{1,0:T(8,128)(2,1)S(1)}, u32[]{:S(2)}, u32[]{:S(2)}) collective-permute-start(bf16[144,768]{1,0:T(8,128)(2,1)S(1)} %get-tuple-element.40), channel_id=1, source_target_pairs={{0,0},{2,2},{4,4},{6,6},{8,8},{10,10},{12,12},{14,14},{16,256},{18... | collective-permute-start | bytes 663560 | tf_op jit(solution)/shard_map/ppermute | solution.py:346
  17.5 7.9 %collective-permute-start.1 = (bf16[144,768]{1,0:T(8,128)(2,1)S(1)}, bf16[144,768]{1,0:T(8,128)(2,1)S(1)}, u32[]{:S(2)}, u32[]{:S(2)}) collective-permute-start(bf16[144,768]{1,0:T(8,128)(2,1)S(1)} %get-tuple-element.40), channel_id=1, source_target_pairs={{0,256},{2,258},{4,260},{6,262},{8,264},{10,266},{12,268},{14,270}... | collective-permute-start | bytes 663560 | tf_op jit(solution)/shard_map/ppermute | solution.py:346
  25.5 10.3 %collective-permute-start.5 = (bf16[288,768]{1,0:T(8,128)(2,1)S(1)}, bf16[288,768]{1,0:T(8,128)(2,1)S(1)}, u32[]{:S(2)}, u32[]{:S(2)}) collective-permute-start(bf16[288,768]{1,0:T(8,128)(2,1)S(1)} %join_kernel.1.refs_0_), channel_id=1, source_target_pairs={{0,97},{2,99},{4,101},{6,103},{8,105},{10,107},{12,109},{14,111},{... | collective-permute-start | bytes 1327112 | tf_op jit(solution)/shard_map/ppermute | solution.py:354
  27.8 14.1 %collective-permute-start.4 = (bf16[288,768]{1,0:T(8,128)(2,1)S(1)}, bf16[288,768]{1,0:T(8,128)(2,1)S(1)}, u32[]{:S(2)}, u32[]{:S(2)}) collective-permute-start(bf16[288,768]{1,0:T(8,128)(2,1)S(1)} %join_kernel.1.refs_0_), channel_id=1, source_target_pairs={{0,1},{2,3},{4,5},{6,7},{8,9},{10,11},{12,13},{14,15},{16,113},{18... | collective-permute-start | bytes 1327112 | tf_op jit(solution)/shard_map/ppermute | solution.py:354
  35.8 20.8 %collective-permute-start.7 = (bf16[288,768]{1,0:T(8,128)(2,1)S(1)}, bf16[288,768]{1,0:T(8,128)(2,1)}, u32[]{:S(2)}, u32[]{:S(2)}) collective-permute-start(bf16[288,768]{1,0:T(8,128)(2,1)S(1)} %collective-permute-done.5.refs_2_), channel_id=1, source_target_pairs={{0,97},{2,99},{4,101},{6,103},{8,105},{10,107},{12,109},{14,111},{... | collective-permute-start | bytes 1327112 | tf_op jit(solution)/shard_map/ppermute | solution.py:358
  41.9 17.0 %collective-permute-start.6 = (bf16[288,768]{1,0:T(8,128)(2,1)S(1)}, bf16[288,768]{1,0:T(8,128)(2,1)}, u32[]{:S(2)}, u32[]{:S(2)}) collective-permute-start(bf16[288,768]{1,0:T(8,128)(2,1)S(1)} %collective-permute-done.4.refs_1_), channel_id=1, source_target_pairs={{0,1},{2,3},{4,5},{6,7},{8,9},{10,11},{12,13},{14,15},{16,113},{18... | collective-permute-start | bytes 1327112 | tf_op jit(solution)/shard_map/ppermute | solution.py:358
  56.6 10.7 %collective-permute-start.9 = (bf16[288,768]{1,0:T(8,128)(2,1)}, bf16[288,768]{1,0:T(8,128)(2,1)S(1)}, u32[]{:S(2)}, u32[]{:S(2)}) collective-permute-start(bf16[288,768]{1,0:T(8,128)(2,1)} %collective-permute-done.7.refs_4_), channel_id=1, source_target_pairs={{0,97},{2,99},{4,101},{6,103},{8,105},{10,107},{12,109},{14,111},{... | collective-permute-start | bytes 1327112 | tf_op jit(solution)/shard_map/ppermute | solution.py:360
  59.0 14.6 %collective-permute-start.8 = (bf16[288,768]{1,0:T(8,128)(2,1)}, bf16[288,768]{1,0:T(8,128)(2,1)S(1)}, u32[]{:S(2)}, u32[]{:S(2)}) collective-permute-start(bf16[288,768]{1,0:T(8,128)(2,1)} %collective-permute-done.6.refs_3_), channel_id=1, source_target_pairs={{0,1},{2,3},{4,5},{6,7},{8,9},{10,11},{12,13},{14,15},{16,113},{18... | collective-permute-start | bytes 1327112 | tf_op jit(solution)/shard_map/ppermute | solution.py:360
  63.6 21.5 %collective-permute-start.12 = (bf16[256,768]{1,0:T(8,128)(2,1)S(1)}, bf16[256,768]{1,0:T(8,128)(2,1)S(1)}, u32[]{:S(2)}, u32[]{:S(2)}) collective-permute-start(bf16[256,768]{1,0:T(8,128)(2,1)S(1)} %bitcast.41), channel_id=1, source_target_pairs={{0,256},{1,257},{2,258},{3,259},{4,260},{5,261},{6,262},{7,263},{8... | collective-permute-start | bytes 1179656 | tf_op jit(solution)/shard_map/ppermute | solution.py:356
  67.4 14.6 %collective-permute-start.11 = (bf16[144,768]{1,0:T(8,128)(2,1)S(1)}, bf16[144,768]{1,0:T(8,128)(2,1)S(1)}, u32[]{:S(2)}, u32[]{:S(2)}) collective-permute-start(bf16[144,768]{1,0:T(8,128)(2,1)S(1)} %slice.24), channel_id=1, source_target_pairs={{0,97},{2,99},{4,101},{6,103},{8,105},{10,107},{12,109},{14,111},{... | collective-permute-start | bytes 663560 | tf_op jit(solution)/shard_map/ppermute | solution.py:362
  73.6 9.7 %collective-permute-start.10 = (bf16[144,768]{1,0:T(8,128)(2,1)S(1)}, bf16[144,768]{1,0:T(8,128)(2,1)S(1)}, u32[]{:S(2)}, u32[]{:S(2)}) collective-permute-start(bf16[144,768]{1,0:T(8,128)(2,1)S(1)} %slice.23), channel_id=1, source_target_pairs={{0,1},{2,3},{4,5},{6,7},{8,9},{10,11},{12,13},{14,15},{16,113},{18... | collective-permute-start | bytes 663560 | tf_op jit(solution)/shard_map/ppermute | solution.py:361
  86.5 8.6 %collective-permute-start.15 = (bf16[64,384]{1,0:T(8,128)(2,1)S(1)}, bf16[64,384]{1,0:T(8,128)(2,1)S(1)}, u32[]{:S(2)}, u32[]{:S(2)}) collective-permute-start(bf16[64,384]{1,0:T(8,128)(2,1)S(1)} %get-tuple-element.49), channel_id=1, source_target_pairs={{0,130},{16,146},{1,131},{17,147},{32,162},{48,178},{33,163},{49,1... | collective-permute-start | bytes 147464 | tf_op jit(solution)/shard_map/ppermute | solution.py:399
  87.8 9.3 %collective-permute-start.13 = (bf16[64,384]{1,0:T(8,128)(2,1)S(1)}, bf16[64,384]{1,0:T(8,128)(2,1)S(1)}, u32[]{:S(2)}, u32[]{:S(2)}) collective-permute-start(bf16[64,384]{1,0:T(8,128)(2,1)S(1)} %get-tuple-element.49), channel_id=1, source_target_pairs={{0,2},{16,18},{1,3},{17,19},{32,34},{48,50},{33,35},{49,51},{64,66... | collective-permute-start | bytes 147464 | tf_op jit(solution)/shard_map/ppermute | solution.py:400
  89.1 8.0 %collective-permute-start.14 = (bf16[64,384]{1,0:T(8,128)(2,1)S(1)}, bf16[64,384]{1,0:T(8,128)(2,1)S(1)}, u32[]{:S(2)}, u32[]{:S(2)}) collective-permute-start(bf16[64,384]{1,0:T(8,128)(2,1)S(1)} %get-tuple-element.49), channel_id=1, source_target_pairs={{0,18},{16,2},{1,19},{17,3},{32,50},{48,34},{33,51},{49,35},{64,82... | collective-permute-start | bytes 147464 | tf_op jit(solution)/shard_map/ppermute | solution.py:401
  97.8 3.2 %collective-permute-start.16 = (bf16[64,384]{1,0:T(8,128)(2,1)S(1)}, bf16[64,384]{1,0:T(8,128)(2,1)S(1)}, u32[]{:S(2)}, u32[]{:S(2)}) collective-permute-start(bf16[64,384]{1,0:T(8,128)(2,1)S(1)} %get-tuple-element.60), channel_id=1, source_target_pairs={{2,4},{18,20},{3,5},{19,21},{34,36},{50,52},{35,37},{51,53},{66,68... | collective-permute-start | bytes 147464 | tf_op jit(solution)/shard_map/ppermute | solution.py:400
  98.5 2.6 %collective-permute-start.17 = (bf16[64,384]{1,0:T(8,128)(2,1)S(1)}, bf16[64,384]{1,0:T(8,128)(2,1)S(1)}, u32[]{:S(2)}, u32[]{:S(2)}) collective-permute-start(bf16[64,384]{1,0:T(8,128)(2,1)S(1)} %get-tuple-element.60), channel_id=1, source_target_pairs={{2,20},{18,4},{3,21},{19,5},{34,52},{50,36},{35,53},{51,37},{66,84... | collective-permute-start | bytes 147464 | tf_op jit(solution)/shard_map/ppermute | solution.py:401
  101.1 2.0 %collective-permute-start.21 = (bf16[64,384]{1,0:T(8,128)(2,1)S(1)}, bf16[64,384]{1,0:T(8,128)(2,1)S(1)}, u32[]{:S(2)}, u32[]{:S(2)}) collective-permute-start(bf16[64,384]{1,0:T(8,128)(2,1)S(1)} %get-tuple-element.62), channel_id=1, source_target_pairs={{4,134},{20,150},{5,135},{21,151},{36,166},{52,182},{37,167},{53,1... | collective-permute-start | bytes 147464 | tf_op jit(solution)/shard_map/ppermute | solution.py:399
  101.8 3.4 %collective-permute-start.19 = (bf16[64,384]{1,0:T(8,128)(2,1)S(1)}, bf16[64,384]{1,0:T(8,128)(2,1)S(1)}, u32[]{:S(2)}, u32[]{:S(2)}) collective-permute-start(bf16[64,384]{1,0:T(8,128)(2,1)S(1)} %get-tuple-element.62), channel_id=1, source_target_pairs={{4,6},{20,22},{5,7},{21,23},{36,38},{52,54},{37,39},{53,55},{68,70... | collective-permute-start | bytes 147464 | tf_op jit(solution)/shard_map/ppermute | solution.py:400
  102.4 2.8 %collective-permute-start.20 = (bf16[64,384]{1,0:T(8,128)(2,1)S(1)}, bf16[64,384]{1,0:T(8,128)(2,1)S(1)}, u32[]{:S(2)}, u32[]{:S(2)}) collective-permute-start(bf16[64,384]{1,0:T(8,128)(2,1)S(1)} %get-tuple-element.62), channel_id=1, source_target_pairs={{4,22},{20,6},{5,23},{21,7},{36,54},{52,38},{37,55},{53,39},{68,86... | collective-permute-start | bytes 147464 | tf_op jit(solution)/shard_map/ppermute | solution.py:401
  105.9 3.2 %collective-permute-start.22 = (bf16[64,384]{1,0:T(8,128)(2,1)S(1)}, bf16[64,384]{1,0:T(8,128)(2,1)S(1)}, u32[]{:S(2)}, u32[]{:S(2)}) collective-permute-start(bf16[64,384]{1,0:T(8,128)(2,1)S(1)} %get-tuple-element.64), channel_id=1, source_target_pairs={{6,8},{22,24},{7,9},{23,25},{38,40},{54,56},{39,41},{55,57},{70,72... | collective-permute-start | bytes 147464 | tf_op jit(solution)/shard_map/ppermute | solution.py:400
  106.5 2.6 %collective-permute-start.23 = (bf16[64,384]{1,0:T(8,128)(2,1)S(1)}, bf16[64,384]{1,0:T(8,128)(2,1)S(1)}, u32[]{:S(2)}, u32[]{:S(2)}) collective-permute-start(bf16[64,384]{1,0:T(8,128)(2,1)S(1)} %get-tuple-element.64), channel_id=1, source_target_pairs={{6,24},{22,8},{7,25},{23,9},{38,56},{54,40},{39,57},{55,41},{70,88... | collective-permute-start | bytes 147464 | tf_op jit(solution)/shard_map/ppermute | solution.py:401
  109.1 10.5 %collective-permute-start.27 = (bf16[64,384]{1,0:T(8,128)(2,1)S(1)}, bf16[64,384]{1,0:T(8,128)(2,1)S(1)}, u32[]{:S(2)}, u32[]{:S(2)}) collective-permute-start(bf16[64,384]{1,0:T(8,128)(2,1)S(1)} %get-tuple-element.66), channel_id=1, source_target_pairs={{0,130},{16,146},{1,131},{17,147},{32,162},{48,178},{33,163},{49,1... | collective-permute-start | bytes 147464 | tf_op jit(solution)/shard_map/ppermute | solution.py:399
  117.0 4.8 %collective-permute-start.25 = (bf16[64,384]{1,0:T(8,128)(2,1)S(1)}, bf16[64,384]{1,0:T(8,128)(2,1)S(1)}, u32[]{:S(2)}, u32[]{:S(2)}) collective-permute-start(bf16[64,384]{1,0:T(8,128)(2,1)S(1)} %get-tuple-element.66), channel_id=1, source_target_pairs={{0,2},{16,18},{1,3},{17,19},{32,34},{48,50},{33,35},{49,51},{64,66... | collective-permute-start | bytes 147464 | tf_op jit(solution)/shard_map/ppermute | solution.py:400
  118.3 3.5 %collective-permute-start.26 = (bf16[64,384]{1,0:T(8,128)(2,1)S(1)}, bf16[64,384]{1,0:T(8,128)(2,1)S(1)}, u32[]{:S(2)}, u32[]{:S(2)}) collective-permute-start(bf16[64,384]{1,0:T(8,128)(2,1)S(1)} %get-tuple-element.66), channel_id=1, source_target_pairs={{0,18},{16,2},{1,19},{17,3},{32,50},{48,34},{33,51},{49,35},{64,82... | collective-permute-start | bytes 147464 | tf_op jit(solution)/shard_map/ppermute | solution.py:401
  121.9 2.0 %collective-permute-start.30 = (bf16[64,384]{1,0:T(8,128)(2,1)S(1)}, bf16[64,384]{1,0:T(8,128)(2,1)S(1)}, u32[]{:S(2)}, u32[]{:S(2)}) collective-permute-start(bf16[64,384]{1,0:T(8,128)(2,1)S(1)} %get-tuple-element.68), channel_id=1, source_target_pairs={{2,132},{18,148},{3,133},{19,149},{34,164},{50,180},{35,165},{51,1... | collective-permute-start | bytes 147464 | tf_op jit(solution)/shard_map/ppermute | solution.py:399
  122.5 3.2 %collective-permute-start.28 = (bf16[64,384]{1,0:T(8,128)(2,1)S(1)}, bf16[64,384]{1,0:T(8,128)(2,1)S(1)}, u32[]{:S(2)}, u32[]{:S(2)}) collective-permute-start(bf16[64,384]{1,0:T(8,128)(2,1)S(1)} %get-tuple-element.68), channel_id=1, source_target_pairs={{2,4},{18,20},{3,5},{19,21},{34,36},{50,52},{35,37},{51,53},{66,68... | collective-permute-start | bytes 147464 | tf_op jit(solution)/shard_map/ppermute | solution.py:400
  123.2 2.6 %collective-permute-start.29 = (bf16[64,384]{1,0:T(8,128)(2,1)S(1)}, bf16[64,384]{1,0:T(8,128)(2,1)S(1)}, u32[]{:S(2)}, u32[]{:S(2)}) collective-permute-start(bf16[64,384]{1,0:T(8,128)(2,1)S(1)} %get-tuple-element.68), channel_id=1, source_target_pairs={{2,20},{18,4},{3,21},{19,5},{34,52},{50,36},{35,53},{51,37},{66,84... | collective-permute-start | bytes 147464 | tf_op jit(solution)/shard_map/ppermute | solution.py:401
  125.8 4.4 %collective-permute-start.33 = (bf16[64,384]{1,0:T(8,128)(2,1)S(1)}, bf16[64,384]{1,0:T(8,128)(2,1)S(1)}, u32[]{:S(2)}, u32[]{:S(2)}) collective-permute-start(bf16[64,384]{1,0:T(8,128)(2,1)S(1)} %get-tuple-element.71), channel_id=1, source_target_pairs={{4,134},{20,150},{5,135},{21,151},{36,166},{52,182},{37,167},{53,1... | collective-permute-start | bytes 147464 | tf_op jit(solution)/shard_map/ppermute | solution.py:399
  126.5 5.7 %collective-permute-start.31 = (bf16[64,384]{1,0:T(8,128)(2,1)S(1)}, bf16[64,384]{1,0:T(8,128)(2,1)S(1)}, u32[]{:S(2)}, u32[]{:S(2)}) collective-permute-start(bf16[64,384]{1,0:T(8,128)(2,1)S(1)} %get-tuple-element.71), channel_id=1, source_target_pairs={{4,6},{20,22},{5,7},{21,23},{36,38},{52,54},{37,39},{53,55},{68,70... | collective-permute-start | bytes 147464 | tf_op jit(solution)/shard_map/ppermute | solution.py:400
  127.2 5.0 %collective-permute-start.32 = (bf16[64,384]{1,0:T(8,128)(2,1)S(1)}, bf16[64,384]{1,0:T(8,128)(2,1)S(1)}, u32[]{:S(2)}, u32[]{:S(2)}) collective-permute-start(bf16[64,384]{1,0:T(8,128)(2,1)S(1)} %get-tuple-element.71), channel_id=1, source_target_pairs={{4,22},{20,6},{5,23},{21,7},{36,54},{52,38},{37,55},{53,39},{68,86... | collective-permute-start | bytes 147464 | tf_op jit(solution)/shard_map/ppermute | solution.py:401
  138.7 28.2 %all-to-all-start.1 = ((bf16[16,2,768]{2,1,0:T(2,128)(2,1)}), bf16[16,2,768]{2,1,0:T(2,128)(2,1)S(1)}, u32[]{:S(2)}, u32[]{:S(2)}) async-start(bf16[16,2,768]{2,1,0:T(2,128)(2,1)} %bitcast.18), calls=%async_computation.1 | async-start | bytes 98304 | tf_op jit(solution)/shard_map/all_to_all | solution.py:408
  (13 other events, 162.3 us)
